TPU v7x, 512 devices: a whole 4x4x16 slice. The times are simulated.
512 devices in a mesh: blk: 8 (over z_lo), grp: 64 (over y, z_hi, x, core).
Axes of the slice: x: 4, y: 4, z: 16 (z_hi: 2, z_lo: 8; z = z_hi * 8 + z_lo), core: 2. Of those that a mesh axis runs over, the one named last changes fastest.
Arguments:
- img_feat: bfloat16 [8192, 1152], P('grp'), may hold values from -6 to 6
- txt_feat: bfloat16 [8192, 1152], P('grp'), may hold values from -6 to 6
- img_proj: bfloat16 [1152, 1152], P(None, 'grp'), may hold values from -5 to 5
- txt_proj: bfloat16 [1152, 1152], P(None, 'grp'), may hold values from -5 to 5
- logit_scale: float32 [1], replicated, may hold values from 5 to 15
- logit_bias: float32 [1], replicated, may hold values from -6 to -3
- loss_weight: float32 [1], replicated, may hold values from 15 to 60
Outputs:
- img_grad: float32 [8192, 1152], P('grp')
- txt_grad: float32 [8192, 1152], P('grp')
- img_proj_grad: float32 [1152, 1152], P(None, 'grp')
- txt_proj_grad: float32 [1152, 1152], P(None, 'grp')
All inputs are finite; a program needn't handle non-finite values.
Results may differ from a plain program's by a relative error of at most 0.014.
Values may be sent and summed in bfloat16 or wider, within the bound.
No kernel may reach another device: no remote copies, remote signals or barrier semaphores. Data moves between devices by JAX's collectives and lax.ppermute only.
A program may use at most 64 MiB of HBM per device.

v0:
```python
import jax
import jax.numpy as jnp
from jax import lax
from jax.sharding import PartitionSpec as P


def shifted(value, axis, steps):
    count = lax.axis_size(axis)
    pairs = [(source, (source + steps) % count) for source in range(count)]
    return lax.ppermute(value, axis, pairs)


def normalize(proj_out):
    inverse = lax.rsqrt(jnp.sum(proj_out * proj_out, axis=1, keepdims=True) + 1e-06)
    return (proj_out * inverse, inverse)


def pull_back(grad_unit, unit, inverse):
    inner = jnp.sum(unit * grad_unit, axis=1, keepdims=True)
    return ((grad_unit - unit * inner) * inverse).astype(jnp.bfloat16)


def contract_last(left, right):
    return lax.dot_general(
        left, right, (((1,), (1,)), ((), ())), preferred_element_type=jnp.float32
    )


def contract_first(left, right):
    return lax.dot_general(
        left, right, (((0,), (0,)), ((), ())), preferred_element_type=jnp.float32
    )


def body(img_feat, txt_feat, img_proj, txt_proj, logit_scale, logit_bias, loss_weight):
    scale = logit_scale[0]
    shift_by = logit_bias[0]
    weight = loss_weight[0]
    rows = img_feat.shape[0]
    n_grp = lax.axis_size("grp")
    n_blk = lax.axis_size("blk")
    blk_at = lax.axis_index("blk")
    grp_at = lax.axis_index("grp")
    sub_rows = rows // n_blk
    own_start = blk_at * sub_rows
    img_mine = lax.dynamic_slice_in_dim(img_feat, own_start, sub_rows, 0)
    txt_mine = lax.dynamic_slice_in_dim(txt_feat, own_start, sub_rows, 0)
    img_full, txt_full = (
        lax.all_gather(img_proj, "grp", axis=1, tiled=True),
        lax.all_gather(txt_proj, "grp", axis=1, tiled=True),
    )
    img_unit, img_inv = normalize(jnp.dot(img_mine, img_full, preferred_element_type=jnp.float32))
    txt_unit, txt_inv = normalize(jnp.dot(txt_mine, txt_full, preferred_element_type=jnp.float32))
    img_emb = img_unit.astype(jnp.bfloat16)
    txt_emb = txt_unit.astype(jnp.bfloat16)
    depth = img_emb.shape[1]
    local_ids = jnp.arange(sub_rows, dtype=jnp.int32)
    image_block, text_block = (
        lax.all_gather(img_emb, "grp", axis=0, tiled=True),
        lax.all_gather(txt_emb, "grp", axis=0, tiled=True),
    )
    block_ids = (
        jnp.arange(n_grp, dtype=jnp.int32)[:, None] * rows + own_start + local_ids[None, :]
    ).reshape(-1)
    start_txt, start_img = (txt_emb, img_emb)
    cur_rows = start_txt.shape[0]

    def weigh(logits, ids):
        sign = jnp.where(ids[:, None] == block_ids[None, :], jnp.float32(1.0), jnp.float32(-1.0))
        return (-weight * sign * jax.nn.sigmoid(-sign * logits)).astype(jnp.bfloat16)

    zero_rows = jnp.zeros((cur_rows, depth), jnp.float32)
    current = (start_txt, start_img)
    carried = (zero_rows, zero_rows)
    for step in range(n_blk):
        owner = (blk_at - step) % n_blk
        tiles_ids = grp_at * rows + owner * sub_rows + local_ids
        coef_text = weigh(scale * contract_last(current[0], image_block) + shift_by, tiles_ids)
        coef_image = weigh(scale * contract_last(current[1], text_block) + shift_by, tiles_ids)
        part_txt = jnp.dot(coef_text, image_block, preferred_element_type=jnp.float32)
        part_img = jnp.dot(coef_image, text_block, preferred_element_type=jnp.float32)
        carried = shifted((carried[0] + part_txt, carried[1] + part_img), "blk", 1)
        if step < n_blk - 1:
            current = shifted((current[0], current[1]), "blk", 1)
    d_txt, d_img = carried
    img_du = pull_back(scale * d_img, img_unit, img_inv)
    txt_du = pull_back(scale * d_txt, txt_unit, txt_inv)
    img_all, txt_all = (
        lax.all_gather(img_du, "blk", axis=0, tiled=True),
        lax.all_gather(txt_du, "blk", axis=0, tiled=True),
    )
    img_grad = contract_last(img_all, img_full)
    txt_grad = contract_last(txt_all, txt_full)
    slab_width = img_feat.shape[1] // n_blk
    slab_start = blk_at * slab_width
    img_part = contract_first(
        lax.dynamic_slice_in_dim(img_feat, slab_start, slab_width, 1), img_all
    )
    txt_part = contract_first(
        lax.dynamic_slice_in_dim(txt_feat, slab_start, slab_width, 1), txt_all
    )
    img_share, txt_share = (
        lax.psum_scatter(img_part, "grp", scatter_dimension=1, tiled=True),
        lax.psum_scatter(txt_part, "grp", scatter_dimension=1, tiled=True),
    )
    img_proj_grad, txt_proj_grad = (
        lax.all_gather(img_share, "blk", axis=0, tiled=True),
        lax.all_gather(txt_share, "blk", axis=0, tiled=True),
    )
    return (img_grad, txt_grad, img_proj_grad, txt_proj_grad)


def solution(mesh):
    return jax.shard_map(
        body,
        mesh=mesh,
        in_specs=(P("grp", None), P("grp", None), P(None, "grp"), P(None, "grp"), P(), P(), P()),
        out_specs=(P("grp", None), P("grp", None), P(None, "grp"), P(None, "grp")),
        check_vma=False,
    )
```

profile of v0, /device:TPU:1, one launch (start us, length us, event | category | flops | bytes accessed | tf_op | source)
XLA Modules:
  0.0 1236.7 jit_solution(16148694722705968315)
XLA Ops:
  8.7 135.4 %all-gather.13.cloned.1.call-done = bf16[64,18,1152]{2,1,0:T(8,128)(2,1)} async-done(((bf16[1,18,1152]{2,1,0:T(8,128)(2,1)}), bf16[64,18,1152]{2,1,0:T(8,128)(2,1)}) %all-gather.13.cloned.1.call-update) | async-done | bytes 2654224 | tf_op jit(solution)/shard_map/all_gather | solution.py:49
  149.8 113.6 %all-gather.15.cloned.1.call-done = bf16[64,18,1152]{2,1,0:T(8,128)(2,1)} async-done(((bf16[1,18,1152]{2,1,0:T(8,128)(2,1)}), bf16[64,18,1152]{2,1,0:T(8,128)(2,1)}) %all-gather.15.cloned.1.call-update) | async-done | bytes 2654224 | tf_op jit(solution)/shard_map/all_gather | solution.py:50
  263.4 5.4 reshape.79
  276.3 7.6 collective-permute-done.16
  287.9 7.4 collective-permute-done.18
  299.6 6.9 collective-permute-done.20
  310.9 7.1 collective-permute-done.22
  322.2 7.1 collective-permute-done.24
  335.5 5.4 collective-permute-done.26
  345.2 26.7 %all-gather.11.cloned.1.call-done = bf16[1024,1152]{1,0:T(8,128)(2,1)} async-done(((bf16[16,1152]{1,0:T(8,128)(2,1)}), bf16[1024,1152]{1,0:T(8,128)(2,1)}) %all-gather.11.cloned.1.call-update) | async-done | bytes 2359312 | tf_op jit(solution)/shard_map/all_gather | solution.py:59
  377.2 106.3 %all-gather.9.cloned.1.call-done = bf16[1024,1152]{1,0:T(8,128)(2,1)} async-done(((bf16[16,1152]{1,0:T(8,128)(2,1)}), bf16[1024,1152]{1,0:T(8,128)(2,1)}) %all-gather.9.cloned.1.call-update) | async-done | bytes 2359312 | tf_op jit(solution)/shard_map/all_gather | solution.py:60
  492.0 7.2 collective-permute-done
  507.6 6.8 collective-permute-done.2
  522.7 6.8 collective-permute-done.4
  537.9 6.8 collective-permute-done.6
  553.0 6.8 collective-permute-done.8
  569.1 5.8 collective-permute-done.10
  584.1 6.0 collective-permute-done.12
  595.7 41.5 %all_gather.29 = bf16[128,1152]{1,0:T(8,128)(2,1)S(1)} all-gather(bf16[16,1152]{1,0:T(8,128)(2,1)S(1)} %multiply_convert_fusion), channel_id=1, replica_groups=mesh['blk'=8,'grp'=64] {'blk'}, dimensions={0}, use_global_device_ids=true | all-gather | bytes 331776 | tf_op jit(solution)/shard_map/all_gather | solution.py:90
  637.5 40.5 %all_gather.27 = bf16[128,1152]{1,0:T(8,128)(2,1)S(1)} all-gather(bf16[16,1152]{1,0:T(8,128)(2,1)S(1)} %multiply_convert_fusion.1), channel_id=1, replica_groups=mesh['blk'=8,'grp'=64] {'blk'}, dimensions={0}, use_global_device_ids=true | all-gather | bytes 331776 | tf_op jit(solution)/shard_map/all_gather | solution.py:89
  679.7 318.6 %fusion.312 = (f32[144,24]{0,1:T(8,128)}, f32[144,24]{0,1:T(8,128)}) fusion(f32[144,1152]{0,1:T(8,128)S(1)} %fusion.158, f32[144,1152]{0,1:T(8,128)S(1)} %fusion.156), kind=kCustom, calls=%all-reduce-scatter.2 | all-reduce-scatter fusion | flops 442369 | bytes 1356800
  1014.7 15.8 %collective-permute-start.39 = (f32[144,24]{0,1:T(8,128)}, f32[144,24]{0,1:T(8,128)}, u32[]{:S(2)}, u32[]{:S(2)}) collective-permute-start(f32[144,24]{0,1:T(8,128)} %get-tuple-element.6), channel_id=1, source_target_pairs={{0,10},{1,11},{2,12},{3,13},{4,14},{5,15},{6,16},{7,17},{8,18},{9,... | collective-permute-start | bytes 41480
  1034.6 10.6 collective-permute-start.36
  1053.7 8.7 collective-permute-start.32
  1070.9 11.2 collective-permute-start.59
  1089.6 4.5 collective-permute-start.55
  1108.3 12.9 %concatenate = f32[144,402]{0,1:T(8,128)S(1)} concatenate(f32[144,18]{0,1:T(8,128)} %collective-permute-done.45, f32[144,24]{0,1:T(8,128)} %collective-permute-done.44, f32[144,24]{0,1:T(8,128)} %collective-permute-done.43, f32[144,24]{0,1:T(8,128)} %collective-permute-done.42, f32[144,24]{0,1:T(8,128)} %collective-permute-done.41, f32[144,24]{0,1:T(8,128)} %collective-permute-done.40, ...), dimensions={1} | concatenate | bytes 463104
  1121.2 3.9 collective-permute-start.50
  1127.5 5.3 collective-permute-start.48
  1139.6 6.9 concatenate.1
  1146.5 41.8 %all-gather.3 = f32[8,144,18]{1,2,0:T(8,128)S(1)} all-gather(f32[1,144,18]{1,2,0:T(8,128)S(1)} %dynamic-slice_bitcast_fusion), channel_id=1, replica_groups=mesh['blk'=8,'grp'=64] {'blk'}, dimensions={0}, use_global_device_ids=true | all-gather | bytes 93312 | tf_op jit(solution)/shard_map/all_gather | solution.py:108
  1189.2 40.2 %all-gather.2 = f32[8,144,18]{1,2,0:T(8,128)S(1)} all-gather(f32[1,144,18]{1,2,0:T(8,128)S(1)} %dynamic-slice_bitcast_fusion.1), channel_id=1, replica_groups=mesh['blk'=8,'grp'=64] {'blk'}, dimensions={0}, use_global_device_ids=true | all-gather | bytes 93312 | tf_op jit(solution)/shard_map/all_gather | solution.py:107
  (185 shorter events, 181.8 us)
Async XLA Ops:
  7.2 136.9 %all-gather.13.cloned.1.call-start = ((), (), s32[]{:S(2)}) async-start(), calls=%async_computation.2 | async-start | bytes 3594240 | tf_op jit(solution)/shard_map/all_gather | solution.py:49
  7.9 255.5 %all-gather.15.cloned.1.call-start = ((), (), s32[]{:S(2)}) async-start(), calls=%async_computation.3 | async-start | bytes 3594240 | tf_op jit(solution)/shard_map/all_gather | solution.py:50
  8.7 363.2 %all-gather.11.cloned.1.call-start = ((), (), s32[]{:S(2)}) async-start(), calls=%async_computation.1 | async-start | bytes 2396160 | tf_op jit(solution)/shard_map/all_gather | solution.py:59
  149.7 333.8 %all-gather.9.cloned.1.call-start = ((), (), s32[]{:S(2)}) async-start(), calls=%async_computation | async-start | bytes 2396160 | tf_op jit(solution)/shard_map/all_gather | solution.py:60
  340.9 239.4 %collective-permute-start.28 = (bf16[16,1152]{1,0:T(8,128)(2,1)}, bf16[16,1152]{1,0:T(8,128)(2,1)}, u32[]{:S(2)}, u32[]{:S(2)}) collective-permute-start(bf16[16,1152]{1,0:T(8,128)(2,1)} %collective-permute-done.26), channel_id=1, source_target_pairs={{0,64},{64,128},{128,192},{192,256},{256,320},{320,384},{384,448},... | collective-permute-start | bytes 110600 | tf_op jit(solution)/shard_map/ppermute | solution.py:10
  343.3 240.8 %collective-permute-start.13 = (bf16[16,1152]{1,0:T(8,128)(2,1)}, bf16[16,1152]{1,0:T(8,128)(2,1)}, u32[]{:S(2)}, u32[]{:S(2)}) collective-permute-start(bf16[16,1152]{1,0:T(8,128)(2,1)} %collective-permute-done.11), channel_id=1, source_target_pairs={{0,64},{64,128},{128,192},{192,256},{256,320},{320,384},{384,448},... | collective-permute-start | bytes 110600 | tf_op jit(solution)/shard_map/ppermute | solution.py:10
  375.3 113.7 %collective-permute-start.15 = (f32[16,1152]{1,0:T(8,128)S(1)}, f32[16,1152]{1,0:T(8,128)S(1)}, u32[]{:S(2)}, u32[]{:S(2)}) collective-permute-start(f32[16,1152]{1,0:T(8,128)S(1)} %fusion.143), channel_id=1, source_target_pairs={{0,64},{64,128},{128,192},{192,256},{256,320},{320,384},{384,448},... | collective-permute-start | bytes 221192 | tf_op jit(solution)/shard_map/ppermute | solution.py:10
  593.5 43.7 %collective-permute-start.14 = (f32[16,1152]{1,0:T(8,128)S(1)}, f32[16,1152]{1,0:T(8,128)S(1)}, u32[]{:S(2)}, u32[]{:S(2)}) collective-permute-start(f32[16,1152]{1,0:T(8,128)S(1)} %fusion.142), channel_id=1, source_target_pairs={{0,64},{64,128},{128,192},{192,256},{256,320},{320,384},{384,448},... | collective-permute-start | bytes 221192 | tf_op jit(solution)/shard_map/ppermute | solution.py:10
  1005.6 24.9 %collective-permute-start.43 = (f32[144,24]{0,1:T(8,128)}, f32[144,24]{0,1:T(8,128)}, u32[]{:S(2)}, u32[]{:S(2)}) collective-permute-start(f32[144,24]{0,1:T(8,128)} %get-tuple-element.6), channel_id=1, source_target_pairs={{0,14},{1,15},{2,16},{3,17},{4,18},{5,19},{6,20},{7,21},{8,22},{9,... | collective-permute-start | bytes 41480
  1009.0 23.4 %collective-permute-start.42 = (f32[144,24]{0,1:T(8,128)}, f32[144,24]{0,1:T(8,128)}, u32[]{:S(2)}, u32[]{:S(2)}) collective-permute-start(f32[144,24]{0,1:T(8,128)} %get-tuple-element.6), channel_id=1, source_target_pairs={{0,13},{1,14},{2,15},{3,16},{4,17},{5,18},{6,19},{7,20},{8,21},{9,... | collective-permute-start | bytes 41480
  1010.9 23.7 %collective-permute-start.41 = (f32[144,24]{0,1:T(8,128)}, f32[144,24]{0,1:T(8,128)}, u32[]{:S(2)}, u32[]{:S(2)}) collective-permute-start(f32[144,24]{0,1:T(8,128)} %get-tuple-element.6), channel_id=1, source_target_pairs={{0,12},{1,13},{2,14},{3,15},{4,16},{5,17},{6,18},{7,19},{8,20},{9,... | collective-permute-start | bytes 41480
  1012.8 32.4 %collective-permute-start.40 = (f32[144,24]{0,1:T(8,128)}, f32[144,24]{0,1:T(8,128)}, u32[]{:S(2)}, u32[]{:S(2)}) collective-permute-start(f32[144,24]{0,1:T(8,128)} %get-tuple-element.6), channel_id=1, source_target_pairs={{0,11},{1,12},{2,13},{3,14},{4,15},{5,16},{6,17},{7,18},{8,19},{9,... | collective-permute-start | bytes 41480
  1014.7 32.4 %collective-permute-start.39 = (f32[144,24]{0,1:T(8,128)}, f32[144,24]{0,1:T(8,128)}, u32[]{:S(2)}, u32[]{:S(2)}) collective-permute-start(f32[144,24]{0,1:T(8,128)} %get-tuple-element.6), channel_id=1, source_target_pairs={{0,10},{1,11},{2,12},{3,13},{4,14},{5,15},{6,16},{7,17},{8,18},{9,... | collective-permute-start | bytes 41480
  1030.5 19.8 %collective-permute-start.38 = (f32[144,24]{0,1:T(8,128)}, f32[144,24]{0,1:T(8,128)}, u32[]{:S(2)}, u32[]{:S(2)}) collective-permute-start(f32[144,24]{0,1:T(8,128)} %get-tuple-element.6), channel_id=1, source_target_pairs={{0,9},{1,10},{2,11},{3,12},{4,13},{5,14},{6,15},{7,16},{8,17},{9,1... | collective-permute-start | bytes 41480
  1032.4 21.3 %collective-permute-start.37 = (f32[144,24]{0,1:T(8,128)}, f32[144,24]{0,1:T(8,128)}, u32[]{:S(2)}, u32[]{:S(2)}) collective-permute-start(f32[144,24]{0,1:T(8,128)} %get-tuple-element.6), channel_id=1, source_target_pairs={{0,8},{1,9},{2,10},{3,11},{4,12},{5,13},{6,14},{7,15},{8,16},{9,17... | collective-permute-start | bytes 41480
  1034.6 27.8 %collective-permute-start.36 = (f32[144,24]{0,1:T(8,128)}, f32[144,24]{0,1:T(8,128)}, u32[]{:S(2)}, u32[]{:S(2)}) collective-permute-start(f32[144,24]{0,1:T(8,128)} %get-tuple-element.6), channel_id=1, source_target_pairs={{0,7},{1,8},{2,9},{3,10},{4,11},{5,12},{6,13},{7,14},{8,15},{9,16}... | collective-permute-start | bytes 41480
  1045.2 19.4 %collective-permute-start.35 = (f32[144,24]{0,1:T(8,128)}, f32[144,24]{0,1:T(8,128)}, u32[]{:S(2)}, u32[]{:S(2)}) collective-permute-start(f32[144,24]{0,1:T(8,128)} %get-tuple-element.6), channel_id=1, source_target_pairs={{0,6},{1,7},{2,8},{3,9},{4,10},{5,11},{6,12},{7,13},{8,14},{9,15},... | collective-permute-start | bytes 41480
  1047.1 22.5 %collective-permute-start.34 = (f32[144,24]{0,1:T(8,128)}, f32[144,24]{0,1:T(8,128)}, u32[]{:S(2)}, u32[]{:S(2)}) collective-permute-start(f32[144,24]{0,1:T(8,128)} %get-tuple-element.6), channel_id=1, source_target_pairs={{0,5},{1,6},{2,7},{3,8},{4,9},{5,10},{6,11},{7,12},{8,13},{9,14},{... | collective-permute-start | bytes 41480
  1050.3 20.6 %collective-permute-start.33 = (f32[144,24]{0,1:T(8,128)}, f32[144,24]{0,1:T(8,128)}, u32[]{:S(2)}, u32[]{:S(2)}) collective-permute-start(f32[144,24]{0,1:T(8,128)} %get-tuple-element.6), channel_id=1, source_target_pairs={{0,4},{1,5},{2,6},{3,7},{4,8},{5,9},{6,10},{7,11},{8,12},{9,13},{1... | collective-permute-start | bytes 41480
  1053.7 28.4 %collective-permute-start.32 = (f32[144,24]{0,1:T(8,128)}, f32[144,24]{0,1:T(8,128)}, u32[]{:S(2)}, u32[]{:S(2)}) collective-permute-start(f32[144,24]{0,1:T(8,128)} %get-tuple-element.6), channel_id=1, source_target_pairs={{0,3},{1,4},{2,5},{3,6},{4,7},{5,8},{6,9},{7,10},{8,11},{9,12},{10... | collective-permute-start | bytes 41480
  1062.4 21.4 %collective-permute-start.31 = (f32[144,24]{0,1:T(8,128)}, f32[144,24]{0,1:T(8,128)}, u32[]{:S(2)}, u32[]{:S(2)}) collective-permute-start(f32[144,24]{0,1:T(8,128)} %get-tuple-element.6), channel_id=1, source_target_pairs={{0,2},{1,3},{2,4},{3,5},{4,6},{5,7},{6,8},{7,9},{8,10},{9,11},{10,... | collective-permute-start | bytes 41480
  1064.6 20.5 %collective-permute-start.30 = (f32[144,24]{0,1:T(8,128)}, f32[144,24]{0,1:T(8,128)}, u32[]{:S(2)}, u32[]{:S(2)}) collective-permute-start(f32[144,24]{0,1:T(8,128)} %get-tuple-element.6), channel_id=1, source_target_pairs={{0,1},{1,2},{2,3},{3,4},{4,5},{5,6},{6,7},{7,8},{8,9},{9,10},{10,1... | collective-permute-start | bytes 41480
  1069.6 20.0 %collective-permute-start.60 = (f32[144,24]{0,1:T(8,128)}, f32[144,24]{0,1:T(8,128)S(1)}, u32[]{:S(2)}, u32[]{:S(2)}) collective-permute-start(f32[144,24]{0,1:T(8,128)} %get-tuple-element.7), channel_id=1, source_target_pairs={{0,15},{1,16},{2,17},{3,18},{4,19},{5,20},{6,21},{7,22},{8,23},{9,... | collective-permute-start | bytes 41480
  1070.9 23.2 %collective-permute-start.59 = (f32[144,24]{0,1:T(8,128)}, f32[144,24]{0,1:T(8,128)S(1)}, u32[]{:S(2)}, u32[]{:S(2)}) collective-permute-start(f32[144,24]{0,1:T(8,128)} %get-tuple-element.7), channel_id=1, source_target_pairs={{0,14},{1,15},{2,16},{3,17},{4,18},{5,19},{6,20},{7,21},{8,22},{9,... | collective-permute-start | bytes 41480
  1083.8 15.9 %collective-permute-start.57 = (f32[144,24]{0,1:T(8,128)}, f32[144,24]{0,1:T(8,128)S(1)}, u32[]{:S(2)}, u32[]{:S(2)}) collective-permute-start(f32[144,24]{0,1:T(8,128)} %get-tuple-element.7), channel_id=1, source_target_pairs={{0,12},{1,13},{2,14},{3,15},{4,16},{5,17},{6,18},{7,19},{8,20},{9,... | collective-permute-start | bytes 41480
  1085.1 17.8 %collective-permute-start.56 = (f32[144,24]{0,1:T(8,128)}, f32[144,24]{0,1:T(8,128)S(1)}, u32[]{:S(2)}, u32[]{:S(2)}) collective-permute-start(f32[144,24]{0,1:T(8,128)} %get-tuple-element.7), channel_id=1, source_target_pairs={{0,11},{1,12},{2,13},{3,14},{4,15},{5,16},{6,17},{7,18},{8,19},{9,... | collective-permute-start | bytes 41480
  1089.6 31.7 %collective-permute-start.55 = (f32[144,24]{0,1:T(8,128)}, f32[144,24]{0,1:T(8,128)S(1)}, u32[]{:S(2)}, u32[]{:S(2)}) collective-permute-start(f32[144,24]{0,1:T(8,128)} %get-tuple-element.7), channel_id=1, source_target_pairs={{0,10},{1,11},{2,12},{3,13},{4,14},{5,15},{6,16},{7,17},{8,18},{9,... | collective-permute-start | bytes 41480
  1094.1 31.1 %collective-permute-start.54 = (f32[144,24]{0,1:T(8,128)}, f32[144,24]{0,1:T(8,128)S(1)}, u32[]{:S(2)}, u32[]{:S(2)}) collective-permute-start(f32[144,24]{0,1:T(8,128)} %get-tuple-element.7), channel_id=1, source_target_pairs={{0,9},{1,10},{2,11},{3,12},{4,13},{5,14},{6,15},{7,16},{8,17},{9,1... | collective-permute-start | bytes 41480
  1096.2 31.3 %collective-permute-start.53 = (f32[144,24]{0,1:T(8,128)}, f32[144,24]{0,1:T(8,128)S(1)}, u32[]{:S(2)}, u32[]{:S(2)}) collective-permute-start(f32[144,24]{0,1:T(8,128)} %get-tuple-element.7), channel_id=1, source_target_pairs={{0,8},{1,9},{2,10},{3,11},{4,12},{5,13},{6,14},{7,15},{8,16},{9,17... | collective-permute-start | bytes 41480
  1099.7 33.1 %collective-permute-start.52 = (f32[144,24]{0,1:T(8,128)}, f32[144,24]{0,1:T(8,128)S(1)}, u32[]{:S(2)}, u32[]{:S(2)}) collective-permute-start(f32[144,24]{0,1:T(8,128)} %get-tuple-element.7), channel_id=1, source_target_pairs={{0,7},{1,8},{2,9},{3,10},{4,11},{5,12},{6,13},{7,14},{8,15},{9,16}... | collective-permute-start | bytes 41480
  1103.0 32.3 %collective-permute-start.51 = (f32[144,24]{0,1:T(8,128)}, f32[144,24]{0,1:T(8,128)S(1)}, u32[]{:S(2)}, u32[]{:S(2)}) collective-permute-start(f32[144,24]{0,1:T(8,128)} %get-tuple-element.7), channel_id=1, source_target_pairs={{0,6},{1,7},{2,8},{3,9},{4,10},{5,11},{6,12},{7,13},{8,14},{9,15},... | collective-permute-start | bytes 41480
  1121.2 17.2 %collective-permute-start.50 = (f32[144,24]{0,1:T(8,128)}, f32[144,24]{0,1:T(8,128)S(1)}, u32[]{:S(2)}, u32[]{:S(2)}) collective-permute-start(f32[144,24]{0,1:T(8,128)} %get-tuple-element.7), channel_id=1, source_target_pairs={{0,5},{1,6},{2,7},{3,8},{4,9},{5,10},{6,11},{7,12},{8,13},{9,14},{... | collective-permute-start | bytes 41480
  (45 other events, 850.6 us)
Sparse Core Ops, SparseCore 0:
  12.4 131.6 all-gather.12
  148.6 114.7 all-gather.14
  268.4 103.4 all-gather.10
  376.7 106.7 all-gather.8
where the time goes:
time: 1260 us; the launch traced here: 1240 us
  blocking collectives  483 us (38%)
  waiting for transfers between devices  474 us (38%)
  starting transfers between devices  176 us (14%)
  matrix products  50 us (4%)
  local copies, waits for them, and re-layouts  33.8 us (3%)
  between operations  17.4 us (1%)
    unnamed x1, blocking collectives  319 us
    all_gather x1, waiting for transfers between devices, body(): lax.all_gather(img_proj, 'grp', axis=1, tiled=True)  135 us
    unnamed x32, starting transfers between devices  119 us
    all_gather x1, waiting for transfers between devices, body(): lax.all_gather(txt_proj, 'grp', axis=1, tiled=True)  114 us
    all_gather x1, waiting for transfers between devices, body(): lax.all_gather(txt_emb, 'grp', axis=0, tiled=True)  106 us
    ppermute x30, waiting for transfers between devices, shifted(): return lax.ppermute(value, axis, pairs)  89.7 us
    ppermute x30, starting transfers between devices, shifted(): return lax.ppermute(value, axis, pairs)  57.6 us
    all_gather x1, blocking collectives, body(): lax.all_gather(txt_share, 'blk', axis=0, tiled=True)  41.8 us
  transfers between devices with their start and end apart: 66, of which 23 were waited for; matrix products, arithmetic and copies ran while one was open for 6% of the time, Pallas kernels for 0%

commit v1 on v0

v1 whole, which is shorter than its diff:
```python
import jax
import jax.numpy as jnp
from jax import lax
from jax.sharding import PartitionSpec as P

BOTH = ("blk", "grp")
N_BLK, N_Y, N_ZH, N_X, N_CORE = 8, 4, 2, 4, 2
N_GRP = N_Y * N_ZH * N_X * N_CORE
PAIR = 40


def place(blk, y, zh, x, core):
    return blk * N_GRP + ((y * N_ZH + zh) * N_X + x) * N_CORE + core


def parts(device):
    blk, grp = divmod(device, N_GRP)
    grp, core = divmod(grp, N_CORE)
    grp, x = divmod(grp, N_X)
    y, zh = divmod(grp, N_ZH)
    return blk, y, zh, x, core


def sibling(device):
    return device ^ 1


def mirror(device):
    blk, y, zh, x, core = parts(device)
    return place(N_BLK - 1 - blk, y, 1 - zh, x, core)


PLANE = [
    [place(blk, y, zh, x, core) for y in range(N_Y) for x in range(N_X)]
    for blk in range(N_BLK)
    for zh in range(N_ZH)
    for core in range(N_CORE)
]
LINE = [
    [place(sub if zh == 0 else N_BLK - 1 - sub, y, zh, x, core) for sub in range(N_BLK)]
    for y in range(N_Y)
    for zh in range(N_ZH)
    for x in range(N_X)
    for core in range(N_CORE)
]


def permuted(value, target):
    pairs = [(source, target(source)) for source in range(N_BLK * N_GRP)]
    return lax.ppermute(value, BOTH, pairs)


def exchanged(value, groups):
    return lax.all_to_all(value, BOTH, 0, 0, axis_index_groups=groups, tiled=True)


def gathered(value, groups):
    count = len(groups[0])
    copies = jnp.broadcast_to(value[None], (count,) + value.shape)
    return exchanged(copies, groups)


def contract_last(left, right):
    return lax.dot_general(
        left, right, (((1,), (1,)), ((), ())), preferred_element_type=jnp.float32
    )


def contract_first(left, right):
    return lax.dot_general(
        left, right, (((0,), (0,)), ((), ())), preferred_element_type=jnp.float32
    )


def body(img_feat, txt_feat, img_proj, txt_proj, logit_scale, logit_bias, loss_weight):
    bf16, f32 = jnp.bfloat16, jnp.float32
    scale, shift_by, weight = logit_scale[0], logit_bias[0], loss_weight[0]
    rows, width = img_feat.shape
    cols = img_proj.shape[1]
    blk = lax.axis_index("blk")
    grp = lax.axis_index("grp")
    core = grp % N_CORE
    x = (grp // N_CORE) % N_X
    zh = (grp // (N_CORE * N_X)) % N_ZH
    y = grp // (N_CORE * N_X * N_ZH)
    first = core == 0
    sub = jnp.where(zh == 0, blk, N_BLK - 1 - blk)
    sub_rows = rows // N_BLK
    own = N_CORE * rows

    img_t, txt_t = img_proj.T, txt_proj.T
    keep_t = jnp.where(first, img_t, txt_t)
    got_t = permuted(jnp.where(first, txt_t, img_t), sibling)
    block = jnp.concatenate(
        [
            jnp.where(first, keep_t, got_t),
            jnp.where(first, got_t, keep_t),
            jnp.zeros((PAIR - N_CORE * cols, width), bf16),
        ],
        0,
    )
    other = permuted(block, mirror)
    keep_f = jnp.where(first, img_feat, txt_feat)
    got_f = permuted(jnp.where(first, txt_feat, img_feat), sibling)
    feat = jnp.stack(
        [keep_f.reshape(N_BLK, sub_rows, width), got_f.reshape(N_BLK, sub_rows, width)], 1
    ).reshape(own, width)
    low = zh == 0
    block = jnp.concatenate([jnp.where(low, block, other), jnp.where(low, other, block)], 0)
    proj = gathered(block, PLANE).reshape(N_Y * N_X * N_ZH * PAIR, width)

    proj_out = contract_last(feat, proj)
    inverse = lax.rsqrt(jnp.sum(proj_out * proj_out, axis=1, keepdims=True) + 1e-06)
    unit = proj_out * inverse
    emb = unit.astype(bf16)

    mine = lax.dynamic_slice_in_dim(emb, sub * N_CORE * sub_rows, N_CORE * sub_rows, 0)
    got = permuted(mine, sibling)
    got = jnp.concatenate([got[sub_rows:], got[:sub_rows]], 0)
    others = gathered(jnp.concatenate([got, permuted(got, mirror)], 0), PLANE)
    others = others.reshape(-1, emb.shape[1])

    logits = scale * contract_last(emb, others) + shift_by
    row = lax.broadcasted_iota(jnp.int32, logits.shape, 0) - sub * (N_CORE * sub_rows)
    col = lax.broadcasted_iota(jnp.int32, logits.shape, 1) - (y * N_X + x) * (
        N_ZH * N_CORE * sub_rows
    )
    same = (row == col) & (row >= 0) & (row < N_CORE * sub_rows)
    sign = jnp.where(same, f32(1.0), f32(-1.0))
    coef = (-weight * sign * jax.nn.sigmoid(-sign * logits)).astype(bf16)
    part = jnp.dot(coef, others, preferred_element_type=f32).astype(bf16)

    pieces = exchanged(part.reshape(N_BLK, N_CORE * sub_rows, -1), LINE)
    grad_unit = scale * jnp.sum(pieces.astype(f32), 0)
    unit_sub = lax.dynamic_slice_in_dim(unit, sub * N_CORE * sub_rows, N_CORE * sub_rows, 0)
    inv_sub = lax.dynamic_slice_in_dim(inverse, sub * N_CORE * sub_rows, N_CORE * sub_rows, 0)
    inner = jnp.sum(unit_sub * grad_unit, axis=1, keepdims=True)
    du = ((grad_unit - unit_sub * inner) * inv_sub).astype(bf16)
    du = gathered(du, LINE).reshape(own, -1)

    terms = contract_first(du, feat).astype(bf16)
    terms = exchanged(terms.reshape(N_Y * N_X, N_ZH * PAIR, width), PLANE)
    terms = jnp.sum(terms.astype(f32), 0)
    lower, upper = terms[:PAIR], terms[PAIR:]
    came = permuted(jnp.where(low, upper, lower).astype(bf16), mirror)
    total = jnp.where(low, lower, upper) + came.astype(f32)
    keep_g = jnp.where(first, total[:cols], total[cols : 2 * cols])
    got_g = permuted(jnp.where(first, total[cols : 2 * cols], total[:cols]), sibling)
    img_proj_grad = jnp.where(first, keep_g, got_g).T
    txt_proj_grad = jnp.where(first, got_g, keep_g).T

    grad = jnp.dot(du, proj, preferred_element_type=f32)
    grad = grad.reshape(N_BLK, N_CORE, sub_rows, width)
    keep_r = grad[:, 0].reshape(rows, width)
    got_r = permuted(grad[:, 1].reshape(rows, width), sibling)
    img_grad = jnp.where(first, keep_r, got_r)
    txt_grad = jnp.where(first, got_r, keep_r)
    return (img_grad, txt_grad, img_proj_grad, txt_proj_grad)


def solution(mesh):
    return jax.shard_map(
        body,
        mesh=mesh,
        in_specs=(P("grp", None), P("grp", None), P(None, "grp"), P(None, "grp"), P(), P(), P()),
        out_specs=(P("grp", None), P("grp", None), P(None, "grp"), P(None, "grp")),
        check_vma=False,
    )
```

time: 1260 us -> 289 us (0.23); the launches traced: 1240 us -> 285 us
  blocking collectives: 483 us -> 45.1 us
  waiting for transfers between devices: 474 us -> 150 us
  starting transfers between devices: 176 us -> 60.7 us
  matrix products: 50 us -> 11.6 us
  local copies, waits for them, and re-layouts: 33.8 us -> 5.42 us
  between operations: 17.4 us -> 2.91 us
    all_gather x4 -> x0, waiting for transfers between devices: 382 us -> none  [the longest x1 135 us: body(): lax.all_gather(img_proj, 'grp', axis=1, tiled=True)]
    unnamed x1 -> x0, blocking collectives: 319 us -> none
    all_gather x4 -> x0, blocking collectives: 164 us -> none  [the longest x1 41.8 us: body(): lax.all_gather(txt_share, 'blk', axis=0, tiled=True)]
    all_to_all x0 -> x4, waiting for transfers between devices: none -> 127 us  [exchanged(): lax.all_to_all(value, BOTH, 0, 0, axis_index_groups=groups, tiled=True)]
    unnamed x32 -> x0, starting transfers between devices: 119 us -> none
    ppermute x30 -> x8, waiting for transfers between devices: 89.7 us -> 22.3 us  [permuted(): return lax.ppermute(value, BOTH, pairs)]
    all_to_all x0 -> x1, blocking collectives: none -> 45.1 us  [exchanged(): lax.all_to_all(value, BOTH, 0, 0, axis_index_groups=groups, tiled=True)]
    dot_general x18 -> x2, matrix products: 43.7 us -> 7.8 us  [the longest x1 4.1 us: body(): grad = jnp.dot(du, proj, preferred_element_type=f32)]
  transfers between devices with their start and end apart: 66 -> 12, of which waited for: 23 -> 9; matrix products, arithmetic and copies ran while one was open for 6% -> 3% of each run, Pallas kernels for 0% -> 0%
where the time goes in v1:
time: 289 us; the launch traced here: 285 us
  waiting for transfers between devices  150 us (52%)
  starting transfers between devices  60.7 us (21%)
  blocking collectives  45.1 us (16%)
  matrix products  11.6 us (4%)
  other arithmetic  9.71 us (3%)
  local copies, waits for them, and re-layouts  5.42 us (2%)
  between operations  2.91 us (1%)
    all_to_all x4, waiting for transfers between devices, exchanged(): lax.all_to_all(value, BOTH, 0, 0, axis_index_groups=groups, tiled=True)  127 us
    all_to_all x1, blocking collectives, exchanged(): lax.all_to_all(value, BOTH, 0, 0, axis_index_groups=groups, tiled=True)  45.1 us
    ppermute x8, starting transfers between devices, permuted(): return lax.ppermute(value, BOTH, pairs)  39.9 us
    ppermute x8, waiting for transfers between devices, permuted(): return lax.ppermute(value, BOTH, pairs)  22.3 us
    all_to_all x4, starting transfers between devices, exchanged(): lax.all_to_all(value, BOTH, 0, 0, axis_index_groups=groups, tiled=True)  20.8 us
  transfers between devices with their start and end apart: 12, of which 9 were waited for; matrix products, arithmetic and copies ran while one was open for 3% of the time, Pallas kernels for 0%

profile of v1, /device:TPU:1, one launch (start us, length us, event | category | flops | bytes accessed | tf_op | source)
XLA Modules:
  0.0 285.2 jit_solution(15762524849565569892)
XLA Ops:
  1.5 8.8 %collective-permute-start.1 = (bf16[18,1152]{1,0:T(8,128)(2,1)S(1)}, bf16[18,1152]{1,0:T(8,128)(2,1)S(1)}, u32[]{:S(2)}, u32[]{:S(2)}) collective-permute-start(bf16[18,1152]{1,0:T(8,128)(2,1)S(1)} %select_bitcast_fusion.2), channel_id=1, source_target_pairs={{0,1},{1,0},{2,3},{3,2},{4,5},{5,4},{6,7},{7,6},{8,9},{9,8},{10,11... | collective-permute-start | bytes 124424 | tf_op jit(solution)/shard_map/ppermute | solution.py:50
  12.1 5.7 %collective-permute-start.2 = (bf16[40,1152]{1,0:T(8,128)(2,1)S(1)}, bf16[40,1152]{1,0:T(8,128)(2,1)S(1)}, u32[]{:S(2)}, u32[]{:S(2)}) collective-permute-start(bf16[40,1152]{1,0:T(8,128)(2,1)S(1)} %maximum_maximum_fusion), channel_id=1, source_target_pairs={{0,456},{1,457},{2,458},{3,459},{4,460},{5,461},{6,462},{7,463},{8... | collective-permute-start | bytes 276488 | tf_op jit(solution)/shard_map/ppermute | solution.py:50
  17.9 8.6 %collective-permute-done.2 = bf16[40,1152]{1,0:T(8,128)(2,1)S(1)} collective-permute-done((bf16[40,1152]{1,0:T(8,128)(2,1)S(1)}, bf16[40,1152]{1,0:T(8,128)(2,1)S(1)}, u32[]{:S(2)}, u32[]{:S(2)}) %collective-permute-start.2) | collective-permute-done | bytes 92192 | tf_op jit(solution)/shard_map/ppermute | solution.py:50
  26.6 1.8 broadcast_in_dim.34
  28.4 6.9 %all-to-all-start = ((bf16[16,80,1152]{2,1,0:T(8,128)(2,1)}), bf16[16,80,1152]{2,1,0:T(8,128)(2,1)S(1)}, u32[]{:S(2)}, u32[]{:S(2)}) async-start(bf16[16,80,1152]{2,1,0:T(8,128)(2,1)} %broadcast_in_dim.34), calls=%async_computation | async-start | bytes 5898240 | tf_op jit(solution)/shard_map/all_to_all | solution.py:54
  36.2 3.0 %collective-permute-start = (bf16[128,1152]{1,0:T(8,128)(2,1)}, bf16[128,1152]{1,0:T(8,128)(2,1)S(1)}, u32[]{:S(2)}, u32[]{:S(2)}) collective-permute-start(bf16[128,1152]{1,0:T(8,128)(2,1)} %get-tuple-element.11), channel_id=1, source_target_pairs={{0,1},{1,0},{2,3},{3,2},{4,5},{5,4},{6,7},{7,6},{8,9},{9,8},{10,11... | collective-permute-start | bytes 884744 | tf_op jit(solution)/shard_map/ppermute | solution.py:50
  39.3 1.4 collective-permute-done
  41.4 1.1 pad_maximum_fusion
  42.5 36.0 %all-to-all-done = bf16[16,80,1152]{2,1,0:T(8,128)(2,1)S(1)} async-done(((bf16[16,80,1152]{2,1,0:T(8,128)(2,1)}), bf16[16,80,1152]{2,1,0:T(8,128)(2,1)S(1)}, u32[]{:S(2)}, u32[]{:S(2)}) %all-to-all-start) | async-done | bytes 2949152 | tf_op jit(solution)/shard_map/all_to_all | solution.py:54
  78.5 1.1 multiply_reduce_fusion
  79.6 1.3 fusion.21
  81.8 3.9 %collective-permute-start.3 = (bf16[32,1280]{1,0:T(8,128)(2,1)S(1)}, bf16[32,1280]{1,0:T(8,128)(2,1)S(1)}, u32[]{:S(2)}, u32[]{:S(2)}) collective-permute-start(bf16[32,1280]{1,0:T(8,128)(2,1)S(1)} %constant_dynamic-slice_fusion), channel_id=1, source_target_pairs={{0,1},{1,0},{2,3},{3,2},{4,5},{5,4},{6,7},{7,6},{8,9},{9,8},{10,11... | collective-permute-start | bytes 245768 | tf_op jit(solution)/shard_map/ppermute | solution.py:50
  85.7 0.9 collective-permute-done.3
  86.6 1.9 collective-permute-start.4
  88.5 10.6 %collective-permute-done.4 = bf16[32,1280]{1,0:T(8,128)(2,1)S(1)} collective-permute-done((bf16[32,1280]{1,0:T(8,128)(2,1)S(1)}, bf16[32,1280]{1,0:T(8,128)(2,1)S(1)}, u32[]{:S(2)}, u32[]{:S(2)}) %collective-permute-start.4) | collective-permute-done | bytes 81952 | tf_op jit(solution)/shard_map/ppermute | solution.py:50
  99.1 1.8 broadcast_in_dim.35
  100.9 3.7 %all-to-all-start.1 = ((bf16[16,64,1280]{2,1,0:T(8,128)(2,1)}), bf16[16,64,1280]{2,1,0:T(8,128)(2,1)S(1)}, u32[]{:S(2)}, u32[]{:S(2)}) async-start(bf16[16,64,1280]{2,1,0:T(8,128)(2,1)} %broadcast_in_dim.35), calls=%async_computation.1 | async-start | bytes 5242880 | tf_op jit(solution)/shard_map/all_to_all | solution.py:54
  106.7 37.2 %all-to-all-done.1 = bf16[16,64,1280]{2,1,0:T(8,128)(2,1)S(1)} async-done(((bf16[16,64,1280]{2,1,0:T(8,128)(2,1)}), bf16[16,64,1280]{2,1,0:T(8,128)(2,1)S(1)}, u32[]{:S(2)}, u32[]{:S(2)}) %all-to-all-start.1) | async-done | bytes 2621472 | tf_op jit(solution)/shard_map/all_to_all | solution.py:54
  143.9 3.7 %convolution_convert_fusion.1 = bf16[256,1280]{1,0:T(8,128)(2,1)} fusion(bf16[1024,1280]{1,0:T(8,128)(2,1)S(1)} %bitcast.46, bf16[256,1280]{1,0:T(8,128)(2,1)} %copy-done.3, f32[]{:T(128)} %bitcast.41, f32[]{:T(128)} %bitcast.39, s32[1024]{0:T(1024)S(1)} %iota_subtract_fusion, f32[]{:T(128)} %bitcast.1, s32[256]{0:T(256)S(1)} %iota_subtract_fusion.1, ...), kind=kOutput, calls=%fused_computation.2 | convolution fusion | flops 1346174976 | bytes 3937804 | tf_op jit(solution)/shard_map/dot_general | solution.py:131
  147.6 6.3 %all-to-all-start.2 = ((bf16[8,32,1280]{2,1,0:T(8,128)(2,1)}), bf16[8,32,1280]{2,1,0:T(8,128)(2,1)S(1)}, u32[]{:S(2)}, u32[]{:S(2)}) async-start(bf16[8,32,1280]{2,1,0:T(8,128)(2,1)} %bitcast.50), calls=%async_computation.2 | async-start | bytes 1310720 | tf_op jit(solution)/shard_map/all_to_all | solution.py:54
  154.0 24.0 %all-to-all-done.2 = bf16[8,32,1280]{2,1,0:T(8,128)(2,1)S(1)} async-done(((bf16[8,32,1280]{2,1,0:T(8,128)(2,1)}), bf16[8,32,1280]{2,1,0:T(8,128)(2,1)S(1)}, u32[]{:S(2)}, u32[]{:S(2)}) %all-to-all-start.2) | async-done | bytes 655392 | tf_op jit(solution)/shard_map/all_to_all | solution.py:54
  178.1 1.1 multiply_reduce_fusion.1
  179.1 1.0 multiply_convert_fusion
  180.2 45.1 %all_to_all.25 = bf16[8,32,1280]{2,1,0:T(8,128)(2,1)S(1)} all-to-all(bf16[8,32,1280]{2,1,0:T(8,128)(2,1)S(1)} %broadcast_in_dim.36), channel_id=1, replica_groups={{0,64,128,192,256,320,384,448},{1,65,129,193,257,321,385,449},{2,66,130..., dimensions={0} | all-to-all | bytes 1310720 | tf_op jit(solution)/shard_map/all_to_all | solution.py:54
  225.3 2.7 convolution_convert_fusion
  228.0 3.9 %all-to-all-start.4 = ((bf16[16,80,1152]{2,1,0:T(8,128)(2,1)}), bf16[16,80,1152]{2,1,0:T(8,128)(2,1)S(1)}, u32[]{:S(2)}, u32[]{:S(2)}) async-start(bf16[16,80,1152]{2,1,0:T(8,128)(2,1)} %bitcast.17), calls=%async_computation.4 | async-start | bytes 5898240 | tf_op jit(solution)/shard_map/all_to_all | solution.py:54
  231.8 4.1 %fusion.24 = f32[8,2,16,1152]{3,2,1,0:T(8,128)} fusion(bf16[8,2,16,1280]{3,2,1,0:T(8,128)(2,1)} %bitcast.43, bf16[1280,1152,1,1]{1,0,3,2:T(8,128)(2,1)} %bitcast.45), kind=kOutput, calls=%fused_computation.60 | convolution fusion | flops 754974720 | bytes 4784128 | tf_op jit(solution)/shard_map/dot_general | solution.py:152
  235.9 30.3 %all-to-all-done.4 = bf16[16,80,1152]{2,1,0:T(8,128)(2,1)S(1)} async-done(((bf16[16,80,1152]{2,1,0:T(8,128)(2,1)}), bf16[16,80,1152]{2,1,0:T(8,128)(2,1)S(1)}, u32[]{:S(2)}, u32[]{:S(2)}) %all-to-all-start.4) | async-done | bytes 2949152 | tf_op jit(solution)/shard_map/all_to_all | solution.py:54
  266.7 1.9 collective-permute-start.6
  268.7 9.0 %collective-permute-start.5 = (f32[128,1152]{1,0:T(8,128)S(1)}, f32[128,1152]{1,0:T(8,128)S(1)}, u32[]{:S(2)}, u32[]{:S(2)}) collective-permute-start(f32[128,1152]{1,0:T(8,128)S(1)} %bitcast.51), channel_id=1, source_target_pairs={{0,1},{1,0},{2,3},{3,2},{4,5},{5,4},{6,7},{7,6},{8,9},{9,8},{10,11... | collective-permute-start | bytes 1769480 | tf_op jit(solution)/shard_map/ppermute | solution.py:50
  277.7 5.6 %collective-permute-start.7 = (f32[18,1152]{1,0:T(8,128)S(1)}, f32[18,1152]{1,0:T(8,128)S(1)}, u32[]{:S(2)}, u32[]{:S(2)}) collective-permute-start(f32[18,1152]{1,0:T(8,128)S(1)} %slice_select_fusion), channel_id=1, source_target_pairs={{0,1},{1,0},{2,3},{3,2},{4,5},{5,4},{6,7},{7,6},{8,9},{9,8},{10,11... | collective-permute-start | bytes 248840 | tf_op jit(solution)/shard_map/ppermute | solution.py:50
  283.3 1.1 bitcast_select_fusion
  (43 shorter events, 6.7 us)
Async XLA Ops:
  1.5 9.7 %collective-permute-start.1 = (bf16[18,1152]{1,0:T(8,128)(2,1)S(1)}, bf16[18,1152]{1,0:T(8,128)(2,1)S(1)}, u32[]{:S(2)}, u32[]{:S(2)}) collective-permute-start(bf16[18,1152]{1,0:T(8,128)(2,1)S(1)} %select_bitcast_fusion.2), channel_id=1, source_target_pairs={{0,1},{1,0},{2,3},{3,2},{4,5},{5,4},{6,7},{7,6},{8,9},{9,8},{10,11... | collective-permute-start | bytes 124424 | tf_op jit(solution)/shard_map/ppermute | solution.py:50
  12.1 14.4 %collective-permute-start.2 = (bf16[40,1152]{1,0:T(8,128)(2,1)S(1)}, bf16[40,1152]{1,0:T(8,128)(2,1)S(1)}, u32[]{:S(2)}, u32[]{:S(2)}) collective-permute-start(bf16[40,1152]{1,0:T(8,128)(2,1)S(1)} %maximum_maximum_fusion), channel_id=1, source_target_pairs={{0,456},{1,457},{2,458},{3,459},{4,460},{5,461},{6,462},{7,463},{8... | collective-permute-start | bytes 276488 | tf_op jit(solution)/shard_map/ppermute | solution.py:50
  28.4 6.9 %copy-start.4 = (bf16[128,1152]{1,0:T(8,128)(2,1)S(1)}, bf16[128,1152]{1,0:T(8,128)(2,1)}, u32[]{:S(2)}) copy-start(bf16[128,1152]{1,0:T(8,128)(2,1)} %param.7) | copy-start | bytes 884740
  28.4 6.9 %copy-start.5 = (bf16[128,1152]{1,0:T(8,128)(2,1)S(1)}, bf16[128,1152]{1,0:T(8,128)(2,1)}, u32[]{:S(2)}) copy-start(bf16[128,1152]{1,0:T(8,128)(2,1)} %param.8) | copy-start | bytes 884740
  28.4 50.0 %all-to-all-start = ((bf16[16,80,1152]{2,1,0:T(8,128)(2,1)}), bf16[16,80,1152]{2,1,0:T(8,128)(2,1)S(1)}, u32[]{:S(2)}, u32[]{:S(2)}) async-start(bf16[16,80,1152]{2,1,0:T(8,128)(2,1)} %broadcast_in_dim.34), calls=%async_computation | async-start | bytes 5898240 | tf_op jit(solution)/shard_map/all_to_all | solution.py:54
  36.2 4.4 %collective-permute-start = (bf16[128,1152]{1,0:T(8,128)(2,1)}, bf16[128,1152]{1,0:T(8,128)(2,1)S(1)}, u32[]{:S(2)}, u32[]{:S(2)}) collective-permute-start(bf16[128,1152]{1,0:T(8,128)(2,1)} %get-tuple-element.11), channel_id=1, source_target_pairs={{0,1},{1,0},{2,3},{3,2},{4,5},{5,4},{6,7},{7,6},{8,9},{9,8},{10,11... | collective-permute-start | bytes 884744 | tf_op jit(solution)/shard_map/ppermute | solution.py:50
  40.6 0.7 copy-start.6
  78.5 2.4 copy-start.1
  80.9 0.8 copy-start.3
  81.8 4.8 %collective-permute-start.3 = (bf16[32,1280]{1,0:T(8,128)(2,1)S(1)}, bf16[32,1280]{1,0:T(8,128)(2,1)S(1)}, u32[]{:S(2)}, u32[]{:S(2)}) collective-permute-start(bf16[32,1280]{1,0:T(8,128)(2,1)S(1)} %constant_dynamic-slice_fusion), channel_id=1, source_target_pairs={{0,1},{1,0},{2,3},{3,2},{4,5},{5,4},{6,7},{7,6},{8,9},{9,8},{10,11... | collective-permute-start | bytes 245768 | tf_op jit(solution)/shard_map/ppermute | solution.py:50
  86.6 12.5 %collective-permute-start.4 = (bf16[32,1280]{1,0:T(8,128)(2,1)S(1)}, bf16[32,1280]{1,0:T(8,128)(2,1)S(1)}, u32[]{:S(2)}, u32[]{:S(2)}) collective-permute-start(bf16[32,1280]{1,0:T(8,128)(2,1)S(1)} %pad_maximum_fusion.3), channel_id=1, source_target_pairs={{0,456},{1,457},{2,458},{3,459},{4,460},{5,461},{6,462},{7,463},{8... | collective-permute-start | bytes 245768 | tf_op jit(solution)/shard_map/ppermute | solution.py:50
  100.9 43.0 %all-to-all-start.1 = ((bf16[16,64,1280]{2,1,0:T(8,128)(2,1)}), bf16[16,64,1280]{2,1,0:T(8,128)(2,1)S(1)}, u32[]{:S(2)}, u32[]{:S(2)}) async-start(bf16[16,64,1280]{2,1,0:T(8,128)(2,1)} %broadcast_in_dim.35), calls=%async_computation.1 | async-start | bytes 5242880 | tf_op jit(solution)/shard_map/all_to_all | solution.py:54
  147.6 30.4 %all-to-all-start.2 = ((bf16[8,32,1280]{2,1,0:T(8,128)(2,1)}), bf16[8,32,1280]{2,1,0:T(8,128)(2,1)S(1)}, u32[]{:S(2)}, u32[]{:S(2)}) async-start(bf16[8,32,1280]{2,1,0:T(8,128)(2,1)} %bitcast.50), calls=%async_computation.2 | async-start | bytes 1310720 | tf_op jit(solution)/shard_map/all_to_all | solution.py:54
  225.3 2.7 copy-start
  228.0 38.2 %all-to-all-start.4 = ((bf16[16,80,1152]{2,1,0:T(8,128)(2,1)}), bf16[16,80,1152]{2,1,0:T(8,128)(2,1)S(1)}, u32[]{:S(2)}, u32[]{:S(2)}) async-start(bf16[16,80,1152]{2,1,0:T(8,128)(2,1)} %bitcast.17), calls=%async_computation.4 | async-start | bytes 5898240 | tf_op jit(solution)/shard_map/all_to_all | solution.py:54
  266.2 2.4 copy-start.2
  266.7 11.0 %collective-permute-start.6 = (bf16[40,1152]{1,0:T(8,128)(2,1)S(1)}, bf16[40,1152]{1,0:T(8,128)(2,1)S(1)}, u32[]{:S(2)}, u32[]{:S(2)}) collective-permute-start(bf16[40,1152]{1,0:T(8,128)(2,1)S(1)} %select_convert_fusion), channel_id=1, source_target_pairs={{0,456},{1,457},{2,458},{3,459},{4,460},{5,461},{6,462},{7,463},{8... | collective-permute-start | bytes 276488 | tf_op jit(solution)/shard_map/ppermute | solution.py:50
  268.7 14.7 %collective-permute-start.5 = (f32[128,1152]{1,0:T(8,128)S(1)}, f32[128,1152]{1,0:T(8,128)S(1)}, u32[]{:S(2)}, u32[]{:S(2)}) collective-permute-start(f32[128,1152]{1,0:T(8,128)S(1)} %bitcast.51), channel_id=1, source_target_pairs={{0,1},{1,0},{2,3},{3,2},{4,5},{5,4},{6,7},{7,6},{8,9},{9,8},{10,11... | collective-permute-start | bytes 1769480 | tf_op jit(solution)/shard_map/ppermute | solution.py:50
  277.7 6.8 %collective-permute-start.7 = (f32[18,1152]{1,0:T(8,128)S(1)}, f32[18,1152]{1,0:T(8,128)S(1)}, u32[]{:S(2)}, u32[]{:S(2)}) collective-permute-start(f32[18,1152]{1,0:T(8,128)S(1)} %slice_select_fusion), channel_id=1, source_target_pairs={{0,1},{1,0},{2,3},{3,2},{4,5},{5,4},{6,7},{7,6},{8,9},{9,8},{10,11... | collective-permute-start | bytes 248840 | tf_op jit(solution)/shard_map/ppermute | solution.py:50

commit v2 on v1

--- a/solution.py
+++ b/solution.py
@@ -6,7 +6,6 @@
 BOTH = ("blk", "grp")
 N_BLK, N_Y, N_ZH, N_X, N_CORE = 8, 4, 2, 4, 2
 N_GRP = N_Y * N_ZH * N_X * N_CORE
-PAIR = 40
 
 
 def place(blk, y, zh, x, core):
@@ -40,6 +39,12 @@
     [place(sub if zh == 0 else N_BLK - 1 - sub, y, zh, x, core) for sub in range(N_BLK)]
     for y in range(N_Y)
     for zh in range(N_ZH)
+    for x in range(N_X)
+    for core in range(N_CORE)
+]
+RING = [
+    LINE[(y * N_ZH * N_X + x) * N_CORE + core] + LINE[(y * N_ZH * N_X + N_X + x) * N_CORE + core]
+    for y in range(N_Y)
     for x in range(N_X)
     for core in range(N_CORE)
 ]
@@ -92,22 +97,19 @@
     keep_t = jnp.where(first, img_t, txt_t)
     got_t = permuted(jnp.where(first, txt_t, img_t), sibling)
     block = jnp.concatenate(
-        [
-            jnp.where(first, keep_t, got_t),
-            jnp.where(first, got_t, keep_t),
-            jnp.zeros((PAIR - N_CORE * cols, width), bf16),
-        ],
-        0,
+        [jnp.where(first, keep_t, got_t), jnp.where(first, got_t, keep_t)], 0
     )
-    other = permuted(block, mirror)
+    near = gathered(block, PLANE)
+    far = gathered(permuted(block, mirror), PLANE)
     keep_f = jnp.where(first, img_feat, txt_feat)
     got_f = permuted(jnp.where(first, txt_feat, img_feat), sibling)
     feat = jnp.stack(
         [keep_f.reshape(N_BLK, sub_rows, width), got_f.reshape(N_BLK, sub_rows, width)], 1
     ).reshape(own, width)
     low = zh == 0
-    block = jnp.concatenate([jnp.where(low, block, other), jnp.where(low, other, block)], 0)
-    proj = gathered(block, PLANE).reshape(N_Y * N_X * N_ZH * PAIR, width)
+    proj = jnp.stack([jnp.where(low, near, far), jnp.where(low, far, near)], 1)
+    proj = proj.reshape(-1, width)
+    embed = proj.shape[0]
 
     proj_out = contract_last(feat, proj)
     inverse = lax.rsqrt(jnp.sum(proj_out * proj_out, axis=1, keepdims=True) + 1e-06)
@@ -115,40 +117,42 @@
     emb = unit.astype(bf16)
 
     mine = lax.dynamic_slice_in_dim(emb, sub * N_CORE * sub_rows, N_CORE * sub_rows, 0)
+    far = gathered(permuted(mine, lambda device: mirror(sibling(device))), PLANE)
     got = permuted(mine, sibling)
-    got = jnp.concatenate([got[sub_rows:], got[:sub_rows]], 0)
-    others = gathered(jnp.concatenate([got, permuted(got, mirror)], 0), PLANE)
-    others = others.reshape(-1, emb.shape[1])
+    near = gathered(jnp.concatenate([got[sub_rows:], got[:sub_rows]], 0), PLANE)
 
-    logits = scale * contract_last(emb, others) + shift_by
-    row = lax.broadcasted_iota(jnp.int32, logits.shape, 0) - sub * (N_CORE * sub_rows)
-    col = lax.broadcasted_iota(jnp.int32, logits.shape, 1) - (y * N_X + x) * (
-        N_ZH * N_CORE * sub_rows
-    )
-    same = (row == col) & (row >= 0) & (row < N_CORE * sub_rows)
-    sign = jnp.where(same, f32(1.0), f32(-1.0))
-    coef = (-weight * sign * jax.nn.sigmoid(-sign * logits)).astype(bf16)
-    part = jnp.dot(coef, others, preferred_element_type=f32).astype(bf16)
+    def weigh(others, with_own):
+        logits = scale * contract_last(emb, others) + shift_by
+        sign = f32(-1.0)
+        if with_own:
+            row = lax.broadcasted_iota(jnp.int32, logits.shape, 0) - sub * (N_CORE * sub_rows)
+            col = lax.broadcasted_iota(jnp.int32, logits.shape, 1) - (y * N_X + x) * (
+                N_CORE * sub_rows
+            )
+            same = (row == col) & (row >= 0) & (row < N_CORE * sub_rows)
+            sign = jnp.where(same, f32(1.0), f32(-1.0))
+        coef = (-weight * sign * jax.nn.sigmoid(-sign * logits)).astype(bf16)
+        return jnp.dot(coef, others, preferred_element_type=f32)
 
-    pieces = exchanged(part.reshape(N_BLK, N_CORE * sub_rows, -1), LINE)
-    grad_unit = scale * jnp.sum(pieces.astype(f32), 0)
-    unit_sub = lax.dynamic_slice_in_dim(unit, sub * N_CORE * sub_rows, N_CORE * sub_rows, 0)
-    inv_sub = lax.dynamic_slice_in_dim(inverse, sub * N_CORE * sub_rows, N_CORE * sub_rows, 0)
-    inner = jnp.sum(unit_sub * grad_unit, axis=1, keepdims=True)
-    du = ((grad_unit - unit_sub * inner) * inv_sub).astype(bf16)
-    du = gathered(du, LINE).reshape(own, -1)
+    near, far = near.reshape(-1, embed), far.reshape(-1, embed)
+    grad_unit = scale * (weigh(near, True) + weigh(far, False))
+    inner = jnp.sum(unit * grad_unit, axis=1, keepdims=True)
+    part = ((grad_unit - unit * inner) * inverse).astype(bf16)
 
-    terms = contract_first(du, feat).astype(bf16)
-    terms = exchanged(terms.reshape(N_Y * N_X, N_ZH * PAIR, width), PLANE)
-    terms = jnp.sum(terms.astype(f32), 0)
-    lower, upper = terms[:PAIR], terms[PAIR:]
-    came = permuted(jnp.where(low, upper, lower).astype(bf16), mirror)
-    total = jnp.where(low, lower, upper) + came.astype(f32)
+    terms = contract_first(part, feat).astype(bf16)
+    terms = exchanged(terms.reshape(N_Y * N_X, embed // (N_Y * N_X), width), PLANE)
+    pieces = exchanged(part.reshape(N_BLK, N_CORE * sub_rows, embed), LINE)
+    terms = jnp.sum(terms.astype(f32), 0).astype(bf16).reshape(N_ZH, N_CORE * cols, width)
+    terms = jnp.pad(terms, ((0, 0), (0, -N_CORE * cols % N_BLK), (0, 0)))
+    terms = exchanged(terms.reshape(N_ZH * N_BLK, -1, width), RING)
+    terms = gathered(jnp.sum(terms.astype(f32), 0).astype(bf16), LINE)
+    total = terms.reshape(-1, width).astype(f32)
     keep_g = jnp.where(first, total[:cols], total[cols : 2 * cols])
     got_g = permuted(jnp.where(first, total[cols : 2 * cols], total[:cols]), sibling)
     img_proj_grad = jnp.where(first, keep_g, got_g).T
     txt_proj_grad = jnp.where(first, got_g, keep_g).T
 
+    du = gathered(jnp.sum(pieces.astype(f32), 0).astype(bf16), LINE).reshape(own, embed)
     grad = jnp.dot(du, proj, preferred_element_type=f32)
     grad = grad.reshape(N_BLK, N_CORE, sub_rows, width)
     keep_r = grad[:, 0].reshape(rows, width)

time: 289 us -> 310 us (1.073)
  waiting for transfers between devices: 150 us -> 104 us
  starting transfers between devices: 60.7 us -> 90.5 us
  blocking collectives: 45.1 us -> 64 us
  local copies, waits for them, and re-layouts: 5.42 us -> 16.9 us
  matrix products: 11.6 us -> 16.3 us
  other arithmetic: 9.71 us -> 14 us
    all_to_all x4 -> x7, waiting for transfers between devices: 127 us -> 83.7 us  [exchanged(): lax.all_to_all(value, BOTH, 0, 0, axis_index_groups=groups, tiled=True)]
    all_to_all x4 -> x7, starting transfers between devices: 20.8 us -> 42.5 us  [exchanged(): lax.all_to_all(value, BOTH, 0, 0, axis_index_groups=groups, tiled=True)]
    all_to_all x1 -> x2, blocking collectives: 45.1 us -> 64 us  [exchanged(): lax.all_to_all(value, BOTH, 0, 0, axis_index_groups=groups, tiled=True)]
    ppermute x8 -> x7, starting transfers between devices: 39.9 us -> 48 us  [permuted(): return lax.ppermute(value, BOTH, pairs)]
    broadcast_in_dim x3 -> x6, local copies, waits for them, and re-layouts: 3.61 us -> 8.74 us  [gathered(): copies = jnp.broadcast_to(value[None], (count,) + value.shape)]
    dot_general x1 -> x2, matrix products: 3.7 us -> 8.6 us  [weigh(): return jnp.dot(coef, others, preferred_element_type=f32)]
    reshape x0 -> x4, local copies, waits for them, and re-layouts: none -> 4.54 us  [the longest x2 4.43 us: body(): proj = proj.reshape(-1, width)]
    ppermute x8 -> x7, waiting for transfers between devices: 22.3 us -> 20.3 us  [permuted(): return lax.ppermute(value, BOTH, pairs)]
  transfers between devices with their start and end apart: 12 -> 14, of which waited for: 9 -> 13; matrix products, arithmetic and copies ran while one was open for 3% -> 4% of each run, Pallas kernels for 0% -> 0%
where the time goes in v2:
time: 310 us; the launch traced here: 309 us
  waiting for transfers between devices  104 us (34%)
  starting transfers between devices  90.5 us (29%)
  blocking collectives  64 us (21%)
  local copies, waits for them, and re-layouts  16.9 us (5%)
  matrix products  16.3 us (5%)
  other arithmetic  14 us (5%)
    all_to_all x7, waiting for transfers between devices, exchanged(): lax.all_to_all(value, BOTH, 0, 0, axis_index_groups=groups, tiled=True)  83.7 us
    all_to_all x2, blocking collectives, exchanged(): lax.all_to_all(value, BOTH, 0, 0, axis_index_groups=groups, tiled=True)  64 us
    ppermute x7, starting transfers between devices, permuted(): return lax.ppermute(value, BOTH, pairs)  48 us
    all_to_all x7, starting transfers between devices, exchanged(): lax.all_to_all(value, BOTH, 0, 0, axis_index_groups=groups, tiled=True)  42.5 us
    ppermute x7, waiting for transfers between devices, permuted(): return lax.ppermute(value, BOTH, pairs)  20.3 us
    broadcast_in_dim x6, local copies, waits for them, and re-layouts, gathered(): copies = jnp.broadcast_to(value[None], (count,) + value.shape)  8.74 us
    dot_general x2, matrix products, weigh(): return jnp.dot(coef, others, preferred_element_type=f32)  8.6 us
  transfers between devices with their start and end apart: 14, of which 13 were waited for; matrix products, arithmetic and copies ran while one was open for 4% of the time, Pallas kernels for 0%

profile of v2, /device:TPU:1, one launch (start us, length us, event | category | flops | bytes accessed | tf_op | source)
XLA Modules:
  0.0 308.6 jit_solution(17400939247937701180)
XLA Ops:
  1.5 8.8 %collective-permute-start.1 = (bf16[18,1152]{1,0:T(8,128)(2,1)S(1)}, bf16[18,1152]{1,0:T(8,128)(2,1)S(1)}, u32[]{:S(2)}, u32[]{:S(2)}) collective-permute-start(bf16[18,1152]{1,0:T(8,128)(2,1)S(1)} %select_bitcast_fusion.4), channel_id=1, source_target_pairs={{0,1},{1,0},{2,3},{3,2},{4,5},{5,4},{6,7},{7,6},{8,9},{9,8},{10,11... | collective-permute-start | bytes 124424 | tf_op jit(solution)/shard_map/ppermute | solution.py:55
  13.3 3.7 %all-to-all-start = ((bf16[16,36,1152]{2,1,0:T(8,128)(2,1)}), bf16[16,36,1152]{2,1,0:T(8,128)(2,1)S(1)}, u32[]{:S(2)}, u32[]{:S(2)}) async-start(bf16[16,36,1152]{2,1,0:T(8,128)(2,1)} %broadcast_in_dim.22), calls=%async_computation | async-start | bytes 2949120 | tf_op jit(solution)/shard_map/all_to_all | solution.py:59
  17.0 8.8 %collective-permute-start.2 = (bf16[36,1152]{1,0:T(8,128)(2,1)S(1)}, bf16[36,1152]{1,0:T(8,128)(2,1)S(1)}, u32[]{:S(2)}, u32[]{:S(2)}) collective-permute-start(bf16[36,1152]{1,0:T(8,128)(2,1)S(1)} %pad_maximum_fusion.2), channel_id=1, source_target_pairs={{0,456},{1,457},{2,458},{3,459},{4,460},{5,461},{6,462},{7,463},{8... | collective-permute-start | bytes 248840 | tf_op jit(solution)/shard_map/ppermute | solution.py:55
  25.8 8.6 %collective-permute-done.2 = bf16[36,1152]{1,0:T(8,128)(2,1)S(1)} collective-permute-done((bf16[36,1152]{1,0:T(8,128)(2,1)S(1)}, bf16[36,1152]{1,0:T(8,128)(2,1)S(1)}, u32[]{:S(2)}, u32[]{:S(2)}) %collective-permute-start.2) | collective-permute-done | bytes 82976 | tf_op jit(solution)/shard_map/ppermute | solution.py:55
  34.4 6.3 %all-to-all-done = bf16[16,36,1152]{2,1,0:T(8,128)(2,1)S(1)} async-done(((bf16[16,36,1152]{2,1,0:T(8,128)(2,1)}), bf16[16,36,1152]{2,1,0:T(8,128)(2,1)S(1)}, u32[]{:S(2)}, u32[]{:S(2)}) %all-to-all-start) | async-done | bytes 1327136 | tf_op jit(solution)/shard_map/all_to_all | solution.py:59
  42.0 3.8 %all-to-all-start.1 = ((bf16[16,36,1152]{2,1,0:T(8,128)(2,1)}), bf16[16,36,1152]{2,1,0:T(8,128)(2,1)S(1)}, u32[]{:S(2)}, u32[]{:S(2)}) async-start(bf16[16,36,1152]{2,1,0:T(8,128)(2,1)} %broadcast_in_dim.23), calls=%async_computation.1 | async-start | bytes 2949120 | tf_op jit(solution)/shard_map/all_to_all | solution.py:59
  46.7 3.1 collective-permute-start
  53.0 13.2 %all-to-all-done.1 = bf16[16,36,1152]{2,1,0:T(8,128)(2,1)S(1)} async-done(((bf16[16,36,1152]{2,1,0:T(8,128)(2,1)}), bf16[16,36,1152]{2,1,0:T(8,128)(2,1)S(1)}, u32[]{:S(2)}, u32[]{:S(2)}) %all-to-all-start.1) | async-done | bytes 1327136 | tf_op jit(solution)/shard_map/all_to_all | solution.py:59
  66.8 2.2 reshape.54
  69.0 2.9 multiply_reduce_fusion.1
  73.9 5.3 %collective-permute-start.3 = (bf16[32,1152]{1,0:T(8,128)(2,1)S(1)}, bf16[32,1152]{1,0:T(8,128)(2,1)S(1)}, u32[]{:S(2)}, u32[]{:S(2)}) collective-permute-start(bf16[32,1152]{1,0:T(8,128)(2,1)S(1)} %constant_dynamic-slice_fusion), channel_id=1, source_target_pairs={{0,1},{1,0},{2,3},{3,2},{4,5},{5,4},{6,7},{7,6},{8,9},{9,8},{10,11... | collective-permute-start | bytes 221192 | tf_op jit(solution)/shard_map/ppermute | solution.py:55
  81.3 4.4 %all-to-all-start.2 = ((bf16[16,32,1152]{2,1,0:T(8,128)(2,1)}), bf16[16,32,1152]{2,1,0:T(8,128)(2,1)}, u32[]{:S(2)}, u32[]{:S(2)}) async-start(bf16[16,32,1152]{2,1,0:T(8,128)(2,1)} %broadcast_in_dim.24), calls=%async_computation.2 | async-start | bytes 2359296 | tf_op jit(solution)/shard_map/all_to_all | solution.py:59
  85.7 8.1 %collective-permute-start.4 = (bf16[32,1152]{1,0:T(8,128)(2,1)}, bf16[32,1152]{1,0:T(8,128)(2,1)}, u32[]{:S(2)}, u32[]{:S(2)}) collective-permute-start(bf16[32,1152]{1,0:T(8,128)(2,1)} %copy-done.5), channel_id=1, source_target_pairs={{0,457},{1,456},{2,459},{3,458},{4,461},{5,460},{6,463},{7,462},{8... | collective-permute-start | bytes 221192 | tf_op jit(solution)/shard_map/ppermute | solution.py:55
  93.8 7.3 %collective-permute-done.4 = bf16[32,1152]{1,0:T(8,128)(2,1)} collective-permute-done((bf16[32,1152]{1,0:T(8,128)(2,1)}, bf16[32,1152]{1,0:T(8,128)(2,1)}, u32[]{:S(2)}, u32[]{:S(2)}) %collective-permute-start.4) | collective-permute-done | bytes 73760 | tf_op jit(solution)/shard_map/ppermute | solution.py:55
  101.1 3.9 %all-to-all-done.2 = bf16[16,32,1152]{2,1,0:T(8,128)(2,1)} async-done(((bf16[16,32,1152]{2,1,0:T(8,128)(2,1)}), bf16[16,32,1152]{2,1,0:T(8,128)(2,1)}, u32[]{:S(2)}, u32[]{:S(2)}) %all-to-all-start.2) | async-done | bytes 1179680 | tf_op jit(solution)/shard_map/all_to_all | solution.py:59
  107.0 4.4 %all-to-all-start.3 = ((bf16[16,32,1152]{2,1,0:T(8,128)(2,1)}), bf16[16,32,1152]{2,1,0:T(8,128)(2,1)}, u32[]{:S(2)}, u32[]{:S(2)}) async-start(bf16[16,32,1152]{2,1,0:T(8,128)(2,1)} %broadcast_in_dim.25), calls=%async_computation.3 | async-start | bytes 2359296 | tf_op jit(solution)/shard_map/all_to_all | solution.py:59
  114.0 4.0 %fusion.18 = f32[256,1152]{1,0:T(8,128)} fusion(bf16[512,1152]{1,0:T(8,128)(2,1)} %bitcast.10, bf16[256,1152]{1,0:T(8,128)(2,1)} %copy-done.1, f32[]{:T(128)} %bitcast.46, f32[]{:T(128)} %bitcast.45, s32[512]{0:T(512)S(1)} %iota_subtract_fusion, f32[]{:T(128)} %bitcast.1, s32[256]{0:T(256)S(1)} %iota_subtract_fusion.1, ...), kind=kOutput, calls=%fused_computation.28 | convolution fusion | flops 605814784 | bytes 2952716 | tf_op jit(solution)/shard_map/dot_general | solution.py:135
  117.9 10.3 %all-to-all-done.3 = bf16[16,32,1152]{2,1,0:T(8,128)(2,1)} async-done(((bf16[16,32,1152]{2,1,0:T(8,128)(2,1)}), bf16[16,32,1152]{2,1,0:T(8,128)(2,1)}, u32[]{:S(2)}, u32[]{:S(2)}) %all-to-all-start.3) | async-done | bytes 1179680 | tf_op jit(solution)/shard_map/all_to_all | solution.py:59
  128.3 4.6 %multiply_reduce_fusion = (f32[256]{0:T(256)S(1)}, f32[256,1152]{1,0:T(8,128)}) fusion(f32[256,1152]{1,0:T(8,128)} %copy-done, f32[256]{0:T(256)S(1)} %add_rsqrt_fusion, f32[256,1152]{1,0:T(8,128)} %fusion.18, bf16[512,1152]{1,0:T(8,128)(2,1)} %bitcast.12, bf16[256,1152]{1,0:T(8,128)(2,1)} %copy-done.1, f32[]{:T(128)S(6)} %mul.89, f32[]{:T(128)} %bitcast.47, ...), kind=kOutput, calls=%fused_computation.26 | convolution fusion | flops 606371584 | bytes 5310476 | tf_op jit(solution)/shard_map/dot_general | solution.py:135
  132.9 2.7 multiply_convert_fusion
  137.6 38.0 %all_to_all.45 = bf16[16,72,1152]{2,1,0:T(8,128)(2,1)} all-to-all(bf16[16,72,1152]{2,1,0:T(8,128)(2,1)S(1)} %bitcast.48), channel_id=1, replica_groups={{0,2,4,6,16,18,20,22,32,34,36,38,48,50,52,54},{1,3,5,7,17,19,21,23,33,3..., dimensions={0} | all-to-all | bytes 5308416 | tf_op jit(solution)/shard_map/all_to_all | solution.py:59
  175.7 2.2 reduce_sum.57
  178.0 25.9 %all_to_all.46 = bf16[16,5,1152]{2,1,0:T(8,128)(2,1)} all-to-all(bf16[16,5,1152]{2,1,0:T(8,128)(2,1)S(1)} %reshape.60), channel_id=1, replica_groups={{0,64,128,192,256,320,384,448,456,392,328,264,200,136,72,8},{1,65,129,1..., dimensions={0} | all-to-all | bytes 368640 | tf_op jit(solution)/shard_map/all_to_all | solution.py:59
  203.9 8.0 %all-to-all-start.4 = ((bf16[8,32,1152]{2,1,0:T(8,128)(2,1)}), bf16[8,32,1152]{2,1,0:T(8,128)(2,1)S(1)}, u32[]{:S(2)}, u32[]{:S(2)}) async-start(bf16[8,32,1152]{2,1,0:T(8,128)(2,1)} %bitcast.13), calls=%async_computation.4 | async-start | bytes 1179648 | tf_op jit(solution)/shard_map/all_to_all | solution.py:59
  213.6 20.8 %all-to-all-done.4 = bf16[8,32,1152]{2,1,0:T(8,128)(2,1)S(1)} async-done(((bf16[8,32,1152]{2,1,0:T(8,128)(2,1)}), bf16[8,32,1152]{2,1,0:T(8,128)(2,1)S(1)}, u32[]{:S(2)}, u32[]{:S(2)}) %all-to-all-start.4) | async-done | bytes 589856 | tf_op jit(solution)/shard_map/all_to_all | solution.py:59
  235.8 12.5 %all-to-all-start.8 = ((bf16[8,5,1152]{2,1,0:T(8,128)(2,1)}), bf16[8,5,1152]{2,1,0:T(8,128)(2,1)}, u32[]{:S(2)}, u32[]{:S(2)}) async-start(bf16[8,5,1152]{2,1,0:T(8,128)(2,1)} %broadcast_in_dim.27), calls=%async_computation.8 | async-start | bytes 294912 | tf_op jit(solution)/shard_map/all_to_all | solution.py:59
  249.0 10.0 %all-to-all-done.8 = bf16[8,5,1152]{2,1,0:T(8,128)(2,1)} async-done(((bf16[8,5,1152]{2,1,0:T(8,128)(2,1)}), bf16[8,5,1152]{2,1,0:T(8,128)(2,1)}, u32[]{:S(2)}, u32[]{:S(2)}) %all-to-all-start.8) | async-done | bytes 92192 | tf_op jit(solution)/shard_map/all_to_all | solution.py:59
  260.7 5.7 %all-to-all-start.5 = ((bf16[8,32,1152]{2,1,0:T(8,128)(2,1)}), bf16[8,32,1152]{2,1,0:T(8,128)(2,1)S(1)}, u32[]{:S(2)}, u32[]{:S(2)}) async-start(bf16[8,32,1152]{2,1,0:T(8,128)(2,1)} %broadcast_in_dim.26), calls=%async_computation.5 | async-start | bytes 1179648 | tf_op jit(solution)/shard_map/all_to_all | solution.py:59
  266.4 2.2 reshape.62
  269.5 19.2 %all-to-all-done.5 = bf16[8,32,1152]{2,1,0:T(8,128)(2,1)S(1)} async-done(((bf16[8,32,1152]{2,1,0:T(8,128)(2,1)}), bf16[8,32,1152]{2,1,0:T(8,128)(2,1)S(1)}, u32[]{:S(2)}, u32[]{:S(2)}) %all-to-all-start.5) | async-done | bytes 589856 | tf_op jit(solution)/shard_map/all_to_all | solution.py:59
  288.7 2.7 fusion.1
  291.6 12.0 %collective-permute-start.5 = (f32[128,1152]{1,0:T(8,128)S(1)}, f32[128,1152]{1,0:T(8,128)S(1)}, u32[]{:S(2)}, u32[]{:S(2)}) collective-permute-start(f32[128,1152]{1,0:T(8,128)S(1)} %bitcast.53), channel_id=1, source_target_pairs={{0,1},{1,0},{2,3},{3,2},{4,5},{5,4},{6,7},{7,6},{8,9},{9,8},{10,11... | collective-permute-start | bytes 1769480 | tf_op jit(solution)/shard_map/ppermute | solution.py:55
  (50 shorter events, 30.0 us)
Async XLA Ops:
  1.5 9.7 %collective-permute-start.1 = (bf16[18,1152]{1,0:T(8,128)(2,1)S(1)}, bf16[18,1152]{1,0:T(8,128)(2,1)S(1)}, u32[]{:S(2)}, u32[]{:S(2)}) collective-permute-start(bf16[18,1152]{1,0:T(8,128)(2,1)S(1)} %select_bitcast_fusion.4), channel_id=1, source_target_pairs={{0,1},{1,0},{2,3},{3,2},{4,5},{5,4},{6,7},{7,6},{8,9},{9,8},{10,11... | collective-permute-start | bytes 124424 | tf_op jit(solution)/shard_map/ppermute | solution.py:55
  13.3 27.4 %all-to-all-start = ((bf16[16,36,1152]{2,1,0:T(8,128)(2,1)}), bf16[16,36,1152]{2,1,0:T(8,128)(2,1)S(1)}, u32[]{:S(2)}, u32[]{:S(2)}) async-start(bf16[16,36,1152]{2,1,0:T(8,128)(2,1)} %broadcast_in_dim.22), calls=%async_computation | async-start | bytes 2949120 | tf_op jit(solution)/shard_map/all_to_all | solution.py:59
  17.0 17.4 %collective-permute-start.2 = (bf16[36,1152]{1,0:T(8,128)(2,1)S(1)}, bf16[36,1152]{1,0:T(8,128)(2,1)S(1)}, u32[]{:S(2)}, u32[]{:S(2)}) collective-permute-start(bf16[36,1152]{1,0:T(8,128)(2,1)S(1)} %pad_maximum_fusion.2), channel_id=1, source_target_pairs={{0,456},{1,457},{2,458},{3,459},{4,460},{5,461},{6,462},{7,463},{8... | collective-permute-start | bytes 248840 | tf_op jit(solution)/shard_map/ppermute | solution.py:55
  41.9 3.9 %copy-start.2 = (bf16[128,1152]{1,0:T(8,128)(2,1)S(1)}, bf16[128,1152]{1,0:T(8,128)(2,1)}, u32[]{:S(2)}) copy-start(bf16[128,1152]{1,0:T(8,128)(2,1)} %param.7) | copy-start | bytes 884740
  42.0 3.9 %copy-start.3 = (bf16[128,1152]{1,0:T(8,128)(2,1)S(1)}, bf16[128,1152]{1,0:T(8,128)(2,1)}, u32[]{:S(2)}) copy-start(bf16[128,1152]{1,0:T(8,128)(2,1)} %param.8) | copy-start | bytes 884740
  42.0 24.2 %all-to-all-start.1 = ((bf16[16,36,1152]{2,1,0:T(8,128)(2,1)}), bf16[16,36,1152]{2,1,0:T(8,128)(2,1)S(1)}, u32[]{:S(2)}, u32[]{:S(2)}) async-start(bf16[16,36,1152]{2,1,0:T(8,128)(2,1)} %broadcast_in_dim.23), calls=%async_computation.1 | async-start | bytes 2949120 | tf_op jit(solution)/shard_map/all_to_all | solution.py:59
  46.7 4.5 %collective-permute-start = (bf16[128,1152]{1,0:T(8,128)(2,1)}, bf16[128,1152]{1,0:T(8,128)(2,1)S(1)}, u32[]{:S(2)}, u32[]{:S(2)}) collective-permute-start(bf16[128,1152]{1,0:T(8,128)(2,1)} %get-tuple-element.11), channel_id=1, source_target_pairs={{0,1},{1,0},{2,3},{3,2},{4,5},{5,4},{6,7},{7,6},{8,9},{9,8},{10,11... | collective-permute-start | bytes 884744 | tf_op jit(solution)/shard_map/ppermute | solution.py:55
  51.2 0.7 copy-start.4
  71.9 1.0 copy-start
  73.1 0.8 copy-start.1
  73.9 5.3 %copy-start.5 = (bf16[32,1152]{1,0:T(8,128)(2,1)}, bf16[32,1152]{1,0:T(8,128)(2,1)S(1)}, u32[]{:S(2)}) copy-start(bf16[32,1152]{1,0:T(8,128)(2,1)S(1)} %constant_dynamic-slice_fusion) | copy-start | bytes 221188
  73.9 6.2 %collective-permute-start.3 = (bf16[32,1152]{1,0:T(8,128)(2,1)S(1)}, bf16[32,1152]{1,0:T(8,128)(2,1)S(1)}, u32[]{:S(2)}, u32[]{:S(2)}) collective-permute-start(bf16[32,1152]{1,0:T(8,128)(2,1)S(1)} %constant_dynamic-slice_fusion), channel_id=1, source_target_pairs={{0,1},{1,0},{2,3},{3,2},{4,5},{5,4},{6,7},{7,6},{8,9},{9,8},{10,11... | collective-permute-start | bytes 221192 | tf_op jit(solution)/shard_map/ppermute | solution.py:55
  81.3 23.7 %all-to-all-start.2 = ((bf16[16,32,1152]{2,1,0:T(8,128)(2,1)}), bf16[16,32,1152]{2,1,0:T(8,128)(2,1)}, u32[]{:S(2)}, u32[]{:S(2)}) async-start(bf16[16,32,1152]{2,1,0:T(8,128)(2,1)} %broadcast_in_dim.24), calls=%async_computation.2 | async-start | bytes 2359296 | tf_op jit(solution)/shard_map/all_to_all | solution.py:59
  85.7 15.5 %collective-permute-start.4 = (bf16[32,1152]{1,0:T(8,128)(2,1)}, bf16[32,1152]{1,0:T(8,128)(2,1)}, u32[]{:S(2)}, u32[]{:S(2)}) collective-permute-start(bf16[32,1152]{1,0:T(8,128)(2,1)} %copy-done.5), channel_id=1, source_target_pairs={{0,457},{1,456},{2,459},{3,458},{4,461},{5,460},{6,463},{7,462},{8... | collective-permute-start | bytes 221192 | tf_op jit(solution)/shard_map/ppermute | solution.py:55
  107.0 21.3 %all-to-all-start.3 = ((bf16[16,32,1152]{2,1,0:T(8,128)(2,1)}), bf16[16,32,1152]{2,1,0:T(8,128)(2,1)}, u32[]{:S(2)}, u32[]{:S(2)}) async-start(bf16[16,32,1152]{2,1,0:T(8,128)(2,1)} %broadcast_in_dim.25), calls=%async_computation.3 | async-start | bytes 2359296 | tf_op jit(solution)/shard_map/all_to_all | solution.py:59
  203.9 30.5 %all-to-all-start.4 = ((bf16[8,32,1152]{2,1,0:T(8,128)(2,1)}), bf16[8,32,1152]{2,1,0:T(8,128)(2,1)S(1)}, u32[]{:S(2)}, u32[]{:S(2)}) async-start(bf16[8,32,1152]{2,1,0:T(8,128)(2,1)} %bitcast.13), calls=%async_computation.4 | async-start | bytes 1179648 | tf_op jit(solution)/shard_map/all_to_all | solution.py:59
  235.8 23.2 %all-to-all-start.8 = ((bf16[8,5,1152]{2,1,0:T(8,128)(2,1)}), bf16[8,5,1152]{2,1,0:T(8,128)(2,1)}, u32[]{:S(2)}, u32[]{:S(2)}) async-start(bf16[8,5,1152]{2,1,0:T(8,128)(2,1)} %broadcast_in_dim.27), calls=%async_computation.8 | async-start | bytes 294912 | tf_op jit(solution)/shard_map/all_to_all | solution.py:59
  260.7 28.0 %all-to-all-start.5 = ((bf16[8,32,1152]{2,1,0:T(8,128)(2,1)}), bf16[8,32,1152]{2,1,0:T(8,128)(2,1)S(1)}, u32[]{:S(2)}, u32[]{:S(2)}) async-start(bf16[8,32,1152]{2,1,0:T(8,128)(2,1)} %broadcast_in_dim.26), calls=%async_computation.5 | async-start | bytes 1179648 | tf_op jit(solution)/shard_map/all_to_all | solution.py:59
  291.6 16.0 %collective-permute-start.5 = (f32[128,1152]{1,0:T(8,128)S(1)}, f32[128,1152]{1,0:T(8,128)S(1)}, u32[]{:S(2)}, u32[]{:S(2)}) collective-permute-start(f32[128,1152]{1,0:T(8,128)S(1)} %bitcast.53), channel_id=1, source_target_pairs={{0,1},{1,0},{2,3},{3,2},{4,5},{5,4},{6,7},{7,6},{8,9},{9,8},{10,11... | collective-permute-start | bytes 1769480 | tf_op jit(solution)/shard_map/ppermute | solution.py:55
  303.6 3.2 %collective-permute-start.6 = (f32[18,1152]{1,0:T(8,128)S(1)}, f32[18,1152]{1,0:T(8,128)S(1)}, u32[]{:S(2)}, u32[]{:S(2)}) collective-permute-start(f32[18,1152]{1,0:T(8,128)S(1)} %slice_select_fusion), channel_id=1, source_target_pairs={{0,1},{1,0},{2,3},{3,2},{4,5},{5,4},{6,7},{7,6},{8,9},{9,8},{10,11... | collective-permute-start | bytes 248840 | tf_op jit(solution)/shard_map/ppermute | solution.py:55

commit v3 on v2

--- a/solution.py
+++ b/solution.py
@@ -29,26 +29,16 @@
     return place(N_BLK - 1 - blk, y, 1 - zh, x, core)
 
 
+def along(hop):
+    return lambda device: device ^ (hop * N_GRP)
+
+
 PLANE = [
     [place(blk, y, zh, x, core) for y in range(N_Y) for x in range(N_X)]
     for blk in range(N_BLK)
     for zh in range(N_ZH)
     for core in range(N_CORE)
 ]
-LINE = [
-    [place(sub if zh == 0 else N_BLK - 1 - sub, y, zh, x, core) for sub in range(N_BLK)]
-    for y in range(N_Y)
-    for zh in range(N_ZH)
-    for x in range(N_X)
-    for core in range(N_CORE)
-]
-RING = [
-    LINE[(y * N_ZH * N_X + x) * N_CORE + core] + LINE[(y * N_ZH * N_X + N_X + x) * N_CORE + core]
-    for y in range(N_Y)
-    for x in range(N_X)
-    for core in range(N_CORE)
-]
-
 
 def permuted(value, target):
     pairs = [(source, target(source)) for source in range(N_BLK * N_GRP)]
@@ -89,7 +79,8 @@
     zh = (grp // (N_CORE * N_X)) % N_ZH
     y = grp // (N_CORE * N_X * N_ZH)
     first = core == 0
-    sub = jnp.where(zh == 0, blk, N_BLK - 1 - blk)
+    steps = jnp.where(zh == 0, blk, N_BLK - 1 - blk)
+    sub = (steps & 1) * 4 + (steps & 2) + (steps & 4) // 4
     sub_rows = rows // N_BLK
     own = N_CORE * rows
 
@@ -141,18 +132,31 @@
 
     terms = contract_first(part, feat).astype(bf16)
     terms = exchanged(terms.reshape(N_Y * N_X, embed // (N_Y * N_X), width), PLANE)
-    pieces = exchanged(part.reshape(N_BLK, N_CORE * sub_rows, embed), LINE)
-    terms = jnp.sum(terms.astype(f32), 0).astype(bf16).reshape(N_ZH, N_CORE * cols, width)
-    terms = jnp.pad(terms, ((0, 0), (0, -N_CORE * cols % N_BLK), (0, 0)))
-    terms = exchanged(terms.reshape(N_ZH * N_BLK, -1, width), RING)
-    terms = gathered(jnp.sum(terms.astype(f32), 0).astype(bf16), LINE)
-    total = terms.reshape(-1, width).astype(f32)
+    held = part.astype(f32)
+    for bit, hop in ((4, 1), (2, 2), (1, 4)):
+        half = held.shape[0] // 2
+        high = (sub & bit) // bit
+        send = lax.dynamic_slice_in_dim(held, (1 - high) * half, half, 0).astype(bf16)
+        stay = lax.dynamic_slice_in_dim(held, high * half, half, 0)
+        held = stay + permuted(send, along(hop)).astype(f32)
+    du = held.astype(bf16)
+    for bit, hop in ((1, 4), (2, 2), (4, 1)):
+        came = permuted(du, along(hop))
+        high = (sub & bit) > 0
+        du = jnp.concatenate([jnp.where(high, came, du), jnp.where(high, du, came)], 0)
+
+    terms = jnp.sum(terms.astype(f32), 0)
+    lower, upper = terms[: N_CORE * cols], terms[N_CORE * cols :]
+    came = permuted(jnp.where(low, upper, lower).astype(bf16), mirror)
+    total = jnp.where(low, lower, upper) + came.astype(f32)
+    for hop in (1, 2, 4):
+        sent = total.astype(bf16)
+        total = sent.astype(f32) + permuted(sent, along(hop)).astype(f32)
     keep_g = jnp.where(first, total[:cols], total[cols : 2 * cols])
     got_g = permuted(jnp.where(first, total[cols : 2 * cols], total[:cols]), sibling)
     img_proj_grad = jnp.where(first, keep_g, got_g).T
     txt_proj_grad = jnp.where(first, got_g, keep_g).T
 
-    du = gathered(jnp.sum(pieces.astype(f32), 0).astype(bf16), LINE).reshape(own, embed)
     grad = jnp.dot(du, proj, preferred_element_type=f32)
     grad = grad.reshape(N_BLK, N_CORE, sub_rows, width)
     keep_r = grad[:, 0].reshape(rows, width)

time: 310 us -> 252 us (0.81)
  the two profiles are of different devices: /device:TPU:1 before, /device:TPU:5 now
where the time goes in v3:
time: 252 us; the launch traced here: 251 us
  starting transfers between devices  114 us (45%)
  waiting for transfers between devices  88.6 us (35%)
  local copies, waits for them, and re-layouts  16 us (6%)
  matrix products  14.7 us (6%)
  other arithmetic  14.4 us (6%)
  between operations  3.15 us (1%)
    ppermute x17, starting transfers between devices, permuted(): return lax.ppermute(value, BOTH, pairs)  78.5 us
    ppermute x17, waiting for transfers between devices, permuted(): return lax.ppermute(value, BOTH, pairs)  61.6 us
    all_to_all x5, starting transfers between devices, exchanged(): lax.all_to_all(value, BOTH, 0, 0, axis_index_groups=groups, tiled=True)  35.6 us
    all_to_all x5, waiting for transfers between devices, exchanged(): lax.all_to_all(value, BOTH, 0, 0, axis_index_groups=groups, tiled=True)  27 us
    dot_general x2, matrix products, weigh(): return jnp.dot(coef, others, preferred_element_type=f32)  8.28 us
    broadcast_in_dim x4, local copies, waits for them, and re-layouts, gathered(): copies = jnp.broadcast_to(value[None], (count,) + value.shape)  5.63 us
  transfers between devices with their start and end apart: 22, of which 18 were waited for; matrix products, arithmetic and copies ran while one was open for 7% of the time, Pallas kernels for 0%

profile of v3, /device:TPU:5, one launch (start us, length us, event | category | flops | bytes accessed | tf_op | source)
XLA Modules:
  0.0 251.0 jit_solution(4332282391577667525)
XLA Ops:
  1.5 2.6 %collective-permute-start.1 = (bf16[18,1152]{1,0:T(8,128)(2,1)S(1)}, bf16[18,1152]{1,0:T(8,128)(2,1)S(1)}, u32[]{:S(2)}, u32[]{:S(2)}) collective-permute-start(bf16[18,1152]{1,0:T(8,128)(2,1)S(1)} %select_bitcast_fusion.4), channel_id=1, source_target_pairs={{0,1},{1,0},{2,3},{3,2},{4,5},{5,4},{6,7},{7,6},{8,9},{9,8},{10,11... | collective-permute-start | bytes 124424 | tf_op jit(solution)/shard_map/ppermute | solution.py:45
  7.1 9.1 %all-to-all-start = ((bf16[16,36,1152]{2,1,0:T(8,128)(2,1)}), bf16[16,36,1152]{2,1,0:T(8,128)(2,1)S(1)}, u32[]{:S(2)}, u32[]{:S(2)}) async-start(bf16[16,36,1152]{2,1,0:T(8,128)(2,1)} %broadcast_in_dim.16), calls=%async_computation | async-start | bytes 2949120 | tf_op jit(solution)/shard_map/all_to_all | solution.py:49
  16.2 8.9 %collective-permute-start.2 = (bf16[36,1152]{1,0:T(8,128)(2,1)S(1)}, bf16[36,1152]{1,0:T(8,128)(2,1)S(1)}, u32[]{:S(2)}, u32[]{:S(2)}) collective-permute-start(bf16[36,1152]{1,0:T(8,128)(2,1)S(1)} %pad_maximum_fusion.5), channel_id=1, source_target_pairs={{0,456},{1,457},{2,458},{3,459},{4,460},{5,461},{6,462},{7,463},{8... | collective-permute-start | bytes 248840 | tf_op jit(solution)/shard_map/ppermute | solution.py:45
  25.1 8.6 %collective-permute-done.2 = bf16[36,1152]{1,0:T(8,128)(2,1)S(1)} collective-permute-done((bf16[36,1152]{1,0:T(8,128)(2,1)S(1)}, bf16[36,1152]{1,0:T(8,128)(2,1)S(1)}, u32[]{:S(2)}, u32[]{:S(2)}) %collective-permute-start.2) | collective-permute-done | bytes 82976 | tf_op jit(solution)/shard_map/ppermute | solution.py:45
  33.7 3.4 %all-to-all-done = bf16[16,36,1152]{2,1,0:T(8,128)(2,1)S(1)} async-done(((bf16[16,36,1152]{2,1,0:T(8,128)(2,1)}), bf16[16,36,1152]{2,1,0:T(8,128)(2,1)S(1)}, u32[]{:S(2)}, u32[]{:S(2)}) %all-to-all-start) | async-done | bytes 1327136 | tf_op jit(solution)/shard_map/all_to_all | solution.py:49
  38.3 6.7 %all-to-all-start.1 = ((bf16[16,36,1152]{2,1,0:T(8,128)(2,1)}), bf16[16,36,1152]{2,1,0:T(8,128)(2,1)S(1)}, u32[]{:S(2)}, u32[]{:S(2)}) async-start(bf16[16,36,1152]{2,1,0:T(8,128)(2,1)} %broadcast_in_dim.17), calls=%async_computation.1 | async-start | bytes 2949120 | tf_op jit(solution)/shard_map/all_to_all | solution.py:49
  45.9 3.4 %collective-permute-start = (bf16[128,1152]{1,0:T(8,128)(2,1)}, bf16[128,1152]{1,0:T(8,128)(2,1)S(1)}, u32[]{:S(2)}, u32[]{:S(2)}) collective-permute-start(bf16[128,1152]{1,0:T(8,128)(2,1)} %get-tuple-element.15), channel_id=1, source_target_pairs={{0,1},{1,0},{2,3},{3,2},{4,5},{5,4},{6,7},{7,6},{8,9},{9,8},{10,11... | collective-permute-start | bytes 884744 | tf_op jit(solution)/shard_map/ppermute | solution.py:45
  52.5 12.4 %all-to-all-done.1 = bf16[16,36,1152]{2,1,0:T(8,128)(2,1)S(1)} async-done(((bf16[16,36,1152]{2,1,0:T(8,128)(2,1)}), bf16[16,36,1152]{2,1,0:T(8,128)(2,1)S(1)}, u32[]{:S(2)}, u32[]{:S(2)}) %all-to-all-start.1) | async-done | bytes 1327136 | tf_op jit(solution)/shard_map/all_to_all | solution.py:49
  67.8 2.9 %multiply_reduce_fusion.1 = (f32[256]{0:T(256)S(1)}, f32[256,1152]{1,0:T(8,128)S(1)}) fusion(bf16[256,1152]{1,0:T(8,128)(2,1)S(1)} %bitcast.48, bf16[1152,1152]{1,0:T(8,128)(2,1)} %reshape.38), kind=kOutput, calls=%fused_computation.28 | convolution fusion | flops 680066816 | bytes 4424704 | tf_op jit(solution)/shard_map/dot_general | solution.py:59
  71.9 2.4 collective-permute-start.3
  76.4 7.7 %all-to-all-start.2 = ((bf16[16,32,1152]{2,1,0:T(8,128)(2,1)}), bf16[16,32,1152]{2,1,0:T(8,128)(2,1)}, u32[]{:S(2)}, u32[]{:S(2)}) async-start(bf16[16,32,1152]{2,1,0:T(8,128)(2,1)} %broadcast_in_dim.18), calls=%async_computation.2 | async-start | bytes 2359296 | tf_op jit(solution)/shard_map/all_to_all | solution.py:49
  84.1 8.4 %collective-permute-start.4 = (bf16[32,1152]{1,0:T(8,128)(2,1)}, bf16[32,1152]{1,0:T(8,128)(2,1)}, u32[]{:S(2)}, u32[]{:S(2)}) collective-permute-start(bf16[32,1152]{1,0:T(8,128)(2,1)} %copy-done.11), channel_id=1, source_target_pairs={{0,457},{1,456},{2,459},{3,458},{4,461},{5,460},{6,463},{7,462},{8... | collective-permute-start | bytes 221192 | tf_op jit(solution)/shard_map/ppermute | solution.py:45
  92.5 7.3 %collective-permute-done.4 = bf16[32,1152]{1,0:T(8,128)(2,1)} collective-permute-done((bf16[32,1152]{1,0:T(8,128)(2,1)}, bf16[32,1152]{1,0:T(8,128)(2,1)}, u32[]{:S(2)}, u32[]{:S(2)}) %collective-permute-start.4) | collective-permute-done | bytes 73760 | tf_op jit(solution)/shard_map/ppermute | solution.py:45
  102.9 6.9 %all-to-all-start.3 = ((bf16[16,32,1152]{2,1,0:T(8,128)(2,1)}), bf16[16,32,1152]{2,1,0:T(8,128)(2,1)}, u32[]{:S(2)}, u32[]{:S(2)}) async-start(bf16[16,32,1152]{2,1,0:T(8,128)(2,1)} %broadcast_in_dim.21), calls=%async_computation.3 | async-start | bytes 2359296 | tf_op jit(solution)/shard_map/all_to_all | solution.py:49
  112.3 3.8 %fusion.18 = f32[256,1152]{1,0:T(8,128)} fusion(bf16[512,1152]{1,0:T(8,128)(2,1)} %bitcast.10, bf16[256,1152]{1,0:T(8,128)(2,1)S(1)} %multiply_convert_fusion.1, f32[]{:T(128)} %bitcast.45, f32[]{:T(128)} %bitcast.44, s32[512]{0:T(512)S(1)} %iota_subtract_fusion, f32[]{:T(128)} %bitcast.1, s32[256]{0:T(256)S(1)} %iota_subtract_fusion.1, ...), kind=kOutput, calls=%fused_computation.29 | convolution fusion | flops 605814784 | bytes 2952716 | tf_op jit(solution)/shard_map/dot_general | solution.py:126
  116.1 10.2 %all-to-all-done.3 = bf16[16,32,1152]{2,1,0:T(8,128)(2,1)} async-done(((bf16[16,32,1152]{2,1,0:T(8,128)(2,1)}), bf16[16,32,1152]{2,1,0:T(8,128)(2,1)}, u32[]{:S(2)}, u32[]{:S(2)}) %all-to-all-start.3) | async-done | bytes 1179680 | tf_op jit(solution)/shard_map/all_to_all | solution.py:49
  126.3 4.5 %multiply_reduce_fusion = (f32[256]{0:T(256)S(1)}, f32[256,1152]{1,0:T(8,128)}) fusion(f32[256,1152]{1,0:T(8,128)} %copy-done, f32[256]{0:T(256)S(1)} %add_rsqrt_fusion, f32[256,1152]{1,0:T(8,128)} %fusion.18, bf16[512,1152]{1,0:T(8,128)(2,1)} %bitcast.12, bf16[256,1152]{1,0:T(8,128)(2,1)S(1)} %multiply_convert_fusion.1, f32[]{:T(128)S(6)} %mul.111, ...), kind=kOutput, calls=%fused_computation.27 | convolution fusion | flops 606371584 | bytes 5310476 | tf_op jit(solution)/shard_map/dot_general | solution.py:126
  136.4 7.9 %collective-permute-done.5 = bf16[128,1152]{1,0:T(8,128)(2,1)} collective-permute-done((bf16[128,1152]{1,0:T(8,128)(2,1)}, bf16[128,1152]{1,0:T(8,128)(2,1)}, u32[]{:S(2)}, u32[]{:S(2)}) %collective-permute-start.5) | collective-permute-done | bytes 294944 | tf_op jit(solution)/shard_map/ppermute | solution.py:45
  149.1 2.5 %convolution_convert_fusion = bf16[1152,1152]{1,0:T(8,128)(2,1)} fusion(bf16[256,1152]{1,0:T(8,128)(2,1)S(1)} %get-tuple-element.5, bf16[256,1152]{1,0:T(8,128)(2,1)S(1)} %bitcast.49), kind=kOutput, calls=%fused_computation | convolution fusion | flops 680804352 | bytes 3833856 | tf_op jit(solution)/shard_map/dot_general | solution.py:65
  151.6 5.1 %all-to-all-start.4 = ((bf16[16,72,1152]{2,1,0:T(8,128)(2,1)}), bf16[16,72,1152]{2,1,0:T(8,128)(2,1)}, u32[]{:S(2)}, u32[]{:S(2)}) async-start(bf16[16,72,1152]{2,1,0:T(8,128)(2,1)} %bitcast.47), calls=%async_computation.4 | async-start | bytes 5308416 | tf_op jit(solution)/shard_map/all_to_all | solution.py:49
  160.5 6.8 %collective-permute-start.7 = (bf16[32,1152]{1,0:T(8,128)(2,1)S(1)}, bf16[32,1152]{1,0:T(8,128)(2,1)S(1)}, u32[]{:S(2)}, u32[]{:S(2)}) collective-permute-start(bf16[32,1152]{1,0:T(8,128)(2,1)S(1)} %dynamic-slice_convert_fusion.2), channel_id=1, source_target_pairs={{0,256},{1,257},{2,258},{3,259},{4,260},{5,261},{6,262},{7,263},{8... | collective-permute-start | bytes 221192 | tf_op jit(solution)/shard_map/ppermute | solution.py:45
  167.3 7.3 %collective-permute-done.7 = bf16[32,1152]{1,0:T(8,128)(2,1)S(1)} collective-permute-done((bf16[32,1152]{1,0:T(8,128)(2,1)S(1)}, bf16[32,1152]{1,0:T(8,128)(2,1)S(1)}, u32[]{:S(2)}, u32[]{:S(2)}) %collective-permute-start.7) | collective-permute-done | bytes 73760 | tf_op jit(solution)/shard_map/ppermute | solution.py:45
  177.7 11.0 %collective-permute-done.8 = bf16[32,1152]{1,0:T(8,128)(2,1)S(1)} collective-permute-done((bf16[32,1152]{1,0:T(8,128)(2,1)S(1)}, bf16[32,1152]{1,0:T(8,128)(2,1)S(1)}, u32[]{:S(2)}, u32[]{:S(2)}) %collective-permute-start.8) | collective-permute-done | bytes 73760 | tf_op jit(solution)/shard_map/ppermute | solution.py:45
  192.9 3.5 %collective-permute-done.9 = bf16[64,1152]{1,0:T(8,128)(2,1)S(1)} collective-permute-done((bf16[64,1152]{1,0:T(8,128)(2,1)S(1)}, bf16[64,1152]{1,0:T(8,128)(2,1)S(1)}, u32[]{:S(2)}, u32[]{:S(2)}) %collective-permute-start.9) | collective-permute-done | bytes 147488 | tf_op jit(solution)/shard_map/ppermute | solution.py:45
  200.6 9.0 %collective-permute-start.12 = (bf16[36,1152]{1,0:T(8,128)(2,1)S(1)}, bf16[36,1152]{1,0:T(8,128)(2,1)S(1)}, u32[]{:S(2)}, u32[]{:S(2)}) collective-permute-start(bf16[36,1152]{1,0:T(8,128)(2,1)S(1)} %select_convert_fusion), channel_id=1, source_target_pairs={{0,456},{1,457},{2,458},{3,459},{4,460},{5,461},{6,462},{7,463},{8... | collective-permute-start | bytes 248840 | tf_op jit(solution)/shard_map/ppermute | solution.py:45
  209.8 2.6 %collective-permute-done.12 = bf16[36,1152]{1,0:T(8,128)(2,1)S(1)} collective-permute-done((bf16[36,1152]{1,0:T(8,128)(2,1)S(1)}, bf16[36,1152]{1,0:T(8,128)(2,1)S(1)}, u32[]{:S(2)}, u32[]{:S(2)}) %collective-permute-start.12) | collective-permute-done | bytes 82976 | tf_op jit(solution)/shard_map/ppermute | solution.py:45
  212.5 9.9 %collective-permute-start.13 = (bf16[36,1152]{1,0:T(8,128)(2,1)S(1)}, bf16[36,1152]{1,0:T(8,128)(2,1)S(1)}, u32[]{:S(2)}, u32[]{:S(2)}) collective-permute-start(bf16[36,1152]{1,0:T(8,128)(2,1)S(1)} %add_convert_fusion.2), channel_id=1, source_target_pairs={{0,64},{1,65},{2,66},{3,67},{4,68},{5,69},{6,70},{7,71},{8,72},{9,... | collective-permute-start | bytes 248840 | tf_op jit(solution)/shard_map/ppermute | solution.py:45
  227.2 3.3 %collective-permute-done.14 = bf16[36,1152]{1,0:T(8,128)(2,1)S(1)} collective-permute-done((bf16[36,1152]{1,0:T(8,128)(2,1)S(1)}, bf16[36,1152]{1,0:T(8,128)(2,1)S(1)}, u32[]{:S(2)}, u32[]{:S(2)}) %collective-permute-start.14) | collective-permute-done | bytes 82976 | tf_op jit(solution)/shard_map/ppermute | solution.py:45
  230.5 5.2 %collective-permute-start.15 = (bf16[36,1152]{1,0:T(8,128)(2,1)S(1)}, bf16[36,1152]{1,0:T(8,128)(2,1)S(1)}, u32[]{:S(2)}, u32[]{:S(2)}) collective-permute-start(bf16[36,1152]{1,0:T(8,128)(2,1)S(1)} %add_convert_fusion), channel_id=1, source_target_pairs={{0,256},{1,257},{2,258},{3,259},{4,260},{5,261},{6,262},{7,263},{8... | collective-permute-start | bytes 248840 | tf_op jit(solution)/shard_map/ppermute | solution.py:45
  235.8 5.3 %collective-permute-start.11 = (f32[128,1152]{1,0:T(8,128)S(1)}, f32[128,1152]{1,0:T(8,128)S(1)}, u32[]{:S(2)}, u32[]{:S(2)}) collective-permute-start(f32[128,1152]{1,0:T(8,128)S(1)} %bitcast.52), channel_id=1, source_target_pairs={{0,1},{1,0},{2,3},{3,2},{4,5},{5,4},{6,7},{7,6},{8,9},{9,8},{10,11... | collective-permute-start | bytes 1769480 | tf_op jit(solution)/shard_map/ppermute | solution.py:45
  241.1 3.1 %collective-permute-done.15 = bf16[36,1152]{1,0:T(8,128)(2,1)S(1)} collective-permute-done((bf16[36,1152]{1,0:T(8,128)(2,1)S(1)}, bf16[36,1152]{1,0:T(8,128)(2,1)S(1)}, u32[]{:S(2)}, u32[]{:S(2)}) %collective-permute-start.15) | collective-permute-done | bytes 82976 | tf_op jit(solution)/shard_map/ppermute | solution.py:45
  244.2 4.9 %collective-permute-start.16 = (f32[18,1152]{1,0:T(8,128)S(1)}, f32[18,1152]{1,0:T(8,128)S(1)}, u32[]{:S(2)}, u32[]{:S(2)}) collective-permute-start(f32[18,1152]{1,0:T(8,128)S(1)} %slice_select_fusion), channel_id=1, source_target_pairs={{0,1},{1,0},{2,3},{3,2},{4,5},{5,4},{6,7},{7,6},{8,9},{9,8},{10,11... | collective-permute-start | bytes 248840 | tf_op jit(solution)/shard_map/ppermute | solution.py:45
  (85 shorter events, 51.4 us)
Async XLA Ops:
  1.5 3.5 %collective-permute-start.1 = (bf16[18,1152]{1,0:T(8,128)(2,1)S(1)}, bf16[18,1152]{1,0:T(8,128)(2,1)S(1)}, u32[]{:S(2)}, u32[]{:S(2)}) collective-permute-start(bf16[18,1152]{1,0:T(8,128)(2,1)S(1)} %select_bitcast_fusion.4), channel_id=1, source_target_pairs={{0,1},{1,0},{2,3},{3,2},{4,5},{5,4},{6,7},{7,6},{8,9},{9,8},{10,11... | collective-permute-start | bytes 124424 | tf_op jit(solution)/shard_map/ppermute | solution.py:45
  7.1 29.9 %all-to-all-start = ((bf16[16,36,1152]{2,1,0:T(8,128)(2,1)}), bf16[16,36,1152]{2,1,0:T(8,128)(2,1)S(1)}, u32[]{:S(2)}, u32[]{:S(2)}) async-start(bf16[16,36,1152]{2,1,0:T(8,128)(2,1)} %broadcast_in_dim.16), calls=%async_computation | async-start | bytes 2949120 | tf_op jit(solution)/shard_map/all_to_all | solution.py:49
  16.2 17.5 %collective-permute-start.2 = (bf16[36,1152]{1,0:T(8,128)(2,1)S(1)}, bf16[36,1152]{1,0:T(8,128)(2,1)S(1)}, u32[]{:S(2)}, u32[]{:S(2)}) collective-permute-start(bf16[36,1152]{1,0:T(8,128)(2,1)S(1)} %pad_maximum_fusion.5), channel_id=1, source_target_pairs={{0,456},{1,457},{2,458},{3,459},{4,460},{5,461},{6,462},{7,463},{8... | collective-permute-start | bytes 248840 | tf_op jit(solution)/shard_map/ppermute | solution.py:45
  38.3 6.7 %copy-start.8 = (bf16[128,1152]{1,0:T(8,128)(2,1)S(1)}, bf16[128,1152]{1,0:T(8,128)(2,1)}, u32[]{:S(2)}) copy-start(bf16[128,1152]{1,0:T(8,128)(2,1)} %param.7) | copy-start | bytes 884740
  38.3 6.8 %copy-start.9 = (bf16[128,1152]{1,0:T(8,128)(2,1)S(1)}, bf16[128,1152]{1,0:T(8,128)(2,1)}, u32[]{:S(2)}) copy-start(bf16[128,1152]{1,0:T(8,128)(2,1)} %param.8) | copy-start | bytes 884740
  38.3 26.7 %all-to-all-start.1 = ((bf16[16,36,1152]{2,1,0:T(8,128)(2,1)}), bf16[16,36,1152]{2,1,0:T(8,128)(2,1)S(1)}, u32[]{:S(2)}, u32[]{:S(2)}) async-start(bf16[16,36,1152]{2,1,0:T(8,128)(2,1)} %broadcast_in_dim.17), calls=%async_computation.1 | async-start | bytes 2949120 | tf_op jit(solution)/shard_map/all_to_all | solution.py:49
  45.9 4.8 %collective-permute-start = (bf16[128,1152]{1,0:T(8,128)(2,1)}, bf16[128,1152]{1,0:T(8,128)(2,1)S(1)}, u32[]{:S(2)}, u32[]{:S(2)}) collective-permute-start(bf16[128,1152]{1,0:T(8,128)(2,1)} %get-tuple-element.15), channel_id=1, source_target_pairs={{0,1},{1,0},{2,3},{3,2},{4,5},{5,4},{6,7},{7,6},{8,9},{9,8},{10,11... | collective-permute-start | bytes 884744 | tf_op jit(solution)/shard_map/ppermute | solution.py:45
  52.5 15.3 %copy-start.3 = (bf16[8,2,16,1152]{3,2,1,0:T(8,128)(2,1)}, bf16[8,2,16,1152]{3,2,1,0:T(8,128)(2,1)S(1)}, u32[]{:S(2)}) copy-start(bf16[8,2,16,1152]{3,2,1,0:T(8,128)(2,1)S(1)} %pad_maximum_fusion.1) | copy-start | bytes 1769476
  70.7 1.0 copy-start
  71.9 2.4 copy-start.11
  71.9 3.3 %collective-permute-start.3 = (bf16[32,1152]{1,0:T(8,128)(2,1)S(1)}, bf16[32,1152]{1,0:T(8,128)(2,1)S(1)}, u32[]{:S(2)}, u32[]{:S(2)}) collective-permute-start(bf16[32,1152]{1,0:T(8,128)(2,1)S(1)} %constant_dynamic-slice_fusion), channel_id=1, source_target_pairs={{0,1},{1,0},{2,3},{3,2},{4,5},{5,4},{6,7},{7,6},{8,9},{9,8},{10,11... | collective-permute-start | bytes 221192 | tf_op jit(solution)/shard_map/ppermute | solution.py:45
  76.4 24.5 %all-to-all-start.2 = ((bf16[16,32,1152]{2,1,0:T(8,128)(2,1)}), bf16[16,32,1152]{2,1,0:T(8,128)(2,1)}, u32[]{:S(2)}, u32[]{:S(2)}) async-start(bf16[16,32,1152]{2,1,0:T(8,128)(2,1)} %broadcast_in_dim.18), calls=%async_computation.2 | async-start | bytes 2359296 | tf_op jit(solution)/shard_map/all_to_all | solution.py:49
  84.1 15.7 %collective-permute-start.4 = (bf16[32,1152]{1,0:T(8,128)(2,1)}, bf16[32,1152]{1,0:T(8,128)(2,1)}, u32[]{:S(2)}, u32[]{:S(2)}) collective-permute-start(bf16[32,1152]{1,0:T(8,128)(2,1)} %copy-done.11), channel_id=1, source_target_pairs={{0,457},{1,456},{2,459},{3,458},{4,461},{5,460},{6,463},{7,462},{8... | collective-permute-start | bytes 221192 | tf_op jit(solution)/shard_map/ppermute | solution.py:45
  102.9 23.4 %all-to-all-start.3 = ((bf16[16,32,1152]{2,1,0:T(8,128)(2,1)}), bf16[16,32,1152]{2,1,0:T(8,128)(2,1)}, u32[]{:S(2)}, u32[]{:S(2)}) async-start(bf16[16,32,1152]{2,1,0:T(8,128)(2,1)} %broadcast_in_dim.21), calls=%async_computation.3 | async-start | bytes 2359296 | tf_op jit(solution)/shard_map/all_to_all | solution.py:49
  132.6 1.0 copy-start.1
  134.4 9.9 %collective-permute-start.5 = (bf16[128,1152]{1,0:T(8,128)(2,1)}, bf16[128,1152]{1,0:T(8,128)(2,1)}, u32[]{:S(2)}, u32[]{:S(2)}) collective-permute-start(bf16[128,1152]{1,0:T(8,128)(2,1)} %dynamic-slice_convert_fusion), channel_id=1, source_target_pairs={{0,64},{1,65},{2,66},{3,67},{4,68},{5,69},{6,70},{7,71},{8,72},{9,... | collective-permute-start | bytes 884744 | tf_op jit(solution)/shard_map/ppermute | solution.py:45
  136.4 12.7 %copy-start.4 = (bf16[8,2,16,1152]{3,2,1,0:T(8,128)(2,1)S(1)}, bf16[8,2,16,1152]{3,2,1,0:T(8,128)(2,1)}, u32[]{:S(2)}) copy-start(bf16[8,2,16,1152]{3,2,1,0:T(8,128)(2,1)} %copy-done.3) | copy-start | bytes 1769476
  145.5 0.8 copy-start.5
  147.0 11.8 %collective-permute-start.6 = (bf16[64,1152]{1,0:T(8,128)(2,1)}, bf16[64,1152]{1,0:T(8,128)(2,1)}, u32[]{:S(2)}, u32[]{:S(2)}) collective-permute-start(bf16[64,1152]{1,0:T(8,128)(2,1)} %dynamic-slice_convert_fusion.1), channel_id=1, source_target_pairs={{0,128},{1,129},{2,130},{3,131},{4,132},{5,133},{6,134},{7,135},{8... | collective-permute-start | bytes 442376 | tf_op jit(solution)/shard_map/ppermute | solution.py:45
  151.6 7.2 %copy-start.6 = (f32[128,1152]{1,0:T(8,128)S(1)}, f32[128,1152]{1,0:T(8,128)}, u32[]{:S(2)}) copy-start(f32[128,1152]{1,0:T(8,128)} %copy-done.5) | copy-start | bytes 1769476
  151.6 46.8 %all-to-all-start.4 = ((bf16[16,72,1152]{2,1,0:T(8,128)(2,1)}), bf16[16,72,1152]{2,1,0:T(8,128)(2,1)}, u32[]{:S(2)}, u32[]{:S(2)}) async-start(bf16[16,72,1152]{2,1,0:T(8,128)(2,1)} %bitcast.47), calls=%async_computation.4 | async-start | bytes 5308416 | tf_op jit(solution)/shard_map/all_to_all | solution.py:49
  160.5 14.1 %collective-permute-start.7 = (bf16[32,1152]{1,0:T(8,128)(2,1)S(1)}, bf16[32,1152]{1,0:T(8,128)(2,1)S(1)}, u32[]{:S(2)}, u32[]{:S(2)}) collective-permute-start(bf16[32,1152]{1,0:T(8,128)(2,1)S(1)} %dynamic-slice_convert_fusion.2), channel_id=1, source_target_pairs={{0,256},{1,257},{2,258},{3,259},{4,260},{5,261},{6,262},{7,263},{8... | collective-permute-start | bytes 221192 | tf_op jit(solution)/shard_map/ppermute | solution.py:45
  175.5 13.1 %collective-permute-start.8 = (bf16[32,1152]{1,0:T(8,128)(2,1)S(1)}, bf16[32,1152]{1,0:T(8,128)(2,1)S(1)}, u32[]{:S(2)}, u32[]{:S(2)}) collective-permute-start(bf16[32,1152]{1,0:T(8,128)(2,1)S(1)} %add_convert_fusion.3), channel_id=1, source_target_pairs={{0,256},{1,257},{2,258},{3,259},{4,260},{5,261},{6,262},{7,263},{8... | collective-permute-start | bytes 221192 | tf_op jit(solution)/shard_map/ppermute | solution.py:45
  188.7 7.7 %collective-permute-start.9 = (bf16[64,1152]{1,0:T(8,128)(2,1)S(1)}, bf16[64,1152]{1,0:T(8,128)(2,1)S(1)}, u32[]{:S(2)}, u32[]{:S(2)}) collective-permute-start(bf16[64,1152]{1,0:T(8,128)(2,1)S(1)} %pad_maximum_fusion.4), channel_id=1, source_target_pairs={{0,128},{1,129},{2,130},{3,131},{4,132},{5,133},{6,134},{7,135},{8... | collective-permute-start | bytes 442376 | tf_op jit(solution)/shard_map/ppermute | solution.py:45
  196.5 13.2 %collective-permute-start.10 = (bf16[128,1152]{1,0:T(8,128)(2,1)S(1)}, bf16[128,1152]{1,0:T(8,128)(2,1)S(1)}, u32[]{:S(2)}, u32[]{:S(2)}) collective-permute-start(bf16[128,1152]{1,0:T(8,128)(2,1)S(1)} %pad_maximum_fusion.3), channel_id=1, source_target_pairs={{0,64},{1,65},{2,66},{3,67},{4,68},{5,69},{6,70},{7,71},{8,72},{9,... | collective-permute-start | bytes 884744 | tf_op jit(solution)/shard_map/ppermute | solution.py:45
  200.6 11.8 %collective-permute-start.12 = (bf16[36,1152]{1,0:T(8,128)(2,1)S(1)}, bf16[36,1152]{1,0:T(8,128)(2,1)S(1)}, u32[]{:S(2)}, u32[]{:S(2)}) collective-permute-start(bf16[36,1152]{1,0:T(8,128)(2,1)S(1)} %select_convert_fusion), channel_id=1, source_target_pairs={{0,456},{1,457},{2,458},{3,459},{4,460},{5,461},{6,462},{7,463},{8... | collective-permute-start | bytes 248840 | tf_op jit(solution)/shard_map/ppermute | solution.py:45
  209.7 16.6 %copy-start.2 = (bf16[1152,1152,1,1]{1,0,2,3:T(8,128)(2,1)S(1)}, bf16[1152,1152,1,1]{1,0,2,3:T(8,128)(2,1)}, u32[]{:S(2)}) copy-start(bf16[1152,1152,1,1]{1,0,2,3:T(8,128)(2,1)} %reshape.42) | copy-start | bytes 7962628
  212.5 11.8 %collective-permute-start.13 = (bf16[36,1152]{1,0:T(8,128)(2,1)S(1)}, bf16[36,1152]{1,0:T(8,128)(2,1)S(1)}, u32[]{:S(2)}, u32[]{:S(2)}) collective-permute-start(bf16[36,1152]{1,0:T(8,128)(2,1)S(1)} %add_convert_fusion.2), channel_id=1, source_target_pairs={{0,64},{1,65},{2,66},{3,67},{4,68},{5,69},{6,70},{7,71},{8,72},{9,... | collective-permute-start | bytes 248840 | tf_op jit(solution)/shard_map/ppermute | solution.py:45
  224.3 6.2 %collective-permute-start.14 = (bf16[36,1152]{1,0:T(8,128)(2,1)S(1)}, bf16[36,1152]{1,0:T(8,128)(2,1)S(1)}, u32[]{:S(2)}, u32[]{:S(2)}) collective-permute-start(bf16[36,1152]{1,0:T(8,128)(2,1)S(1)} %add_convert_fusion.1), channel_id=1, source_target_pairs={{0,128},{1,129},{2,130},{3,131},{4,132},{5,133},{6,134},{7,135},{8... | collective-permute-start | bytes 248840 | tf_op jit(solution)/shard_map/ppermute | solution.py:45
  230.5 13.6 %collective-permute-start.15 = (bf16[36,1152]{1,0:T(8,128)(2,1)S(1)}, bf16[36,1152]{1,0:T(8,128)(2,1)S(1)}, u32[]{:S(2)}, u32[]{:S(2)}) collective-permute-start(bf16[36,1152]{1,0:T(8,128)(2,1)S(1)} %add_convert_fusion), channel_id=1, source_target_pairs={{0,256},{1,257},{2,258},{3,259},{4,260},{5,261},{6,262},{7,263},{8... | collective-permute-start | bytes 248840 | tf_op jit(solution)/shard_map/ppermute | solution.py:45
  235.8 13.3 %collective-permute-start.11 = (f32[128,1152]{1,0:T(8,128)S(1)}, f32[128,1152]{1,0:T(8,128)S(1)}, u32[]{:S(2)}, u32[]{:S(2)}) collective-permute-start(f32[128,1152]{1,0:T(8,128)S(1)} %bitcast.52), channel_id=1, source_target_pairs={{0,1},{1,0},{2,3},{3,2},{4,5},{5,4},{6,7},{7,6},{8,9},{9,8},{10,11... | collective-permute-start | bytes 1769480 | tf_op jit(solution)/shard_map/ppermute | solution.py:45
  244.2 6.0 %collective-permute-start.16 = (f32[18,1152]{1,0:T(8,128)S(1)}, f32[18,1152]{1,0:T(8,128)S(1)}, u32[]{:S(2)}, u32[]{:S(2)}) collective-permute-start(f32[18,1152]{1,0:T(8,128)S(1)} %slice_select_fusion), channel_id=1, source_target_pairs={{0,1},{1,0},{2,3},{3,2},{4,5},{5,4},{6,7},{7,6},{8,9},{9,8},{10,11... | collective-permute-start | bytes 248840 | tf_op jit(solution)/shard_map/ppermute | solution.py:45
  (2 other events, 1.4 us)

commit v4 on v3

--- a/solution.py
+++ b/solution.py
@@ -33,12 +33,26 @@
     return lambda device: device ^ (hop * N_GRP)
 
 
-PLANE = [
-    [place(blk, y, zh, x, core) for y in range(N_Y) for x in range(N_X)]
-    for blk in range(N_BLK)
-    for zh in range(N_ZH)
-    for core in range(N_CORE)
-]
+def crossed(first_axis):
+    groups = []
+    for blk in range(N_BLK):
+        for zh in range(N_ZH):
+            for core in range(N_CORE):
+                along_x = (first_axis == "x") == (core == 0)
+                for fixed in range(4):
+                    groups.append(
+                        [
+                            place(blk, fixed, zh, at, core)
+                            if along_x
+                            else place(blk, at, zh, fixed, core)
+                            for at in range(4)
+                        ]
+                    )
+    return groups
+
+
+INNER, OUTER = crossed("x"), crossed("y")
+
 
 def permuted(value, target):
     pairs = [(source, target(source)) for source in range(N_BLK * N_GRP)]
@@ -53,6 +67,21 @@
     count = len(groups[0])
     copies = jnp.broadcast_to(value[None], (count,) + value.shape)
     return exchanged(copies, groups)
+
+
+def plane_gathered(value):
+    return gathered(gathered(value, INNER), OUTER)
+
+
+def summed(own, beside, across, both):
+    own, beside, across, both = (v.astype(jnp.float32) for v in (own, beside, across, both))
+    return (own + beside) + (across + both)
+
+
+def block_transposed(value):
+    side = value.shape[1] // (N_Y * N_X)
+    value = value.reshape(-1, N_Y, N_X, side).transpose(0, 2, 1, 3)
+    return value.reshape(-1, N_Y * N_X * side)
 
 
 def contract_last(left, right):
@@ -90,48 +119,49 @@
     block = jnp.concatenate(
         [jnp.where(first, keep_t, got_t), jnp.where(first, got_t, keep_t)], 0
     )
-    near = gathered(block, PLANE)
-    far = gathered(permuted(block, mirror), PLANE)
+    low = zh == 0
+    other = permuted(block, mirror)
+    block = jnp.concatenate([jnp.where(low, block, other), jnp.where(low, other, block)], 0)
+    proj = plane_gathered(block).reshape(-1, width)
+    embed = proj.shape[0]
     keep_f = jnp.where(first, img_feat, txt_feat)
     got_f = permuted(jnp.where(first, txt_feat, img_feat), sibling)
     feat = jnp.stack(
         [keep_f.reshape(N_BLK, sub_rows, width), got_f.reshape(N_BLK, sub_rows, width)], 1
     ).reshape(own, width)
-    low = zh == 0
-    proj = jnp.stack([jnp.where(low, near, far), jnp.where(low, far, near)], 1)
-    proj = proj.reshape(-1, width)
-    embed = proj.shape[0]
-
     proj_out = contract_last(feat, proj)
     inverse = lax.rsqrt(jnp.sum(proj_out * proj_out, axis=1, keepdims=True) + 1e-06)
     unit = proj_out * inverse
     emb = unit.astype(bf16)
 
     mine = lax.dynamic_slice_in_dim(emb, sub * N_CORE * sub_rows, N_CORE * sub_rows, 0)
-    far = gathered(permuted(mine, lambda device: mirror(sibling(device))), PLANE)
+    far = permuted(mine, lambda device: mirror(sibling(device)))
     got = permuted(mine, sibling)
-    near = gathered(jnp.concatenate([got[sub_rows:], got[:sub_rows]], 0), PLANE)
+    near = jnp.concatenate([got[sub_rows:], got[:sub_rows]], 0)
+    near = plane_gathered(block_transposed(near)).reshape(-1, embed)
+    far = plane_gathered(block_transposed(far)).reshape(-1, embed)
+    spot = jnp.where(first, y * N_X + x, x * N_Y + y) * (N_CORE * sub_rows)
 
     def weigh(others, with_own):
         logits = scale * contract_last(emb, others) + shift_by
         sign = f32(-1.0)
         if with_own:
             row = lax.broadcasted_iota(jnp.int32, logits.shape, 0) - sub * (N_CORE * sub_rows)
-            col = lax.broadcasted_iota(jnp.int32, logits.shape, 1) - (y * N_X + x) * (
-                N_CORE * sub_rows
-            )
+            col = lax.broadcasted_iota(jnp.int32, logits.shape, 1) - spot
             same = (row == col) & (row >= 0) & (row < N_CORE * sub_rows)
             sign = jnp.where(same, f32(1.0), f32(-1.0))
         coef = (-weight * sign * jax.nn.sigmoid(-sign * logits)).astype(bf16)
         return jnp.dot(coef, others, preferred_element_type=f32)
 
-    near, far = near.reshape(-1, embed), far.reshape(-1, embed)
     grad_unit = scale * (weigh(near, True) + weigh(far, False))
     inner = jnp.sum(unit * grad_unit, axis=1, keepdims=True)
     part = ((grad_unit - unit * inner) * inverse).astype(bf16)
 
     terms = contract_first(part, feat).astype(bf16)
-    terms = exchanged(terms.reshape(N_Y * N_X, embed // (N_Y * N_X), width), PLANE)
+    part, terms = lax.optimization_barrier((part, terms))
+    terms = exchanged(terms.reshape(N_Y, embed // N_Y, width), OUTER)
+    terms = jnp.sum(terms.astype(f32), 0).astype(bf16)
+    terms = exchanged(terms.reshape(N_X, embed // (N_Y * N_X), width), INNER)
     held = part.astype(f32)
     for bit, hop in ((4, 1), (2, 2), (1, 4)):
         half = held.shape[0] // 2
@@ -145,13 +175,16 @@
         high = (sub & bit) > 0
         du = jnp.concatenate([jnp.where(high, came, du), jnp.where(high, du, came)], 0)
 
-    terms = jnp.sum(terms.astype(f32), 0)
+    terms = jnp.sum(terms.astype(f32), 0).astype(bf16)
     lower, upper = terms[: N_CORE * cols], terms[N_CORE * cols :]
-    came = permuted(jnp.where(low, upper, lower).astype(bf16), mirror)
-    total = jnp.where(low, lower, upper) + came.astype(f32)
-    for hop in (1, 2, 4):
-        sent = total.astype(bf16)
-        total = sent.astype(f32) + permuted(sent, along(hop)).astype(f32)
+    stay, send = jnp.where(low, lower, upper), jnp.where(low, upper, lower)
+    total = summed(
+        stay,
+        permuted(stay, along(4)),
+        permuted(send, mirror),
+        permuted(send, lambda device: mirror(along(4)(device))),
+    ).astype(bf16)
+    total = summed(total, *(permuted(total, along(hop)) for hop in (1, 2, 3)))
     keep_g = jnp.where(first, total[:cols], total[cols : 2 * cols])
     got_g = permuted(jnp.where(first, total[cols : 2 * cols], total[:cols]), sibling)
     img_proj_grad = jnp.where(first, keep_g, got_g).T

time: 252 us -> 256 us (1.016)
  the two profiles are of different devices: /device:TPU:5 before, /device:TPU:1 now
where the time goes in v4:
time: 256 us; the launch traced here: 255 us
  starting transfers between devices  102 us (40%)
  waiting for transfers between devices  77.9 us (30%)
  blocking collectives  35.3 us (14%)
  matrix products  14.6 us (6%)
  other arithmetic  14 us (5%)
  local copies, waits for them, and re-layouts  7.7 us (3%)
  between operations  3.25 us (1%)
    ppermute x19, starting transfers between devices, permuted(): return lax.ppermute(value, BOTH, pairs)  83.9 us
    ppermute x19, waiting for transfers between devices, permuted(): return lax.ppermute(value, BOTH, pairs)  59 us
    all_to_all x3, blocking collectives, exchanged(): lax.all_to_all(value, BOTH, 0, 0, axis_index_groups=groups, tiled=True)  35.3 us
    all_to_all x5, waiting for transfers between devices, exchanged(): lax.all_to_all(value, BOTH, 0, 0, axis_index_groups=groups, tiled=True)  18.8 us
    all_to_all x5, starting transfers between devices, exchanged(): lax.all_to_all(value, BOTH, 0, 0, axis_index_groups=groups, tiled=True)  18 us
    dot_general x2, matrix products, weigh(): return jnp.dot(coef, others, preferred_element_type=f32)  7.13 us
  transfers between devices with their start and end apart: 24, of which 15 were waited for; matrix products, arithmetic and copies ran while one was open for 6% of the time, Pallas kernels for 0%

profile of v4, /device:TPU:1, one launch (start us, length us, event | category | flops | bytes accessed | tf_op | source)
XLA Modules:
  0.0 254.6 jit_solution(9632485740333095901)
XLA Ops:
  1.5 8.8 %collective-permute-start.1 = (bf16[18,1152]{1,0:T(8,128)(2,1)S(1)}, bf16[18,1152]{1,0:T(8,128)(2,1)S(1)}, u32[]{:S(2)}, u32[]{:S(2)}) collective-permute-start(bf16[18,1152]{1,0:T(8,128)(2,1)S(1)} %select_bitcast_fusion.2), channel_id=1, source_target_pairs={{0,1},{1,0},{2,3},{3,2},{4,5},{5,4},{6,7},{7,6},{8,9},{9,8},{10,11... | collective-permute-start | bytes 124424 | tf_op jit(solution)/shard_map/ppermute | solution.py:59
  12.0 5.7 %collective-permute-start.2 = (bf16[36,1152]{1,0:T(8,128)(2,1)S(1)}, bf16[36,1152]{1,0:T(8,128)(2,1)S(1)}, u32[]{:S(2)}, u32[]{:S(2)}) collective-permute-start(bf16[36,1152]{1,0:T(8,128)(2,1)S(1)} %pad_maximum_fusion.5), channel_id=1, source_target_pairs={{0,456},{1,457},{2,458},{3,459},{4,460},{5,461},{6,462},{7,463},{8... | collective-permute-start | bytes 248840 | tf_op jit(solution)/shard_map/ppermute | solution.py:59
  17.8 8.6 %collective-permute-done.2 = bf16[36,1152]{1,0:T(8,128)(2,1)S(1)} collective-permute-done((bf16[36,1152]{1,0:T(8,128)(2,1)S(1)}, bf16[36,1152]{1,0:T(8,128)(2,1)S(1)}, u32[]{:S(2)}, u32[]{:S(2)}) %collective-permute-start.2) | collective-permute-done | bytes 82976 | tf_op jit(solution)/shard_map/ppermute | solution.py:59
  26.6 11.9 %all_to_all.40 = bf16[4,72,1152]{2,1,0:T(8,128)(2,1)S(1)} all-to-all(bf16[4,72,1152]{2,1,0:T(8,128)(2,1)S(1)} %broadcast_in_dim.24), channel_id=1, replica_groups={{0,2,4,6},{16,18,20,22},{32,34,36,38},{48,50,52,54},{1,17,33,49},{3,19,..., dimensions={0} | all-to-all | bytes 1327104 | tf_op jit(solution)/shard_map/all_to_all | solution.py:63
  40.2 3.9 %all-to-all-start.1 = ((bf16[4,4,72,1152]{3,2,1,0:T(8,128)(2,1)}), bf16[4,4,72,1152]{3,2,1,0:T(8,128)(2,1)S(1)}, u32[]{:S(2)}, u32[]{:S(2)}) async-start(bf16[4,4,72,1152]{3,2,1,0:T(8,128)(2,1)} %broadcast_in_dim.27), calls=%async_computation.1 | async-start | bytes 5308416 | tf_op jit(solution)/shard_map/all_to_all | solution.py:63
  44.9 4.5 %collective-permute-start = (bf16[128,1152]{1,0:T(8,128)(2,1)}, bf16[128,1152]{1,0:T(8,128)(2,1)S(1)}, u32[]{:S(2)}, u32[]{:S(2)}) collective-permute-start(bf16[128,1152]{1,0:T(8,128)(2,1)} %get-tuple-element.15), channel_id=1, source_target_pairs={{0,1},{1,0},{2,3},{3,2},{4,5},{5,4},{6,7},{7,6},{8,9},{9,8},{10,11... | collective-permute-start | bytes 884744 | tf_op jit(solution)/shard_map/ppermute | solution.py:59
  52.5 10.3 %all-to-all-done.1 = bf16[4,4,72,1152]{3,2,1,0:T(8,128)(2,1)S(1)} async-done(((bf16[4,4,72,1152]{3,2,1,0:T(8,128)(2,1)}), bf16[4,4,72,1152]{3,2,1,0:T(8,128)(2,1)S(1)}, u32[]{:S(2)}, u32[]{:S(2)}) %all-to-all-start.1) | async-done | bytes 2654240 | tf_op jit(solution)/shard_map/all_to_all | solution.py:63
  67.3 5.3 %collective-permute-start.3 = (bf16[32,1152]{1,0:T(8,128)(2,1)S(1)}, bf16[32,1152]{1,0:T(8,128)(2,1)S(1)}, u32[]{:S(2)}, u32[]{:S(2)}) collective-permute-start(bf16[32,1152]{1,0:T(8,128)(2,1)S(1)} %constant_dynamic-slice_fusion), channel_id=1, source_target_pairs={{0,1},{1,0},{2,3},{3,2},{4,5},{5,4},{6,7},{7,6},{8,9},{9,8},{10,11... | collective-permute-start | bytes 221192 | tf_op jit(solution)/shard_map/ppermute | solution.py:59
  74.7 3.5 %all-to-all-start.2 = ((bf16[4,32,1152]{2,1,0:T(8,128)(2,1)}), bf16[4,32,1152]{2,1,0:T(8,128)(2,1)S(1)}, u32[]{:S(2)}, u32[]{:S(2)}) async-start(bf16[4,32,1152]{2,1,0:T(8,128)(2,1)} %broadcast_in_dim.53), calls=%async_computation.2 | async-start | bytes 589824 | tf_op jit(solution)/shard_map/all_to_all | solution.py:63
  78.2 4.8 %collective-permute-start.4 = (bf16[32,1152]{1,0:T(8,128)(2,1)S(1)}, bf16[32,1152]{1,0:T(8,128)(2,1)S(1)}, u32[]{:S(2)}, u32[]{:S(2)}) collective-permute-start(bf16[32,1152]{1,0:T(8,128)(2,1)S(1)} %constant_dynamic-slice_fusion), channel_id=1, source_target_pairs={{0,457},{1,456},{2,459},{3,458},{4,461},{5,460},{6,463},{7,462},{8... | collective-permute-start | bytes 221192 | tf_op jit(solution)/shard_map/ppermute | solution.py:59
  83.0 7.3 %collective-permute-done.4 = bf16[32,1152]{1,0:T(8,128)(2,1)S(1)} collective-permute-done((bf16[32,1152]{1,0:T(8,128)(2,1)S(1)}, bf16[32,1152]{1,0:T(8,128)(2,1)S(1)}, u32[]{:S(2)}, u32[]{:S(2)}) %collective-permute-start.4) | collective-permute-done | bytes 73760 | tf_op jit(solution)/shard_map/ppermute | solution.py:59
  90.8 9.5 %all_to_all.41 = bf16[4,32,1152]{2,1,0:T(8,128)(2,1)S(1)} all-to-all(bf16[4,32,1152]{2,1,0:T(8,128)(2,1)S(1)} %broadcast_in_dim.56), channel_id=1, replica_groups={{0,2,4,6},{16,18,20,22},{32,34,36,38},{48,50,52,54},{1,17,33,49},{3,19,..., dimensions={0} | all-to-all | bytes 589824 | tf_op jit(solution)/shard_map/all_to_all | solution.py:63
  100.3 13.9 %all_to_all.42 = bf16[4,4,32,1152]{3,2,1,0:T(8,128)(2,1)} all-to-all(bf16[4,4,32,1152]{3,2,1,0:T(8,128)(2,1)S(1)} %broadcast_in_dim.54), channel_id=1, replica_groups={{0,16,32,48},{2,18,34,50},{4,20,36,52},{6,22,38,54},{1,3,5,7},{17,19,21..., dimensions={0} | all-to-all | bytes 2359296 | tf_op jit(solution)/shard_map/all_to_all | solution.py:63
  115.4 3.5 %all-to-all-start.5 = ((bf16[4,4,32,1152]{3,2,1,0:T(8,128)(2,1)}), bf16[4,4,32,1152]{3,2,1,0:T(8,128)(2,1)S(1)}, u32[]{:S(2)}, u32[]{:S(2)}) async-start(bf16[4,4,32,1152]{3,2,1,0:T(8,128)(2,1)} %broadcast_in_dim.57), calls=%async_computation.5 | async-start | bytes 2359296 | tf_op jit(solution)/shard_map/all_to_all | solution.py:63
  121.4 3.8 %fusion.16 = f32[256,1152]{1,0:T(8,128)} fusion(bf16[512,1152]{1,0:T(8,128)(2,1)} %bitcast.57, bf16[256,1152]{1,0:T(8,128)(2,1)S(1)} %multiply_convert_fusion.1, f32[]{:T(128)} %bitcast.49, f32[]{:T(128)} %bitcast.48, s32[512]{0:T(512)S(1)} %iota_subtract_fusion, f32[]{:T(128)} %bitcast.1, s32[256]{0:T(256)S(1)} %iota_subtract_fusion.1, ...), kind=kOutput, calls=%fused_computation.23 | convolution fusion | flops 605814784 | bytes 2952716 | tf_op jit(solution)/shard_map/dot_general | solution.py:154
  125.2 4.1 %all-to-all-done.5 = bf16[4,4,32,1152]{3,2,1,0:T(8,128)(2,1)S(1)} async-done(((bf16[4,4,32,1152]{3,2,1,0:T(8,128)(2,1)}), bf16[4,4,32,1152]{3,2,1,0:T(8,128)(2,1)S(1)}, u32[]{:S(2)}, u32[]{:S(2)}) %all-to-all-start.5) | async-done | bytes 1179680 | tf_op jit(solution)/shard_map/all_to_all | solution.py:63
  129.3 3.4 %multiply_reduce_fusion = (f32[256]{0:T(256)S(1)}, f32[256,1152]{1,0:T(8,128)}) fusion(f32[256,1152]{1,0:T(8,128)S(1)} %get-tuple-element.31, f32[256]{0:T(256)S(1)} %add_rsqrt_fusion, f32[256,1152]{1,0:T(8,128)} %fusion.16, bf16[512,1152]{1,0:T(8,128)(2,1)S(1)} %bitcast.56, bf16[256,1152]{1,0:T(8,128)(2,1)S(1)} %multiply_convert_fusion.1, f32[]{:T(128)S(6)} %mul.115, ...), kind=kOutput, calls=%fused_computation.21 | convolution fusion | flops 606371584 | bytes 5310476 | tf_op jit(solution)/shard_map/dot_general | solution.py:154
  138.9 5.5 %collective-permute-done.5 = bf16[128,1152]{1,0:T(8,128)(2,1)S(1)} collective-permute-done((bf16[128,1152]{1,0:T(8,128)(2,1)S(1)}, bf16[128,1152]{1,0:T(8,128)(2,1)S(1)}, u32[]{:S(2)}, u32[]{:S(2)}) %collective-permute-start.5) | collective-permute-done | bytes 294944 | tf_op jit(solution)/shard_map/ppermute | solution.py:59
  146.3 6.2 %collective-permute-done.6 = bf16[64,1152]{1,0:T(8,128)(2,1)S(1)} collective-permute-done((bf16[64,1152]{1,0:T(8,128)(2,1)S(1)}, bf16[64,1152]{1,0:T(8,128)(2,1)S(1)}, u32[]{:S(2)}, u32[]{:S(2)}) %collective-permute-start.6) | collective-permute-done | bytes 147488 | tf_op jit(solution)/shard_map/ppermute | solution.py:59
  155.0 3.7 %all-to-all-start.6 = ((bf16[4,288,1152]{2,1,0:T(8,128)(2,1)}), bf16[4,288,1152]{2,1,0:T(8,128)(2,1)S(1)}, u32[]{:S(2)}, u32[]{:S(2)}) async-start(bf16[4,288,1152]{2,1,0:T(8,128)(2,1)} %bitcast.18), calls=%async_computation.6 | async-start | bytes 5308416 | tf_op jit(solution)/shard_map/all_to_all | solution.py:63
  158.7 4.1 %collective-permute-done.7 = bf16[32,1152]{1,0:T(8,128)(2,1)S(1)} collective-permute-done((bf16[32,1152]{1,0:T(8,128)(2,1)S(1)}, bf16[32,1152]{1,0:T(8,128)(2,1)S(1)}, u32[]{:S(2)}, u32[]{:S(2)}) %collective-permute-start.7) | collective-permute-done | bytes 73760 | tf_op jit(solution)/shard_map/ppermute | solution.py:59
  165.5 7.7 %collective-permute-done.8 = bf16[32,1152]{1,0:T(8,128)(2,1)S(1)} collective-permute-done((bf16[32,1152]{1,0:T(8,128)(2,1)S(1)}, bf16[32,1152]{1,0:T(8,128)(2,1)S(1)}, u32[]{:S(2)}, u32[]{:S(2)}) %collective-permute-start.8) | collective-permute-done | bytes 73760 | tf_op jit(solution)/shard_map/ppermute | solution.py:59
  175.2 7.6 %collective-permute-done.9 = bf16[64,1152]{1,0:T(8,128)(2,1)S(1)} collective-permute-done((bf16[64,1152]{1,0:T(8,128)(2,1)S(1)}, bf16[64,1152]{1,0:T(8,128)(2,1)S(1)}, u32[]{:S(2)}, u32[]{:S(2)}) %collective-permute-start.9) | collective-permute-done | bytes 147488 | tf_op jit(solution)/shard_map/ppermute | solution.py:59
  187.7 3.5 %all-to-all-start.7 = ((bf16[4,72,1152]{2,1,0:T(8,128)(2,1)}), bf16[4,72,1152]{2,1,0:T(8,128)(2,1)S(1)}, u32[]{:S(2)}, u32[]{:S(2)}) async-start(bf16[4,72,1152]{2,1,0:T(8,128)(2,1)} %bitcast.53), calls=%async_computation.7 | async-start | bytes 1327104 | tf_op jit(solution)/shard_map/all_to_all | solution.py:63
  194.3 4.5 %all-to-all-done.7 = bf16[4,72,1152]{2,1,0:T(8,128)(2,1)S(1)} async-done(((bf16[4,72,1152]{2,1,0:T(8,128)(2,1)}), bf16[4,72,1152]{2,1,0:T(8,128)(2,1)S(1)}, u32[]{:S(2)}, u32[]{:S(2)}) %all-to-all-start.7) | async-done | bytes 663584 | tf_op jit(solution)/shard_map/all_to_all | solution.py:63
  200.6 5.1 %collective-permute-start.13 = (bf16[36,1152]{1,0:T(8,128)(2,1)S(1)}, bf16[36,1152]{1,0:T(8,128)(2,1)S(1)}, u32[]{:S(2)}, u32[]{:S(2)}) collective-permute-start(bf16[36,1152]{1,0:T(8,128)(2,1)S(1)} %get-tuple-element.23), channel_id=1, source_target_pairs={{0,456},{1,457},{2,458},{3,459},{4,460},{5,461},{6,462},{7,463},{8... | collective-permute-start | bytes 248840 | tf_op jit(solution)/shard_map/ppermute | solution.py:59
  205.7 5.1 %collective-permute-start.14 = (bf16[36,1152]{1,0:T(8,128)(2,1)S(1)}, bf16[36,1152]{1,0:T(8,128)(2,1)S(1)}, u32[]{:S(2)}, u32[]{:S(2)}) collective-permute-start(bf16[36,1152]{1,0:T(8,128)(2,1)S(1)} %get-tuple-element.23), channel_id=1, source_target_pairs={{0,200},{1,201},{2,202},{3,203},{4,204},{5,205},{6,206},{7,207},{8... | collective-permute-start | bytes 248840 | tf_op jit(solution)/shard_map/ppermute | solution.py:59
  210.8 3.8 %collective-permute-start.12 = (bf16[36,1152]{1,0:T(8,128)(2,1)S(1)}, bf16[36,1152]{1,0:T(8,128)(2,1)S(1)}, u32[]{:S(2)}, u32[]{:S(2)}) collective-permute-start(bf16[36,1152]{1,0:T(8,128)(2,1)S(1)} %get-tuple-element.22), channel_id=1, source_target_pairs={{0,256},{1,257},{2,258},{3,259},{4,260},{5,261},{6,262},{7,263},{8... | collective-permute-start | bytes 248840 | tf_op jit(solution)/shard_map/ppermute | solution.py:59
  216.7 7.9 %collective-permute-done.12 = bf16[36,1152]{1,0:T(8,128)(2,1)S(1)} collective-permute-done((bf16[36,1152]{1,0:T(8,128)(2,1)S(1)}, bf16[36,1152]{1,0:T(8,128)(2,1)S(1)}, u32[]{:S(2)}, u32[]{:S(2)}) %collective-permute-start.12) | collective-permute-done | bytes 82976 | tf_op jit(solution)/shard_map/ppermute | solution.py:59
  228.5 5.4 %collective-permute-start.17 = (bf16[36,1152]{1,0:T(8,128)(2,1)S(1)}, bf16[36,1152]{1,0:T(8,128)(2,1)S(1)}, u32[]{:S(2)}, u32[]{:S(2)}) collective-permute-start(bf16[36,1152]{1,0:T(8,128)(2,1)S(1)} %add_convert_fusion), channel_id=1, source_target_pairs={{0,192},{1,193},{2,194},{3,195},{4,196},{5,197},{6,198},{7,199},{8... | collective-permute-start | bytes 248840 | tf_op jit(solution)/shard_map/ppermute | solution.py:59
  234.0 15.3 %collective-permute-start.11 = (f32[128,1152]{1,0:T(8,128)S(1)}, f32[128,1152]{1,0:T(8,128)S(1)}, u32[]{:S(2)}, u32[]{:S(2)}) collective-permute-start(f32[128,1152]{1,0:T(8,128)S(1)} %bitcast.60), channel_id=1, source_target_pairs={{0,1},{1,0},{2,3},{3,2},{4,5},{5,4},{6,7},{7,6},{8,9},{9,8},{10,11... | collective-permute-start | bytes 1769480 | tf_op jit(solution)/shard_map/ppermute | solution.py:59
  249.4 3.4 %collective-permute-start.18 = (f32[18,1152]{1,0:T(8,128)S(1)}, f32[18,1152]{1,0:T(8,128)S(1)}, u32[]{:S(2)}, u32[]{:S(2)}) collective-permute-start(f32[18,1152]{1,0:T(8,128)S(1)} %slice_select_fusion), channel_id=1, source_target_pairs={{0,1},{1,0},{2,3},{3,2},{4,5},{5,4},{6,7},{7,6},{8,9},{9,8},{10,11... | collective-permute-start | bytes 248840 | tf_op jit(solution)/shard_map/ppermute | solution.py:59
  (86 shorter events, 50.1 us)
Async XLA Ops:
  1.5 9.7 %collective-permute-start.1 = (bf16[18,1152]{1,0:T(8,128)(2,1)S(1)}, bf16[18,1152]{1,0:T(8,128)(2,1)S(1)}, u32[]{:S(2)}, u32[]{:S(2)}) collective-permute-start(bf16[18,1152]{1,0:T(8,128)(2,1)S(1)} %select_bitcast_fusion.2), channel_id=1, source_target_pairs={{0,1},{1,0},{2,3},{3,2},{4,5},{5,4},{6,7},{7,6},{8,9},{9,8},{10,11... | collective-permute-start | bytes 124424 | tf_op jit(solution)/shard_map/ppermute | solution.py:59
  12.0 14.4 %collective-permute-start.2 = (bf16[36,1152]{1,0:T(8,128)(2,1)S(1)}, bf16[36,1152]{1,0:T(8,128)(2,1)S(1)}, u32[]{:S(2)}, u32[]{:S(2)}) collective-permute-start(bf16[36,1152]{1,0:T(8,128)(2,1)S(1)} %pad_maximum_fusion.5), channel_id=1, source_target_pairs={{0,456},{1,457},{2,458},{3,459},{4,460},{5,461},{6,462},{7,463},{8... | collective-permute-start | bytes 248840 | tf_op jit(solution)/shard_map/ppermute | solution.py:59
  40.2 3.9 %copy-start.3 = (bf16[128,1152]{1,0:T(8,128)(2,1)S(1)}, bf16[128,1152]{1,0:T(8,128)(2,1)}, u32[]{:S(2)}) copy-start(bf16[128,1152]{1,0:T(8,128)(2,1)} %param.7) | copy-start | bytes 884740
  40.2 3.9 %copy-start.4 = (bf16[128,1152]{1,0:T(8,128)(2,1)S(1)}, bf16[128,1152]{1,0:T(8,128)(2,1)}, u32[]{:S(2)}) copy-start(bf16[128,1152]{1,0:T(8,128)(2,1)} %param.8) | copy-start | bytes 884740
  40.2 22.5 %all-to-all-start.1 = ((bf16[4,4,72,1152]{3,2,1,0:T(8,128)(2,1)}), bf16[4,4,72,1152]{3,2,1,0:T(8,128)(2,1)S(1)}, u32[]{:S(2)}, u32[]{:S(2)}) async-start(bf16[4,4,72,1152]{3,2,1,0:T(8,128)(2,1)} %broadcast_in_dim.27), calls=%async_computation.1 | async-start | bytes 5308416 | tf_op jit(solution)/shard_map/all_to_all | solution.py:63
  44.9 5.9 %collective-permute-start = (bf16[128,1152]{1,0:T(8,128)(2,1)}, bf16[128,1152]{1,0:T(8,128)(2,1)S(1)}, u32[]{:S(2)}, u32[]{:S(2)}) collective-permute-start(bf16[128,1152]{1,0:T(8,128)(2,1)} %get-tuple-element.15), channel_id=1, source_target_pairs={{0,1},{1,0},{2,3},{3,2},{4,5},{5,4},{6,7},{7,6},{8,9},{9,8},{10,11... | collective-permute-start | bytes 884744 | tf_op jit(solution)/shard_map/ppermute | solution.py:59
  50.7 0.7 copy-start.5
  62.7 1.5 copy-start
  67.3 6.2 %collective-permute-start.3 = (bf16[32,1152]{1,0:T(8,128)(2,1)S(1)}, bf16[32,1152]{1,0:T(8,128)(2,1)S(1)}, u32[]{:S(2)}, u32[]{:S(2)}) collective-permute-start(bf16[32,1152]{1,0:T(8,128)(2,1)S(1)} %constant_dynamic-slice_fusion), channel_id=1, source_target_pairs={{0,1},{1,0},{2,3},{3,2},{4,5},{5,4},{6,7},{7,6},{8,9},{9,8},{10,11... | collective-permute-start | bytes 221192 | tf_op jit(solution)/shard_map/ppermute | solution.py:59
  74.7 16.0 %all-to-all-start.2 = ((bf16[4,32,1152]{2,1,0:T(8,128)(2,1)}), bf16[4,32,1152]{2,1,0:T(8,128)(2,1)S(1)}, u32[]{:S(2)}, u32[]{:S(2)}) async-start(bf16[4,32,1152]{2,1,0:T(8,128)(2,1)} %broadcast_in_dim.53), calls=%async_computation.2 | async-start | bytes 589824 | tf_op jit(solution)/shard_map/all_to_all | solution.py:63
  78.2 12.1 %collective-permute-start.4 = (bf16[32,1152]{1,0:T(8,128)(2,1)S(1)}, bf16[32,1152]{1,0:T(8,128)(2,1)S(1)}, u32[]{:S(2)}, u32[]{:S(2)}) collective-permute-start(bf16[32,1152]{1,0:T(8,128)(2,1)S(1)} %constant_dynamic-slice_fusion), channel_id=1, source_target_pairs={{0,457},{1,456},{2,459},{3,458},{4,461},{5,460},{6,463},{7,462},{8... | collective-permute-start | bytes 221192 | tf_op jit(solution)/shard_map/ppermute | solution.py:59
  115.4 13.9 %all-to-all-start.5 = ((bf16[4,4,32,1152]{3,2,1,0:T(8,128)(2,1)}), bf16[4,4,32,1152]{3,2,1,0:T(8,128)(2,1)S(1)}, u32[]{:S(2)}, u32[]{:S(2)}) async-start(bf16[4,4,32,1152]{3,2,1,0:T(8,128)(2,1)} %broadcast_in_dim.57), calls=%async_computation.5 | async-start | bytes 2359296 | tf_op jit(solution)/shard_map/all_to_all | solution.py:63
  136.8 7.5 %collective-permute-start.5 = (bf16[128,1152]{1,0:T(8,128)(2,1)S(1)}, bf16[128,1152]{1,0:T(8,128)(2,1)S(1)}, u32[]{:S(2)}, u32[]{:S(2)}) collective-permute-start(bf16[128,1152]{1,0:T(8,128)(2,1)S(1)} %dynamic-slice_convert_fusion), channel_id=1, source_target_pairs={{0,64},{1,65},{2,66},{3,67},{4,68},{5,69},{6,70},{7,71},{8,72},{9,... | collective-permute-start | bytes 884744 | tf_op jit(solution)/shard_map/ppermute | solution.py:59
  144.4 8.2 %collective-permute-start.6 = (bf16[64,1152]{1,0:T(8,128)(2,1)S(1)}, bf16[64,1152]{1,0:T(8,128)(2,1)S(1)}, u32[]{:S(2)}, u32[]{:S(2)}) collective-permute-start(bf16[64,1152]{1,0:T(8,128)(2,1)S(1)} %dynamic-slice_convert_fusion.1), channel_id=1, source_target_pairs={{0,128},{1,129},{2,130},{3,131},{4,132},{5,133},{6,134},{7,135},{8... | collective-permute-start | bytes 442376 | tf_op jit(solution)/shard_map/ppermute | solution.py:59
  152.6 10.2 %collective-permute-start.7 = (bf16[32,1152]{1,0:T(8,128)(2,1)S(1)}, bf16[32,1152]{1,0:T(8,128)(2,1)S(1)}, u32[]{:S(2)}, u32[]{:S(2)}) collective-permute-start(bf16[32,1152]{1,0:T(8,128)(2,1)S(1)} %dynamic-slice_convert_fusion.2), channel_id=1, source_target_pairs={{0,256},{1,257},{2,258},{3,259},{4,260},{5,261},{6,262},{7,263},{8... | collective-permute-start | bytes 221192 | tf_op jit(solution)/shard_map/ppermute | solution.py:59
  155.0 31.2 %all-to-all-start.6 = ((bf16[4,288,1152]{2,1,0:T(8,128)(2,1)}), bf16[4,288,1152]{2,1,0:T(8,128)(2,1)S(1)}, u32[]{:S(2)}, u32[]{:S(2)}) async-start(bf16[4,288,1152]{2,1,0:T(8,128)(2,1)} %bitcast.18), calls=%async_computation.6 | async-start | bytes 5308416 | tf_op jit(solution)/shard_map/all_to_all | solution.py:63
  162.8 10.4 %collective-permute-start.8 = (bf16[32,1152]{1,0:T(8,128)(2,1)S(1)}, bf16[32,1152]{1,0:T(8,128)(2,1)S(1)}, u32[]{:S(2)}, u32[]{:S(2)}) collective-permute-start(bf16[32,1152]{1,0:T(8,128)(2,1)S(1)} %add_convert_fusion.1), channel_id=1, source_target_pairs={{0,256},{1,257},{2,258},{3,259},{4,260},{5,261},{6,262},{7,263},{8... | collective-permute-start | bytes 221192 | tf_op jit(solution)/shard_map/ppermute | solution.py:59
  173.3 9.6 %collective-permute-start.9 = (bf16[64,1152]{1,0:T(8,128)(2,1)S(1)}, bf16[64,1152]{1,0:T(8,128)(2,1)S(1)}, u32[]{:S(2)}, u32[]{:S(2)}) collective-permute-start(bf16[64,1152]{1,0:T(8,128)(2,1)S(1)} %pad_maximum_fusion.4), channel_id=1, source_target_pairs={{0,128},{1,129},{2,130},{3,131},{4,132},{5,133},{6,134},{7,135},{8... | collective-permute-start | bytes 442376 | tf_op jit(solution)/shard_map/ppermute | solution.py:59
  182.9 0.7 copy-start.2
  184.3 7.9 %collective-permute-start.10 = (bf16[128,1152]{1,0:T(8,128)(2,1)}, bf16[128,1152]{1,0:T(8,128)(2,1)}, u32[]{:S(2)}, u32[]{:S(2)}) collective-permute-start(bf16[128,1152]{1,0:T(8,128)(2,1)} %pad_maximum_fusion.2), channel_id=1, source_target_pairs={{0,64},{1,65},{2,66},{3,67},{4,68},{5,69},{6,70},{7,71},{8,72},{9,... | collective-permute-start | bytes 884744 | tf_op jit(solution)/shard_map/ppermute | solution.py:59
  187.7 11.1 %all-to-all-start.7 = ((bf16[4,72,1152]{2,1,0:T(8,128)(2,1)}), bf16[4,72,1152]{2,1,0:T(8,128)(2,1)S(1)}, u32[]{:S(2)}, u32[]{:S(2)}) async-start(bf16[4,72,1152]{2,1,0:T(8,128)(2,1)} %bitcast.53), calls=%async_computation.7 | async-start | bytes 1327104 | tf_op jit(solution)/shard_map/all_to_all | solution.py:63
  192.2 22.4 %copy-start.1 = (bf16[4,4,72,1152]{3,2,1,0:T(8,128)(2,1)S(1)}, bf16[4,4,72,1152]{3,2,1,0:T(8,128)(2,1)}, u32[]{:S(2)}) copy-start(bf16[4,4,72,1152]{3,2,1,0:T(8,128)(2,1)} %copy-done) | copy-start | bytes 7962628
  200.6 24.0 %collective-permute-start.13 = (bf16[36,1152]{1,0:T(8,128)(2,1)S(1)}, bf16[36,1152]{1,0:T(8,128)(2,1)S(1)}, u32[]{:S(2)}, u32[]{:S(2)}) collective-permute-start(bf16[36,1152]{1,0:T(8,128)(2,1)S(1)} %get-tuple-element.23), channel_id=1, source_target_pairs={{0,456},{1,457},{2,458},{3,459},{4,460},{5,461},{6,462},{7,463},{8... | collective-permute-start | bytes 248840 | tf_op jit(solution)/shard_map/ppermute | solution.py:59
  205.7 18.9 %collective-permute-start.14 = (bf16[36,1152]{1,0:T(8,128)(2,1)S(1)}, bf16[36,1152]{1,0:T(8,128)(2,1)S(1)}, u32[]{:S(2)}, u32[]{:S(2)}) collective-permute-start(bf16[36,1152]{1,0:T(8,128)(2,1)S(1)} %get-tuple-element.23), channel_id=1, source_target_pairs={{0,200},{1,201},{2,202},{3,203},{4,204},{5,205},{6,206},{7,207},{8... | collective-permute-start | bytes 248840 | tf_op jit(solution)/shard_map/ppermute | solution.py:59
  210.8 13.8 %collective-permute-start.12 = (bf16[36,1152]{1,0:T(8,128)(2,1)S(1)}, bf16[36,1152]{1,0:T(8,128)(2,1)S(1)}, u32[]{:S(2)}, u32[]{:S(2)}) collective-permute-start(bf16[36,1152]{1,0:T(8,128)(2,1)S(1)} %get-tuple-element.22), channel_id=1, source_target_pairs={{0,256},{1,257},{2,258},{3,259},{4,260},{5,261},{6,262},{7,263},{8... | collective-permute-start | bytes 248840 | tf_op jit(solution)/shard_map/ppermute | solution.py:59
  224.6 24.6 %collective-permute-start.15 = (bf16[36,1152]{1,0:T(8,128)(2,1)S(1)}, bf16[36,1152]{1,0:T(8,128)(2,1)S(1)}, u32[]{:S(2)}, u32[]{:S(2)}) collective-permute-start(bf16[36,1152]{1,0:T(8,128)(2,1)S(1)} %add_convert_fusion), channel_id=1, source_target_pairs={{0,64},{1,65},{2,66},{3,67},{4,68},{5,69},{6,70},{7,71},{8,72},{9,... | collective-permute-start | bytes 248840 | tf_op jit(solution)/shard_map/ppermute | solution.py:59
  226.5 22.7 %collective-permute-start.16 = (bf16[36,1152]{1,0:T(8,128)(2,1)S(1)}, bf16[36,1152]{1,0:T(8,128)(2,1)S(1)}, u32[]{:S(2)}, u32[]{:S(2)}) collective-permute-start(bf16[36,1152]{1,0:T(8,128)(2,1)S(1)} %add_convert_fusion), channel_id=1, source_target_pairs={{0,128},{1,129},{2,130},{3,131},{4,132},{5,133},{6,134},{7,135},{8... | collective-permute-start | bytes 248840 | tf_op jit(solution)/shard_map/ppermute | solution.py:59
  228.5 20.8 %collective-permute-start.17 = (bf16[36,1152]{1,0:T(8,128)(2,1)S(1)}, bf16[36,1152]{1,0:T(8,128)(2,1)S(1)}, u32[]{:S(2)}, u32[]{:S(2)}) collective-permute-start(bf16[36,1152]{1,0:T(8,128)(2,1)S(1)} %add_convert_fusion), channel_id=1, source_target_pairs={{0,192},{1,193},{2,194},{3,195},{4,196},{5,197},{6,198},{7,199},{8... | collective-permute-start | bytes 248840 | tf_op jit(solution)/shard_map/ppermute | solution.py:59
  234.0 18.7 %collective-permute-start.11 = (f32[128,1152]{1,0:T(8,128)S(1)}, f32[128,1152]{1,0:T(8,128)S(1)}, u32[]{:S(2)}, u32[]{:S(2)}) collective-permute-start(f32[128,1152]{1,0:T(8,128)S(1)} %bitcast.60), channel_id=1, source_target_pairs={{0,1},{1,0},{2,3},{3,2},{4,5},{5,4},{6,7},{7,6},{8,9},{9,8},{10,11... | collective-permute-start | bytes 1769480 | tf_op jit(solution)/shard_map/ppermute | solution.py:59
  249.4 4.5 %collective-permute-start.18 = (f32[18,1152]{1,0:T(8,128)S(1)}, f32[18,1152]{1,0:T(8,128)S(1)}, u32[]{:S(2)}, u32[]{:S(2)}) collective-permute-start(f32[18,1152]{1,0:T(8,128)S(1)} %slice_select_fusion), channel_id=1, source_target_pairs={{0,1},{1,0},{2,3},{3,2},{4,5},{5,4},{6,7},{7,6},{8,9},{9,8},{10,11... | collective-permute-start | bytes 248840 | tf_op jit(solution)/shard_map/ppermute | solution.py:59

commit v5 on v3

--- a/solution.py
+++ b/solution.py
@@ -33,12 +33,37 @@
     return lambda device: device ^ (hop * N_GRP)
 
 
+def crossed(first_axis):
+    groups = []
+    for blk in range(N_BLK):
+        for zh in range(N_ZH):
+            for core in range(N_CORE):
+                along_x = (first_axis == "x") == (core == 0)
+                for fixed in range(4):
+                    groups.append(
+                        [
+                            place(blk, fixed, zh, at, core)
+                            if along_x
+                            else place(blk, at, zh, fixed, core)
+                            for at in range(4)
+                        ]
+                    )
+    return groups
+
+
+INNER, OUTER = crossed("x"), crossed("y")
 PLANE = [
-    [place(blk, y, zh, x, core) for y in range(N_Y) for x in range(N_X)]
+    [
+        place(blk, slow, zh, fast, core) if core == 0 else place(blk, fast, zh, slow, core)
+        for slow in range(4)
+        for fast in range(4)
+    ]
     for blk in range(N_BLK)
     for zh in range(N_ZH)
     for core in range(N_CORE)
 ]
+LINE = [[place(blk, *rest) for blk in range(N_BLK)] for rest in map(lambda d: parts(d)[1:], range(N_GRP))]
+
 
 def permuted(value, target):
     pairs = [(source, target(source)) for source in range(N_BLK * N_GRP)]
@@ -84,53 +109,62 @@
     sub_rows = rows // N_BLK
     own = N_CORE * rows
 
+    low = zh == 0
     img_t, txt_t = img_proj.T, txt_proj.T
     keep_t = jnp.where(first, img_t, txt_t)
-    got_t = permuted(jnp.where(first, txt_t, img_t), sibling)
-    block = jnp.concatenate(
-        [jnp.where(first, keep_t, got_t), jnp.where(first, got_t, keep_t)], 0
-    )
-    near = gathered(block, PLANE)
-    far = gathered(permuted(block, mirror), PLANE)
     keep_f = jnp.where(first, img_feat, txt_feat)
-    got_f = permuted(jnp.where(first, txt_feat, img_feat), sibling)
+    give_f = jnp.where(first, txt_feat, img_feat)
+    give_sub = lax.dynamic_slice_in_dim(keep_f, sub * sub_rows, sub_rows, 0)
+    keep_sub = lax.dynamic_slice_in_dim(give_f, sub * sub_rows, sub_rows, 0)
+    got = permuted(jnp.concatenate([jnp.where(first, txt_t, img_t), give_sub], 0), sibling)
+    got_t, got_sub = got[:cols], got[cols:]
+    pair = N_CORE * cols
+    near = jnp.concatenate(
+        [jnp.where(first, keep_t, got_t), jnp.where(first, got_t, keep_t), keep_sub, got_sub], 0
+    )
+    far = gathered(permuted(near, mirror), INNER)
+    near = gathered(near, INNER)
+    proj = jnp.concatenate(
+        [
+            jnp.where(low, near[:, :pair], far[:, :pair]),
+            jnp.where(low, far[:, :pair], near[:, :pair]),
+        ],
+        1,
+    )
+    others = jnp.concatenate([near[:, pair:], far[:, pair:]], 1)
+    proj, others = lax.optimization_barrier((gathered(proj, OUTER), others))
+    others = gathered(others, OUTER).reshape(-1, width)
+    other_proj = permuted(proj, sibling).transpose(1, 0, 2, 3).reshape(-1, width)
+    proj = proj.reshape(-1, width)
+    embed = proj.shape[0]
+
+    got_f = permuted(give_f, sibling)
     feat = jnp.stack(
         [keep_f.reshape(N_BLK, sub_rows, width), got_f.reshape(N_BLK, sub_rows, width)], 1
     ).reshape(own, width)
-    low = zh == 0
-    proj = jnp.stack([jnp.where(low, near, far), jnp.where(low, far, near)], 1)
-    proj = proj.reshape(-1, width)
-    embed = proj.shape[0]
-
-    proj_out = contract_last(feat, proj)
-    inverse = lax.rsqrt(jnp.sum(proj_out * proj_out, axis=1, keepdims=True) + 1e-06)
-    unit = proj_out * inverse
+
+    def embedded(rows_of, columns_of):
+        proj_out = contract_last(rows_of, columns_of)
+        inverse = lax.rsqrt(jnp.sum(proj_out * proj_out, axis=1, keepdims=True) + 1e-06)
+        return proj_out * inverse, inverse
+
+    unit, inverse = embedded(feat, proj)
     emb = unit.astype(bf16)
-
-    mine = lax.dynamic_slice_in_dim(emb, sub * N_CORE * sub_rows, N_CORE * sub_rows, 0)
-    far = gathered(permuted(mine, lambda device: mirror(sibling(device))), PLANE)
-    got = permuted(mine, sibling)
-    near = gathered(jnp.concatenate([got[sub_rows:], got[:sub_rows]], 0), PLANE)
-
-    def weigh(others, with_own):
-        logits = scale * contract_last(emb, others) + shift_by
-        sign = f32(-1.0)
-        if with_own:
-            row = lax.broadcasted_iota(jnp.int32, logits.shape, 0) - sub * (N_CORE * sub_rows)
-            col = lax.broadcasted_iota(jnp.int32, logits.shape, 1) - (y * N_X + x) * (
-                N_CORE * sub_rows
-            )
-            same = (row == col) & (row >= 0) & (row < N_CORE * sub_rows)
-            sign = jnp.where(same, f32(1.0), f32(-1.0))
-        coef = (-weight * sign * jax.nn.sigmoid(-sign * logits)).astype(bf16)
-        return jnp.dot(coef, others, preferred_element_type=f32)
-
-    near, far = near.reshape(-1, embed), far.reshape(-1, embed)
-    grad_unit = scale * (weigh(near, True) + weigh(far, False))
+    others = embedded(others, other_proj)[0].astype(bf16)
+    spot = jnp.where(first, y * N_X + x, x * N_Y + y) * (N_ZH * N_CORE * sub_rows)
+
+    logits = scale * contract_last(emb, others) + shift_by
+    row = lax.broadcasted_iota(jnp.int32, logits.shape, 0) - sub * (N_CORE * sub_rows)
+    col = lax.broadcasted_iota(jnp.int32, logits.shape, 1) - spot
+    same = (row == col) & (row >= 0) & (row < N_CORE * sub_rows)
+    sign = jnp.where(same, f32(1.0), f32(-1.0))
+    coef = (-weight * sign * jax.nn.sigmoid(-sign * logits)).astype(bf16)
+    grad_unit = scale * jnp.dot(coef, others, preferred_element_type=f32)
     inner = jnp.sum(unit * grad_unit, axis=1, keepdims=True)
     part = ((grad_unit - unit * inner) * inverse).astype(bf16)
 
     terms = contract_first(part, feat).astype(bf16)
+    part, terms = lax.optimization_barrier((part, terms))
     terms = exchanged(terms.reshape(N_Y * N_X, embed // (N_Y * N_X), width), PLANE)
     held = part.astype(f32)
     for bit, hop in ((4, 1), (2, 2), (1, 4)):
@@ -139,19 +173,19 @@
         send = lax.dynamic_slice_in_dim(held, (1 - high) * half, half, 0).astype(bf16)
         stay = lax.dynamic_slice_in_dim(held, high * half, half, 0)
         held = stay + permuted(send, along(hop)).astype(f32)
-    du = held.astype(bf16)
+    du, terms = lax.optimization_barrier((held.astype(bf16), terms))
     for bit, hop in ((1, 4), (2, 2), (4, 1)):
         came = permuted(du, along(hop))
         high = (sub & bit) > 0
         du = jnp.concatenate([jnp.where(high, came, du), jnp.where(high, du, came)], 0)
 
     terms = jnp.sum(terms.astype(f32), 0)
-    lower, upper = terms[: N_CORE * cols], terms[N_CORE * cols :]
+    lower, upper = terms[:pair], terms[pair:]
     came = permuted(jnp.where(low, upper, lower).astype(bf16), mirror)
-    total = jnp.where(low, lower, upper) + came.astype(f32)
-    for hop in (1, 2, 4):
-        sent = total.astype(bf16)
-        total = sent.astype(f32) + permuted(sent, along(hop)).astype(f32)
+    terms = (jnp.where(low, lower, upper) + came.astype(f32)).astype(bf16)
+    terms = jnp.pad(terms, ((0, -pair % N_BLK), (0, 0))).reshape(N_BLK, -1, width)
+    terms = jnp.sum(exchanged(terms, LINE).astype(f32), 0).astype(bf16)
+    total = gathered(terms, LINE).reshape(-1, width).astype(f32)
     keep_g = jnp.where(first, total[:cols], total[cols : 2 * cols])
     got_g = permuted(jnp.where(first, total[cols : 2 * cols], total[:cols]), sibling)
     img_proj_grad = jnp.where(first, keep_g, got_g).T

time: 252 us -> 225 us (0.89)
  the two profiles are of different devices: /device:TPU:5 before, /device:TPU:1 now
where the time goes in v5:
time: 225 us; the launch traced here: 224 us
  starting transfers between devices  82.8 us (37%)
  waiting for transfers between devices  82.3 us (37%)
  matrix products  19.8 us (9%)
  local copies, waits for them, and re-layouts  12.4 us (6%)
  blocking collectives  12 us (5%)
  other arithmetic  11.7 us (5%)
  between operations  3.2 us (1%)
    ppermute x13, starting transfers between devices, permuted(): return lax.ppermute(value, BOTH, pairs)  56.1 us
    ppermute x13, waiting for transfers between devices, permuted(): return lax.ppermute(value, BOTH, pairs)  50.8 us
    all_to_all x6, waiting for transfers between devices, exchanged(): lax.all_to_all(value, BOTH, 0, 0, axis_index_groups=groups, tiled=True)  31.4 us
    all_to_all x6, starting transfers between devices, exchanged(): lax.all_to_all(value, BOTH, 0, 0, axis_index_groups=groups, tiled=True)  26.7 us
    all_to_all x1, blocking collectives, exchanged(): lax.all_to_all(value, BOTH, 0, 0, axis_index_groups=groups, tiled=True)  12 us
    dot_general x2, matrix products, contract_last(): lax.dot_general(left, right, (((1,), (1,)), ((), ())), preferred_element_...  9.5 us
    dot_general x1, matrix products, body(): grad_unit = scale * jnp.dot(coef, others, preferred_element_type=f32)  6.75 us
    broadcast_in_dim x5, local copies, waits for them, and re-layouts, gathered(): copies = jnp.broadcast_to(value[None], (count,) + value.shape)  5.01 us
  transfers between devices with their start and end apart: 19, of which 12 were waited for; matrix products, arithmetic and copies ran while one was open for 7% of the time, Pallas kernels for 0%

profile of v5, /device:TPU:1, one launch (start us, length us, event | category | flops | bytes accessed | tf_op | source)
XLA Modules:
  0.0 224.0 jit_solution(7734051422990997863)
XLA Ops:
  3.4 8.8 %collective-permute-start.1 = (bf16[34,1152]{1,0:T(8,128)(2,1)S(1)}, bf16[34,1152]{1,0:T(8,128)(2,1)S(1)}, u32[]{:S(2)}, u32[]{:S(2)}) collective-permute-start(bf16[34,1152]{1,0:T(8,128)(2,1)S(1)} %pad_maximum_fusion.7), channel_id=1, source_target_pairs={{0,1},{1,0},{2,3},{3,2},{4,5},{5,4},{6,7},{7,6},{8,9},{9,8},{10,11... | collective-permute-start | bytes 235016 | tf_op jit(solution)/shard_map/ppermute | solution.py:70
  14.9 3.5 %all-to-all-start = ((bf16[4,68,1152]{2,1,0:T(8,128)(2,1)}), bf16[4,68,1152]{2,1,0:T(8,128)(2,1)S(1)}, u32[]{:S(2)}, u32[]{:S(2)}) async-start(bf16[4,68,1152]{2,1,0:T(8,128)(2,1)} %broadcast_in_dim.18), calls=%async_computation | async-start | bytes 1327104 | tf_op jit(solution)/shard_map/all_to_all | solution.py:74
  18.4 6.4 %collective-permute-start.2 = (bf16[68,1152]{1,0:T(8,128)(2,1)S(1)}, bf16[68,1152]{1,0:T(8,128)(2,1)S(1)}, u32[]{:S(2)}, u32[]{:S(2)}) collective-permute-start(bf16[68,1152]{1,0:T(8,128)(2,1)S(1)} %pad_maximum_fusion.5), channel_id=1, source_target_pairs={{0,456},{1,457},{2,458},{3,459},{4,460},{5,461},{6,462},{7,463},{8... | collective-permute-start | bytes 470024 | tf_op jit(solution)/shard_map/ppermute | solution.py:70
  24.8 15.0 %collective-permute-done.2 = bf16[68,1152]{1,0:T(8,128)(2,1)S(1)} collective-permute-done((bf16[68,1152]{1,0:T(8,128)(2,1)S(1)}, bf16[68,1152]{1,0:T(8,128)(2,1)S(1)}, u32[]{:S(2)}, u32[]{:S(2)}) %collective-permute-start.2) | collective-permute-done | bytes 156704 | tf_op jit(solution)/shard_map/ppermute | solution.py:70
  39.9 12.0 %all_to_all.35 = bf16[4,68,1152]{2,1,0:T(8,128)(2,1)S(1)} all-to-all(bf16[4,68,1152]{2,1,0:T(8,128)(2,1)S(1)} %broadcast_in_dim.19), channel_id=1, replica_groups={{0,2,4,6},{16,18,20,22},{32,34,36,38},{48,50,52,54},{1,17,33,49},{3,19,..., dimensions={0} | all-to-all | bytes 1253376 | tf_op jit(solution)/shard_map/all_to_all | solution.py:74
  54.5 3.7 %all-to-all-start.2 = ((bf16[4,4,72,1152]{3,2,1,0:T(8,128)(2,1)}), bf16[4,4,72,1152]{3,2,1,0:T(8,128)(2,1)S(1)}, u32[]{:S(2)}, u32[]{:S(2)}) async-start(bf16[4,4,72,1152]{3,2,1,0:T(8,128)(2,1)} %broadcast_in_dim.22), calls=%async_computation.2 | async-start | bytes 5308416 | tf_op jit(solution)/shard_map/all_to_all | solution.py:74
  59.4 17.4 %all-to-all-done.2 = bf16[4,4,72,1152]{3,2,1,0:T(8,128)(2,1)S(1)} async-done(((bf16[4,4,72,1152]{3,2,1,0:T(8,128)(2,1)}), bf16[4,4,72,1152]{3,2,1,0:T(8,128)(2,1)S(1)}, u32[]{:S(2)}, u32[]{:S(2)}) %all-to-all-start.2) | async-done | bytes 2654240 | tf_op jit(solution)/shard_map/all_to_all | solution.py:74
  76.8 5.4 %collective-permute-start.3 = (bf16[4,4,72,1152]{3,2,1,0:T(8,128)(2,1)S(1)}, bf16[4,4,72,1152]{3,2,1,0:T(8,128)(2,1)}, u32[]{:S(2)}, u32[]{:S(2)}) collective-permute-start(bf16[4,4,72,1152]{3,2,1,0:T(8,128)(2,1)S(1)} %all-to-all-done.2), channel_id=1, source_target_pairs={{0,1},{1,0},{2,3},{3,2},{4,5},{5,4},{6,7},{7,6},{8,9},{9,8},{10,11... | collective-permute-start | bytes 7962632 | tf_op jit(solution)/shard_map/ppermute | solution.py:70
  84.0 4.6 %all-to-all-start.3 = ((bf16[4,4,64,1152]{3,2,1,0:T(8,128)(2,1)}), bf16[4,4,64,1152]{3,2,1,0:T(8,128)(2,1)}, u32[]{:S(2)}, u32[]{:S(2)}) async-start(bf16[4,4,64,1152]{3,2,1,0:T(8,128)(2,1)} %broadcast_in_dim.23), calls=%async_computation.3 | async-start | bytes 4718592 | tf_op jit(solution)/shard_map/all_to_all | solution.py:74
  88.6 1.9 collective-permute-start
  94.9 2.1 multiply_reduce_fusion.2
  97.0 2.0 copy.11
  98.9 6.8 %all-to-all-done.3 = bf16[4,4,64,1152]{3,2,1,0:T(8,128)(2,1)} async-done(((bf16[4,4,64,1152]{3,2,1,0:T(8,128)(2,1)}), bf16[4,4,64,1152]{3,2,1,0:T(8,128)(2,1)}, u32[]{:S(2)}, u32[]{:S(2)}) %all-to-all-start.3) | async-done | bytes 2359328 | tf_op jit(solution)/shard_map/all_to_all | solution.py:74
  105.7 7.4 %multiply_reduce_fusion = (f32[1024]{0:T(1024)S(1)}, f32[1024,1152]{1,0:T(8,128)}) fusion(bf16[1024,1152]{1,0:T(8,128)(2,1)} %bitcast.8, bf16[1152,1152]{1,0:T(8,128)(2,1)S(1)} %bitcast.41), kind=kOutput, calls=%fused_computation.3 | convolution fusion | flops 2720267264 | bytes 9736192 | tf_op jit(solution)/shard_map/dot_general | solution.py:84
  113.2 6.8 %multiply_reduce_fusion.1 = (f32[256]{0:T(256)S(1)}, f32[256,1152]{1,0:T(8,128)S(1)}) fusion(f32[256,1152]{1,0:T(8,128)} %get-tuple-element.37, f32[256]{0:T(256)S(1)} %add_rsqrt_fusion.1, f32[1024,1152]{1,0:T(8,128)} %get-tuple-element.35, f32[1024]{0:T(1024)S(1)} %add_rsqrt_fusion, f32[]{:T(128)} %bitcast.38, f32[]{:T(128)} %bitcast.37, ...), kind=kOutput, calls=%fused_computation.17 | convolution fusion | flops 1218117376 | bytes 7089676 | tf_op jit(solution)/shard_map/dot_general | solution.py:162
  120.2 2.5 %convolution_convert_fusion = bf16[1152,1152]{1,0:T(8,128)(2,1)} fusion(bf16[256,1152]{1,0:T(8,128)(2,1)S(1)} %multiply_convert_fusion.1, bf16[256,1152]{1,0:T(8,128)(2,1)S(1)} %bitcast.43), kind=kOutput, calls=%fused_computation | convolution fusion | flops 680804352 | bytes 3833856 | tf_op jit(solution)/shard_map/dot_general | solution.py:90
  123.8 3.7 %all-to-all-start.4 = ((bf16[16,72,1152]{2,1,0:T(8,128)(2,1)}), bf16[16,72,1152]{2,1,0:T(8,128)(2,1)S(1)}, u32[]{:S(2)}, u32[]{:S(2)}) async-start(bf16[16,72,1152]{2,1,0:T(8,128)(2,1)} %bitcast.12), calls=%async_computation.4 | async-start | bytes 5308416 | tf_op jit(solution)/shard_map/all_to_all | solution.py:74
  130.6 7.6 %collective-permute-done.4 = bf16[128,1152]{1,0:T(8,128)(2,1)S(1)} collective-permute-done((bf16[128,1152]{1,0:T(8,128)(2,1)S(1)}, bf16[128,1152]{1,0:T(8,128)(2,1)S(1)}, u32[]{:S(2)}, u32[]{:S(2)}) %collective-permute-start.4) | collective-permute-done | bytes 294944 | tf_op jit(solution)/shard_map/ppermute | solution.py:70
  139.4 1.9 collective-permute-start.5
  141.3 9.5 %collective-permute-done.5 = bf16[64,1152]{1,0:T(8,128)(2,1)} collective-permute-done((bf16[64,1152]{1,0:T(8,128)(2,1)S(1)}, bf16[64,1152]{1,0:T(8,128)(2,1)}, u32[]{:S(2)}, u32[]{:S(2)}) %collective-permute-start.5) | collective-permute-done | bytes 147488 | tf_op jit(solution)/shard_map/ppermute | solution.py:70
  151.9 3.0 %collective-permute-start.6 = (bf16[32,1152]{1,0:T(8,128)(2,1)S(1)}, bf16[32,1152]{1,0:T(8,128)(2,1)S(1)}, u32[]{:S(2)}, u32[]{:S(2)}) collective-permute-start(bf16[32,1152]{1,0:T(8,128)(2,1)S(1)} %dynamic-slice_convert_fusion.2), channel_id=1, source_target_pairs={{0,256},{1,257},{2,258},{3,259},{4,260},{5,261},{6,262},{7,263},{8... | collective-permute-start | bytes 221192 | tf_op jit(solution)/shard_map/ppermute | solution.py:70
  154.9 9.4 %collective-permute-done.6 = bf16[32,1152]{1,0:T(8,128)(2,1)S(1)} collective-permute-done((bf16[32,1152]{1,0:T(8,128)(2,1)S(1)}, bf16[32,1152]{1,0:T(8,128)(2,1)S(1)}, u32[]{:S(2)}, u32[]{:S(2)}) %collective-permute-start.6) | collective-permute-done | bytes 73760 | tf_op jit(solution)/shard_map/ppermute | solution.py:70
  166.7 4.6 %collective-permute-start.11 = (bf16[36,1152]{1,0:T(8,128)(2,1)S(1)}, bf16[36,1152]{1,0:T(8,128)(2,1)S(1)}, u32[]{:S(2)}, u32[]{:S(2)}) collective-permute-start(bf16[36,1152]{1,0:T(8,128)(2,1)S(1)} %select_convert_fusion), channel_id=1, source_target_pairs={{0,456},{1,457},{2,458},{3,459},{4,460},{5,461},{6,462},{7,463},{8... | collective-permute-start | bytes 248840 | tf_op jit(solution)/shard_map/ppermute | solution.py:70
  171.3 5.5 %collective-permute-done.7 = bf16[32,1152]{1,0:T(8,128)(2,1)S(1)} collective-permute-done((bf16[32,1152]{1,0:T(8,128)(2,1)S(1)}, bf16[32,1152]{1,0:T(8,128)(2,1)S(1)}, u32[]{:S(2)}, u32[]{:S(2)}) %collective-permute-start.7) | collective-permute-done | bytes 73760 | tf_op jit(solution)/shard_map/ppermute | solution.py:70
  176.8 1.9 collective-permute-start.8
  179.5 7.7 %all-to-all-start.5 = ((bf16[8,5,1152]{2,1,0:T(8,128)(2,1)}), bf16[8,5,1152]{2,1,0:T(8,128)(2,1)S(1)}, u32[]{:S(2)}, u32[]{:S(2)}) async-start(bf16[8,5,1152]{2,1,0:T(8,128)(2,1)} %reshape.55), calls=%async_computation.5 | async-start | bytes 294912 | tf_op jit(solution)/shard_map/all_to_all | solution.py:74
  187.2 2.0 collective-permute-done.8
  189.3 1.9 collective-permute-start.9
  191.3 6.6 %all-to-all-done.5 = bf16[8,5,1152]{2,1,0:T(8,128)(2,1)S(1)} async-done(((bf16[8,5,1152]{2,1,0:T(8,128)(2,1)}), bf16[8,5,1152]{2,1,0:T(8,128)(2,1)S(1)}, u32[]{:S(2)}, u32[]{:S(2)}) %all-to-all-start.5) | async-done | bytes 92192 | tf_op jit(solution)/shard_map/all_to_all | solution.py:74
  198.6 3.4 %all-to-all-start.6 = ((bf16[8,5,1152]{2,1,0:T(8,128)(2,1)}), bf16[8,5,1152]{2,1,0:T(8,128)(2,1)S(1)}, u32[]{:S(2)}, u32[]{:S(2)}) async-start(bf16[8,5,1152]{2,1,0:T(8,128)(2,1)} %broadcast_in_dim.24), calls=%async_computation.6 | async-start | bytes 294912 | tf_op jit(solution)/shard_map/all_to_all | solution.py:74
  204.2 7.6 %collective-permute-start.10 = (f32[128,1152]{1,0:T(8,128)S(1)}, f32[128,1152]{1,0:T(8,128)S(1)}, u32[]{:S(2)}, u32[]{:S(2)}) collective-permute-start(f32[128,1152]{1,0:T(8,128)S(1)} %bitcast.46), channel_id=1, source_target_pairs={{0,1},{1,0},{2,3},{3,2},{4,5},{5,4},{6,7},{7,6},{8,9},{9,8},{10,11... | collective-permute-start | bytes 1769480 | tf_op jit(solution)/shard_map/ppermute | solution.py:70
  212.5 8.8 %collective-permute-start.12 = (f32[18,1152]{1,0:T(8,128)S(1)}, f32[18,1152]{1,0:T(8,128)S(1)}, u32[]{:S(2)}, u32[]{:S(2)}) collective-permute-start(f32[18,1152]{1,0:T(8,128)S(1)} %slice_select_fusion), channel_id=1, source_target_pairs={{0,1},{1,0},{2,3},{3,2},{4,5},{5,4},{6,7},{7,6},{8,9},{9,8},{10,11... | collective-permute-start | bytes 248840 | tf_op jit(solution)/shard_map/ppermute | solution.py:70
  (84 shorter events, 29.3 us)
Async XLA Ops:
  1.8 0.7 copy-start.3
  1.8 12.1 %copy-start.6 = (bf16[128,1152]{1,0:T(8,128)(2,1)}, bf16[128,1152]{1,0:T(8,128)(2,1)S(1)}, u32[]{:S(2)}) copy-start(bf16[128,1152]{1,0:T(8,128)(2,1)S(1)} %get-tuple-element.24) | copy-start | bytes 884740
  3.4 9.7 %collective-permute-start.1 = (bf16[34,1152]{1,0:T(8,128)(2,1)S(1)}, bf16[34,1152]{1,0:T(8,128)(2,1)S(1)}, u32[]{:S(2)}, u32[]{:S(2)}) collective-permute-start(bf16[34,1152]{1,0:T(8,128)(2,1)S(1)} %pad_maximum_fusion.7), channel_id=1, source_target_pairs={{0,1},{1,0},{2,3},{3,2},{4,5},{5,4},{6,7},{7,6},{8,9},{9,8},{10,11... | collective-permute-start | bytes 235016 | tf_op jit(solution)/shard_map/ppermute | solution.py:70
  14.9 24.9 %all-to-all-start = ((bf16[4,68,1152]{2,1,0:T(8,128)(2,1)}), bf16[4,68,1152]{2,1,0:T(8,128)(2,1)S(1)}, u32[]{:S(2)}, u32[]{:S(2)}) async-start(bf16[4,68,1152]{2,1,0:T(8,128)(2,1)} %broadcast_in_dim.18), calls=%async_computation | async-start | bytes 1327104 | tf_op jit(solution)/shard_map/all_to_all | solution.py:74
  18.4 21.4 %collective-permute-start.2 = (bf16[68,1152]{1,0:T(8,128)(2,1)S(1)}, bf16[68,1152]{1,0:T(8,128)(2,1)S(1)}, u32[]{:S(2)}, u32[]{:S(2)}) collective-permute-start(bf16[68,1152]{1,0:T(8,128)(2,1)S(1)} %pad_maximum_fusion.5), channel_id=1, source_target_pairs={{0,456},{1,457},{2,458},{3,459},{4,460},{5,461},{6,462},{7,463},{8... | collective-permute-start | bytes 470024 | tf_op jit(solution)/shard_map/ppermute | solution.py:70
  51.8 0.9 copy-start.2
  54.5 22.3 %all-to-all-start.2 = ((bf16[4,4,72,1152]{3,2,1,0:T(8,128)(2,1)}), bf16[4,4,72,1152]{3,2,1,0:T(8,128)(2,1)S(1)}, u32[]{:S(2)}, u32[]{:S(2)}) async-start(bf16[4,4,72,1152]{3,2,1,0:T(8,128)(2,1)} %broadcast_in_dim.22), calls=%async_computation.2 | async-start | bytes 5308416 | tf_op jit(solution)/shard_map/all_to_all | solution.py:74
  76.8 18.1 %copy-start = (bf16[4,4,72,1152]{3,2,1,0:T(8,128)(2,1)}, bf16[4,4,72,1152]{3,2,1,0:T(8,128)(2,1)S(1)}, u32[]{:S(2)}) copy-start(bf16[4,4,72,1152]{3,2,1,0:T(8,128)(2,1)S(1)} %all-to-all-done.2) | copy-start | bytes 7962628
  76.8 20.2 %collective-permute-start.3 = (bf16[4,4,72,1152]{3,2,1,0:T(8,128)(2,1)S(1)}, bf16[4,4,72,1152]{3,2,1,0:T(8,128)(2,1)}, u32[]{:S(2)}, u32[]{:S(2)}) collective-permute-start(bf16[4,4,72,1152]{3,2,1,0:T(8,128)(2,1)S(1)} %all-to-all-done.2), channel_id=1, source_target_pairs={{0,1},{1,0},{2,3},{3,2},{4,5},{5,4},{6,7},{7,6},{8,9},{9,8},{10,11... | collective-permute-start | bytes 7962632 | tf_op jit(solution)/shard_map/ppermute | solution.py:70
  84.0 4.6 %copy-start.7 = (bf16[128,1152]{1,0:T(8,128)(2,1)S(1)}, bf16[128,1152]{1,0:T(8,128)(2,1)}, u32[]{:S(2)}) copy-start(bf16[128,1152]{1,0:T(8,128)(2,1)} %copy-done.6) | copy-start | bytes 884740
  84.0 9.9 %copy-start.4 = (bf16[128,1152]{1,0:T(8,128)(2,1)S(1)}, bf16[128,1152]{1,0:T(8,128)(2,1)}, u32[]{:S(2)}) copy-start(bf16[128,1152]{1,0:T(8,128)(2,1)} %copy-done.3) | copy-start | bytes 884740
  84.0 21.8 %all-to-all-start.3 = ((bf16[4,4,64,1152]{3,2,1,0:T(8,128)(2,1)}), bf16[4,4,64,1152]{3,2,1,0:T(8,128)(2,1)}, u32[]{:S(2)}, u32[]{:S(2)}) async-start(bf16[4,4,64,1152]{3,2,1,0:T(8,128)(2,1)} %broadcast_in_dim.23), calls=%async_computation.3 | async-start | bytes 4718592 | tf_op jit(solution)/shard_map/all_to_all | solution.py:74
  88.6 4.5 %collective-permute-start = (bf16[128,1152]{1,0:T(8,128)(2,1)S(1)}, bf16[128,1152]{1,0:T(8,128)(2,1)S(1)}, u32[]{:S(2)}, u32[]{:S(2)}) collective-permute-start(bf16[128,1152]{1,0:T(8,128)(2,1)S(1)} %copy-done.7), channel_id=1, source_target_pairs={{0,1},{1,0},{2,3},{3,2},{4,5},{5,4},{6,7},{7,6},{8,9},{9,8},{10,11... | collective-permute-start | bytes 884744 | tf_op jit(solution)/shard_map/ppermute | solution.py:70
  93.2 0.7 copy-start.8
  105.7 7.4 %copy-start.9 = (pred[256]{0:T(512)(128)(4,1)S(1)}, pred[256]{0:T(512)(128)(4,1)}, u32[]{:S(2)}) copy-start(pred[256]{0:T(512)(128)(4,1)} %get-tuple-element.40) | copy-start | bytes 772
  105.7 7.4 %copy-start.10 = (pred[256]{0:T(512)(128)(4,1)S(1)}, pred[256]{0:T(512)(128)(4,1)}, u32[]{:S(2)}) copy-start(pred[256]{0:T(512)(128)(4,1)} %get-tuple-element.41) | copy-start | bytes 772
  113.2 6.8 %copy-start.5 = (f32[256,1152]{1,0:T(8,128)S(1)}, f32[256,1152]{1,0:T(8,128)}, u32[]{:S(2)}) copy-start(f32[256,1152]{1,0:T(8,128)} %get-tuple-element.37) | copy-start | bytes 3538948
  123.8 40.5 %all-to-all-start.4 = ((bf16[16,72,1152]{2,1,0:T(8,128)(2,1)}), bf16[16,72,1152]{2,1,0:T(8,128)(2,1)S(1)}, u32[]{:S(2)}, u32[]{:S(2)}) async-start(bf16[16,72,1152]{2,1,0:T(8,128)(2,1)} %bitcast.12), calls=%async_computation.4 | async-start | bytes 5308416 | tf_op jit(solution)/shard_map/all_to_all | solution.py:74
  128.7 9.6 %collective-permute-start.4 = (bf16[128,1152]{1,0:T(8,128)(2,1)S(1)}, bf16[128,1152]{1,0:T(8,128)(2,1)S(1)}, u32[]{:S(2)}, u32[]{:S(2)}) collective-permute-start(bf16[128,1152]{1,0:T(8,128)(2,1)S(1)} %dynamic-slice_convert_fusion), channel_id=1, source_target_pairs={{0,64},{1,65},{2,66},{3,67},{4,68},{5,69},{6,70},{7,71},{8,72},{9,... | collective-permute-start | bytes 884744 | tf_op jit(solution)/shard_map/ppermute | solution.py:70
  139.4 11.5 %collective-permute-start.5 = (bf16[64,1152]{1,0:T(8,128)(2,1)S(1)}, bf16[64,1152]{1,0:T(8,128)(2,1)}, u32[]{:S(2)}, u32[]{:S(2)}) collective-permute-start(bf16[64,1152]{1,0:T(8,128)(2,1)S(1)} %dynamic-slice_convert_fusion.1), channel_id=1, source_target_pairs={{0,128},{1,129},{2,130},{3,131},{4,132},{5,133},{6,134},{7,135},{8... | collective-permute-start | bytes 442376 | tf_op jit(solution)/shard_map/ppermute | solution.py:70
  151.9 12.4 %collective-permute-start.6 = (bf16[32,1152]{1,0:T(8,128)(2,1)S(1)}, bf16[32,1152]{1,0:T(8,128)(2,1)S(1)}, u32[]{:S(2)}, u32[]{:S(2)}) collective-permute-start(bf16[32,1152]{1,0:T(8,128)(2,1)S(1)} %dynamic-slice_convert_fusion.2), channel_id=1, source_target_pairs={{0,256},{1,257},{2,258},{3,259},{4,260},{5,261},{6,262},{7,263},{8... | collective-permute-start | bytes 221192 | tf_op jit(solution)/shard_map/ppermute | solution.py:70
  164.7 12.0 %collective-permute-start.7 = (bf16[32,1152]{1,0:T(8,128)(2,1)S(1)}, bf16[32,1152]{1,0:T(8,128)(2,1)S(1)}, u32[]{:S(2)}, u32[]{:S(2)}) collective-permute-start(bf16[32,1152]{1,0:T(8,128)(2,1)S(1)} %add_convert_fusion.1), channel_id=1, source_target_pairs={{0,256},{1,257},{2,258},{3,259},{4,260},{5,261},{6,262},{7,263},{8... | collective-permute-start | bytes 221192 | tf_op jit(solution)/shard_map/ppermute | solution.py:70
  166.7 12.0 %collective-permute-start.11 = (bf16[36,1152]{1,0:T(8,128)(2,1)S(1)}, bf16[36,1152]{1,0:T(8,128)(2,1)S(1)}, u32[]{:S(2)}, u32[]{:S(2)}) collective-permute-start(bf16[36,1152]{1,0:T(8,128)(2,1)S(1)} %select_convert_fusion), channel_id=1, source_target_pairs={{0,456},{1,457},{2,458},{3,459},{4,460},{5,461},{6,462},{7,463},{8... | collective-permute-start | bytes 248840 | tf_op jit(solution)/shard_map/ppermute | solution.py:70
  176.8 12.5 %collective-permute-start.8 = (bf16[64,1152]{1,0:T(8,128)(2,1)S(1)}, bf16[64,1152]{1,0:T(8,128)(2,1)S(1)}, u32[]{:S(2)}, u32[]{:S(2)}) collective-permute-start(bf16[64,1152]{1,0:T(8,128)(2,1)S(1)} %pad_maximum_fusion.6), channel_id=1, source_target_pairs={{0,128},{1,129},{2,130},{3,131},{4,132},{5,133},{6,134},{7,135},{8... | collective-permute-start | bytes 442376 | tf_op jit(solution)/shard_map/ppermute | solution.py:70
  178.8 24.3 %copy-start.1 = (bf16[4,4,72,1152]{3,2,1,0:T(8,128)(2,1)S(1)}, bf16[4,4,72,1152]{3,2,1,0:T(8,128)(2,1)}, u32[]{:S(2)}) copy-start(bf16[4,4,72,1152]{3,2,1,0:T(8,128)(2,1)} %copy-done) | copy-start | bytes 7962628
  179.5 18.4 %all-to-all-start.5 = ((bf16[8,5,1152]{2,1,0:T(8,128)(2,1)}), bf16[8,5,1152]{2,1,0:T(8,128)(2,1)S(1)}, u32[]{:S(2)}, u32[]{:S(2)}) async-start(bf16[8,5,1152]{2,1,0:T(8,128)(2,1)} %reshape.55), calls=%async_computation.5 | async-start | bytes 294912 | tf_op jit(solution)/shard_map/all_to_all | solution.py:74
  189.3 12.7 %collective-permute-start.9 = (bf16[128,1152]{1,0:T(8,128)(2,1)S(1)}, bf16[128,1152]{1,0:T(8,128)(2,1)}, u32[]{:S(2)}, u32[]{:S(2)}) collective-permute-start(bf16[128,1152]{1,0:T(8,128)(2,1)S(1)} %pad_maximum_fusion.4), channel_id=1, source_target_pairs={{0,64},{1,65},{2,66},{3,67},{4,68},{5,69},{6,70},{7,71},{8,72},{9,... | collective-permute-start | bytes 884744 | tf_op jit(solution)/shard_map/ppermute | solution.py:70
  198.6 13.8 %all-to-all-start.6 = ((bf16[8,5,1152]{2,1,0:T(8,128)(2,1)}), bf16[8,5,1152]{2,1,0:T(8,128)(2,1)S(1)}, u32[]{:S(2)}, u32[]{:S(2)}) async-start(bf16[8,5,1152]{2,1,0:T(8,128)(2,1)} %broadcast_in_dim.24), calls=%async_computation.6 | async-start | bytes 294912 | tf_op jit(solution)/shard_map/all_to_all | solution.py:74
  204.2 18.7 %collective-permute-start.10 = (f32[128,1152]{1,0:T(8,128)S(1)}, f32[128,1152]{1,0:T(8,128)S(1)}, u32[]{:S(2)}, u32[]{:S(2)}) collective-permute-start(f32[128,1152]{1,0:T(8,128)S(1)} %bitcast.46), channel_id=1, source_target_pairs={{0,1},{1,0},{2,3},{3,2},{4,5},{5,4},{6,7},{7,6},{8,9},{9,8},{10,11... | collective-permute-start | bytes 1769480 | tf_op jit(solution)/shard_map/ppermute | solution.py:70
  212.5 9.7 %collective-permute-start.12 = (f32[18,1152]{1,0:T(8,128)S(1)}, f32[18,1152]{1,0:T(8,128)S(1)}, u32[]{:S(2)}, u32[]{:S(2)}) collective-permute-start(f32[18,1152]{1,0:T(8,128)S(1)} %slice_select_fusion), channel_id=1, source_target_pairs={{0,1},{1,0},{2,3},{3,2},{4,5},{5,4},{6,7},{7,6},{8,9},{9,8},{10,11... | collective-permute-start | bytes 248840 | tf_op jit(solution)/shard_map/ppermute | solution.py:70

commit v6 on v5

--- a/solution.py
+++ b/solution.py
@@ -53,11 +53,7 @@
 
 INNER, OUTER = crossed("x"), crossed("y")
 PLANE = [
-    [
-        place(blk, slow, zh, fast, core) if core == 0 else place(blk, fast, zh, slow, core)
-        for slow in range(4)
-        for fast in range(4)
-    ]
+    [place(blk, y, zh, x, core) for y in range(N_Y) for x in range(N_X)]
     for blk in range(N_BLK)
     for zh in range(N_ZH)
     for core in range(N_CORE)
@@ -111,47 +107,64 @@
 
     low = zh == 0
     img_t, txt_t = img_proj.T, txt_proj.T
-    keep_t = jnp.where(first, img_t, txt_t)
-    keep_f = jnp.where(first, img_feat, txt_feat)
-    give_f = jnp.where(first, txt_feat, img_feat)
-    give_sub = lax.dynamic_slice_in_dim(keep_f, sub * sub_rows, sub_rows, 0)
-    keep_sub = lax.dynamic_slice_in_dim(give_f, sub * sub_rows, sub_rows, 0)
-    got = permuted(jnp.concatenate([jnp.where(first, txt_t, img_t), give_sub], 0), sibling)
-    got_t, got_sub = got[:cols], got[cols:]
+    own_f, other_f = jnp.where(first, img_feat, txt_feat), jnp.where(first, txt_feat, img_feat)
+    own_sub = lax.dynamic_slice_in_dim(own_f, sub * sub_rows, sub_rows, 0)
+    other_sub = lax.dynamic_slice_in_dim(other_f, sub * sub_rows, sub_rows, 0)
+    ours = jnp.concatenate([own_sub, jnp.where(first, img_t, txt_t)], 0)
+    theirs = jnp.concatenate([other_sub, jnp.where(first, txt_t, img_t)], 0)
+
+    def joined(mine, siblings):
+        mine_t, siblings_t = mine[sub_rows:], siblings[sub_rows:]
+        return jnp.concatenate(
+            [
+                mine[:sub_rows],
+                siblings[:sub_rows],
+                jnp.where(first, mine_t, siblings_t),
+                jnp.where(first, siblings_t, mine_t),
+            ],
+            0,
+        )
+
+    far = joined(
+        permuted(ours, mirror), permuted(theirs, lambda device: mirror(sibling(device)))
+    )
+    near = gathered(joined(ours, permuted(theirs, sibling)), INNER)
+    far = gathered(far, INNER)
+    picked = N_CORE * sub_rows
     pair = N_CORE * cols
-    near = jnp.concatenate(
-        [jnp.where(first, keep_t, got_t), jnp.where(first, got_t, keep_t), keep_sub, got_sub], 0
-    )
-    far = gathered(permuted(near, mirror), INNER)
-    near = gathered(near, INNER)
-    proj = jnp.concatenate(
+    both = jnp.concatenate(
         [
-            jnp.where(low, near[:, :pair], far[:, :pair]),
-            jnp.where(low, far[:, :pair], near[:, :pair]),
+            near[:, :picked],
+            far[:, :picked],
+            jnp.where(low, near[:, picked:], far[:, picked:]),
+            jnp.where(low, far[:, picked:], near[:, picked:]),
         ],
         1,
     )
-    others = jnp.concatenate([near[:, pair:], far[:, pair:]], 1)
-    proj, others = lax.optimization_barrier((gathered(proj, OUTER), others))
-    others = gathered(others, OUTER).reshape(-1, width)
-    other_proj = permuted(proj, sibling).transpose(1, 0, 2, 3).reshape(-1, width)
-    proj = proj.reshape(-1, width)
+    both = gathered(both, OUTER)
+    others = both[:, :, : N_ZH * picked].reshape(-1, width)
+    proj = both[:, :, N_ZH * picked :]
+    proj = jnp.where(first, proj, proj.transpose(1, 0, 2, 3)).reshape(-1, width)
     embed = proj.shape[0]
 
-    got_f = permuted(give_f, sibling)
-    feat = jnp.stack(
-        [keep_f.reshape(N_BLK, sub_rows, width), got_f.reshape(N_BLK, sub_rows, width)], 1
-    ).reshape(own, width)
-
-    def embedded(rows_of, columns_of):
-        proj_out = contract_last(rows_of, columns_of)
+    sib_feat = permuted(jnp.concatenate([own_f, other_f], 0), sibling)
+    sib_other, sib_own = sib_feat[:rows], sib_feat[rows:]
+
+    def interleaved(one, two):
+        shape = (N_BLK, sub_rows, width)
+        return jnp.stack([one.reshape(shape), two.reshape(shape)], 1).reshape(own, width)
+
+    feat = interleaved(other_f, sib_other)
+
+    def normalized(proj_out):
         inverse = lax.rsqrt(jnp.sum(proj_out * proj_out, axis=1, keepdims=True) + 1e-06)
         return proj_out * inverse, inverse
 
-    unit, inverse = embedded(feat, proj)
+    made = contract_last(interleaved(sib_own, own_f), proj)
+    unit, inverse = normalized(permuted(made, sibling))
     emb = unit.astype(bf16)
-    others = embedded(others, other_proj)[0].astype(bf16)
-    spot = jnp.where(first, y * N_X + x, x * N_Y + y) * (N_ZH * N_CORE * sub_rows)
+    others = normalized(contract_last(others, proj))[0].astype(bf16)
+    spot = jnp.where(first, y * N_X + x, x * N_Y + y) * (N_ZH * picked)
 
     logits = scale * contract_last(emb, others) + shift_by
     row = lax.broadcasted_iota(jnp.int32, logits.shape, 0) - sub * (N_CORE * sub_rows)
@@ -186,17 +199,17 @@
     terms = jnp.pad(terms, ((0, -pair % N_BLK), (0, 0))).reshape(N_BLK, -1, width)
     terms = jnp.sum(exchanged(terms, LINE).astype(f32), 0).astype(bf16)
     total = gathered(terms, LINE).reshape(-1, width).astype(f32)
-    keep_g = jnp.where(first, total[:cols], total[cols : 2 * cols])
-    got_g = permuted(jnp.where(first, total[cols : 2 * cols], total[:cols]), sibling)
-    img_proj_grad = jnp.where(first, keep_g, got_g).T
-    txt_proj_grad = jnp.where(first, got_g, keep_g).T
-
-    grad = jnp.dot(du, proj, preferred_element_type=f32)
+    keep_g = jnp.where(first, total[:cols], total[cols:pair])
+    got_g = permuted(jnp.where(first, total[cols:pair], total[:cols]), sibling)
+    img_proj_grad = jnp.where(first, got_g, keep_g).T
+    txt_proj_grad = jnp.where(first, keep_g, got_g).T
+
+    grad = jnp.dot(du, permuted(proj, sibling), preferred_element_type=f32)
     grad = grad.reshape(N_BLK, N_CORE, sub_rows, width)
     keep_r = grad[:, 0].reshape(rows, width)
     got_r = permuted(grad[:, 1].reshape(rows, width), sibling)
-    img_grad = jnp.where(first, keep_r, got_r)
-    txt_grad = jnp.where(first, got_r, keep_r)
+    img_grad = jnp.where(first, got_r, keep_r)
+    txt_grad = jnp.where(first, keep_r, got_r)
     return (img_grad, txt_grad, img_proj_grad, txt_proj_grad)
 
 

time: 225 us -> 227 us (level)
  starting transfers between devices: 82.8 us -> 97 us
  blocking collectives: 12 us -> 0 us
    all_to_all x6, waiting for transfers between devices: 31.4 us -> 49.8 us  [exchanged(): lax.all_to_all(value, BOTH, 0, 0, axis_index_groups=groups, tiled=True)]
    ppermute x13 -> x15, waiting for transfers between devices: 50.8 us -> 34.3 us  [permuted(): return lax.ppermute(value, BOTH, pairs)]
    ppermute x13 -> x15, starting transfers between devices: 56.1 us -> 68.9 us  [permuted(): return lax.ppermute(value, BOTH, pairs)]
    all_to_all x1 -> x0, blocking collectives: 12 us -> none  [exchanged(): lax.all_to_all(value, BOTH, 0, 0, axis_index_groups=groups, tiled=True)]
    slice x3 -> x8, local copies, waits for them, and re-layouts: 1.16 us -> 4.09 us  [the longest x1 2.03 us: body(): others = both[:, :, :N_ZH * picked].reshape(-1, width)]
    broadcast_in_dim x5 -> x4, local copies, waits for them, and re-layouts: 5.01 us -> 5.1 us  [gathered(): copies = jnp.broadcast_to(value[None], (count,) + value.shape)]
  transfers between devices with their start and end apart: 19 -> 21, of which waited for: 12 -> 13; matrix products, arithmetic and copies ran while one was open for 7% -> 8% of each run, Pallas kernels for 0% -> 0%
where the time goes in v6:
time: 227 us; the launch traced here: 226 us
  starting transfers between devices  97 us (43%)
  waiting for transfers between devices  84.1 us (37%)
  matrix products  18.7 us (8%)
  local copies, waits for them, and re-layouts  13.1 us (6%)
  other arithmetic  9.74 us (4%)
  between operations  3.23 us (1%)
    ppermute x15, starting transfers between devices, permuted(): return lax.ppermute(value, BOTH, pairs)  68.9 us
    all_to_all x6, waiting for transfers between devices, exchanged(): lax.all_to_all(value, BOTH, 0, 0, axis_index_groups=groups, tiled=True)  49.8 us
    ppermute x15, waiting for transfers between devices, permuted(): return lax.ppermute(value, BOTH, pairs)  34.3 us
    all_to_all x6, starting transfers between devices, exchanged(): lax.all_to_all(value, BOTH, 0, 0, axis_index_groups=groups, tiled=True)  28 us
    dot_general x2, matrix products, contract_last(): lax.dot_general(left, right, (((1,), (1,)), ((), ())), preferred_element_...  7.43 us
    dot_general x1, matrix products, body(): grad_unit = scale * jnp.dot(coef, others, preferred_element_type=f32)  5.97 us
    broadcast_in_dim x4, local copies, waits for them, and re-layouts, gathered(): copies = jnp.broadcast_to(value[None], (count,) + value.shape)  5.1 us
  transfers between devices with their start and end apart: 21, of which 13 were waited for; matrix products, arithmetic and copies ran while one was open for 8% of the time, Pallas kernels for 0%

profile of v6, /device:TPU:1, one launch (start us, length us, event | category | flops | bytes accessed | tf_op | source)
XLA Modules:
  0.0 225.8 jit_solution(17029605558276343174)
XLA Ops:
  2.7 8.8 %collective-permute-start.1 = (bf16[34,1152]{1,0:T(8,128)(2,1)S(1)}, bf16[34,1152]{1,0:T(8,128)(2,1)S(1)}, u32[]{:S(2)}, u32[]{:S(2)}) collective-permute-start(bf16[34,1152]{1,0:T(8,128)(2,1)S(1)} %pad_maximum_fusion.8), channel_id=1, source_target_pairs={{0,1},{1,0},{2,3},{3,2},{4,5},{5,4},{6,7},{7,6},{8,9},{9,8},{10,11... | collective-permute-start | bytes 235016 | tf_op jit(solution)/shard_map/ppermute | solution.py:66
  11.5 5.6 %collective-permute-start.3 = (bf16[34,1152]{1,0:T(8,128)(2,1)S(1)}, bf16[34,1152]{1,0:T(8,128)(2,1)S(1)}, u32[]{:S(2)}, u32[]{:S(2)}) collective-permute-start(bf16[34,1152]{1,0:T(8,128)(2,1)S(1)} %pad_maximum_fusion.8), channel_id=1, source_target_pairs={{0,457},{1,456},{2,459},{3,458},{4,461},{5,460},{6,463},{7,462},{8... | collective-permute-start | bytes 235016 | tf_op jit(solution)/shard_map/ppermute | solution.py:66
  21.0 4.2 %all-to-all-start = ((bf16[4,68,1152]{2,1,0:T(8,128)(2,1)}), bf16[4,68,1152]{2,1,0:T(8,128)(2,1)S(1)}, u32[]{:S(2)}, u32[]{:S(2)}) async-start(bf16[4,68,1152]{2,1,0:T(8,128)(2,1)} %broadcast_in_dim.18), calls=%async_computation | async-start | bytes 1327104 | tf_op jit(solution)/shard_map/all_to_all | solution.py:70
  25.2 5.3 %collective-permute-done.3 = bf16[34,1152]{1,0:T(8,128)(2,1)S(1)} collective-permute-done((bf16[34,1152]{1,0:T(8,128)(2,1)S(1)}, bf16[34,1152]{1,0:T(8,128)(2,1)S(1)}, u32[]{:S(2)}, u32[]{:S(2)}) %collective-permute-start.3) | collective-permute-done | bytes 78368 | tf_op jit(solution)/shard_map/ppermute | solution.py:66
  30.5 3.6 %collective-permute-done.2 = bf16[34,1152]{1,0:T(8,128)(2,1)S(1)} collective-permute-done((bf16[34,1152]{1,0:T(8,128)(2,1)S(1)}, bf16[34,1152]{1,0:T(8,128)(2,1)S(1)}, u32[]{:S(2)}, u32[]{:S(2)}) %collective-permute-start.2) | collective-permute-done | bytes 78368 | tf_op jit(solution)/shard_map/ppermute | solution.py:66
  35.0 4.2 %all-to-all-start.1 = ((bf16[4,68,1152]{2,1,0:T(8,128)(2,1)}), bf16[4,68,1152]{2,1,0:T(8,128)(2,1)S(1)}, u32[]{:S(2)}, u32[]{:S(2)}) async-start(bf16[4,68,1152]{2,1,0:T(8,128)(2,1)} %broadcast_in_dim.19), calls=%async_computation.1 | async-start | bytes 1327104 | tf_op jit(solution)/shard_map/all_to_all | solution.py:70
  39.2 7.9 %all-to-all-done.1 = bf16[4,68,1152]{2,1,0:T(8,128)(2,1)S(1)} async-done(((bf16[4,68,1152]{2,1,0:T(8,128)(2,1)}), bf16[4,68,1152]{2,1,0:T(8,128)(2,1)S(1)}, u32[]{:S(2)}, u32[]{:S(2)}) %all-to-all-start.1) | async-done | bytes 626720 | tf_op jit(solution)/shard_map/all_to_all | solution.py:70
  50.1 5.0 %all-to-all-start.2 = ((bf16[4,4,136,1152]{3,2,1,0:T(8,128)(2,1)}), bf16[4,4,136,1152]{3,2,1,0:T(8,128)(2,1)}, u32[]{:S(2)}, u32[]{:S(2)}) async-start(bf16[4,4,136,1152]{3,2,1,0:T(8,128)(2,1)} %broadcast_in_dim.20), calls=%async_computation.2 | async-start | bytes 10027008 | tf_op jit(solution)/shard_map/all_to_all | solution.py:70
  55.1 3.5 %collective-permute-start = (bf16[256,1152]{1,0:T(8,128)(2,1)S(1)}, bf16[256,1152]{1,0:T(8,128)(2,1)S(1)}, u32[]{:S(2)}, u32[]{:S(2)}) collective-permute-start(bf16[256,1152]{1,0:T(8,128)(2,1)S(1)} %pad_maximum_fusion.1), channel_id=1, source_target_pairs={{0,1},{1,0},{2,3},{3,2},{4,5},{5,4},{6,7},{7,6},{8,9},{9,8},{10,11... | collective-permute-start | bytes 1769480 | tf_op jit(solution)/shard_map/ppermute | solution.py:66
  60.3 26.1 %all-to-all-done.2 = bf16[4,4,136,1152]{3,2,1,0:T(8,128)(2,1)} async-done(((bf16[4,4,136,1152]{3,2,1,0:T(8,128)(2,1)}), bf16[4,4,136,1152]{3,2,1,0:T(8,128)(2,1)}, u32[]{:S(2)}, u32[]{:S(2)}) %all-to-all-start.2) | async-done | bytes 5013536 | tf_op jit(solution)/shard_map/all_to_all | solution.py:70
  92.3 4.3 %collective-permute-start.4 = (f32[256,1152]{1,0:T(8,128)}, f32[256,1152]{1,0:T(8,128)S(1)}, u32[]{:S(2)}, u32[]{:S(2)}) collective-permute-start(f32[256,1152]{1,0:T(8,128)} %fusion.33), channel_id=1, source_target_pairs={{0,1},{1,0},{2,3},{3,2},{4,5},{5,4},{6,7},{7,6},{8,9},{9,8},{10,11... | collective-permute-start | bytes 3538952 | tf_op jit(solution)/shard_map/ppermute | solution.py:66
  101.1 5.3 %multiply_reduce_fusion = (f32[1024]{0:T(1024)S(1)}, f32[1024,1152]{1,0:T(8,128)}) fusion(bf16[1024,1152]{1,0:T(8,128)(2,1)S(1)} %bitcast.43, bf16[1152,1152]{1,0:T(8,128)(2,1)S(1)} %bitcast.41), kind=kOutput, calls=%fused_computation.3 | convolution fusion | flops 2720267264 | bytes 9736192 | tf_op jit(solution)/shard_map/dot_general | solution.py:80
  106.6 6.0 %multiply_reduce_fusion.1 = (f32[256]{0:T(256)S(1)}, f32[256,1152]{1,0:T(8,128)S(1)}) fusion(f32[256,1152]{1,0:T(8,128)S(1)} %collective-permute-done.4, f32[256]{0:T(256)S(1)} %add_rsqrt_fusion.1, f32[1024,1152]{1,0:T(8,128)} %get-tuple-element.35, f32[1024]{0:T(1024)S(1)} %add_rsqrt_fusion, f32[]{:T(128)} %bitcast.36, f32[]{:T(128)} %bitcast.35, ...), kind=kOutput, calls=%fused_computation.19 | convolution fusion | flops 1218117376 | bytes 7089676 | tf_op jit(solution)/shard_map/dot_general | solution.py:175
  116.4 3.7 %all-to-all-start.3 = ((bf16[16,72,1152]{2,1,0:T(8,128)(2,1)}), bf16[16,72,1152]{2,1,0:T(8,128)(2,1)S(1)}, u32[]{:S(2)}, u32[]{:S(2)}) async-start(bf16[16,72,1152]{2,1,0:T(8,128)(2,1)} %bitcast.14), calls=%async_computation.3 | async-start | bytes 5308416 | tf_op jit(solution)/shard_map/all_to_all | solution.py:70
  123.8 8.0 %collective-permute-done.5 = bf16[128,1152]{1,0:T(8,128)(2,1)S(1)} collective-permute-done((bf16[128,1152]{1,0:T(8,128)(2,1)S(1)}, bf16[128,1152]{1,0:T(8,128)(2,1)S(1)}, u32[]{:S(2)}, u32[]{:S(2)}) %collective-permute-start.5) | collective-permute-done | bytes 294944 | tf_op jit(solution)/shard_map/ppermute | solution.py:66
  132.9 4.1 %collective-permute-start.6 = (bf16[64,1152]{1,0:T(8,128)(2,1)S(1)}, bf16[64,1152]{1,0:T(8,128)(2,1)}, u32[]{:S(2)}, u32[]{:S(2)}) collective-permute-start(bf16[64,1152]{1,0:T(8,128)(2,1)S(1)} %dynamic-slice_convert_fusion.1), channel_id=1, source_target_pairs={{0,128},{1,129},{2,130},{3,131},{4,132},{5,133},{6,134},{7,135},{8... | collective-permute-start | bytes 442376 | tf_op jit(solution)/shard_map/ppermute | solution.py:66
  137.1 6.7 %collective-permute-done.6 = bf16[64,1152]{1,0:T(8,128)(2,1)} collective-permute-done((bf16[64,1152]{1,0:T(8,128)(2,1)S(1)}, bf16[64,1152]{1,0:T(8,128)(2,1)}, u32[]{:S(2)}, u32[]{:S(2)}) %collective-permute-start.6) | collective-permute-done | bytes 147488 | tf_op jit(solution)/shard_map/ppermute | solution.py:66
  144.8 7.7 %collective-permute-start.7 = (bf16[32,1152]{1,0:T(8,128)(2,1)S(1)}, bf16[32,1152]{1,0:T(8,128)(2,1)S(1)}, u32[]{:S(2)}, u32[]{:S(2)}) collective-permute-start(bf16[32,1152]{1,0:T(8,128)(2,1)S(1)} %dynamic-slice_convert_fusion.2), channel_id=1, source_target_pairs={{0,256},{1,257},{2,258},{3,259},{4,260},{5,261},{6,262},{7,263},{8... | collective-permute-start | bytes 221192 | tf_op jit(solution)/shard_map/ppermute | solution.py:66
  152.5 2.7 %collective-permute-start.11 = (bf16[1152,1152]{1,0:T(8,128)(2,1)}, bf16[1152,1152]{1,0:T(8,128)(2,1)}, u32[]{:S(2)}, u32[]{:S(2)}) collective-permute-start(bf16[1152,1152]{1,0:T(8,128)(2,1)} %bitcast.40), channel_id=1, source_target_pairs={{0,1},{1,0},{2,3},{3,2},{4,5},{5,4},{6,7},{7,6},{8,9},{9,8},{10,11... | collective-permute-start | bytes 7962632 | tf_op jit(solution)/shard_map/ppermute | solution.py:66
  155.2 2.7 %collective-permute-done.7 = bf16[32,1152]{1,0:T(8,128)(2,1)S(1)} collective-permute-done((bf16[32,1152]{1,0:T(8,128)(2,1)S(1)}, bf16[32,1152]{1,0:T(8,128)(2,1)S(1)}, u32[]{:S(2)}, u32[]{:S(2)}) %collective-permute-start.7) | collective-permute-done | bytes 73760 | tf_op jit(solution)/shard_map/ppermute | solution.py:66
  157.9 4.3 %all-to-all-done.3 = bf16[16,72,1152]{2,1,0:T(8,128)(2,1)S(1)} async-done(((bf16[16,72,1152]{2,1,0:T(8,128)(2,1)}), bf16[16,72,1152]{2,1,0:T(8,128)(2,1)S(1)}, u32[]{:S(2)}, u32[]{:S(2)}) %all-to-all-start.3) | async-done | bytes 2654240 | tf_op jit(solution)/shard_map/all_to_all | solution.py:70
  162.6 6.9 %collective-permute-start.8 = (bf16[32,1152]{1,0:T(8,128)(2,1)S(1)}, bf16[32,1152]{1,0:T(8,128)(2,1)S(1)}, u32[]{:S(2)}, u32[]{:S(2)}) collective-permute-start(bf16[32,1152]{1,0:T(8,128)(2,1)S(1)} %add_convert_fusion.1), channel_id=1, source_target_pairs={{0,256},{1,257},{2,258},{3,259},{4,260},{5,261},{6,262},{7,263},{8... | collective-permute-start | bytes 221192 | tf_op jit(solution)/shard_map/ppermute | solution.py:66
  169.6 7.5 %collective-permute-start.13 = (bf16[36,1152]{1,0:T(8,128)(2,1)S(1)}, bf16[36,1152]{1,0:T(8,128)(2,1)S(1)}, u32[]{:S(2)}, u32[]{:S(2)}) collective-permute-start(bf16[36,1152]{1,0:T(8,128)(2,1)S(1)} %select_convert_fusion), channel_id=1, source_target_pairs={{0,456},{1,457},{2,458},{3,459},{4,460},{5,461},{6,462},{7,463},{8... | collective-permute-start | bytes 248840 | tf_op jit(solution)/shard_map/ppermute | solution.py:66
  179.0 5.5 %collective-permute-done.13 = bf16[36,1152]{1,0:T(8,128)(2,1)S(1)} collective-permute-done((bf16[36,1152]{1,0:T(8,128)(2,1)S(1)}, bf16[36,1152]{1,0:T(8,128)(2,1)S(1)}, u32[]{:S(2)}, u32[]{:S(2)}) %collective-permute-start.13) | collective-permute-done | bytes 82976 | tf_op jit(solution)/shard_map/ppermute | solution.py:66
  185.3 5.1 %all-to-all-start.4 = ((bf16[8,5,1152]{2,1,0:T(8,128)(2,1)}), bf16[8,5,1152]{2,1,0:T(8,128)(2,1)S(1)}, u32[]{:S(2)}, u32[]{:S(2)}) async-start(bf16[8,5,1152]{2,1,0:T(8,128)(2,1)} %reshape.56), calls=%async_computation.4 | async-start | bytes 294912 | tf_op jit(solution)/shard_map/all_to_all | solution.py:70
  190.5 3.4 %collective-permute-start.10 = (bf16[128,1152]{1,0:T(8,128)(2,1)S(1)}, bf16[128,1152]{1,0:T(8,128)(2,1)S(1)}, u32[]{:S(2)}, u32[]{:S(2)}) collective-permute-start(bf16[128,1152]{1,0:T(8,128)(2,1)S(1)} %pad_maximum_fusion.4), channel_id=1, source_target_pairs={{0,64},{1,65},{2,66},{3,67},{4,68},{5,69},{6,70},{7,71},{8,72},{9,... | collective-permute-start | bytes 884744 | tf_op jit(solution)/shard_map/ppermute | solution.py:66
  193.8 7.2 %all-to-all-done.4 = bf16[8,5,1152]{2,1,0:T(8,128)(2,1)S(1)} async-done(((bf16[8,5,1152]{2,1,0:T(8,128)(2,1)}), bf16[8,5,1152]{2,1,0:T(8,128)(2,1)S(1)}, u32[]{:S(2)}, u32[]{:S(2)}) %all-to-all-start.4) | async-done | bytes 92192 | tf_op jit(solution)/shard_map/all_to_all | solution.py:70
  201.8 5.8 %all-to-all-start.5 = ((bf16[8,5,1152]{2,1,0:T(8,128)(2,1)}), bf16[8,5,1152]{2,1,0:T(8,128)(2,1)S(1)}, u32[]{:S(2)}, u32[]{:S(2)}) async-start(bf16[8,5,1152]{2,1,0:T(8,128)(2,1)} %broadcast_in_dim.21), calls=%async_computation.5 | async-start | bytes 294912 | tf_op jit(solution)/shard_map/all_to_all | solution.py:70
  207.8 2.7 %fusion.11 = f32[256,1152]{1,0:T(8,128)S(1)} fusion(bf16[1152,1152]{1,0:T(8,128)(2,1)} %collective-permute-done.11, bf16[128,1152]{1,0:T(8,128)(2,1)S(1)} %get-tuple-element.21, bf16[128,1152]{1,0:T(8,128)(2,1)S(1)} %get-tuple-element.20), kind=kOutput, calls=%fused_computation.28 | convolution fusion | flops 680656896 | bytes 4423680 | tf_op jit(solution)/shard_map/dot_general | solution.py:207
  210.6 3.2 %collective-permute-start.12 = (f32[128,1152]{1,0:T(8,128)S(1)}, f32[128,1152]{1,0:T(8,128)S(1)}, u32[]{:S(2)}, u32[]{:S(2)}) collective-permute-start(f32[128,1152]{1,0:T(8,128)S(1)} %bitcast.48), channel_id=1, source_target_pairs={{0,1},{1,0},{2,3},{3,2},{4,5},{5,4},{6,7},{7,6},{8,9},{9,8},{10,11... | collective-permute-start | bytes 1769480 | tf_op jit(solution)/shard_map/ppermute | solution.py:66
  213.8 4.3 %all-to-all-done.5 = bf16[8,5,1152]{2,1,0:T(8,128)(2,1)S(1)} async-done(((bf16[8,5,1152]{2,1,0:T(8,128)(2,1)}), bf16[8,5,1152]{2,1,0:T(8,128)(2,1)S(1)}, u32[]{:S(2)}, u32[]{:S(2)}) %all-to-all-start.5) | async-done | bytes 92192 | tf_op jit(solution)/shard_map/all_to_all | solution.py:70
  218.2 4.8 %collective-permute-start.14 = (f32[18,1152]{1,0:T(8,128)S(1)}, f32[18,1152]{1,0:T(8,128)S(1)}, u32[]{:S(2)}, u32[]{:S(2)}) collective-permute-start(f32[18,1152]{1,0:T(8,128)S(1)} %slice_select_fusion.1), channel_id=1, source_target_pairs={{0,1},{1,0},{2,3},{3,2},{4,5},{5,4},{6,7},{7,6},{8,9},{9,8},{10,11... | collective-permute-start | bytes 248840 | tf_op jit(solution)/shard_map/ppermute | solution.py:66
  (78 shorter events, 36.5 us)
Async XLA Ops:
  2.7 14.5 %collective-permute-start.1 = (bf16[34,1152]{1,0:T(8,128)(2,1)S(1)}, bf16[34,1152]{1,0:T(8,128)(2,1)S(1)}, u32[]{:S(2)}, u32[]{:S(2)}) collective-permute-start(bf16[34,1152]{1,0:T(8,128)(2,1)S(1)} %pad_maximum_fusion.8), channel_id=1, source_target_pairs={{0,1},{1,0},{2,3},{3,2},{4,5},{5,4},{6,7},{7,6},{8,9},{9,8},{10,11... | collective-permute-start | bytes 235016 | tf_op jit(solution)/shard_map/ppermute | solution.py:66
  11.5 19.0 %collective-permute-start.3 = (bf16[34,1152]{1,0:T(8,128)(2,1)S(1)}, bf16[34,1152]{1,0:T(8,128)(2,1)S(1)}, u32[]{:S(2)}, u32[]{:S(2)}) collective-permute-start(bf16[34,1152]{1,0:T(8,128)(2,1)S(1)} %pad_maximum_fusion.8), channel_id=1, source_target_pairs={{0,457},{1,456},{2,459},{3,458},{4,461},{5,460},{6,463},{7,462},{8... | collective-permute-start | bytes 235016 | tf_op jit(solution)/shard_map/ppermute | solution.py:66
  18.0 16.0 %collective-permute-start.2 = (bf16[34,1152]{1,0:T(8,128)(2,1)S(1)}, bf16[34,1152]{1,0:T(8,128)(2,1)S(1)}, u32[]{:S(2)}, u32[]{:S(2)}) collective-permute-start(bf16[34,1152]{1,0:T(8,128)(2,1)S(1)} %pad_maximum_fusion.9), channel_id=1, source_target_pairs={{0,456},{1,457},{2,458},{3,459},{4,460},{5,461},{6,462},{7,463},{8... | collective-permute-start | bytes 235016 | tf_op jit(solution)/shard_map/ppermute | solution.py:66
  21.0 13.1 %all-to-all-start = ((bf16[4,68,1152]{2,1,0:T(8,128)(2,1)}), bf16[4,68,1152]{2,1,0:T(8,128)(2,1)S(1)}, u32[]{:S(2)}, u32[]{:S(2)}) async-start(bf16[4,68,1152]{2,1,0:T(8,128)(2,1)} %broadcast_in_dim.18), calls=%async_computation | async-start | bytes 1327104 | tf_op jit(solution)/shard_map/all_to_all | solution.py:70
  35.0 12.2 %all-to-all-start.1 = ((bf16[4,68,1152]{2,1,0:T(8,128)(2,1)}), bf16[4,68,1152]{2,1,0:T(8,128)(2,1)S(1)}, u32[]{:S(2)}, u32[]{:S(2)}) async-start(bf16[4,68,1152]{2,1,0:T(8,128)(2,1)} %broadcast_in_dim.19), calls=%async_computation.1 | async-start | bytes 1327104 | tf_op jit(solution)/shard_map/all_to_all | solution.py:70
  50.1 36.3 %all-to-all-start.2 = ((bf16[4,4,136,1152]{3,2,1,0:T(8,128)(2,1)}), bf16[4,4,136,1152]{3,2,1,0:T(8,128)(2,1)}, u32[]{:S(2)}, u32[]{:S(2)}) async-start(bf16[4,4,136,1152]{3,2,1,0:T(8,128)(2,1)} %broadcast_in_dim.20), calls=%async_computation.2 | async-start | bytes 10027008 | tf_op jit(solution)/shard_map/all_to_all | solution.py:70
  55.1 5.1 %collective-permute-start = (bf16[256,1152]{1,0:T(8,128)(2,1)S(1)}, bf16[256,1152]{1,0:T(8,128)(2,1)S(1)}, u32[]{:S(2)}, u32[]{:S(2)}) collective-permute-start(bf16[256,1152]{1,0:T(8,128)(2,1)S(1)} %pad_maximum_fusion.1), channel_id=1, source_target_pairs={{0,1},{1,0},{2,3},{3,2},{4,5},{5,4},{6,7},{7,6},{8,9},{9,8},{10,11... | collective-permute-start | bytes 1769480 | tf_op jit(solution)/shard_map/ppermute | solution.py:66
  88.7 1.5 copy-start
  92.3 14.1 %collective-permute-start.4 = (f32[256,1152]{1,0:T(8,128)}, f32[256,1152]{1,0:T(8,128)S(1)}, u32[]{:S(2)}, u32[]{:S(2)}) collective-permute-start(f32[256,1152]{1,0:T(8,128)} %fusion.33), channel_id=1, source_target_pairs={{0,1},{1,0},{2,3},{3,2},{4,5},{5,4},{6,7},{7,6},{8,9},{9,8},{10,11... | collective-permute-start | bytes 3538952 | tf_op jit(solution)/shard_map/ppermute | solution.py:66
  98.6 2.5 %copy-start.1 = (bf16[4,4,72,1152]{3,2,1,0:T(8,128)(2,1)S(1)}, bf16[4,4,72,1152]{3,2,1,0:T(8,128)(2,1)}, u32[]{:S(2)}) copy-start(bf16[4,4,72,1152]{3,2,1,0:T(8,128)(2,1)} %copy-done) | copy-start | bytes 7962628
  116.4 45.8 %all-to-all-start.3 = ((bf16[16,72,1152]{2,1,0:T(8,128)(2,1)}), bf16[16,72,1152]{2,1,0:T(8,128)(2,1)S(1)}, u32[]{:S(2)}, u32[]{:S(2)}) async-start(bf16[16,72,1152]{2,1,0:T(8,128)(2,1)} %bitcast.14), calls=%async_computation.3 | async-start | bytes 5308416 | tf_op jit(solution)/shard_map/all_to_all | solution.py:70
  121.3 10.5 %collective-permute-start.5 = (bf16[128,1152]{1,0:T(8,128)(2,1)S(1)}, bf16[128,1152]{1,0:T(8,128)(2,1)S(1)}, u32[]{:S(2)}, u32[]{:S(2)}) collective-permute-start(bf16[128,1152]{1,0:T(8,128)(2,1)S(1)} %dynamic-slice_convert_fusion), channel_id=1, source_target_pairs={{0,64},{1,65},{2,66},{3,67},{4,68},{5,69},{6,70},{7,71},{8,72},{9,... | collective-permute-start | bytes 884744 | tf_op jit(solution)/shard_map/ppermute | solution.py:66
  132.9 10.9 %collective-permute-start.6 = (bf16[64,1152]{1,0:T(8,128)(2,1)S(1)}, bf16[64,1152]{1,0:T(8,128)(2,1)}, u32[]{:S(2)}, u32[]{:S(2)}) collective-permute-start(bf16[64,1152]{1,0:T(8,128)(2,1)S(1)} %dynamic-slice_convert_fusion.1), channel_id=1, source_target_pairs={{0,128},{1,129},{2,130},{3,131},{4,132},{5,133},{6,134},{7,135},{8... | collective-permute-start | bytes 442376 | tf_op jit(solution)/shard_map/ppermute | solution.py:66
  144.8 13.2 %collective-permute-start.7 = (bf16[32,1152]{1,0:T(8,128)(2,1)S(1)}, bf16[32,1152]{1,0:T(8,128)(2,1)S(1)}, u32[]{:S(2)}, u32[]{:S(2)}) collective-permute-start(bf16[32,1152]{1,0:T(8,128)(2,1)S(1)} %dynamic-slice_convert_fusion.2), channel_id=1, source_target_pairs={{0,256},{1,257},{2,258},{3,259},{4,260},{5,261},{6,262},{7,263},{8... | collective-permute-start | bytes 221192 | tf_op jit(solution)/shard_map/ppermute | solution.py:66
  152.5 55.3 %collective-permute-start.11 = (bf16[1152,1152]{1,0:T(8,128)(2,1)}, bf16[1152,1152]{1,0:T(8,128)(2,1)}, u32[]{:S(2)}, u32[]{:S(2)}) collective-permute-start(bf16[1152,1152]{1,0:T(8,128)(2,1)} %bitcast.40), channel_id=1, source_target_pairs={{0,1},{1,0},{2,3},{3,2},{4,5},{5,4},{6,7},{7,6},{8,9},{9,8},{10,11... | collective-permute-start | bytes 7962632 | tf_op jit(solution)/shard_map/ppermute | solution.py:66
  162.6 14.5 %collective-permute-start.8 = (bf16[32,1152]{1,0:T(8,128)(2,1)S(1)}, bf16[32,1152]{1,0:T(8,128)(2,1)S(1)}, u32[]{:S(2)}, u32[]{:S(2)}) collective-permute-start(bf16[32,1152]{1,0:T(8,128)(2,1)S(1)} %add_convert_fusion.1), channel_id=1, source_target_pairs={{0,256},{1,257},{2,258},{3,259},{4,260},{5,261},{6,262},{7,263},{8... | collective-permute-start | bytes 221192 | tf_op jit(solution)/shard_map/ppermute | solution.py:66
  169.6 14.9 %collective-permute-start.13 = (bf16[36,1152]{1,0:T(8,128)(2,1)S(1)}, bf16[36,1152]{1,0:T(8,128)(2,1)S(1)}, u32[]{:S(2)}, u32[]{:S(2)}) collective-permute-start(bf16[36,1152]{1,0:T(8,128)(2,1)S(1)} %select_convert_fusion), channel_id=1, source_target_pairs={{0,456},{1,457},{2,458},{3,459},{4,460},{5,461},{6,462},{7,463},{8... | collective-permute-start | bytes 248840 | tf_op jit(solution)/shard_map/ppermute | solution.py:66
  177.1 13.2 %collective-permute-start.9 = (bf16[64,1152]{1,0:T(8,128)(2,1)S(1)}, bf16[64,1152]{1,0:T(8,128)(2,1)S(1)}, u32[]{:S(2)}, u32[]{:S(2)}) collective-permute-start(bf16[64,1152]{1,0:T(8,128)(2,1)S(1)} %pad_maximum_fusion.7), channel_id=1, source_target_pairs={{0,128},{1,129},{2,130},{3,131},{4,132},{5,133},{6,134},{7,135},{8... | collective-permute-start | bytes 442376 | tf_op jit(solution)/shard_map/ppermute | solution.py:66
  185.3 15.8 %all-to-all-start.4 = ((bf16[8,5,1152]{2,1,0:T(8,128)(2,1)}), bf16[8,5,1152]{2,1,0:T(8,128)(2,1)S(1)}, u32[]{:S(2)}, u32[]{:S(2)}) async-start(bf16[8,5,1152]{2,1,0:T(8,128)(2,1)} %reshape.56), calls=%async_computation.4 | async-start | bytes 294912 | tf_op jit(solution)/shard_map/all_to_all | solution.py:70
  190.5 17.2 %collective-permute-start.10 = (bf16[128,1152]{1,0:T(8,128)(2,1)S(1)}, bf16[128,1152]{1,0:T(8,128)(2,1)S(1)}, u32[]{:S(2)}, u32[]{:S(2)}) collective-permute-start(bf16[128,1152]{1,0:T(8,128)(2,1)S(1)} %pad_maximum_fusion.4), channel_id=1, source_target_pairs={{0,64},{1,65},{2,66},{3,67},{4,68},{5,69},{6,70},{7,71},{8,72},{9,... | collective-permute-start | bytes 884744 | tf_op jit(solution)/shard_map/ppermute | solution.py:66
  201.8 16.4 %all-to-all-start.5 = ((bf16[8,5,1152]{2,1,0:T(8,128)(2,1)}), bf16[8,5,1152]{2,1,0:T(8,128)(2,1)S(1)}, u32[]{:S(2)}, u32[]{:S(2)}) async-start(bf16[8,5,1152]{2,1,0:T(8,128)(2,1)} %broadcast_in_dim.21), calls=%async_computation.5 | async-start | bytes 294912 | tf_op jit(solution)/shard_map/all_to_all | solution.py:70
  210.6 14.0 %collective-permute-start.12 = (f32[128,1152]{1,0:T(8,128)S(1)}, f32[128,1152]{1,0:T(8,128)S(1)}, u32[]{:S(2)}, u32[]{:S(2)}) collective-permute-start(f32[128,1152]{1,0:T(8,128)S(1)} %bitcast.48), channel_id=1, source_target_pairs={{0,1},{1,0},{2,3},{3,2},{4,5},{5,4},{6,7},{7,6},{8,9},{9,8},{10,11... | collective-permute-start | bytes 1769480 | tf_op jit(solution)/shard_map/ppermute | solution.py:66
  218.2 5.7 %collective-permute-start.14 = (f32[18,1152]{1,0:T(8,128)S(1)}, f32[18,1152]{1,0:T(8,128)S(1)}, u32[]{:S(2)}, u32[]{:S(2)}) collective-permute-start(f32[18,1152]{1,0:T(8,128)S(1)} %slice_select_fusion.1), channel_id=1, source_target_pairs={{0,1},{1,0},{2,3},{3,2},{4,5},{5,4},{6,7},{7,6},{8,9},{9,8},{10,11... | collective-permute-start | bytes 248840 | tf_op jit(solution)/shard_map/ppermute | solution.py:66

commit v7 on v6

--- a/solution.py
+++ b/solution.py
@@ -58,7 +58,6 @@
     for zh in range(N_ZH)
     for core in range(N_CORE)
 ]
-LINE = [[place(blk, *rest) for blk in range(N_BLK)] for rest in map(lambda d: parts(d)[1:], range(N_GRP))]
 
 
 def permuted(value, target):
@@ -176,15 +175,18 @@
     inner = jnp.sum(unit * grad_unit, axis=1, keepdims=True)
     part = ((grad_unit - unit * inner) * inverse).astype(bf16)
 
-    terms = contract_first(part, feat).astype(bf16)
-    part, terms = lax.optimization_barrier((part, terms))
-    terms = exchanged(terms.reshape(N_Y * N_X, embed // (N_Y * N_X), width), PLANE)
-    held = part.astype(f32)
-    for bit, hop in ((4, 1), (2, 2), (1, 4)):
-        half = held.shape[0] // 2
+    part = part.astype(f32) + permuted(part, along(1)).astype(f32)
+    odd = (steps & 1) == 1
+    half = width // 2
+    terms = contract_first(part.astype(bf16), jnp.where(odd, feat[:, half:], feat[:, :half]))
+    part, terms = lax.optimization_barrier((part, terms.astype(bf16)))
+    terms = exchanged(terms.reshape(N_Y * N_X, embed // (N_Y * N_X), half), PLANE)
+    held = lax.dynamic_slice_in_dim(part, (steps & 1) * (own // 2), own // 2, 0)
+    for bit, hop in ((2, 2), (1, 4)):
+        count = held.shape[0] // 2
         high = (sub & bit) // bit
-        send = lax.dynamic_slice_in_dim(held, (1 - high) * half, half, 0).astype(bf16)
-        stay = lax.dynamic_slice_in_dim(held, high * half, half, 0)
+        send = lax.dynamic_slice_in_dim(held, (1 - high) * count, count, 0).astype(bf16)
+        stay = lax.dynamic_slice_in_dim(held, high * count, count, 0)
         held = stay + permuted(send, along(hop)).astype(f32)
     du, terms = lax.optimization_barrier((held.astype(bf16), terms))
     for bit, hop in ((1, 4), (2, 2), (4, 1)):
@@ -195,10 +197,12 @@
     terms = jnp.sum(terms.astype(f32), 0)
     lower, upper = terms[:pair], terms[pair:]
     came = permuted(jnp.where(low, upper, lower).astype(bf16), mirror)
-    terms = (jnp.where(low, lower, upper) + came.astype(f32)).astype(bf16)
-    terms = jnp.pad(terms, ((0, -pair % N_BLK), (0, 0))).reshape(N_BLK, -1, width)
-    terms = jnp.sum(exchanged(terms, LINE).astype(f32), 0).astype(bf16)
-    total = gathered(terms, LINE).reshape(-1, width).astype(f32)
+    total = jnp.where(low, lower, upper) + came.astype(f32)
+    for hop in (2, 4):
+        total = total.astype(bf16)
+        total = total.astype(f32) + permuted(total, along(hop)).astype(f32)
+    came = permuted(total, along(1))
+    total = jnp.concatenate([jnp.where(odd, came, total), jnp.where(odd, total, came)], 1)
     keep_g = jnp.where(first, total[:cols], total[cols:pair])
     got_g = permuted(jnp.where(first, total[cols:pair], total[:cols]), sibling)
     img_proj_grad = jnp.where(first, got_g, keep_g).T

time: 227 us -> 226 us (level)
  waiting for transfers between devices: 84.1 us -> 94.7 us
  starting transfers between devices: 97 us -> 93.2 us
  other arithmetic: 9.74 us -> 6.52 us
  matrix products: 18.7 us -> 15.8 us
    ppermute x15 -> x18, waiting for transfers between devices: 34.3 us -> 57.1 us  [permuted(): return lax.ppermute(value, BOTH, pairs)]
    all_to_all x6 -> x4, waiting for transfers between devices: 49.8 us -> 37.6 us  [exchanged(): lax.all_to_all(value, BOTH, 0, 0, axis_index_groups=groups, tiled=True)]
    all_to_all x6 -> x4, starting transfers between devices: 28 us -> 17.1 us  [exchanged(): lax.all_to_all(value, BOTH, 0, 0, axis_index_groups=groups, tiled=True)]
    ppermute x15 -> x18, starting transfers between devices: 68.9 us -> 76.1 us  [permuted(): return lax.ppermute(value, BOTH, pairs)]
    broadcast_in_dim x4 -> x3, local copies, waits for them, and re-layouts: 5.1 us -> 4.42 us  [gathered(): copies = jnp.broadcast_to(value[None], (count,) + value.shape)]
  transfers between devices with their start and end apart: 21 -> 22, of which waited for: 13 -> 15; matrix products, arithmetic and copies ran while one was open for 8% -> 6% of each run, Pallas kernels for 0% -> 0%
where the time goes in v7:
time: 226 us; the launch traced here: 225 us
  waiting for transfers between devices  94.7 us (42%)
  starting transfers between devices  93.2 us (41%)
  matrix products  15.8 us (7%)
  local copies, waits for them, and re-layouts  11.5 us (5%)
  other arithmetic  6.52 us (3%)
  between operations  3.26 us (1%)
    ppermute x18, starting transfers between devices, permuted(): return lax.ppermute(value, BOTH, pairs)  76.1 us
    ppermute x18, waiting for transfers between devices, permuted(): return lax.ppermute(value, BOTH, pairs)  57.1 us
    all_to_all x4, waiting for transfers between devices, exchanged(): lax.all_to_all(value, BOTH, 0, 0, axis_index_groups=groups, tiled=True)  37.6 us
    all_to_all x4, starting transfers between devices, exchanged(): lax.all_to_all(value, BOTH, 0, 0, axis_index_groups=groups, tiled=True)  17.1 us
    dot_general x2, matrix products, contract_last(): lax.dot_general(left, right, (((1,), (1,)), ((), ())), preferred_element_...  6.31 us
    dot_general x1, matrix products, body(): grad_unit = scale * jnp.dot(coef, others, preferred_element_type=f32)  5.98 us
  transfers between devices with their start and end apart: 22, of which 15 were waited for; matrix products, arithmetic and copies ran while one was open for 6% of the time, Pallas kernels for 0%

profile of v7, /device:TPU:1, one launch (start us, length us, event | category | flops | bytes accessed | tf_op | source)
XLA Modules:
  0.0 224.9 jit_solution(13860720045134331423)
XLA Ops:
  1.9 8.8 %collective-permute-start.1 = (bf16[34,1152]{1,0:T(8,128)(2,1)S(1)}, bf16[34,1152]{1,0:T(8,128)(2,1)S(1)}, u32[]{:S(2)}, u32[]{:S(2)}) collective-permute-start(bf16[34,1152]{1,0:T(8,128)(2,1)S(1)} %pad_maximum_fusion.9), channel_id=1, source_target_pairs={{0,1},{1,0},{2,3},{3,2},{4,5},{5,4},{6,7},{7,6},{8,9},{9,8},{10,11... | collective-permute-start | bytes 235016 | tf_op jit(solution)/shard_map/ppermute | solution.py:65
  10.7 5.6 %collective-permute-start.3 = (bf16[34,1152]{1,0:T(8,128)(2,1)S(1)}, bf16[34,1152]{1,0:T(8,128)(2,1)S(1)}, u32[]{:S(2)}, u32[]{:S(2)}) collective-permute-start(bf16[34,1152]{1,0:T(8,128)(2,1)S(1)} %pad_maximum_fusion.9), channel_id=1, source_target_pairs={{0,457},{1,456},{2,459},{3,458},{4,461},{5,460},{6,463},{7,462},{8... | collective-permute-start | bytes 235016 | tf_op jit(solution)/shard_map/ppermute | solution.py:65
  19.4 4.2 %all-to-all-start = ((bf16[4,68,1152]{2,1,0:T(8,128)(2,1)}), bf16[4,68,1152]{2,1,0:T(8,128)(2,1)S(1)}, u32[]{:S(2)}, u32[]{:S(2)}) async-start(bf16[4,68,1152]{2,1,0:T(8,128)(2,1)} %broadcast_in_dim.14), calls=%async_computation | async-start | bytes 1327104 | tf_op jit(solution)/shard_map/all_to_all | solution.py:69
  23.6 8.1 %collective-permute-done.3 = bf16[34,1152]{1,0:T(8,128)(2,1)S(1)} collective-permute-done((bf16[34,1152]{1,0:T(8,128)(2,1)S(1)}, bf16[34,1152]{1,0:T(8,128)(2,1)S(1)}, u32[]{:S(2)}, u32[]{:S(2)}) %collective-permute-start.3) | collective-permute-done | bytes 78368 | tf_op jit(solution)/shard_map/ppermute | solution.py:65
  34.3 4.2 %all-to-all-start.1 = ((bf16[4,68,1152]{2,1,0:T(8,128)(2,1)}), bf16[4,68,1152]{2,1,0:T(8,128)(2,1)S(1)}, u32[]{:S(2)}, u32[]{:S(2)}) async-start(bf16[4,68,1152]{2,1,0:T(8,128)(2,1)} %broadcast_in_dim.15), calls=%async_computation.1 | async-start | bytes 1327104 | tf_op jit(solution)/shard_map/all_to_all | solution.py:69
  38.5 7.9 %all-to-all-done.1 = bf16[4,68,1152]{2,1,0:T(8,128)(2,1)S(1)} async-done(((bf16[4,68,1152]{2,1,0:T(8,128)(2,1)}), bf16[4,68,1152]{2,1,0:T(8,128)(2,1)S(1)}, u32[]{:S(2)}, u32[]{:S(2)}) %all-to-all-start.1) | async-done | bytes 626720 | tf_op jit(solution)/shard_map/all_to_all | solution.py:69
  46.7 2.6 %broadcast_in_dim.18 = bf16[4,4,136,1152]{3,2,1,0:T(8,128)(2,1)} broadcast(bf16[4,136,1152]{2,1,0:T(8,128)(2,1)S(1)} %pad_maximum_fusion), dimensions={1,2,3} | broadcast | bytes 6266880 | tf_op jit(solution)/shard_map/broadcast_in_dim | solution.py:74
  49.3 5.0 %all-to-all-start.2 = ((bf16[4,4,136,1152]{3,2,1,0:T(8,128)(2,1)}), bf16[4,4,136,1152]{3,2,1,0:T(8,128)(2,1)}, u32[]{:S(2)}, u32[]{:S(2)}) async-start(bf16[4,4,136,1152]{3,2,1,0:T(8,128)(2,1)} %broadcast_in_dim.18), calls=%async_computation.2 | async-start | bytes 10027008 | tf_op jit(solution)/shard_map/all_to_all | solution.py:69
  54.4 3.5 %collective-permute-start = (bf16[256,1152]{1,0:T(8,128)(2,1)S(1)}, bf16[256,1152]{1,0:T(8,128)(2,1)S(1)}, u32[]{:S(2)}, u32[]{:S(2)}) collective-permute-start(bf16[256,1152]{1,0:T(8,128)(2,1)S(1)} %pad_maximum_fusion.1), channel_id=1, source_target_pairs={{0,1},{1,0},{2,3},{3,2},{4,5},{5,4},{6,7},{7,6},{8,9},{9,8},{10,11... | collective-permute-start | bytes 1769480 | tf_op jit(solution)/shard_map/ppermute | solution.py:65
  59.6 26.1 %all-to-all-done.2 = bf16[4,4,136,1152]{3,2,1,0:T(8,128)(2,1)} async-done(((bf16[4,4,136,1152]{3,2,1,0:T(8,128)(2,1)}), bf16[4,4,136,1152]{3,2,1,0:T(8,128)(2,1)}, u32[]{:S(2)}, u32[]{:S(2)}) %all-to-all-start.2) | async-done | bytes 5013536 | tf_op jit(solution)/shard_map/all_to_all | solution.py:69
  89.4 4.3 %collective-permute-start.4 = (f32[256,1152]{1,0:T(8,128)S(1)}, f32[256,1152]{1,0:T(8,128)S(1)}, u32[]{:S(2)}, u32[]{:S(2)}) collective-permute-start(f32[256,1152]{1,0:T(8,128)S(1)} %fusion.37), channel_id=1, source_target_pairs={{0,1},{1,0},{2,3},{3,2},{4,5},{5,4},{6,7},{7,6},{8,9},{9,8},{10,11... | collective-permute-start | bytes 3538952 | tf_op jit(solution)/shard_map/ppermute | solution.py:65
  98.7 5.3 %multiply_reduce_fusion = (f32[1024]{0:T(1024)S(1)}, f32[1024,1152]{1,0:T(8,128)}) fusion(bf16[1024,1152]{1,0:T(8,128)(2,1)S(1)} %bitcast.40, bf16[1152,1152]{1,0:T(8,128)(2,1)S(1)} %bitcast.39), kind=kOutput, calls=%fused_computation.1 | convolution fusion | flops 2720267264 | bytes 9736192 | tf_op jit(solution)/shard_map/dot_general | solution.py:79
  104.1 6.0 %multiply_reduce_fusion.1 = (f32[256]{0:T(256)S(1)}, f32[256,1152]{1,0:T(8,128)S(1)}) fusion(f32[256,1152]{1,0:T(8,128)S(1)} %collective-permute-done.4, f32[256]{0:T(256)S(1)} %add_rsqrt_fusion.1, f32[1024,1152]{1,0:T(8,128)} %get-tuple-element.37, f32[1024]{0:T(1024)S(1)} %add_rsqrt_fusion, f32[]{:T(128)} %bitcast.34, f32[]{:T(128)} %bitcast.33, ...), kind=kOutput, calls=%fused_computation.20 | convolution fusion | flops 1218117376 | bytes 7089676 | tf_op jit(solution)/shard_map/dot_general | solution.py:174
  112.4 14.8 %collective-permute-done.5 = bf16[256,1152]{1,0:T(8,128)(2,1)S(1)} collective-permute-done((bf16[256,1152]{1,0:T(8,128)(2,1)S(1)}, bf16[256,1152]{1,0:T(8,128)(2,1)S(1)}, u32[]{:S(2)}, u32[]{:S(2)}) %collective-permute-start.5) | collective-permute-done | bytes 589856 | tf_op jit(solution)/shard_map/ppermute | solution.py:65
  128.4 3.3 %collective-permute-start.6 = (bf16[64,1152]{1,0:T(8,128)(2,1)S(1)}, bf16[64,1152]{1,0:T(8,128)(2,1)S(1)}, u32[]{:S(2)}, u32[]{:S(2)}) collective-permute-start(bf16[64,1152]{1,0:T(8,128)(2,1)S(1)} %dynamic-slice_convert_fusion), channel_id=1, source_target_pairs={{0,128},{1,129},{2,130},{3,131},{4,132},{5,133},{6,134},{7,135},{8... | collective-permute-start | bytes 442376 | tf_op jit(solution)/shard_map/ppermute | solution.py:65
  133.4 3.7 %all-to-all-start.3 = ((bf16[16,72,576]{2,1,0:T(8,128)(2,1)}), bf16[16,72,576]{2,1,0:T(8,128)(2,1)S(1)}, u32[]{:S(2)}, u32[]{:S(2)}) async-start(bf16[16,72,576]{2,1,0:T(8,128)(2,1)} %bitcast.14), calls=%async_computation.3 | async-start | bytes 2949120 | tf_op jit(solution)/shard_map/all_to_all | solution.py:69
  137.1 2.9 %collective-permute-done.6 = bf16[64,1152]{1,0:T(8,128)(2,1)S(1)} collective-permute-done((bf16[64,1152]{1,0:T(8,128)(2,1)S(1)}, bf16[64,1152]{1,0:T(8,128)(2,1)S(1)}, u32[]{:S(2)}, u32[]{:S(2)}) %collective-permute-start.6) | collective-permute-done | bytes 147488 | tf_op jit(solution)/shard_map/ppermute | solution.py:65
  141.0 6.0 %collective-permute-start.7 = (bf16[32,1152]{1,0:T(8,128)(2,1)S(1)}, bf16[32,1152]{1,0:T(8,128)(2,1)S(1)}, u32[]{:S(2)}, u32[]{:S(2)}) collective-permute-start(bf16[32,1152]{1,0:T(8,128)(2,1)S(1)} %dynamic-slice_convert_fusion.1), channel_id=1, source_target_pairs={{0,256},{1,257},{2,258},{3,259},{4,260},{5,261},{6,262},{7,263},{8... | collective-permute-start | bytes 221192 | tf_op jit(solution)/shard_map/ppermute | solution.py:65
  147.1 7.7 %collective-permute-done.7 = bf16[32,1152]{1,0:T(8,128)(2,1)S(1)} collective-permute-done((bf16[32,1152]{1,0:T(8,128)(2,1)S(1)}, bf16[32,1152]{1,0:T(8,128)(2,1)S(1)}, u32[]{:S(2)}, u32[]{:S(2)}) %collective-permute-start.7) | collective-permute-done | bytes 73760 | tf_op jit(solution)/shard_map/ppermute | solution.py:65
  154.8 3.6 %all-to-all-done.3 = bf16[16,72,576]{2,1,0:T(8,128)(2,1)S(1)} async-done(((bf16[16,72,576]{2,1,0:T(8,128)(2,1)}), bf16[16,72,576]{2,1,0:T(8,128)(2,1)S(1)}, u32[]{:S(2)}, u32[]{:S(2)}) %all-to-all-start.3) | async-done | bytes 1327136 | tf_op jit(solution)/shard_map/all_to_all | solution.py:69
  158.6 8.1 %collective-permute-start.13 = (bf16[36,576]{1,0:T(8,128)(2,1)S(1)}, bf16[36,576]{1,0:T(8,128)(2,1)S(1)}, u32[]{:S(2)}, u32[]{:S(2)}) collective-permute-start(bf16[36,576]{1,0:T(8,128)(2,1)S(1)} %select_convert_fusion), channel_id=1, source_target_pairs={{0,456},{1,457},{2,458},{3,459},{4,460},{5,461},{6,462},{7,463},{8... | collective-permute-start | bytes 124424 | tf_op jit(solution)/shard_map/ppermute | solution.py:65
  166.7 4.7 %collective-permute-start.11 = (bf16[1152,1152]{1,0:T(8,128)(2,1)}, bf16[1152,1152]{1,0:T(8,128)(2,1)}, u32[]{:S(2)}, u32[]{:S(2)}) collective-permute-start(bf16[1152,1152]{1,0:T(8,128)(2,1)} %bitcast.38), channel_id=1, source_target_pairs={{0,1},{1,0},{2,3},{3,2},{4,5},{5,4},{6,7},{7,6},{8,9},{9,8},{10,11... | collective-permute-start | bytes 7962632 | tf_op jit(solution)/shard_map/ppermute | solution.py:65
  171.4 7.3 %collective-permute-start.8 = (bf16[32,1152]{1,0:T(8,128)(2,1)S(1)}, bf16[32,1152]{1,0:T(8,128)(2,1)S(1)}, u32[]{:S(2)}, u32[]{:S(2)}) collective-permute-start(bf16[32,1152]{1,0:T(8,128)(2,1)S(1)} %add_convert_fusion), channel_id=1, source_target_pairs={{0,256},{1,257},{2,258},{3,259},{4,260},{5,261},{6,262},{7,263},{8... | collective-permute-start | bytes 221192 | tf_op jit(solution)/shard_map/ppermute | solution.py:65
  178.7 2.2 collective-permute-start.14
  181.2 4.4 %collective-permute-done.14 = bf16[36,576]{1,0:T(8,128)(2,1)S(1)} collective-permute-done((bf16[36,576]{1,0:T(8,128)(2,1)S(1)}, bf16[36,576]{1,0:T(8,128)(2,1)S(1)}, u32[]{:S(2)}, u32[]{:S(2)}) %collective-permute-start.14) | collective-permute-done | bytes 41504 | tf_op jit(solution)/shard_map/ppermute | solution.py:65
  185.7 3.6 %collective-permute-start.15 = (bf16[36,576]{1,0:T(8,128)(2,1)S(1)}, bf16[36,576]{1,0:T(8,128)(2,1)S(1)}, u32[]{:S(2)}, u32[]{:S(2)}) collective-permute-start(bf16[36,576]{1,0:T(8,128)(2,1)S(1)} %add_convert_fusion.1), channel_id=1, source_target_pairs={{0,256},{1,257},{2,258},{3,259},{4,260},{5,261},{6,262},{7,263},{8... | collective-permute-start | bytes 124424 | tf_op jit(solution)/shard_map/ppermute | solution.py:65
  189.3 5.6 %collective-permute-start.9 = (bf16[64,1152]{1,0:T(8,128)(2,1)S(1)}, bf16[64,1152]{1,0:T(8,128)(2,1)S(1)}, u32[]{:S(2)}, u32[]{:S(2)}) collective-permute-start(bf16[64,1152]{1,0:T(8,128)(2,1)S(1)} %pad_maximum_fusion.7), channel_id=1, source_target_pairs={{0,128},{1,129},{2,130},{3,131},{4,132},{5,133},{6,134},{7,135},{8... | collective-permute-start | bytes 442376 | tf_op jit(solution)/shard_map/ppermute | solution.py:65
  194.9 2.9 %collective-permute-done.15 = bf16[36,576]{1,0:T(8,128)(2,1)S(1)} collective-permute-done((bf16[36,576]{1,0:T(8,128)(2,1)S(1)}, bf16[36,576]{1,0:T(8,128)(2,1)S(1)}, u32[]{:S(2)}, u32[]{:S(2)}) %collective-permute-start.15) | collective-permute-done | bytes 41504 | tf_op jit(solution)/shard_map/ppermute | solution.py:65
  199.7 3.7 %collective-permute-done.9 = bf16[64,1152]{1,0:T(8,128)(2,1)S(1)} collective-permute-done((bf16[64,1152]{1,0:T(8,128)(2,1)S(1)}, bf16[64,1152]{1,0:T(8,128)(2,1)S(1)}, u32[]{:S(2)}, u32[]{:S(2)}) %collective-permute-start.9) | collective-permute-done | bytes 147488 | tf_op jit(solution)/shard_map/ppermute | solution.py:65
  205.5 7.9 %collective-permute-done.10 = bf16[128,1152]{1,0:T(8,128)(2,1)S(1)} collective-permute-done((bf16[128,1152]{1,0:T(8,128)(2,1)S(1)}, bf16[128,1152]{1,0:T(8,128)(2,1)S(1)}, u32[]{:S(2)}, u32[]{:S(2)}) %collective-permute-start.10) | collective-permute-done | bytes 294944 | tf_op jit(solution)/shard_map/ppermute | solution.py:65
  213.5 2.7 %fusion.11 = f32[256,1152]{1,0:T(8,128)S(1)} fusion(bf16[1152,1152]{1,0:T(8,128)(2,1)} %collective-permute-done.11, bf16[128,1152]{1,0:T(8,128)(2,1)S(1)} %get-tuple-element.21, bf16[128,1152]{1,0:T(8,128)(2,1)S(1)} %get-tuple-element.20), kind=kOutput, calls=%fused_computation.29 | convolution fusion | flops 680656896 | bytes 4423680 | tf_op jit(solution)/shard_map/dot_general | solution.py:211
  216.3 3.4 %collective-permute-start.12 = (f32[128,1152]{1,0:T(8,128)S(1)}, f32[128,1152]{1,0:T(8,128)S(1)}, u32[]{:S(2)}, u32[]{:S(2)}) collective-permute-start(f32[128,1152]{1,0:T(8,128)S(1)} %bitcast.46), channel_id=1, source_target_pairs={{0,1},{1,0},{2,3},{3,2},{4,5},{5,4},{6,7},{7,6},{8,9},{9,8},{10,11... | collective-permute-start | bytes 1769480 | tf_op jit(solution)/shard_map/ppermute | solution.py:65
  (83 shorter events, 31.6 us)
Async XLA Ops:
  0.6 1.2 copy-start.3
  0.6 1.2 copy-start.4
  1.9 14.5 %collective-permute-start.1 = (bf16[34,1152]{1,0:T(8,128)(2,1)S(1)}, bf16[34,1152]{1,0:T(8,128)(2,1)S(1)}, u32[]{:S(2)}, u32[]{:S(2)}) collective-permute-start(bf16[34,1152]{1,0:T(8,128)(2,1)S(1)} %pad_maximum_fusion.9), channel_id=1, source_target_pairs={{0,1},{1,0},{2,3},{3,2},{4,5},{5,4},{6,7},{7,6},{8,9},{9,8},{10,11... | collective-permute-start | bytes 235016 | tf_op jit(solution)/shard_map/ppermute | solution.py:65
  10.7 21.0 %collective-permute-start.3 = (bf16[34,1152]{1,0:T(8,128)(2,1)S(1)}, bf16[34,1152]{1,0:T(8,128)(2,1)S(1)}, u32[]{:S(2)}, u32[]{:S(2)}) collective-permute-start(bf16[34,1152]{1,0:T(8,128)(2,1)S(1)} %pad_maximum_fusion.9), channel_id=1, source_target_pairs={{0,457},{1,456},{2,459},{3,458},{4,461},{5,460},{6,463},{7,462},{8... | collective-permute-start | bytes 235016 | tf_op jit(solution)/shard_map/ppermute | solution.py:65
  16.4 16.9 %collective-permute-start.2 = (bf16[34,1152]{1,0:T(8,128)(2,1)S(1)}, bf16[34,1152]{1,0:T(8,128)(2,1)S(1)}, u32[]{:S(2)}, u32[]{:S(2)}) collective-permute-start(bf16[34,1152]{1,0:T(8,128)(2,1)S(1)} %pad_maximum_fusion.10), channel_id=1, source_target_pairs={{0,456},{1,457},{2,458},{3,459},{4,460},{5,461},{6,462},{7,463},{8... | collective-permute-start | bytes 235016 | tf_op jit(solution)/shard_map/ppermute | solution.py:65
  19.4 13.9 %all-to-all-start = ((bf16[4,68,1152]{2,1,0:T(8,128)(2,1)}), bf16[4,68,1152]{2,1,0:T(8,128)(2,1)S(1)}, u32[]{:S(2)}, u32[]{:S(2)}) async-start(bf16[4,68,1152]{2,1,0:T(8,128)(2,1)} %broadcast_in_dim.14), calls=%async_computation | async-start | bytes 1327104 | tf_op jit(solution)/shard_map/all_to_all | solution.py:69
  34.3 12.2 %all-to-all-start.1 = ((bf16[4,68,1152]{2,1,0:T(8,128)(2,1)}), bf16[4,68,1152]{2,1,0:T(8,128)(2,1)S(1)}, u32[]{:S(2)}, u32[]{:S(2)}) async-start(bf16[4,68,1152]{2,1,0:T(8,128)(2,1)} %broadcast_in_dim.15), calls=%async_computation.1 | async-start | bytes 1327104 | tf_op jit(solution)/shard_map/all_to_all | solution.py:69
  49.3 36.4 %all-to-all-start.2 = ((bf16[4,4,136,1152]{3,2,1,0:T(8,128)(2,1)}), bf16[4,4,136,1152]{3,2,1,0:T(8,128)(2,1)}, u32[]{:S(2)}, u32[]{:S(2)}) async-start(bf16[4,4,136,1152]{3,2,1,0:T(8,128)(2,1)} %broadcast_in_dim.18), calls=%async_computation.2 | async-start | bytes 10027008 | tf_op jit(solution)/shard_map/all_to_all | solution.py:69
  54.4 5.1 %collective-permute-start = (bf16[256,1152]{1,0:T(8,128)(2,1)S(1)}, bf16[256,1152]{1,0:T(8,128)(2,1)S(1)}, u32[]{:S(2)}, u32[]{:S(2)}) collective-permute-start(bf16[256,1152]{1,0:T(8,128)(2,1)S(1)} %pad_maximum_fusion.1), channel_id=1, source_target_pairs={{0,1},{1,0},{2,3},{3,2},{4,5},{5,4},{6,7},{7,6},{8,9},{9,8},{10,11... | collective-permute-start | bytes 1769480 | tf_op jit(solution)/shard_map/ppermute | solution.py:65
  87.9 1.5 copy-start
  89.4 14.5 %collective-permute-start.4 = (f32[256,1152]{1,0:T(8,128)S(1)}, f32[256,1152]{1,0:T(8,128)S(1)}, u32[]{:S(2)}, u32[]{:S(2)}) collective-permute-start(f32[256,1152]{1,0:T(8,128)S(1)} %fusion.37), channel_id=1, source_target_pairs={{0,1},{1,0},{2,3},{3,2},{4,5},{5,4},{6,7},{7,6},{8,9},{9,8},{10,11... | collective-permute-start | bytes 3538952 | tf_op jit(solution)/shard_map/ppermute | solution.py:65
  96.2 2.5 %copy-start.1 = (bf16[4,4,72,1152]{3,2,1,0:T(8,128)(2,1)S(1)}, bf16[4,4,72,1152]{3,2,1,0:T(8,128)(2,1)}, u32[]{:S(2)}) copy-start(bf16[4,4,72,1152]{3,2,1,0:T(8,128)(2,1)} %copy-done) | copy-start | bytes 7962628
  110.4 16.8 %collective-permute-start.5 = (bf16[256,1152]{1,0:T(8,128)(2,1)S(1)}, bf16[256,1152]{1,0:T(8,128)(2,1)S(1)}, u32[]{:S(2)}, u32[]{:S(2)}) collective-permute-start(bf16[256,1152]{1,0:T(8,128)(2,1)S(1)} %multiply_convert_fusion.1), channel_id=1, source_target_pairs={{0,64},{1,65},{2,66},{3,67},{4,68},{5,69},{6,70},{7,71},{8,72},{9,... | collective-permute-start | bytes 1769480 | tf_op jit(solution)/shard_map/ppermute | solution.py:65
  127.3 1.0 copy-start.2
  128.4 11.6 %collective-permute-start.6 = (bf16[64,1152]{1,0:T(8,128)(2,1)S(1)}, bf16[64,1152]{1,0:T(8,128)(2,1)S(1)}, u32[]{:S(2)}, u32[]{:S(2)}) collective-permute-start(bf16[64,1152]{1,0:T(8,128)(2,1)S(1)} %dynamic-slice_convert_fusion), channel_id=1, source_target_pairs={{0,128},{1,129},{2,130},{3,131},{4,132},{5,133},{6,134},{7,135},{8... | collective-permute-start | bytes 442376 | tf_op jit(solution)/shard_map/ppermute | solution.py:65
  133.4 25.0 %all-to-all-start.3 = ((bf16[16,72,576]{2,1,0:T(8,128)(2,1)}), bf16[16,72,576]{2,1,0:T(8,128)(2,1)S(1)}, u32[]{:S(2)}, u32[]{:S(2)}) async-start(bf16[16,72,576]{2,1,0:T(8,128)(2,1)} %bitcast.14), calls=%async_computation.3 | async-start | bytes 2949120 | tf_op jit(solution)/shard_map/all_to_all | solution.py:69
  141.0 13.7 %collective-permute-start.7 = (bf16[32,1152]{1,0:T(8,128)(2,1)S(1)}, bf16[32,1152]{1,0:T(8,128)(2,1)S(1)}, u32[]{:S(2)}, u32[]{:S(2)}) collective-permute-start(bf16[32,1152]{1,0:T(8,128)(2,1)S(1)} %dynamic-slice_convert_fusion.1), channel_id=1, source_target_pairs={{0,256},{1,257},{2,258},{3,259},{4,260},{5,261},{6,262},{7,263},{8... | collective-permute-start | bytes 221192 | tf_op jit(solution)/shard_map/ppermute | solution.py:65
  158.6 20.1 %collective-permute-start.13 = (bf16[36,576]{1,0:T(8,128)(2,1)S(1)}, bf16[36,576]{1,0:T(8,128)(2,1)S(1)}, u32[]{:S(2)}, u32[]{:S(2)}) collective-permute-start(bf16[36,576]{1,0:T(8,128)(2,1)S(1)} %select_convert_fusion), channel_id=1, source_target_pairs={{0,456},{1,457},{2,458},{3,459},{4,460},{5,461},{6,462},{7,463},{8... | collective-permute-start | bytes 124424 | tf_op jit(solution)/shard_map/ppermute | solution.py:65
  166.7 46.8 %collective-permute-start.11 = (bf16[1152,1152]{1,0:T(8,128)(2,1)}, bf16[1152,1152]{1,0:T(8,128)(2,1)}, u32[]{:S(2)}, u32[]{:S(2)}) collective-permute-start(bf16[1152,1152]{1,0:T(8,128)(2,1)} %bitcast.38), channel_id=1, source_target_pairs={{0,1},{1,0},{2,3},{3,2},{4,5},{5,4},{6,7},{7,6},{8,9},{9,8},{10,11... | collective-permute-start | bytes 7962632 | tf_op jit(solution)/shard_map/ppermute | solution.py:65
  171.4 9.8 %collective-permute-start.8 = (bf16[32,1152]{1,0:T(8,128)(2,1)S(1)}, bf16[32,1152]{1,0:T(8,128)(2,1)S(1)}, u32[]{:S(2)}, u32[]{:S(2)}) collective-permute-start(bf16[32,1152]{1,0:T(8,128)(2,1)S(1)} %add_convert_fusion), channel_id=1, source_target_pairs={{0,256},{1,257},{2,258},{3,259},{4,260},{5,261},{6,262},{7,263},{8... | collective-permute-start | bytes 221192 | tf_op jit(solution)/shard_map/ppermute | solution.py:65
  178.7 6.9 %collective-permute-start.14 = (bf16[36,576]{1,0:T(8,128)(2,1)S(1)}, bf16[36,576]{1,0:T(8,128)(2,1)S(1)}, u32[]{:S(2)}, u32[]{:S(2)}) collective-permute-start(bf16[36,576]{1,0:T(8,128)(2,1)S(1)} %add_convert_fusion.2), channel_id=1, source_target_pairs={{0,128},{1,129},{2,130},{3,131},{4,132},{5,133},{6,134},{7,135},{8... | collective-permute-start | bytes 124424 | tf_op jit(solution)/shard_map/ppermute | solution.py:65
  185.7 12.1 %collective-permute-start.15 = (bf16[36,576]{1,0:T(8,128)(2,1)S(1)}, bf16[36,576]{1,0:T(8,128)(2,1)S(1)}, u32[]{:S(2)}, u32[]{:S(2)}) collective-permute-start(bf16[36,576]{1,0:T(8,128)(2,1)S(1)} %add_convert_fusion.1), channel_id=1, source_target_pairs={{0,256},{1,257},{2,258},{3,259},{4,260},{5,261},{6,262},{7,263},{8... | collective-permute-start | bytes 124424 | tf_op jit(solution)/shard_map/ppermute | solution.py:65
  189.3 14.2 %collective-permute-start.9 = (bf16[64,1152]{1,0:T(8,128)(2,1)S(1)}, bf16[64,1152]{1,0:T(8,128)(2,1)S(1)}, u32[]{:S(2)}, u32[]{:S(2)}) collective-permute-start(bf16[64,1152]{1,0:T(8,128)(2,1)S(1)} %pad_maximum_fusion.7), channel_id=1, source_target_pairs={{0,128},{1,129},{2,130},{3,131},{4,132},{5,133},{6,134},{7,135},{8... | collective-permute-start | bytes 442376 | tf_op jit(solution)/shard_map/ppermute | solution.py:65
  197.8 7.7 %collective-permute-start.16 = (f32[36,576]{1,0:T(8,128)S(1)}, f32[36,576]{1,0:T(8,128)S(1)}, u32[]{:S(2)}, u32[]{:S(2)}) collective-permute-start(f32[36,576]{1,0:T(8,128)S(1)} %convert_add_fusion.2), channel_id=1, source_target_pairs={{0,64},{1,65},{2,66},{3,67},{4,68},{5,69},{6,70},{7,71},{8,72},{9,... | collective-permute-start | bytes 248840 | tf_op jit(solution)/shard_map/ppermute | solution.py:65
  203.5 9.9 %collective-permute-start.10 = (bf16[128,1152]{1,0:T(8,128)(2,1)S(1)}, bf16[128,1152]{1,0:T(8,128)(2,1)S(1)}, u32[]{:S(2)}, u32[]{:S(2)}) collective-permute-start(bf16[128,1152]{1,0:T(8,128)(2,1)S(1)} %pad_maximum_fusion.4), channel_id=1, source_target_pairs={{0,64},{1,65},{2,66},{3,67},{4,68},{5,69},{6,70},{7,71},{8,72},{9,... | collective-permute-start | bytes 884744 | tf_op jit(solution)/shard_map/ppermute | solution.py:65
  216.3 7.5 %collective-permute-start.12 = (f32[128,1152]{1,0:T(8,128)S(1)}, f32[128,1152]{1,0:T(8,128)S(1)}, u32[]{:S(2)}, u32[]{:S(2)}) collective-permute-start(f32[128,1152]{1,0:T(8,128)S(1)} %bitcast.46), channel_id=1, source_target_pairs={{0,1},{1,0},{2,3},{3,2},{4,5},{5,4},{6,7},{7,6},{8,9},{9,8},{10,11... | collective-permute-start | bytes 1769480 | tf_op jit(solution)/shard_map/ppermute | solution.py:65
  219.8 3.2 %collective-permute-start.17 = (f32[18,1152]{1,0:T(8,128)S(1)}, f32[18,1152]{1,0:T(8,128)S(1)}, u32[]{:S(2)}, u32[]{:S(2)}) collective-permute-start(f32[18,1152]{1,0:T(8,128)S(1)} %broadcast_select_fusion.11), channel_id=1, source_target_pairs={{0,1},{1,0},{2,3},{3,2},{4,5},{5,4},{6,7},{7,6},{8,9},{9,8},{10,11... | collective-permute-start | bytes 248840 | tf_op jit(solution)/shard_map/ppermute | solution.py:65

commit v8 on v7

--- a/solution.py
+++ b/solution.py
@@ -1,6 +1,10 @@
+import functools
+
 import jax
 import jax.numpy as jnp
 from jax import lax
+from jax.experimental import pallas as pl
+from jax.experimental.pallas import tpu as pltpu
 from jax.sharding import PartitionSpec as P
 
 BOTH = ("blk", "grp")
@@ -59,6 +63,18 @@
     for core in range(N_CORE)
 ]
 
+RING = [
+    [
+        place(step if zh == 0 else N_BLK - 1 - step, y, zh, x, core)
+        for zh in range(N_ZH)
+        for step in range(odd, N_BLK, 2)
+    ]
+    for odd in range(2)
+    for y in range(N_Y)
+    for x in range(N_X)
+    for core in range(N_CORE)
+]
+
 
 def permuted(value, target):
     pairs = [(source, target(source)) for source in range(N_BLK * N_GRP)]
@@ -85,6 +101,95 @@
     return lax.dot_general(
         left, right, (((0,), (0,)), ((), ())), preferred_element_type=jnp.float32
     )
+
+
+def embed_kernel(feat_ref, proj_ref, emb_ref):
+    proj_out = contract_last(feat_ref[...].reshape(emb_ref.shape), proj_ref[...])
+    inverse = lax.rsqrt(jnp.sum(proj_out * proj_out, axis=1, keepdims=True) + 1e-06)
+    emb_ref[...] = (proj_out * inverse).astype(jnp.bfloat16)
+
+
+def embedded(both, picked, proj):
+    count, _, width = both.shape
+    embed = proj.shape[0]
+    group = 4
+    rows = count * picked
+    return pl.pallas_call(
+        embed_kernel,
+        grid=(count // group,),
+        in_specs=[
+            pl.BlockSpec((group, picked, width), lambda i: (i, 0, 0)),
+            pl.BlockSpec((embed, width), lambda i: (0, 0)),
+        ],
+        out_specs=pl.BlockSpec((group * picked, embed), lambda i: (i, 0)),
+        out_shape=jax.ShapeDtypeStruct((rows, embed), jnp.bfloat16),
+        compiler_params=pltpu.CompilerParams(vmem_limit_bytes=40 * 2**20),
+        cost_estimate=pl.CostEstimate(
+            flops=2 * rows * embed * width,
+            bytes_accessed=2 * (rows * width + rows * embed + embed * width),
+            transcendentals=rows,
+        ),
+    )(both, proj)
+
+
+def partial_kernel(at_ref, par_ref, made_ref, others_ref, part_ref, emb_ref, acc_ref, *, block):
+    step = pl.program_id(0)
+    scale, shift_by, weight = par_ref[0], par_ref[1], par_ref[2]
+
+    def unit_of():
+        made = made_ref[...]
+        inverse = lax.rsqrt(jnp.sum(made * made, axis=1, keepdims=True) + 1e-06)
+        return made * inverse, inverse
+
+    @pl.when(step == 0)
+    def _():
+        emb_ref[...] = unit_of()[0].astype(jnp.bfloat16)
+        acc_ref[...] = jnp.zeros_like(acc_ref)
+
+    others = others_ref[...]
+    logits = scale * contract_last(emb_ref[...], others) + shift_by
+    row = lax.broadcasted_iota(jnp.int32, logits.shape, 0) - at_ref[0]
+    col = lax.broadcasted_iota(jnp.int32, logits.shape, 1) + (step * logits.shape[1] - at_ref[1])
+    same = (row == col) & (row >= 0) & (row < block)
+    coef = jnp.where(same, -weight, weight) * jax.nn.sigmoid(jnp.where(same, -logits, logits))
+    acc_ref[...] += jnp.dot(
+        coef.astype(jnp.bfloat16), others, preferred_element_type=jnp.float32
+    )
+
+    @pl.when(step == pl.num_programs(0) - 1)
+    def _():
+        unit, inverse = unit_of()
+        grad_unit = scale * acc_ref[...]
+        inner = jnp.sum(unit * grad_unit, axis=1, keepdims=True)
+        part_ref[...] = ((grad_unit - unit * inner) * inverse).astype(jnp.bfloat16)
+
+
+def partial_grads(at, params, made, others, block):
+    own, embed = made.shape
+    count = others.shape[0]
+    tile = 256
+    return pl.pallas_call(
+        functools.partial(partial_kernel, block=block),
+        grid=(count // tile,),
+        in_specs=[
+            pl.BlockSpec(memory_space=pltpu.SMEM),
+            pl.BlockSpec(memory_space=pltpu.SMEM),
+            pl.BlockSpec((own, embed), lambda i: (0, 0)),
+            pl.BlockSpec((tile, embed), lambda i: (i, 0)),
+        ],
+        out_specs=pl.BlockSpec((own, embed), lambda i: (0, 0)),
+        out_shape=jax.ShapeDtypeStruct((own, embed), jnp.bfloat16),
+        scratch_shapes=[
+            pltpu.VMEM((own, embed), jnp.bfloat16),
+            pltpu.VMEM((own, embed), jnp.float32),
+        ],
+        compiler_params=pltpu.CompilerParams(vmem_limit_bytes=40 * 2**20),
+        cost_estimate=pl.CostEstimate(
+            flops=4 * own * count * embed,
+            bytes_accessed=2 * count * embed + 6 * own * embed,
+            transcendentals=own * count,
+        ),
+    )(at, params, made, others)
 
 
 def body(img_feat, txt_feat, img_proj, txt_proj, logit_scale, logit_bias, loss_weight):
@@ -141,7 +246,6 @@
         1,
     )
     both = gathered(both, OUTER)
-    others = both[:, :, : N_ZH * picked].reshape(-1, width)
     proj = both[:, :, N_ZH * picked :]
     proj = jnp.where(first, proj, proj.transpose(1, 0, 2, 3)).reshape(-1, width)
     embed = proj.shape[0]
@@ -155,25 +259,12 @@
 
     feat = interleaved(other_f, sib_other)
 
-    def normalized(proj_out):
-        inverse = lax.rsqrt(jnp.sum(proj_out * proj_out, axis=1, keepdims=True) + 1e-06)
-        return proj_out * inverse, inverse
-
-    made = contract_last(interleaved(sib_own, own_f), proj)
-    unit, inverse = normalized(permuted(made, sibling))
-    emb = unit.astype(bf16)
-    others = normalized(contract_last(others, proj))[0].astype(bf16)
+    made = permuted(contract_last(interleaved(sib_own, own_f), proj), sibling)
+    others = embedded(both.reshape(N_Y * N_X, -1, width), N_ZH * picked, proj)
     spot = jnp.where(first, y * N_X + x, x * N_Y + y) * (N_ZH * picked)
-
-    logits = scale * contract_last(emb, others) + shift_by
-    row = lax.broadcasted_iota(jnp.int32, logits.shape, 0) - sub * (N_CORE * sub_rows)
-    col = lax.broadcasted_iota(jnp.int32, logits.shape, 1) - spot
-    same = (row == col) & (row >= 0) & (row < N_CORE * sub_rows)
-    sign = jnp.where(same, f32(1.0), f32(-1.0))
-    coef = (-weight * sign * jax.nn.sigmoid(-sign * logits)).astype(bf16)
-    grad_unit = scale * jnp.dot(coef, others, preferred_element_type=f32)
-    inner = jnp.sum(unit * grad_unit, axis=1, keepdims=True)
-    part = ((grad_unit - unit * inner) * inverse).astype(bf16)
+    at = jnp.stack([sub * picked, spot]).astype(jnp.int32)
+    part = partial_grads(at, jnp.stack([scale, shift_by, weight]), made, others, picked)
+    part, other_proj = lax.optimization_barrier((part, permuted(proj, sibling)))
 
     part = part.astype(f32) + permuted(part, along(1)).astype(f32)
     odd = (steps & 1) == 1
@@ -195,12 +286,10 @@
         du = jnp.concatenate([jnp.where(high, came, du), jnp.where(high, du, came)], 0)
 
     terms = jnp.sum(terms.astype(f32), 0)
-    lower, upper = terms[:pair], terms[pair:]
-    came = permuted(jnp.where(low, upper, lower).astype(bf16), mirror)
-    total = jnp.where(low, lower, upper) + came.astype(f32)
-    for hop in (2, 4):
-        total = total.astype(bf16)
-        total = total.astype(f32) + permuted(total, along(hop)).astype(f32)
+    terms = terms.astype(bf16).reshape(N_ZH, pair, half)
+    terms = jnp.broadcast_to(terms[:, None], (N_ZH, N_BLK // 2, pair, half))
+    terms = exchanged(terms.reshape(N_BLK, pair, half), RING)
+    total = jnp.sum(terms.astype(f32), 0)
     came = permuted(total, along(1))
     total = jnp.concatenate([jnp.where(odd, came, total), jnp.where(odd, total, came)], 1)
     keep_g = jnp.where(first, total[:cols], total[cols:pair])
@@ -208,7 +297,7 @@
     img_proj_grad = jnp.where(first, got_g, keep_g).T
     txt_proj_grad = jnp.where(first, keep_g, got_g).T
 
-    grad = jnp.dot(du, permuted(proj, sibling), preferred_element_type=f32)
+    grad = jnp.dot(du, other_proj, preferred_element_type=f32)
     grad = grad.reshape(N_BLK, N_CORE, sub_rows, width)
     keep_r = grad[:, 0].reshape(rows, width)
     got_r = permuted(grad[:, 1].reshape(rows, width), sibling)

time: 226 us -> 238 us (1.053)
  the two profiles are of different devices: /device:TPU:1 before, /device:TPU:13 now
where the time goes in v8:
time: 238 us; the launch traced here: 237 us
  waiting for transfers between devices  113 us (47%)
  starting transfers between devices  84.4 us (35%)
  Pallas kernels  11.6 us (5%)
  local copies, waits for them, and re-layouts  11.2 us (5%)
  other arithmetic  7.69 us (3%)
  matrix products  5.63 us (2%)
  between operations  3.16 us (1%)
    all_to_all x5, waiting for transfers between devices, exchanged(): lax.all_to_all(value, BOTH, 0, 0, axis_index_groups=groups, tiled=True)  59.2 us
    ppermute x15, waiting for transfers between devices, permuted(): return lax.ppermute(value, BOTH, pairs)  53.7 us
    ppermute x15, starting transfers between devices, permuted(): return lax.ppermute(value, BOTH, pairs)  51.7 us
    all_to_all x5, starting transfers between devices, exchanged(): lax.all_to_all(value, BOTH, 0, 0, axis_index_groups=groups, tiled=True)  32.7 us
    pallas_call x1, Pallas kernels, partial_grads(): pl.pallas_call(functools.partial(partial_kernel, block=block), grid=(coun...  5.81 us
    pallas_call x1, Pallas kernels, embedded(): pl.pallas_call(embed_kernel, grid=(count // group,), in_specs=[pl.BlockSp...  5.79 us
  transfers between devices with their start and end apart: 20, of which 11 were waited for; matrix products, arithmetic and copies ran while one was open for 7% of the time, Pallas kernels for 5%

profile of v8, /device:TPU:13, one launch (start us, length us, event | category | flops | bytes accessed | tf_op | source)
XLA Modules:
  0.0 236.5 jit_solution(10547850057683752993)
XLA Ops:
  1.9 2.6 %collective-permute-start.1 = (bf16[34,1152]{1,0:T(8,128)(2,1)S(1)}, bf16[34,1152]{1,0:T(8,128)(2,1)S(1)}, u32[]{:S(2)}, u32[]{:S(2)}) collective-permute-start(bf16[34,1152]{1,0:T(8,128)(2,1)S(1)} %pad_maximum_fusion.9), channel_id=1, source_target_pairs={{0,1},{1,0},{2,3},{3,2},{4,5},{5,4},{6,7},{7,6},{8,9},{9,8},{10,11... | collective-permute-start | bytes 235016 | tf_op jit(solution)/shard_map/ppermute | solution.py:81
  4.5 11.0 %collective-permute-start.3 = (bf16[34,1152]{1,0:T(8,128)(2,1)S(1)}, bf16[34,1152]{1,0:T(8,128)(2,1)S(1)}, u32[]{:S(2)}, u32[]{:S(2)}) collective-permute-start(bf16[34,1152]{1,0:T(8,128)(2,1)S(1)} %pad_maximum_fusion.9), channel_id=1, source_target_pairs={{0,457},{1,456},{2,459},{3,458},{4,461},{5,460},{6,463},{7,462},{8... | collective-permute-start | bytes 235016 | tf_op jit(solution)/shard_map/ppermute | solution.py:81
  15.6 2.0 collective-permute-start.2
  18.6 4.3 %all-to-all-start = ((bf16[4,68,1152]{2,1,0:T(8,128)(2,1)}), bf16[4,68,1152]{2,1,0:T(8,128)(2,1)S(1)}, u32[]{:S(2)}, u32[]{:S(2)}) async-start(bf16[4,68,1152]{2,1,0:T(8,128)(2,1)} %broadcast_in_dim.10), calls=%async_computation | async-start | bytes 1327104 | tf_op jit(solution)/shard_map/all_to_all | solution.py:85
  22.9 7.6 %collective-permute-done.3 = bf16[34,1152]{1,0:T(8,128)(2,1)S(1)} collective-permute-done((bf16[34,1152]{1,0:T(8,128)(2,1)S(1)}, bf16[34,1152]{1,0:T(8,128)(2,1)S(1)}, u32[]{:S(2)}, u32[]{:S(2)}) %collective-permute-start.3) | collective-permute-done | bytes 78368 | tf_op jit(solution)/shard_map/ppermute | solution.py:81
  33.4 4.3 %all-to-all-start.1 = ((bf16[4,68,1152]{2,1,0:T(8,128)(2,1)}), bf16[4,68,1152]{2,1,0:T(8,128)(2,1)S(1)}, u32[]{:S(2)}, u32[]{:S(2)}) async-start(bf16[4,68,1152]{2,1,0:T(8,128)(2,1)} %broadcast_in_dim.11), calls=%async_computation.1 | async-start | bytes 1327104 | tf_op jit(solution)/shard_map/all_to_all | solution.py:85
  37.8 6.5 %all-to-all-done.1 = bf16[4,68,1152]{2,1,0:T(8,128)(2,1)S(1)} async-done(((bf16[4,68,1152]{2,1,0:T(8,128)(2,1)}), bf16[4,68,1152]{2,1,0:T(8,128)(2,1)S(1)}, u32[]{:S(2)}, u32[]{:S(2)}) %all-to-all-start.1) | async-done | bytes 626720 | tf_op jit(solution)/shard_map/all_to_all | solution.py:85
  44.5 2.6 %broadcast_in_dim.12 = bf16[4,4,136,1152]{3,2,1,0:T(8,128)(2,1)} broadcast(bf16[4,136,1152]{2,1,0:T(8,128)(2,1)S(1)} %pad_maximum_fusion), dimensions={1,2,3} | broadcast | bytes 6266880 | tf_op jit(solution)/shard_map/broadcast_in_dim | solution.py:90
  47.1 5.5 %all-to-all-start.2 = ((bf16[4,4,136,1152]{3,2,1,0:T(8,128)(2,1)}), bf16[4,4,136,1152]{3,2,1,0:T(8,128)(2,1)}, u32[]{:S(2)}, u32[]{:S(2)}) async-start(bf16[4,4,136,1152]{3,2,1,0:T(8,128)(2,1)} %broadcast_in_dim.12), calls=%async_computation.2 | async-start | bytes 10027008 | tf_op jit(solution)/shard_map/all_to_all | solution.py:85
  53.5 2.2 collective-permute-start
  55.7 25.6 %all-to-all-done.2 = bf16[4,4,136,1152]{3,2,1,0:T(8,128)(2,1)} async-done(((bf16[4,4,136,1152]{3,2,1,0:T(8,128)(2,1)}), bf16[4,4,136,1152]{3,2,1,0:T(8,128)(2,1)}, u32[]{:S(2)}, u32[]{:S(2)}) %all-to-all-start.2) | async-done | bytes 5013536 | tf_op jit(solution)/shard_map/all_to_all | solution.py:85
  81.3 2.0 slice.91
  83.6 4.3 %collective-permute-start.5 = (bf16[1152,1152]{1,0:T(8,128)(2,1)S(1)}, bf16[1152,1152]{1,0:T(8,128)(2,1)}, u32[]{:S(2)}, u32[]{:S(2)}) collective-permute-start(bf16[1152,1152]{1,0:T(8,128)(2,1)S(1)} %bitcast.39), channel_id=1, source_target_pairs={{0,1},{1,0},{2,3},{3,2},{4,5},{5,4},{6,7},{7,6},{8,9},{9,8},{10,11... | collective-permute-start | bytes 7962632 | tf_op jit(solution)/shard_map/ppermute | solution.py:81
  89.8 2.2 fusion.11
  96.0 5.8 %shard_map.102.others_ref = bf16[1024,1152]{1,0:T(8,128)(2,1)S(1)} custom-call(bf16[16,136,1152]{2,1,0:T(8,128)(2,1)} %bitcast.11.feat_ref, bf16[1152,1152]{1,0:T(8,128)(2,1)S(1)} %bitcast.41), custom_call_target="tpu_custom_call" | custom-call | flops 2717908992 | bytes 7372800 | tf_op jit(solution)/shard_map/pallas_call | solution.py:117
  101.8 5.8 %shard_map.103 = bf16[256,1152]{1,0:T(8,128)(2,1)S(1)} custom-call(s32[2]{0:T(128)S(1)} %pad_add_fusion.at_ref, f32[3]{0:T(128)S(1)} %pad_maximum_fusion.11.par_ref, f32[256,1152]{1,0:T(8,128)} %collective-permute-done.4.made_ref, bf16[1024,1152]{1,0:T(8,128)(2,1)S(1)} %shard_map.102.others_ref), custom_call_target="tpu_custom_call" | custom-call | flops 1207959552 | bytes 4128768 | tf_op jit(solution)/shard_map/pallas_call | solution.py:171
  110.7 13.3 %collective-permute-done.6 = bf16[256,1152]{1,0:T(8,128)(2,1)S(1)} collective-permute-done((bf16[256,1152]{1,0:T(8,128)(2,1)S(1)}, bf16[256,1152]{1,0:T(8,128)(2,1)S(1)}, u32[]{:S(2)}, u32[]{:S(2)}) %collective-permute-start.6) | collective-permute-done | bytes 589856 | tf_op jit(solution)/shard_map/ppermute | solution.py:81
  125.1 3.4 %collective-permute-start.7 = (bf16[64,1152]{1,0:T(8,128)(2,1)S(1)}, bf16[64,1152]{1,0:T(8,128)(2,1)S(1)}, u32[]{:S(2)}, u32[]{:S(2)}) collective-permute-start(bf16[64,1152]{1,0:T(8,128)(2,1)S(1)} %dynamic-slice_convert_fusion), channel_id=1, source_target_pairs={{0,128},{1,129},{2,130},{3,131},{4,132},{5,133},{6,134},{7,135},{8... | collective-permute-start | bytes 442376 | tf_op jit(solution)/shard_map/ppermute | solution.py:81
  130.3 7.1 %all-to-all-start.3 = ((bf16[16,72,576]{2,1,0:T(8,128)(2,1)}), bf16[16,72,576]{2,1,0:T(8,128)(2,1)S(1)}, u32[]{:S(2)}, u32[]{:S(2)}) async-start(bf16[16,72,576]{2,1,0:T(8,128)(2,1)} %bitcast.17), calls=%async_computation.3 | async-start | bytes 2949120 | tf_op jit(solution)/shard_map/all_to_all | solution.py:85
  138.4 5.5 %collective-permute-start.8 = (bf16[32,1152]{1,0:T(8,128)(2,1)S(1)}, bf16[32,1152]{1,0:T(8,128)(2,1)S(1)}, u32[]{:S(2)}, u32[]{:S(2)}) collective-permute-start(bf16[32,1152]{1,0:T(8,128)(2,1)S(1)} %dynamic-slice_convert_fusion.1), channel_id=1, source_target_pairs={{0,256},{1,257},{2,258},{3,259},{4,260},{5,261},{6,262},{7,263},{8... | collective-permute-start | bytes 221192 | tf_op jit(solution)/shard_map/ppermute | solution.py:81
  144.0 8.5 %collective-permute-done.8 = bf16[32,1152]{1,0:T(8,128)(2,1)S(1)} collective-permute-done((bf16[32,1152]{1,0:T(8,128)(2,1)S(1)}, bf16[32,1152]{1,0:T(8,128)(2,1)S(1)}, u32[]{:S(2)}, u32[]{:S(2)}) %collective-permute-start.8) | collective-permute-done | bytes 73760 | tf_op jit(solution)/shard_map/ppermute | solution.py:81
  152.5 5.1 %all-to-all-done.3 = bf16[16,72,576]{2,1,0:T(8,128)(2,1)S(1)} async-done(((bf16[16,72,576]{2,1,0:T(8,128)(2,1)}), bf16[16,72,576]{2,1,0:T(8,128)(2,1)S(1)}, u32[]{:S(2)}, u32[]{:S(2)}) %all-to-all-start.3) | async-done | bytes 1327136 | tf_op jit(solution)/shard_map/all_to_all | solution.py:85
  157.6 4.7 %collective-permute-start.9 = (bf16[32,1152]{1,0:T(8,128)(2,1)S(1)}, bf16[32,1152]{1,0:T(8,128)(2,1)S(1)}, u32[]{:S(2)}, u32[]{:S(2)}) collective-permute-start(bf16[32,1152]{1,0:T(8,128)(2,1)S(1)} %add_convert_fusion), channel_id=1, source_target_pairs={{0,256},{1,257},{2,258},{3,259},{4,260},{5,261},{6,262},{7,263},{8... | collective-permute-start | bytes 221192 | tf_op jit(solution)/shard_map/ppermute | solution.py:81
  162.3 9.8 %collective-permute-done.9 = bf16[32,1152]{1,0:T(8,128)(2,1)S(1)} collective-permute-done((bf16[32,1152]{1,0:T(8,128)(2,1)S(1)}, bf16[32,1152]{1,0:T(8,128)(2,1)S(1)}, u32[]{:S(2)}, u32[]{:S(2)}) %collective-permute-start.9) | collective-permute-done | bytes 73760 | tf_op jit(solution)/shard_map/ppermute | solution.py:81
  174.1 8.7 %collective-permute-done.10 = bf16[64,1152]{1,0:T(8,128)(2,1)S(1)} collective-permute-done((bf16[64,1152]{1,0:T(8,128)(2,1)S(1)}, bf16[64,1152]{1,0:T(8,128)(2,1)S(1)}, u32[]{:S(2)}, u32[]{:S(2)}) %collective-permute-start.10) | collective-permute-done | bytes 147488 | tf_op jit(solution)/shard_map/ppermute | solution.py:81
  182.9 1.9 collective-permute-start.11
  185.9 11.4 %all-to-all-start.4 = ((bf16[8,36,576]{2,1,0:T(8,128)(2,1)}), bf16[8,36,576]{2,1,0:T(8,128)(2,1)S(1)}, u32[]{:S(2)}, u32[]{:S(2)}) async-start(bf16[8,36,576]{2,1,0:T(8,128)(2,1)} %bitcast.21), calls=%async_computation.4 | async-start | bytes 819200 | tf_op jit(solution)/shard_map/all_to_all | solution.py:85
  197.4 2.7 %fusion = f32[256,1152]{1,0:T(8,128)S(1)} fusion(bf16[1152,1152]{1,0:T(8,128)(2,1)} %collective-permute-done.5, bf16[128,1152]{1,0:T(8,128)(2,1)S(1)} %get-tuple-element.25, bf16[128,1152]{1,0:T(8,128)(2,1)S(1)} %get-tuple-element.24), kind=kOutput, calls=%fused_computation.8 | convolution fusion | flops 680656896 | bytes 4423680 | tf_op jit(solution)/shard_map/dot_general | solution.py:300
  200.2 3.0 %collective-permute-start.12 = (f32[128,1152]{1,0:T(8,128)S(1)}, f32[128,1152]{1,0:T(8,128)S(1)}, u32[]{:S(2)}, u32[]{:S(2)}) collective-permute-start(f32[128,1152]{1,0:T(8,128)S(1)} %bitcast.49), channel_id=1, source_target_pairs={{0,1},{1,0},{2,3},{3,2},{4,5},{5,4},{6,7},{7,6},{8,9},{9,8},{10,11... | collective-permute-start | bytes 1769480 | tf_op jit(solution)/shard_map/ppermute | solution.py:81
  203.2 22.0 %all-to-all-done.4 = bf16[8,36,576]{2,1,0:T(8,128)(2,1)S(1)} async-done(((bf16[8,36,576]{2,1,0:T(8,128)(2,1)}), bf16[8,36,576]{2,1,0:T(8,128)(2,1)S(1)}, u32[]{:S(2)}, u32[]{:S(2)}) %all-to-all-start.4) | async-done | bytes 331808 | tf_op jit(solution)/shard_map/all_to_all | solution.py:85
  227.3 3.8 %collective-permute-done.13 = f32[36,576]{1,0:T(8,128)S(1)} collective-permute-done((f32[36,576]{1,0:T(8,128)S(1)}, f32[36,576]{1,0:T(8,128)S(1)}, u32[]{:S(2)}, u32[]{:S(2)}) %collective-permute-start.13) | collective-permute-done | bytes 82976 | tf_op jit(solution)/shard_map/ppermute | solution.py:81
  231.2 3.4 %collective-permute-start.14 = (f32[18,1152]{1,0:T(8,128)S(1)}, f32[18,1152]{1,0:T(8,128)S(1)}, u32[]{:S(2)}, u32[]{:S(2)}) collective-permute-start(f32[18,1152]{1,0:T(8,128)S(1)} %broadcast_select_fusion.11), channel_id=1, source_target_pairs={{0,1},{1,0},{2,3},{3,2},{4,5},{5,4},{6,7},{7,6},{8,9},{9,8},{10,11... | collective-permute-start | bytes 248840 | tf_op jit(solution)/shard_map/ppermute | solution.py:81
  (68 shorter events, 24.6 us)
Async XLA Ops:
  0.6 1.2 copy-start.1
  0.6 1.2 copy-start.2
  1.9 13.6 %collective-permute-start.1 = (bf16[34,1152]{1,0:T(8,128)(2,1)S(1)}, bf16[34,1152]{1,0:T(8,128)(2,1)S(1)}, u32[]{:S(2)}, u32[]{:S(2)}) collective-permute-start(bf16[34,1152]{1,0:T(8,128)(2,1)S(1)} %pad_maximum_fusion.9), channel_id=1, source_target_pairs={{0,1},{1,0},{2,3},{3,2},{4,5},{5,4},{6,7},{7,6},{8,9},{9,8},{10,11... | collective-permute-start | bytes 235016 | tf_op jit(solution)/shard_map/ppermute | solution.py:81
  4.5 26.1 %collective-permute-start.3 = (bf16[34,1152]{1,0:T(8,128)(2,1)S(1)}, bf16[34,1152]{1,0:T(8,128)(2,1)S(1)}, u32[]{:S(2)}, u32[]{:S(2)}) collective-permute-start(bf16[34,1152]{1,0:T(8,128)(2,1)S(1)} %pad_maximum_fusion.9), channel_id=1, source_target_pairs={{0,457},{1,456},{2,459},{3,458},{4,461},{5,460},{6,463},{7,462},{8... | collective-permute-start | bytes 235016 | tf_op jit(solution)/shard_map/ppermute | solution.py:81
  15.6 16.9 %collective-permute-start.2 = (bf16[34,1152]{1,0:T(8,128)(2,1)S(1)}, bf16[34,1152]{1,0:T(8,128)(2,1)S(1)}, u32[]{:S(2)}, u32[]{:S(2)}) collective-permute-start(bf16[34,1152]{1,0:T(8,128)(2,1)S(1)} %pad_maximum_fusion.10), channel_id=1, source_target_pairs={{0,456},{1,457},{2,458},{3,459},{4,460},{5,461},{6,462},{7,463},{8... | collective-permute-start | bytes 235016 | tf_op jit(solution)/shard_map/ppermute | solution.py:81
  18.6 13.9 %all-to-all-start = ((bf16[4,68,1152]{2,1,0:T(8,128)(2,1)}), bf16[4,68,1152]{2,1,0:T(8,128)(2,1)S(1)}, u32[]{:S(2)}, u32[]{:S(2)}) async-start(bf16[4,68,1152]{2,1,0:T(8,128)(2,1)} %broadcast_in_dim.10), calls=%async_computation | async-start | bytes 1327104 | tf_op jit(solution)/shard_map/all_to_all | solution.py:85
  33.4 10.9 %all-to-all-start.1 = ((bf16[4,68,1152]{2,1,0:T(8,128)(2,1)}), bf16[4,68,1152]{2,1,0:T(8,128)(2,1)S(1)}, u32[]{:S(2)}, u32[]{:S(2)}) async-start(bf16[4,68,1152]{2,1,0:T(8,128)(2,1)} %broadcast_in_dim.11), calls=%async_computation.1 | async-start | bytes 1327104 | tf_op jit(solution)/shard_map/all_to_all | solution.py:85
  47.1 34.2 %all-to-all-start.2 = ((bf16[4,4,136,1152]{3,2,1,0:T(8,128)(2,1)}), bf16[4,4,136,1152]{3,2,1,0:T(8,128)(2,1)}, u32[]{:S(2)}, u32[]{:S(2)}) async-start(bf16[4,4,136,1152]{3,2,1,0:T(8,128)(2,1)} %broadcast_in_dim.12), calls=%async_computation.2 | async-start | bytes 10027008 | tf_op jit(solution)/shard_map/all_to_all | solution.py:85
  53.5 34.4 %collective-permute-start = (bf16[256,1152]{1,0:T(8,128)(2,1)}, bf16[256,1152]{1,0:T(8,128)(2,1)}, u32[]{:S(2)}, u32[]{:S(2)}) collective-permute-start(bf16[256,1152]{1,0:T(8,128)(2,1)} %pad_maximum_fusion.1), channel_id=1, source_target_pairs={{0,1},{1,0},{2,3},{3,2},{4,5},{5,4},{6,7},{7,6},{8,9},{9,8},{10,11... | collective-permute-start | bytes 1769480 | tf_op jit(solution)/shard_map/ppermute | solution.py:81
  83.6 24.1 %collective-permute-start.5 = (bf16[1152,1152]{1,0:T(8,128)(2,1)S(1)}, bf16[1152,1152]{1,0:T(8,128)(2,1)}, u32[]{:S(2)}, u32[]{:S(2)}) collective-permute-start(bf16[1152,1152]{1,0:T(8,128)(2,1)S(1)} %bitcast.39), channel_id=1, source_target_pairs={{0,1},{1,0},{2,3},{3,2},{4,5},{5,4},{6,7},{7,6},{8,9},{9,8},{10,11... | collective-permute-start | bytes 7962632 | tf_op jit(solution)/shard_map/ppermute | solution.py:81
  92.0 9.9 %collective-permute-start.4 = (f32[256,1152]{1,0:T(8,128)}, f32[256,1152]{1,0:T(8,128)}, u32[]{:S(2)}, u32[]{:S(2)}) collective-permute-start(f32[256,1152]{1,0:T(8,128)} %fusion.11), channel_id=1, source_target_pairs={{0,1},{1,0},{2,3},{3,2},{4,5},{5,4},{6,7},{7,6},{8,9},{9,8},{10,11... | collective-permute-start | bytes 3538952 | tf_op jit(solution)/shard_map/ppermute | solution.py:81
  107.7 16.3 %collective-permute-start.6 = (bf16[256,1152]{1,0:T(8,128)(2,1)S(1)}, bf16[256,1152]{1,0:T(8,128)(2,1)S(1)}, u32[]{:S(2)}, u32[]{:S(2)}) collective-permute-start(bf16[256,1152]{1,0:T(8,128)(2,1)S(1)} %shard_map.103), channel_id=1, source_target_pairs={{0,64},{1,65},{2,66},{3,67},{4,68},{5,69},{6,70},{7,71},{8,72},{9,... | collective-permute-start | bytes 1769480 | tf_op jit(solution)/shard_map/ppermute | solution.py:81
  124.1 1.0 copy-start
  125.1 12.2 %collective-permute-start.7 = (bf16[64,1152]{1,0:T(8,128)(2,1)S(1)}, bf16[64,1152]{1,0:T(8,128)(2,1)S(1)}, u32[]{:S(2)}, u32[]{:S(2)}) collective-permute-start(bf16[64,1152]{1,0:T(8,128)(2,1)S(1)} %dynamic-slice_convert_fusion), channel_id=1, source_target_pairs={{0,128},{1,129},{2,130},{3,131},{4,132},{5,133},{6,134},{7,135},{8... | collective-permute-start | bytes 442376 | tf_op jit(solution)/shard_map/ppermute | solution.py:81
  130.3 27.4 %all-to-all-start.3 = ((bf16[16,72,576]{2,1,0:T(8,128)(2,1)}), bf16[16,72,576]{2,1,0:T(8,128)(2,1)S(1)}, u32[]{:S(2)}, u32[]{:S(2)}) async-start(bf16[16,72,576]{2,1,0:T(8,128)(2,1)} %bitcast.17), calls=%async_computation.3 | async-start | bytes 2949120 | tf_op jit(solution)/shard_map/all_to_all | solution.py:85
  138.4 14.1 %collective-permute-start.8 = (bf16[32,1152]{1,0:T(8,128)(2,1)S(1)}, bf16[32,1152]{1,0:T(8,128)(2,1)S(1)}, u32[]{:S(2)}, u32[]{:S(2)}) collective-permute-start(bf16[32,1152]{1,0:T(8,128)(2,1)S(1)} %dynamic-slice_convert_fusion.1), channel_id=1, source_target_pairs={{0,256},{1,257},{2,258},{3,259},{4,260},{5,261},{6,262},{7,263},{8... | collective-permute-start | bytes 221192 | tf_op jit(solution)/shard_map/ppermute | solution.py:81
  157.6 14.5 %collective-permute-start.9 = (bf16[32,1152]{1,0:T(8,128)(2,1)S(1)}, bf16[32,1152]{1,0:T(8,128)(2,1)S(1)}, u32[]{:S(2)}, u32[]{:S(2)}) collective-permute-start(bf16[32,1152]{1,0:T(8,128)(2,1)S(1)} %add_convert_fusion), channel_id=1, source_target_pairs={{0,256},{1,257},{2,258},{3,259},{4,260},{5,261},{6,262},{7,263},{8... | collective-permute-start | bytes 221192 | tf_op jit(solution)/shard_map/ppermute | solution.py:81
  172.1 10.7 %collective-permute-start.10 = (bf16[64,1152]{1,0:T(8,128)(2,1)S(1)}, bf16[64,1152]{1,0:T(8,128)(2,1)S(1)}, u32[]{:S(2)}, u32[]{:S(2)}) collective-permute-start(bf16[64,1152]{1,0:T(8,128)(2,1)S(1)} %pad_maximum_fusion.7), channel_id=1, source_target_pairs={{0,128},{1,129},{2,130},{3,131},{4,132},{5,133},{6,134},{7,135},{8... | collective-permute-start | bytes 442376 | tf_op jit(solution)/shard_map/ppermute | solution.py:81
  182.9 14.3 %collective-permute-start.11 = (bf16[128,1152]{1,0:T(8,128)(2,1)S(1)}, bf16[128,1152]{1,0:T(8,128)(2,1)S(1)}, u32[]{:S(2)}, u32[]{:S(2)}) collective-permute-start(bf16[128,1152]{1,0:T(8,128)(2,1)S(1)} %pad_maximum_fusion.4), channel_id=1, source_target_pairs={{0,64},{1,65},{2,66},{3,67},{4,68},{5,69},{6,70},{7,71},{8,72},{9,... | collective-permute-start | bytes 884744 | tf_op jit(solution)/shard_map/ppermute | solution.py:81
  185.9 39.3 %all-to-all-start.4 = ((bf16[8,36,576]{2,1,0:T(8,128)(2,1)}), bf16[8,36,576]{2,1,0:T(8,128)(2,1)S(1)}, u32[]{:S(2)}, u32[]{:S(2)}) async-start(bf16[8,36,576]{2,1,0:T(8,128)(2,1)} %bitcast.21), calls=%async_computation.4 | async-start | bytes 819200 | tf_op jit(solution)/shard_map/all_to_all | solution.py:85
  200.2 34.4 %collective-permute-start.12 = (f32[128,1152]{1,0:T(8,128)S(1)}, f32[128,1152]{1,0:T(8,128)S(1)}, u32[]{:S(2)}, u32[]{:S(2)}) collective-permute-start(f32[128,1152]{1,0:T(8,128)S(1)} %bitcast.49), channel_id=1, source_target_pairs={{0,1},{1,0},{2,3},{3,2},{4,5},{5,4},{6,7},{7,6},{8,9},{9,8},{10,11... | collective-permute-start | bytes 1769480 | tf_op jit(solution)/shard_map/ppermute | solution.py:81
  225.4 5.7 %collective-permute-start.13 = (f32[36,576]{1,0:T(8,128)S(1)}, f32[36,576]{1,0:T(8,128)S(1)}, u32[]{:S(2)}, u32[]{:S(2)}) collective-permute-start(f32[36,576]{1,0:T(8,128)S(1)} %convert_reduce_fusion), channel_id=1, source_target_pairs={{0,64},{1,65},{2,66},{3,67},{4,68},{5,69},{6,70},{7,71},{8,72},{9,... | collective-permute-start | bytes 248840 | tf_op jit(solution)/shard_map/ppermute | solution.py:81
  231.2 4.5 %collective-permute-start.14 = (f32[18,1152]{1,0:T(8,128)S(1)}, f32[18,1152]{1,0:T(8,128)S(1)}, u32[]{:S(2)}, u32[]{:S(2)}) collective-permute-start(f32[18,1152]{1,0:T(8,128)S(1)} %broadcast_select_fusion.11), channel_id=1, source_target_pairs={{0,1},{1,0},{2,3},{3,2},{4,5},{5,4},{6,7},{7,6},{8,9},{9,8},{10,11... | collective-permute-start | bytes 248840 | tf_op jit(solution)/shard_map/ppermute | solution.py:81

commit v9 on v8

--- a/solution.py
+++ b/solution.py
@@ -112,7 +112,7 @@
 def embedded(both, picked, proj):
     count, _, width = both.shape
     embed = proj.shape[0]
-    group = 4
+    group = 8
     rows = count * picked
     return pl.pallas_call(
         embed_kernel,
@@ -167,7 +167,7 @@
 def partial_grads(at, params, made, others, block):
     own, embed = made.shape
     count = others.shape[0]
-    tile = 256
+    tile = count
     return pl.pallas_call(
         functools.partial(partial_kernel, block=block),
         grid=(count // tile,),
@@ -245,26 +245,27 @@
         ],
         1,
     )
+    sib_feat = permuted(jnp.concatenate([own_f, other_f], 0), sibling)
+    sib_other, sib_own = sib_feat[:rows], sib_feat[rows:]
+
+    def interleaved(one, two):
+        shape = (N_BLK, sub_rows, width)
+        return jnp.stack([one.reshape(shape), two.reshape(shape)], 1).reshape(own, width)
+
+    feat = interleaved(other_f, sib_other)
+    sib_rows = interleaved(sib_own, own_f)
+    both, feat, sib_rows = lax.optimization_barrier((both, feat, sib_rows))
+
     both = gathered(both, OUTER)
     proj = both[:, :, N_ZH * picked :]
     proj = jnp.where(first, proj, proj.transpose(1, 0, 2, 3)).reshape(-1, width)
     embed = proj.shape[0]
 
-    sib_feat = permuted(jnp.concatenate([own_f, other_f], 0), sibling)
-    sib_other, sib_own = sib_feat[:rows], sib_feat[rows:]
-
-    def interleaved(one, two):
-        shape = (N_BLK, sub_rows, width)
-        return jnp.stack([one.reshape(shape), two.reshape(shape)], 1).reshape(own, width)
-
-    feat = interleaved(other_f, sib_other)
-
-    made = permuted(contract_last(interleaved(sib_own, own_f), proj), sibling)
+    made = permuted(contract_last(sib_rows, proj), sibling)
     others = embedded(both.reshape(N_Y * N_X, -1, width), N_ZH * picked, proj)
     spot = jnp.where(first, y * N_X + x, x * N_Y + y) * (N_ZH * picked)
     at = jnp.stack([sub * picked, spot]).astype(jnp.int32)
     part = partial_grads(at, jnp.stack([scale, shift_by, weight]), made, others, picked)
-    part, other_proj = lax.optimization_barrier((part, permuted(proj, sibling)))
 
     part = part.astype(f32) + permuted(part, along(1)).astype(f32)
     odd = (steps & 1) == 1
@@ -279,16 +280,18 @@
         send = lax.dynamic_slice_in_dim(held, (1 - high) * count, count, 0).astype(bf16)
         stay = lax.dynamic_slice_in_dim(held, high * count, count, 0)
         held = stay + permuted(send, along(hop)).astype(f32)
-    du, terms = lax.optimization_barrier((held.astype(bf16), terms))
+    du, terms, other_proj = lax.optimization_barrier(
+        (held.astype(bf16), terms, permuted(proj, sibling))
+    )
+    terms = jnp.sum(terms.astype(f32), 0).astype(bf16).reshape(N_ZH, pair, half)
+    terms = jnp.broadcast_to(terms[:, None], (N_ZH, N_BLK // 2, pair, half))
+    terms = exchanged(terms.reshape(N_BLK, pair, half), RING)
     for bit, hop in ((1, 4), (2, 2), (4, 1)):
+        if hop == 1:
+            du, terms = lax.optimization_barrier((du, terms))
         came = permuted(du, along(hop))
         high = (sub & bit) > 0
         du = jnp.concatenate([jnp.where(high, came, du), jnp.where(high, du, came)], 0)
-
-    terms = jnp.sum(terms.astype(f32), 0)
-    terms = terms.astype(bf16).reshape(N_ZH, pair, half)
-    terms = jnp.broadcast_to(terms[:, None], (N_ZH, N_BLK // 2, pair, half))
-    terms = exchanged(terms.reshape(N_BLK, pair, half), RING)
     total = jnp.sum(terms.astype(f32), 0)
     came = permuted(total, along(1))
     total = jnp.concatenate([jnp.where(odd, came, total), jnp.where(odd, total, came)], 1)
@@ -297,10 +300,14 @@
     img_proj_grad = jnp.where(first, got_g, keep_g).T
     txt_proj_grad = jnp.where(first, keep_g, got_g).T
 
-    grad = jnp.dot(du, other_proj, preferred_element_type=f32)
-    grad = grad.reshape(N_BLK, N_CORE, sub_rows, width)
-    keep_r = grad[:, 0].reshape(rows, width)
-    got_r = permuted(grad[:, 1].reshape(rows, width), sibling)
+    du = du.reshape(N_BLK, N_CORE, sub_rows, embed)
+
+    def grads(core_at):
+        rows_of = du[:, core_at].reshape(rows, embed)
+        return jnp.dot(rows_of, other_proj, preferred_element_type=f32)
+
+    got_r = permuted(grads(1), sibling)
+    keep_r = grads(0)
     img_grad = jnp.where(first, got_r, keep_r)
     txt_grad = jnp.where(first, keep_r, got_r)
     return (img_grad, txt_grad, img_proj_grad, txt_proj_grad)

time: 238 us -> 235 us (0.987)
  the two profiles are of different devices: /device:TPU:13 before, /device:TPU:1 now
where the time goes in v9:
time: 235 us; the launch traced here: 234 us
  starting transfers between devices  90.4 us (38%)
  waiting for transfers between devices  66.6 us (28%)
  blocking collectives  34.8 us (15%)
  local copies, waits for them, and re-layouts  11.7 us (5%)
  matrix products  10.9 us (5%)
  other arithmetic  8.71 us (4%)
  Pallas kernels  7.81 us (3%)
  between operations  3.23 us (1%)
    ppermute x15, starting transfers between devices, permuted(): return lax.ppermute(value, BOTH, pairs)  69 us
    ppermute x15, waiting for transfers between devices, permuted(): return lax.ppermute(value, BOTH, pairs)  52.3 us
    all_to_all x1, blocking collectives, exchanged(): lax.all_to_all(value, BOTH, 0, 0, axis_index_groups=groups, tiled=True)  34.8 us
    all_to_all x4, starting transfers between devices, exchanged(): lax.all_to_all(value, BOTH, 0, 0, axis_index_groups=groups, tiled=True)  21.5 us
    all_to_all x4, waiting for transfers between devices, exchanged(): lax.all_to_all(value, BOTH, 0, 0, axis_index_groups=groups, tiled=True)  14.3 us
    unnamed x10, local copies, waits for them, and re-layouts  5.72 us
    dot_general x2, matrix products, grads(): return jnp.dot(rows_of, other_proj, preferred_element_type=f32)  5.69 us
  transfers between devices with their start and end apart: 19, of which 10 were waited for; matrix products, arithmetic and copies ran while one was open for 6% of the time, Pallas kernels for 2%

profile of v9, /device:TPU:1, one launch (start us, length us, event | category | flops | bytes accessed | tf_op | source)
XLA Modules:
  0.0 234.2 jit_solution(5625294357296605988)
XLA Ops:
  2.7 8.8 %collective-permute-start = (bf16[34,1152]{1,0:T(8,128)(2,1)S(1)}, bf16[34,1152]{1,0:T(8,128)(2,1)S(1)}, u32[]{:S(2)}, u32[]{:S(2)}) collective-permute-start(bf16[34,1152]{1,0:T(8,128)(2,1)S(1)} %pad_maximum_fusion.10), channel_id=1, source_target_pairs={{0,1},{1,0},{2,3},{3,2},{4,5},{5,4},{6,7},{7,6},{8,9},{9,8},{10,11... | collective-permute-start | bytes 235016 | tf_op jit(solution)/shard_map/ppermute | solution.py:81
  11.5 5.6 %collective-permute-start.2 = (bf16[34,1152]{1,0:T(8,128)(2,1)S(1)}, bf16[34,1152]{1,0:T(8,128)(2,1)S(1)}, u32[]{:S(2)}, u32[]{:S(2)}) collective-permute-start(bf16[34,1152]{1,0:T(8,128)(2,1)S(1)} %pad_maximum_fusion.10), channel_id=1, source_target_pairs={{0,457},{1,456},{2,459},{3,458},{4,461},{5,460},{6,463},{7,462},{8... | collective-permute-start | bytes 235016 | tf_op jit(solution)/shard_map/ppermute | solution.py:81
  17.2 2.4 %collective-permute-start.3 = (bf16[256,1152]{1,0:T(8,128)(2,1)S(1)}, bf16[256,1152]{1,0:T(8,128)(2,1)S(1)}, u32[]{:S(2)}, u32[]{:S(2)}) collective-permute-start(bf16[256,1152]{1,0:T(8,128)(2,1)S(1)} %pad_maximum_fusion.1), channel_id=1, source_target_pairs={{0,1},{1,0},{2,3},{3,2},{4,5},{5,4},{6,7},{7,6},{8,9},{9,8},{10,11... | collective-permute-start | bytes 1769480 | tf_op jit(solution)/shard_map/ppermute | solution.py:81
  22.6 4.2 %all-to-all-start = ((bf16[4,68,1152]{2,1,0:T(8,128)(2,1)}), bf16[4,68,1152]{2,1,0:T(8,128)(2,1)S(1)}, u32[]{:S(2)}, u32[]{:S(2)}) async-start(bf16[4,68,1152]{2,1,0:T(8,128)(2,1)} %broadcast_in_dim.10), calls=%async_computation | async-start | bytes 1327104 | tf_op jit(solution)/shard_map/all_to_all | solution.py:85
  26.8 6.2 %collective-permute-done.1 = bf16[34,1152]{1,0:T(8,128)(2,1)S(1)} collective-permute-done((bf16[34,1152]{1,0:T(8,128)(2,1)S(1)}, bf16[34,1152]{1,0:T(8,128)(2,1)S(1)}, u32[]{:S(2)}, u32[]{:S(2)}) %collective-permute-start.1) | collective-permute-done | bytes 78368 | tf_op jit(solution)/shard_map/ppermute | solution.py:81
  35.7 3.5 %all-to-all-start.1 = ((bf16[4,68,1152]{2,1,0:T(8,128)(2,1)}), bf16[4,68,1152]{2,1,0:T(8,128)(2,1)S(1)}, u32[]{:S(2)}, u32[]{:S(2)}) async-start(bf16[4,68,1152]{2,1,0:T(8,128)(2,1)} %broadcast_in_dim.11), calls=%async_computation.1 | async-start | bytes 1327104 | tf_op jit(solution)/shard_map/all_to_all | solution.py:85
  40.2 6.6 %all-to-all-done.1 = bf16[4,68,1152]{2,1,0:T(8,128)(2,1)S(1)} async-done(((bf16[4,68,1152]{2,1,0:T(8,128)(2,1)}), bf16[4,68,1152]{2,1,0:T(8,128)(2,1)S(1)}, u32[]{:S(2)}, u32[]{:S(2)}) %all-to-all-start.1) | async-done | bytes 626720 | tf_op jit(solution)/shard_map/all_to_all | solution.py:85
  47.4 34.8 %all_to_all.25 = bf16[4,4,136,1152]{3,2,1,0:T(8,128)(2,1)S(1)} all-to-all(bf16[4,4,136,1152]{3,2,1,0:T(8,128)(2,1)S(1)} %broadcast_in_dim.12), channel_id=1, replica_groups={{0,16,32,48},{2,18,34,50},{4,20,36,52},{6,22,38,54},{1,3,5,7},{17,19,21..., dimensions={0} | all-to-all | bytes 10027008 | tf_op jit(solution)/shard_map/all_to_all | solution.py:85
  82.5 2.2 copy-done
  87.1 6.0 %collective-permute-start.4 = (f32[256,1152]{1,0:T(8,128)}, f32[256,1152]{1,0:T(8,128)}, u32[]{:S(2)}, u32[]{:S(2)}) collective-permute-start(f32[256,1152]{1,0:T(8,128)} %fusion.8), channel_id=1, source_target_pairs={{0,1},{1,0},{2,3},{3,2},{4,5},{5,4},{6,7},{7,6},{8,9},{9,8},{10,11... | collective-permute-start | bytes 3538952 | tf_op jit(solution)/shard_map/ppermute | solution.py:81
  95.2 2.4 %copy-done.1 = bf16[4,4,136,1152]{3,2,1,0:T(8,128)(2,1)S(1)} copy-done((bf16[4,4,136,1152]{3,2,1,0:T(8,128)(2,1)S(1)}, bf16[4,4,136,1152]{3,2,1,0:T(8,128)(2,1)}, u32[]{:S(2)}) %copy-start.1) | copy-done | bytes 5013528
  97.6 4.3 %shard_map.102.others_ref = bf16[1024,1152]{1,0:T(8,128)(2,1)S(1)} custom-call(bf16[16,136,1152]{2,1,0:T(8,128)(2,1)S(1)} %bitcast.40, bf16[1152,1152]{1,0:T(8,128)(2,1)S(1)} %bitcast.42), custom_call_target="tpu_custom_call" | custom-call | flops 2717908992 | bytes 7372800 | tf_op jit(solution)/shard_map/pallas_call | solution.py:117
  101.9 3.5 %shard_map.103 = bf16[256,1152]{1,0:T(8,128)(2,1)S(1)} custom-call(s32[2]{0:T(128)S(1)} %pad_add_fusion.at_ref, f32[3]{0:T(128)S(1)} %pad_maximum_fusion.12.par_ref, f32[256,1152]{1,0:T(8,128)} %collective-permute-done.4.made_ref, bf16[1024,1152]{1,0:T(8,128)(2,1)S(1)} %shard_map.102.others_ref), custom_call_target="tpu_custom_call" | custom-call | flops 1207959552 | bytes 4128768 | tf_op jit(solution)/shard_map/pallas_call | solution.py:171
  105.4 3.5 %collective-permute-start.5 = (bf16[256,1152]{1,0:T(8,128)(2,1)S(1)}, bf16[256,1152]{1,0:T(8,128)(2,1)}, u32[]{:S(2)}, u32[]{:S(2)}) collective-permute-start(bf16[256,1152]{1,0:T(8,128)(2,1)S(1)} %shard_map.103), channel_id=1, source_target_pairs={{0,64},{1,65},{2,66},{3,67},{4,68},{5,69},{6,70},{7,71},{8,72},{9,... | collective-permute-start | bytes 1769480 | tf_op jit(solution)/shard_map/ppermute | solution.py:81
  109.0 2.2 collective-permute-start.8
  111.2 11.4 %collective-permute-done.5 = bf16[256,1152]{1,0:T(8,128)(2,1)} collective-permute-done((bf16[256,1152]{1,0:T(8,128)(2,1)S(1)}, bf16[256,1152]{1,0:T(8,128)(2,1)}, u32[]{:S(2)}, u32[]{:S(2)}) %collective-permute-start.5) | collective-permute-done | bytes 589856 | tf_op jit(solution)/shard_map/ppermute | solution.py:81
  122.7 3.1 %convolution_convert_fusion = bf16[1152,576]{0,1:T(8,128)(2,1)} fusion(bf16[256,1152]{1,0:T(8,128)(2,1)} %bitcast.48, pred[]{:T(512)S(6)} %eq.16, bf16[256,1152]{1,0:T(8,128)(2,1)} %collective-permute-done.5, bf16[256,1152]{1,0:T(8,128)(2,1)S(1)} %shard_map.103), kind=kOutput, calls=%fused_computation | convolution fusion | flops 341729280 | bytes 3162113 | tf_op jit(solution)/shard_map/dot_general | solution.py:101
  128.0 4.9 %collective-permute-start.6 = (bf16[64,1152]{1,0:T(8,128)(2,1)S(1)}, bf16[64,1152]{1,0:T(8,128)(2,1)S(1)}, u32[]{:S(2)}, u32[]{:S(2)}) collective-permute-start(bf16[64,1152]{1,0:T(8,128)(2,1)S(1)} %dynamic-slice_convert_fusion), channel_id=1, source_target_pairs={{0,128},{1,129},{2,130},{3,131},{4,132},{5,133},{6,134},{7,135},{8... | collective-permute-start | bytes 442376 | tf_op jit(solution)/shard_map/ppermute | solution.py:81
  132.9 2.6 %copy.38 = bf16[1152,576]{1,0:T(8,128)(2,1)} copy(bf16[1152,576]{0,1:T(8,128)(2,1)} %convolution_convert_fusion) | data formatting | bytes 2654208 | tf_op jit(solution)/shard_map/optimization_barrier | solution.py:274
  135.5 4.4 %all-to-all-start.3 = ((bf16[16,72,576]{2,1,0:T(8,128)(2,1)}), bf16[16,72,576]{2,1,0:T(8,128)(2,1)}, u32[]{:S(2)}, u32[]{:S(2)}) async-start(bf16[16,72,576]{2,1,0:T(8,128)(2,1)} %bitcast.44), calls=%async_computation.3 | async-start | bytes 2949120 | tf_op jit(solution)/shard_map/all_to_all | solution.py:85
  141.0 7.2 %collective-permute-start.7 = (bf16[32,1152]{1,0:T(8,128)(2,1)S(1)}, bf16[32,1152]{1,0:T(8,128)(2,1)S(1)}, u32[]{:S(2)}, u32[]{:S(2)}) collective-permute-start(bf16[32,1152]{1,0:T(8,128)(2,1)S(1)} %dynamic-slice_convert_fusion.1), channel_id=1, source_target_pairs={{0,256},{1,257},{2,258},{3,259},{4,260},{5,261},{6,262},{7,263},{8... | collective-permute-start | bytes 221192 | tf_op jit(solution)/shard_map/ppermute | solution.py:81
  148.2 7.0 %collective-permute-done.7 = bf16[32,1152]{1,0:T(8,128)(2,1)S(1)} collective-permute-done((bf16[32,1152]{1,0:T(8,128)(2,1)S(1)}, bf16[32,1152]{1,0:T(8,128)(2,1)S(1)}, u32[]{:S(2)}, u32[]{:S(2)}) %collective-permute-start.7) | collective-permute-done | bytes 73760 | tf_op jit(solution)/shard_map/ppermute | solution.py:81
  155.2 6.0 %all-to-all-done.3 = bf16[16,72,576]{2,1,0:T(8,128)(2,1)} async-done(((bf16[16,72,576]{2,1,0:T(8,128)(2,1)}), bf16[16,72,576]{2,1,0:T(8,128)(2,1)}, u32[]{:S(2)}, u32[]{:S(2)}) %all-to-all-start.3) | async-done | bytes 1327136 | tf_op jit(solution)/shard_map/all_to_all | solution.py:85
  161.2 5.4 %collective-permute-start.9 = (bf16[32,1152]{1,0:T(8,128)(2,1)S(1)}, bf16[32,1152]{1,0:T(8,128)(2,1)S(1)}, u32[]{:S(2)}, u32[]{:S(2)}) collective-permute-start(bf16[32,1152]{1,0:T(8,128)(2,1)S(1)} %add_convert_fusion), channel_id=1, source_target_pairs={{0,256},{1,257},{2,258},{3,259},{4,260},{5,261},{6,262},{7,263},{8... | collective-permute-start | bytes 221192 | tf_op jit(solution)/shard_map/ppermute | solution.py:81
  169.0 9.4 %all-to-all-start.4 = ((bf16[8,36,576]{2,1,0:T(8,128)(2,1)}), bf16[8,36,576]{2,1,0:T(8,128)(2,1)S(1)}, u32[]{:S(2)}, u32[]{:S(2)}) async-start(bf16[8,36,576]{2,1,0:T(8,128)(2,1)} %bitcast.18), calls=%async_computation.4 | async-start | bytes 819200 | tf_op jit(solution)/shard_map/all_to_all | solution.py:85
  178.5 4.3 %collective-permute-start.10 = (bf16[64,1152]{1,0:T(8,128)(2,1)S(1)}, bf16[64,1152]{1,0:T(8,128)(2,1)S(1)}, u32[]{:S(2)}, u32[]{:S(2)}) collective-permute-start(bf16[64,1152]{1,0:T(8,128)(2,1)S(1)} %pad_maximum_fusion.8), channel_id=1, source_target_pairs={{0,128},{1,129},{2,130},{3,131},{4,132},{5,133},{6,134},{7,135},{8... | collective-permute-start | bytes 442376 | tf_op jit(solution)/shard_map/ppermute | solution.py:81
  182.7 22.4 %collective-permute-done.10 = bf16[64,1152]{1,0:T(8,128)(2,1)S(1)} collective-permute-done((bf16[64,1152]{1,0:T(8,128)(2,1)S(1)}, bf16[64,1152]{1,0:T(8,128)(2,1)S(1)}, u32[]{:S(2)}, u32[]{:S(2)}) %collective-permute-start.10) | collective-permute-done | bytes 147488 | tf_op jit(solution)/shard_map/ppermute | solution.py:81
  207.2 3.4 %collective-permute-start.11 = (bf16[128,1152]{1,0:T(8,128)(2,1)S(1)}, bf16[128,1152]{1,0:T(8,128)(2,1)S(1)}, u32[]{:S(2)}, u32[]{:S(2)}) collective-permute-start(bf16[128,1152]{1,0:T(8,128)(2,1)S(1)} %pad_maximum_fusion.5), channel_id=1, source_target_pairs={{0,64},{1,65},{2,66},{3,67},{4,68},{5,69},{6,70},{7,71},{8,72},{9,... | collective-permute-start | bytes 884744 | tf_op jit(solution)/shard_map/ppermute | solution.py:81
  211.0 3.7 %collective-permute-done.11 = bf16[128,1152]{1,0:T(8,128)(2,1)S(1)} collective-permute-done((bf16[128,1152]{1,0:T(8,128)(2,1)S(1)}, bf16[128,1152]{1,0:T(8,128)(2,1)S(1)}, u32[]{:S(2)}, u32[]{:S(2)}) %collective-permute-start.11) | collective-permute-done | bytes 294944 | tf_op jit(solution)/shard_map/ppermute | solution.py:81
  214.9 2.3 fusion.9
  217.2 9.5 %collective-permute-start.12 = (f32[128,1152]{1,0:T(8,128)S(1)}, f32[128,1152]{1,0:T(8,128)S(1)}, u32[]{:S(2)}, u32[]{:S(2)}) collective-permute-start(f32[128,1152]{1,0:T(8,128)S(1)} %fusion.9), channel_id=1, source_target_pairs={{0,1},{1,0},{2,3},{3,2},{4,5},{5,4},{6,7},{7,6},{8,9},{9,8},{10,11... | collective-permute-start | bytes 1769480 | tf_op jit(solution)/shard_map/ppermute | solution.py:81
  230.9 3.4 %broadcast_select_fusion.4 = (f32[128,1152]{1,0:T(8,128)}, f32[128,1152]{1,0:T(8,128)}) fusion(f32[128,1152]{1,0:T(8,128)S(1)} %collective-permute-done.12, pred[]{:T(512)S(6)} %eq.14, bf16[128,1152]{1,0:T(8,128)(2,1)S(1)} %bitcast.49, bf16[1152,1152]{1,0:T(8,128)(2,1)} %collective-permute-done.8), kind=kOutput, calls=%fused_computation.21 | convolution fusion | flops 340033536 | bytes 4718593 | tf_op jit(solution)/shard_map/dot_general | solution.py:307
  (72 shorter events, 24.5 us)
Async XLA Ops:
  0.7 19.0 %copy-start.3 = (bf16[1152,18]{0,1:T(8,128)(2,1)S(1)}, bf16[1152,18]{0,1:T(8,128)(2,1)}, u32[]{:S(2)}) copy-start(bf16[1152,18]{0,1:T(8,128)(2,1)} %param.10) | copy-start | bytes 124420
  0.7 19.0 %copy-start.4 = (bf16[1152,18]{0,1:T(8,128)(2,1)S(1)}, bf16[1152,18]{0,1:T(8,128)(2,1)}, u32[]{:S(2)}) copy-start(bf16[1152,18]{0,1:T(8,128)(2,1)} %param.9) | copy-start | bytes 124420
  2.7 16.9 %collective-permute-start = (bf16[34,1152]{1,0:T(8,128)(2,1)S(1)}, bf16[34,1152]{1,0:T(8,128)(2,1)S(1)}, u32[]{:S(2)}, u32[]{:S(2)}) collective-permute-start(bf16[34,1152]{1,0:T(8,128)(2,1)S(1)} %pad_maximum_fusion.10), channel_id=1, source_target_pairs={{0,1},{1,0},{2,3},{3,2},{4,5},{5,4},{6,7},{7,6},{8,9},{9,8},{10,11... | collective-permute-start | bytes 235016 | tf_op jit(solution)/shard_map/ppermute | solution.py:81
  11.5 15.3 %collective-permute-start.2 = (bf16[34,1152]{1,0:T(8,128)(2,1)S(1)}, bf16[34,1152]{1,0:T(8,128)(2,1)S(1)}, u32[]{:S(2)}, u32[]{:S(2)}) collective-permute-start(bf16[34,1152]{1,0:T(8,128)(2,1)S(1)} %pad_maximum_fusion.10), channel_id=1, source_target_pairs={{0,457},{1,456},{2,459},{3,458},{4,461},{5,460},{6,463},{7,462},{8... | collective-permute-start | bytes 235016 | tf_op jit(solution)/shard_map/ppermute | solution.py:81
  17.2 22.0 %collective-permute-start.3 = (bf16[256,1152]{1,0:T(8,128)(2,1)S(1)}, bf16[256,1152]{1,0:T(8,128)(2,1)S(1)}, u32[]{:S(2)}, u32[]{:S(2)}) collective-permute-start(bf16[256,1152]{1,0:T(8,128)(2,1)S(1)} %pad_maximum_fusion.1), channel_id=1, source_target_pairs={{0,1},{1,0},{2,3},{3,2},{4,5},{5,4},{6,7},{7,6},{8,9},{9,8},{10,11... | collective-permute-start | bytes 1769480 | tf_op jit(solution)/shard_map/ppermute | solution.py:81
  19.7 13.3 %collective-permute-start.1 = (bf16[34,1152]{1,0:T(8,128)(2,1)S(1)}, bf16[34,1152]{1,0:T(8,128)(2,1)S(1)}, u32[]{:S(2)}, u32[]{:S(2)}) collective-permute-start(bf16[34,1152]{1,0:T(8,128)(2,1)S(1)} %pad_maximum_fusion.11), channel_id=1, source_target_pairs={{0,456},{1,457},{2,458},{3,459},{4,460},{5,461},{6,462},{7,463},{8... | collective-permute-start | bytes 235016 | tf_op jit(solution)/shard_map/ppermute | solution.py:81
  22.6 12.2 %all-to-all-start = ((bf16[4,68,1152]{2,1,0:T(8,128)(2,1)}), bf16[4,68,1152]{2,1,0:T(8,128)(2,1)S(1)}, u32[]{:S(2)}, u32[]{:S(2)}) async-start(bf16[4,68,1152]{2,1,0:T(8,128)(2,1)} %broadcast_in_dim.10), calls=%async_computation | async-start | bytes 1327104 | tf_op jit(solution)/shard_map/all_to_all | solution.py:85
  35.7 11.1 %all-to-all-start.1 = ((bf16[4,68,1152]{2,1,0:T(8,128)(2,1)}), bf16[4,68,1152]{2,1,0:T(8,128)(2,1)S(1)}, u32[]{:S(2)}, u32[]{:S(2)}) async-start(bf16[4,68,1152]{2,1,0:T(8,128)(2,1)} %broadcast_in_dim.11), calls=%async_computation.1 | async-start | bytes 1327104 | tf_op jit(solution)/shard_map/all_to_all | solution.py:85
  82.4 2.3 copy-start
  87.1 14.8 %collective-permute-start.4 = (f32[256,1152]{1,0:T(8,128)}, f32[256,1152]{1,0:T(8,128)}, u32[]{:S(2)}, u32[]{:S(2)}) collective-permute-start(f32[256,1152]{1,0:T(8,128)} %fusion.8), channel_id=1, source_target_pairs={{0,1},{1,0},{2,3},{3,2},{4,5},{5,4},{6,7},{7,6},{8,9},{9,8},{10,11... | collective-permute-start | bytes 3538952 | tf_op jit(solution)/shard_map/ppermute | solution.py:81
  95.2 2.4 %copy-start.1 = (bf16[4,4,136,1152]{3,2,1,0:T(8,128)(2,1)S(1)}, bf16[4,4,136,1152]{3,2,1,0:T(8,128)(2,1)}, u32[]{:S(2)}) copy-start(bf16[4,4,136,1152]{3,2,1,0:T(8,128)(2,1)} %copy-done) | copy-start | bytes 15040516
  105.4 17.2 %collective-permute-start.5 = (bf16[256,1152]{1,0:T(8,128)(2,1)S(1)}, bf16[256,1152]{1,0:T(8,128)(2,1)}, u32[]{:S(2)}, u32[]{:S(2)}) collective-permute-start(bf16[256,1152]{1,0:T(8,128)(2,1)S(1)} %shard_map.103), channel_id=1, source_target_pairs={{0,64},{1,65},{2,66},{3,67},{4,68},{5,69},{6,70},{7,71},{8,72},{9,... | collective-permute-start | bytes 1769480 | tf_op jit(solution)/shard_map/ppermute | solution.py:81
  109.0 46.2 %collective-permute-start.8 = (bf16[1152,1152]{1,0:T(8,128)(2,1)S(1)}, bf16[1152,1152]{1,0:T(8,128)(2,1)}, u32[]{:S(2)}, u32[]{:S(2)}) collective-permute-start(bf16[1152,1152]{1,0:T(8,128)(2,1)S(1)} %bitcast.43), channel_id=1, source_target_pairs={{0,1},{1,0},{2,3},{3,2},{4,5},{5,4},{6,7},{7,6},{8,9},{9,8},{10,11... | collective-permute-start | bytes 7962632 | tf_op jit(solution)/shard_map/ppermute | solution.py:81
  126.9 1.0 copy-start.2
  128.0 11.9 %collective-permute-start.6 = (bf16[64,1152]{1,0:T(8,128)(2,1)S(1)}, bf16[64,1152]{1,0:T(8,128)(2,1)S(1)}, u32[]{:S(2)}, u32[]{:S(2)}) collective-permute-start(bf16[64,1152]{1,0:T(8,128)(2,1)S(1)} %dynamic-slice_convert_fusion), channel_id=1, source_target_pairs={{0,128},{1,129},{2,130},{3,131},{4,132},{5,133},{6,134},{7,135},{8... | collective-permute-start | bytes 442376 | tf_op jit(solution)/shard_map/ppermute | solution.py:81
  135.5 25.7 %all-to-all-start.3 = ((bf16[16,72,576]{2,1,0:T(8,128)(2,1)}), bf16[16,72,576]{2,1,0:T(8,128)(2,1)}, u32[]{:S(2)}, u32[]{:S(2)}) async-start(bf16[16,72,576]{2,1,0:T(8,128)(2,1)} %bitcast.44), calls=%async_computation.3 | async-start | bytes 2949120 | tf_op jit(solution)/shard_map/all_to_all | solution.py:85
  141.0 14.2 %collective-permute-start.7 = (bf16[32,1152]{1,0:T(8,128)(2,1)S(1)}, bf16[32,1152]{1,0:T(8,128)(2,1)S(1)}, u32[]{:S(2)}, u32[]{:S(2)}) collective-permute-start(bf16[32,1152]{1,0:T(8,128)(2,1)S(1)} %dynamic-slice_convert_fusion.1), channel_id=1, source_target_pairs={{0,256},{1,257},{2,258},{3,259},{4,260},{5,261},{6,262},{7,263},{8... | collective-permute-start | bytes 221192 | tf_op jit(solution)/shard_map/ppermute | solution.py:81
  161.2 17.2 %collective-permute-start.9 = (bf16[32,1152]{1,0:T(8,128)(2,1)S(1)}, bf16[32,1152]{1,0:T(8,128)(2,1)S(1)}, u32[]{:S(2)}, u32[]{:S(2)}) collective-permute-start(bf16[32,1152]{1,0:T(8,128)(2,1)S(1)} %add_convert_fusion), channel_id=1, source_target_pairs={{0,256},{1,257},{2,258},{3,259},{4,260},{5,261},{6,262},{7,263},{8... | collective-permute-start | bytes 221192 | tf_op jit(solution)/shard_map/ppermute | solution.py:81
  169.0 36.2 %all-to-all-start.4 = ((bf16[8,36,576]{2,1,0:T(8,128)(2,1)}), bf16[8,36,576]{2,1,0:T(8,128)(2,1)S(1)}, u32[]{:S(2)}, u32[]{:S(2)}) async-start(bf16[8,36,576]{2,1,0:T(8,128)(2,1)} %bitcast.18), calls=%async_computation.4 | async-start | bytes 819200 | tf_op jit(solution)/shard_map/all_to_all | solution.py:85
  178.5 26.7 %collective-permute-start.10 = (bf16[64,1152]{1,0:T(8,128)(2,1)S(1)}, bf16[64,1152]{1,0:T(8,128)(2,1)S(1)}, u32[]{:S(2)}, u32[]{:S(2)}) collective-permute-start(bf16[64,1152]{1,0:T(8,128)(2,1)S(1)} %pad_maximum_fusion.8), channel_id=1, source_target_pairs={{0,128},{1,129},{2,130},{3,131},{4,132},{5,133},{6,134},{7,135},{8... | collective-permute-start | bytes 442376 | tf_op jit(solution)/shard_map/ppermute | solution.py:81
  205.3 5.7 %collective-permute-start.13 = (f32[36,576]{1,0:T(8,128)S(1)}, f32[36,576]{1,0:T(8,128)S(1)}, u32[]{:S(2)}, u32[]{:S(2)}) collective-permute-start(f32[36,576]{1,0:T(8,128)S(1)} %convert_reduce_fusion), channel_id=1, source_target_pairs={{0,64},{1,65},{2,66},{3,67},{4,68},{5,69},{6,70},{7,71},{8,72},{9,... | collective-permute-start | bytes 248840 | tf_op jit(solution)/shard_map/ppermute | solution.py:81
  207.2 7.5 %collective-permute-start.11 = (bf16[128,1152]{1,0:T(8,128)(2,1)S(1)}, bf16[128,1152]{1,0:T(8,128)(2,1)S(1)}, u32[]{:S(2)}, u32[]{:S(2)}) collective-permute-start(bf16[128,1152]{1,0:T(8,128)(2,1)S(1)} %pad_maximum_fusion.5), channel_id=1, source_target_pairs={{0,64},{1,65},{2,66},{3,67},{4,68},{5,69},{6,70},{7,71},{8,72},{9,... | collective-permute-start | bytes 884744 | tf_op jit(solution)/shard_map/ppermute | solution.py:81
  217.2 13.7 %collective-permute-start.12 = (f32[128,1152]{1,0:T(8,128)S(1)}, f32[128,1152]{1,0:T(8,128)S(1)}, u32[]{:S(2)}, u32[]{:S(2)}) collective-permute-start(f32[128,1152]{1,0:T(8,128)S(1)} %fusion.9), channel_id=1, source_target_pairs={{0,1},{1,0},{2,3},{3,2},{4,5},{5,4},{6,7},{7,6},{8,9},{9,8},{10,11... | collective-permute-start | bytes 1769480 | tf_op jit(solution)/shard_map/ppermute | solution.py:81
  226.9 3.2 %collective-permute-start.14 = (f32[18,1152]{1,0:T(8,128)S(1)}, f32[18,1152]{1,0:T(8,128)S(1)}, u32[]{:S(2)}, u32[]{:S(2)}) collective-permute-start(f32[18,1152]{1,0:T(8,128)S(1)} %broadcast_select_fusion.13), channel_id=1, source_target_pairs={{0,1},{1,0},{2,3},{3,2},{4,5},{5,4},{6,7},{7,6},{8,9},{9,8},{10,11... | collective-permute-start | bytes 248840 | tf_op jit(solution)/shard_map/ppermute | solution.py:81

commit v10 on v9

--- a/solution.py
+++ b/solution.py
@@ -63,18 +63,6 @@
     for core in range(N_CORE)
 ]
 
-RING = [
-    [
-        place(step if zh == 0 else N_BLK - 1 - step, y, zh, x, core)
-        for zh in range(N_ZH)
-        for step in range(odd, N_BLK, 2)
-    ]
-    for odd in range(2)
-    for y in range(N_Y)
-    for x in range(N_X)
-    for core in range(N_CORE)
-]
-
 
 def permuted(value, target):
     pairs = [(source, target(source)) for source in range(N_BLK * N_GRP)]
@@ -89,6 +77,11 @@
     count = len(groups[0])
     copies = jnp.broadcast_to(value[None], (count,) + value.shape)
     return exchanged(copies, groups)
+
+
+def summed(own, beside, across, both):
+    own, beside, across, both = (v.astype(jnp.float32) for v in (own, beside, across, both))
+    return (own + beside) + (across + both)
 
 
 def contract_last(left, right):
@@ -267,14 +260,11 @@
     at = jnp.stack([sub * picked, spot]).astype(jnp.int32)
     part = partial_grads(at, jnp.stack([scale, shift_by, weight]), made, others, picked)
 
-    part = part.astype(f32) + permuted(part, along(1)).astype(f32)
-    odd = (steps & 1) == 1
-    half = width // 2
-    terms = contract_first(part.astype(bf16), jnp.where(odd, feat[:, half:], feat[:, :half]))
-    part, terms = lax.optimization_barrier((part, terms.astype(bf16)))
-    terms = exchanged(terms.reshape(N_Y * N_X, embed // (N_Y * N_X), half), PLANE)
-    held = lax.dynamic_slice_in_dim(part, (steps & 1) * (own // 2), own // 2, 0)
-    for bit, hop in ((2, 2), (1, 4)):
+    terms = contract_first(part, feat).astype(bf16)
+    part, terms = lax.optimization_barrier((part, terms))
+    terms = exchanged(terms.reshape(N_Y * N_X, embed // (N_Y * N_X), width), PLANE)
+    held = part.astype(f32)
+    for bit, hop in ((4, 1), (2, 2), (1, 4)):
         count = held.shape[0] // 2
         high = (sub & bit) // bit
         send = lax.dynamic_slice_in_dim(held, (1 - high) * count, count, 0).astype(bf16)
@@ -283,31 +273,26 @@
     du, terms, other_proj = lax.optimization_barrier(
         (held.astype(bf16), terms, permuted(proj, sibling))
     )
-    terms = jnp.sum(terms.astype(f32), 0).astype(bf16).reshape(N_ZH, pair, half)
-    terms = jnp.broadcast_to(terms[:, None], (N_ZH, N_BLK // 2, pair, half))
-    terms = exchanged(terms.reshape(N_BLK, pair, half), RING)
     for bit, hop in ((1, 4), (2, 2), (4, 1)):
-        if hop == 1:
-            du, terms = lax.optimization_barrier((du, terms))
         came = permuted(du, along(hop))
         high = (sub & bit) > 0
         du = jnp.concatenate([jnp.where(high, came, du), jnp.where(high, du, came)], 0)
-    total = jnp.sum(terms.astype(f32), 0)
-    came = permuted(total, along(1))
-    total = jnp.concatenate([jnp.where(odd, came, total), jnp.where(odd, total, came)], 1)
+
+    terms = jnp.sum(terms.astype(f32), 0)
+    lower, upper = terms[:pair], terms[pair:]
+    came = permuted(jnp.where(low, upper, lower).astype(bf16), mirror)
+    total = (jnp.where(low, lower, upper) + came.astype(f32)).astype(bf16)
+    total = (total.astype(f32) + permuted(total, along(4)).astype(f32)).astype(bf16)
+    total = summed(total, *(permuted(total, along(hop)) for hop in (1, 2, 3)))
     keep_g = jnp.where(first, total[:cols], total[cols:pair])
     got_g = permuted(jnp.where(first, total[cols:pair], total[:cols]), sibling)
     img_proj_grad = jnp.where(first, got_g, keep_g).T
     txt_proj_grad = jnp.where(first, keep_g, got_g).T
 
-    du = du.reshape(N_BLK, N_CORE, sub_rows, embed)
-
-    def grads(core_at):
-        rows_of = du[:, core_at].reshape(rows, embed)
-        return jnp.dot(rows_of, other_proj, preferred_element_type=f32)
-
-    got_r = permuted(grads(1), sibling)
-    keep_r = grads(0)
+    grad = jnp.dot(du, other_proj, preferred_element_type=f32)
+    grad = grad.reshape(N_BLK, N_CORE, sub_rows, width)
+    keep_r = grad[:, 0].reshape(rows, width)
+    got_r = permuted(grad[:, 1].reshape(rows, width), sibling)
     img_grad = jnp.where(first, got_r, keep_r)
     txt_grad = jnp.where(first, keep_r, got_r)
     return (img_grad, txt_grad, img_proj_grad, txt_proj_grad)

time: 235 us -> 228 us (0.970)
  waiting for transfers between devices: 66.6 us -> 59.4 us
  starting transfers between devices: 90.4 us -> 93.9 us
  matrix products: 10.9 us -> 7.43 us
  other arithmetic: 8.71 us -> 11.3 us
  local copies, waits for them, and re-layouts: 11.7 us -> 9.15 us
    ppermute x15 -> x19, starting transfers between devices: 69 us -> 81.8 us  [permuted(): return lax.ppermute(value, BOTH, pairs)]
    all_to_all x4 -> x3, starting transfers between devices: 21.5 us -> 12.1 us  [exchanged(): lax.all_to_all(value, BOTH, 0, 0, axis_index_groups=groups, tiled=True)]
    all_to_all x4 -> x3, waiting for transfers between devices: 14.3 us -> 10.5 us  [exchanged(): lax.all_to_all(value, BOTH, 0, 0, axis_index_groups=groups, tiled=True)]
    ppermute x15 -> x19, waiting for transfers between devices: 52.3 us -> 48.8 us  [permuted(): return lax.ppermute(value, BOTH, pairs)]
    dot_general x2 -> x1, matrix products: 5.69 us -> 2.76 us  [body(): grad = jnp.dot(du, other_proj, preferred_element_type=f32)]
    optimization_barrier x1 -> x0, local copies, waits for them, and re-layouts: 2.6 us -> none  [body(): part, terms = lax.optimization_barrier((part, terms.astype(bf16)))]
  transfers between devices with their start and end apart: 19 -> 22, of which waited for: 10 -> 12; matrix products, arithmetic and copies ran while one was open for 6% -> 5% of each run, Pallas kernels for 2% -> 3%
where the time goes in v10:
time: 228 us; the launch traced here: 227 us
  starting transfers between devices  93.9 us (41%)
  waiting for transfers between devices  59.4 us (26%)
  blocking collectives  34.8 us (15%)
  other arithmetic  11.3 us (5%)
  local copies, waits for them, and re-layouts  9.15 us (4%)
  Pallas kernels  7.81 us (3%)
  matrix products  7.43 us (3%)
  between operations  3.28 us (1%)
    ppermute x19, starting transfers between devices, permuted(): return lax.ppermute(value, BOTH, pairs)  81.8 us
    ppermute x19, waiting for transfers between devices, permuted(): return lax.ppermute(value, BOTH, pairs)  48.8 us
    all_to_all x1, blocking collectives, exchanged(): lax.all_to_all(value, BOTH, 0, 0, axis_index_groups=groups, tiled=True)  34.8 us
    all_to_all x3, starting transfers between devices, exchanged(): lax.all_to_all(value, BOTH, 0, 0, axis_index_groups=groups, tiled=True)  12.1 us
    all_to_all x3, waiting for transfers between devices, exchanged(): lax.all_to_all(value, BOTH, 0, 0, axis_index_groups=groups, tiled=True)  10.5 us
    unnamed x10, local copies, waits for them, and re-layouts  5.4 us
  transfers between devices with their start and end apart: 22, of which 12 were waited for; matrix products, arithmetic and copies ran while one was open for 5% of the time, Pallas kernels for 3%

profile of v10, /device:TPU:1, one launch (start us, length us, event | category | flops | bytes accessed | tf_op | source)
XLA Modules:
  0.0 227.1 jit_solution(12156382164718695824)
XLA Ops:
  2.7 8.8 %collective-permute-start = (bf16[34,1152]{1,0:T(8,128)(2,1)S(1)}, bf16[34,1152]{1,0:T(8,128)(2,1)S(1)}, u32[]{:S(2)}, u32[]{:S(2)}) collective-permute-start(bf16[34,1152]{1,0:T(8,128)(2,1)S(1)} %pad_maximum_fusion.8), channel_id=1, source_target_pairs={{0,1},{1,0},{2,3},{3,2},{4,5},{5,4},{6,7},{7,6},{8,9},{9,8},{10,11... | collective-permute-start | bytes 235016 | tf_op jit(solution)/shard_map/ppermute | solution.py:69
  11.5 5.6 %collective-permute-start.2 = (bf16[34,1152]{1,0:T(8,128)(2,1)S(1)}, bf16[34,1152]{1,0:T(8,128)(2,1)S(1)}, u32[]{:S(2)}, u32[]{:S(2)}) collective-permute-start(bf16[34,1152]{1,0:T(8,128)(2,1)S(1)} %pad_maximum_fusion.8), channel_id=1, source_target_pairs={{0,457},{1,456},{2,459},{3,458},{4,461},{5,460},{6,463},{7,462},{8... | collective-permute-start | bytes 235016 | tf_op jit(solution)/shard_map/ppermute | solution.py:69
  17.2 2.4 %collective-permute-start.3 = (bf16[256,1152]{1,0:T(8,128)(2,1)S(1)}, bf16[256,1152]{1,0:T(8,128)(2,1)S(1)}, u32[]{:S(2)}, u32[]{:S(2)}) collective-permute-start(bf16[256,1152]{1,0:T(8,128)(2,1)S(1)} %pad_maximum_fusion.1), channel_id=1, source_target_pairs={{0,1},{1,0},{2,3},{3,2},{4,5},{5,4},{6,7},{7,6},{8,9},{9,8},{10,11... | collective-permute-start | bytes 1769480 | tf_op jit(solution)/shard_map/ppermute | solution.py:69
  22.6 4.2 %all-to-all-start = ((bf16[4,68,1152]{2,1,0:T(8,128)(2,1)}), bf16[4,68,1152]{2,1,0:T(8,128)(2,1)S(1)}, u32[]{:S(2)}, u32[]{:S(2)}) async-start(bf16[4,68,1152]{2,1,0:T(8,128)(2,1)} %broadcast_in_dim.6), calls=%async_computation | async-start | bytes 1327104 | tf_op jit(solution)/shard_map/all_to_all | solution.py:73
  26.8 6.2 %collective-permute-done.1 = bf16[34,1152]{1,0:T(8,128)(2,1)S(1)} collective-permute-done((bf16[34,1152]{1,0:T(8,128)(2,1)S(1)}, bf16[34,1152]{1,0:T(8,128)(2,1)S(1)}, u32[]{:S(2)}, u32[]{:S(2)}) %collective-permute-start.1) | collective-permute-done | bytes 78368 | tf_op jit(solution)/shard_map/ppermute | solution.py:69
  35.7 3.5 %all-to-all-start.1 = ((bf16[4,68,1152]{2,1,0:T(8,128)(2,1)}), bf16[4,68,1152]{2,1,0:T(8,128)(2,1)S(1)}, u32[]{:S(2)}, u32[]{:S(2)}) async-start(bf16[4,68,1152]{2,1,0:T(8,128)(2,1)} %broadcast_in_dim.7), calls=%async_computation.1 | async-start | bytes 1327104 | tf_op jit(solution)/shard_map/all_to_all | solution.py:73
  40.2 6.6 %all-to-all-done.1 = bf16[4,68,1152]{2,1,0:T(8,128)(2,1)S(1)} async-done(((bf16[4,68,1152]{2,1,0:T(8,128)(2,1)}), bf16[4,68,1152]{2,1,0:T(8,128)(2,1)S(1)}, u32[]{:S(2)}, u32[]{:S(2)}) %all-to-all-start.1) | async-done | bytes 626720 | tf_op jit(solution)/shard_map/all_to_all | solution.py:73
  47.4 34.8 %all_to_all.20 = bf16[4,4,136,1152]{3,2,1,0:T(8,128)(2,1)S(1)} all-to-all(bf16[4,4,136,1152]{3,2,1,0:T(8,128)(2,1)S(1)} %broadcast_in_dim.8), channel_id=1, replica_groups={{0,16,32,48},{2,18,34,50},{4,20,36,52},{6,22,38,54},{1,3,5,7},{17,19,21..., dimensions={0} | all-to-all | bytes 10027008 | tf_op jit(solution)/shard_map/all_to_all | solution.py:73
  82.5 2.2 copy-done
  87.9 6.0 %collective-permute-start.4 = (f32[256,1152]{1,0:T(8,128)}, f32[256,1152]{1,0:T(8,128)}, u32[]{:S(2)}, u32[]{:S(2)}) collective-permute-start(f32[256,1152]{1,0:T(8,128)} %fusion.7), channel_id=1, source_target_pairs={{0,1},{1,0},{2,3},{3,2},{4,5},{5,4},{6,7},{7,6},{8,9},{9,8},{10,11... | collective-permute-start | bytes 3538952 | tf_op jit(solution)/shard_map/ppermute | solution.py:69
  98.0 2.4 %copy-done.1 = bf16[4,4,136,1152]{3,2,1,0:T(8,128)(2,1)S(1)} copy-done((bf16[4,4,136,1152]{3,2,1,0:T(8,128)(2,1)S(1)}, bf16[4,4,136,1152]{3,2,1,0:T(8,128)(2,1)}, u32[]{:S(2)}) %copy-start.1) | copy-done | bytes 5013528
  100.4 4.3 %shard_map.102.others_ref = bf16[1024,1152]{1,0:T(8,128)(2,1)S(1)} custom-call(bf16[16,136,1152]{2,1,0:T(8,128)(2,1)S(1)} %bitcast.32, bf16[1152,1152]{1,0:T(8,128)(2,1)S(1)} %bitcast.35), custom_call_target="tpu_custom_call" | custom-call | flops 2717908992 | bytes 7372800 | tf_op jit(solution)/shard_map/pallas_call | solution.py:110
  104.7 3.5 %shard_map.103 = bf16[256,1152]{1,0:T(8,128)(2,1)S(1)} custom-call(s32[2]{0:T(128)S(1)} %pad_add_fusion.at_ref, f32[3]{0:T(128)S(1)} %pad_maximum_fusion.10.par_ref, f32[256,1152]{1,0:T(8,128)} %collective-permute-done.4.made_ref, bf16[1024,1152]{1,0:T(8,128)(2,1)S(1)} %shard_map.102.others_ref), custom_call_target="tpu_custom_call" | custom-call | flops 1207959552 | bytes 4128768 | tf_op jit(solution)/shard_map/pallas_call | solution.py:164
  108.2 2.5 %convolution_convert_fusion = bf16[1152,1152]{1,0:T(8,128)(2,1)} fusion(bf16[256,1152]{1,0:T(8,128)(2,1)S(1)} %shard_map.103, bf16[256,1152]{1,0:T(8,128)(2,1)S(1)} %bitcast.39), kind=kOutput, calls=%fused_computation | convolution fusion | flops 680804352 | bytes 3833856 | tf_op jit(solution)/shard_map/dot_general | solution.py:94
  111.9 4.5 %all-to-all-start.3 = ((bf16[16,72,1152]{2,1,0:T(8,128)(2,1)}), bf16[16,72,1152]{2,1,0:T(8,128)(2,1)}, u32[]{:S(2)}, u32[]{:S(2)}) async-start(bf16[16,72,1152]{2,1,0:T(8,128)(2,1)} %bitcast.36), calls=%async_computation.3 | async-start | bytes 5308416 | tf_op jit(solution)/shard_map/all_to_all | solution.py:73
  117.5 3.5 %collective-permute-start.5 = (bf16[128,1152]{1,0:T(8,128)(2,1)S(1)}, bf16[128,1152]{1,0:T(8,128)(2,1)S(1)}, u32[]{:S(2)}, u32[]{:S(2)}) collective-permute-start(bf16[128,1152]{1,0:T(8,128)(2,1)S(1)} %dynamic-slice_convert_fusion), channel_id=1, source_target_pairs={{0,64},{1,65},{2,66},{3,67},{4,68},{5,69},{6,70},{7,71},{8,72},{9,... | collective-permute-start | bytes 884744 | tf_op jit(solution)/shard_map/ppermute | solution.py:69
  121.1 6.9 %collective-permute-done.5 = bf16[128,1152]{1,0:T(8,128)(2,1)S(1)} collective-permute-done((bf16[128,1152]{1,0:T(8,128)(2,1)S(1)}, bf16[128,1152]{1,0:T(8,128)(2,1)S(1)}, u32[]{:S(2)}, u32[]{:S(2)}) %collective-permute-start.5) | collective-permute-done | bytes 294944 | tf_op jit(solution)/shard_map/ppermute | solution.py:69
  129.1 4.9 %collective-permute-start.6 = (bf16[64,1152]{1,0:T(8,128)(2,1)S(1)}, bf16[64,1152]{1,0:T(8,128)(2,1)}, u32[]{:S(2)}, u32[]{:S(2)}) collective-permute-start(bf16[64,1152]{1,0:T(8,128)(2,1)S(1)} %dynamic-slice_convert_fusion.1), channel_id=1, source_target_pairs={{0,128},{1,129},{2,130},{3,131},{4,132},{5,133},{6,134},{7,135},{8... | collective-permute-start | bytes 442376 | tf_op jit(solution)/shard_map/ppermute | solution.py:69
  134.0 6.5 %collective-permute-done.6 = bf16[64,1152]{1,0:T(8,128)(2,1)} collective-permute-done((bf16[64,1152]{1,0:T(8,128)(2,1)S(1)}, bf16[64,1152]{1,0:T(8,128)(2,1)}, u32[]{:S(2)}, u32[]{:S(2)}) %collective-permute-start.6) | collective-permute-done | bytes 147488 | tf_op jit(solution)/shard_map/ppermute | solution.py:69
  141.5 7.8 %collective-permute-start.7 = (bf16[32,1152]{1,0:T(8,128)(2,1)S(1)}, bf16[32,1152]{1,0:T(8,128)(2,1)S(1)}, u32[]{:S(2)}, u32[]{:S(2)}) collective-permute-start(bf16[32,1152]{1,0:T(8,128)(2,1)S(1)} %dynamic-slice_convert_fusion.2), channel_id=1, source_target_pairs={{0,256},{1,257},{2,258},{3,259},{4,260},{5,261},{6,262},{7,263},{8... | collective-permute-start | bytes 221192 | tf_op jit(solution)/shard_map/ppermute | solution.py:69
  149.4 5.4 %collective-permute-done.7 = bf16[32,1152]{1,0:T(8,128)(2,1)S(1)} collective-permute-done((bf16[32,1152]{1,0:T(8,128)(2,1)S(1)}, bf16[32,1152]{1,0:T(8,128)(2,1)S(1)}, u32[]{:S(2)}, u32[]{:S(2)}) %collective-permute-start.7) | collective-permute-done | bytes 73760 | tf_op jit(solution)/shard_map/ppermute | solution.py:69
  154.8 2.2 all-to-all-done.3
  159.2 7.9 %collective-permute-start.9 = (bf16[32,1152]{1,0:T(8,128)(2,1)S(1)}, bf16[32,1152]{1,0:T(8,128)(2,1)S(1)}, u32[]{:S(2)}, u32[]{:S(2)}) collective-permute-start(bf16[32,1152]{1,0:T(8,128)(2,1)S(1)} %add_convert_fusion.2), channel_id=1, source_target_pairs={{0,256},{1,257},{2,258},{3,259},{4,260},{5,261},{6,262},{7,263},{8... | collective-permute-start | bytes 221192 | tf_op jit(solution)/shard_map/ppermute | solution.py:69
  167.1 7.2 %collective-permute-start.13 = (bf16[36,1152]{1,0:T(8,128)(2,1)S(1)}, bf16[36,1152]{1,0:T(8,128)(2,1)S(1)}, u32[]{:S(2)}, u32[]{:S(2)}) collective-permute-start(bf16[36,1152]{1,0:T(8,128)(2,1)S(1)} %select_convert_fusion), channel_id=1, source_target_pairs={{0,456},{1,457},{2,458},{3,459},{4,460},{5,461},{6,462},{7,463},{8... | collective-permute-start | bytes 248840 | tf_op jit(solution)/shard_map/ppermute | solution.py:69
  174.4 7.3 %collective-permute-done.13 = bf16[36,1152]{1,0:T(8,128)(2,1)S(1)} collective-permute-done((bf16[36,1152]{1,0:T(8,128)(2,1)S(1)}, bf16[36,1152]{1,0:T(8,128)(2,1)S(1)}, u32[]{:S(2)}, u32[]{:S(2)}) %collective-permute-start.13) | collective-permute-done | bytes 82976 | tf_op jit(solution)/shard_map/ppermute | solution.py:69
  181.7 3.6 %collective-permute-start.14 = (bf16[36,1152]{1,0:T(8,128)(2,1)S(1)}, bf16[36,1152]{1,0:T(8,128)(2,1)S(1)}, u32[]{:S(2)}, u32[]{:S(2)}) collective-permute-start(bf16[36,1152]{1,0:T(8,128)(2,1)S(1)} %add_convert_fusion.1), channel_id=1, source_target_pairs={{0,256},{1,257},{2,258},{3,259},{4,260},{5,261},{6,262},{7,263},{8... | collective-permute-start | bytes 248840 | tf_op jit(solution)/shard_map/ppermute | solution.py:69
  185.3 2.9 %collective-permute-start.10 = (bf16[64,1152]{1,0:T(8,128)(2,1)S(1)}, bf16[64,1152]{1,0:T(8,128)(2,1)S(1)}, u32[]{:S(2)}, u32[]{:S(2)}) collective-permute-start(bf16[64,1152]{1,0:T(8,128)(2,1)S(1)} %pad_maximum_fusion.7), channel_id=1, source_target_pairs={{0,128},{1,129},{2,130},{3,131},{4,132},{5,133},{6,134},{7,135},{8... | collective-permute-start | bytes 442376 | tf_op jit(solution)/shard_map/ppermute | solution.py:69
  188.3 8.0 %collective-permute-done.14 = bf16[36,1152]{1,0:T(8,128)(2,1)S(1)} collective-permute-done((bf16[36,1152]{1,0:T(8,128)(2,1)S(1)}, bf16[36,1152]{1,0:T(8,128)(2,1)S(1)}, u32[]{:S(2)}, u32[]{:S(2)}) %collective-permute-start.14) | collective-permute-done | bytes 82976 | tf_op jit(solution)/shard_map/ppermute | solution.py:69
  200.2 5.4 %collective-permute-start.17 = (bf16[36,1152]{1,0:T(8,128)(2,1)S(1)}, bf16[36,1152]{1,0:T(8,128)(2,1)S(1)}, u32[]{:S(2)}, u32[]{:S(2)}) collective-permute-start(bf16[36,1152]{1,0:T(8,128)(2,1)S(1)} %add_convert_fusion), channel_id=1, source_target_pairs={{0,192},{1,193},{2,194},{3,195},{4,196},{5,197},{6,198},{7,199},{8... | collective-permute-start | bytes 248840 | tf_op jit(solution)/shard_map/ppermute | solution.py:69
  208.1 6.9 %collective-permute-done.11 = bf16[128,1152]{1,0:T(8,128)(2,1)S(1)} collective-permute-done((bf16[128,1152]{1,0:T(8,128)(2,1)S(1)}, bf16[128,1152]{1,0:T(8,128)(2,1)S(1)}, u32[]{:S(2)}, u32[]{:S(2)}) %collective-permute-start.11) | collective-permute-done | bytes 294944 | tf_op jit(solution)/shard_map/ppermute | solution.py:69
  215.1 2.8 %fusion = f32[256,1152]{1,0:T(8,128)S(1)} fusion(bf16[1152,1152]{1,0:T(8,128)(2,1)} %collective-permute-done.8, bf16[128,1152]{1,0:T(8,128)(2,1)S(1)} %get-tuple-element.29, bf16[128,1152]{1,0:T(8,128)(2,1)S(1)} %get-tuple-element.28), kind=kOutput, calls=%fused_computation.7 | convolution fusion | flops 680656896 | bytes 4423680 | tf_op jit(solution)/shard_map/dot_general | solution.py:292
  217.9 4.2 %collective-permute-start.12 = (f32[128,1152]{1,0:T(8,128)S(1)}, f32[128,1152]{1,0:T(8,128)S(1)}, u32[]{:S(2)}, u32[]{:S(2)}) collective-permute-start(f32[128,1152]{1,0:T(8,128)S(1)} %bitcast.44), channel_id=1, source_target_pairs={{0,1},{1,0},{2,3},{3,2},{4,5},{5,4},{6,7},{7,6},{8,9},{9,8},{10,11... | collective-permute-start | bytes 1769480 | tf_op jit(solution)/shard_map/ppermute | solution.py:69
  (78 shorter events, 32.9 us)
Async XLA Ops:
  0.6 19.0 %copy-start.3 = (bf16[1152,18]{0,1:T(8,128)(2,1)S(1)}, bf16[1152,18]{0,1:T(8,128)(2,1)}, u32[]{:S(2)}) copy-start(bf16[1152,18]{0,1:T(8,128)(2,1)} %param.10) | copy-start | bytes 124420
  0.6 19.0 %copy-start.4 = (bf16[1152,18]{0,1:T(8,128)(2,1)S(1)}, bf16[1152,18]{0,1:T(8,128)(2,1)}, u32[]{:S(2)}) copy-start(bf16[1152,18]{0,1:T(8,128)(2,1)} %param.9) | copy-start | bytes 124420
  2.7 16.9 %collective-permute-start = (bf16[34,1152]{1,0:T(8,128)(2,1)S(1)}, bf16[34,1152]{1,0:T(8,128)(2,1)S(1)}, u32[]{:S(2)}, u32[]{:S(2)}) collective-permute-start(bf16[34,1152]{1,0:T(8,128)(2,1)S(1)} %pad_maximum_fusion.8), channel_id=1, source_target_pairs={{0,1},{1,0},{2,3},{3,2},{4,5},{5,4},{6,7},{7,6},{8,9},{9,8},{10,11... | collective-permute-start | bytes 235016 | tf_op jit(solution)/shard_map/ppermute | solution.py:69
  11.5 15.3 %collective-permute-start.2 = (bf16[34,1152]{1,0:T(8,128)(2,1)S(1)}, bf16[34,1152]{1,0:T(8,128)(2,1)S(1)}, u32[]{:S(2)}, u32[]{:S(2)}) collective-permute-start(bf16[34,1152]{1,0:T(8,128)(2,1)S(1)} %pad_maximum_fusion.8), channel_id=1, source_target_pairs={{0,457},{1,456},{2,459},{3,458},{4,461},{5,460},{6,463},{7,462},{8... | collective-permute-start | bytes 235016 | tf_op jit(solution)/shard_map/ppermute | solution.py:69
  17.2 22.0 %collective-permute-start.3 = (bf16[256,1152]{1,0:T(8,128)(2,1)S(1)}, bf16[256,1152]{1,0:T(8,128)(2,1)S(1)}, u32[]{:S(2)}, u32[]{:S(2)}) collective-permute-start(bf16[256,1152]{1,0:T(8,128)(2,1)S(1)} %pad_maximum_fusion.1), channel_id=1, source_target_pairs={{0,1},{1,0},{2,3},{3,2},{4,5},{5,4},{6,7},{7,6},{8,9},{9,8},{10,11... | collective-permute-start | bytes 1769480 | tf_op jit(solution)/shard_map/ppermute | solution.py:69
  19.7 13.3 %collective-permute-start.1 = (bf16[34,1152]{1,0:T(8,128)(2,1)S(1)}, bf16[34,1152]{1,0:T(8,128)(2,1)S(1)}, u32[]{:S(2)}, u32[]{:S(2)}) collective-permute-start(bf16[34,1152]{1,0:T(8,128)(2,1)S(1)} %pad_maximum_fusion.9), channel_id=1, source_target_pairs={{0,456},{1,457},{2,458},{3,459},{4,460},{5,461},{6,462},{7,463},{8... | collective-permute-start | bytes 235016 | tf_op jit(solution)/shard_map/ppermute | solution.py:69
  22.6 12.2 %all-to-all-start = ((bf16[4,68,1152]{2,1,0:T(8,128)(2,1)}), bf16[4,68,1152]{2,1,0:T(8,128)(2,1)S(1)}, u32[]{:S(2)}, u32[]{:S(2)}) async-start(bf16[4,68,1152]{2,1,0:T(8,128)(2,1)} %broadcast_in_dim.6), calls=%async_computation | async-start | bytes 1327104 | tf_op jit(solution)/shard_map/all_to_all | solution.py:73
  35.7 11.1 %all-to-all-start.1 = ((bf16[4,68,1152]{2,1,0:T(8,128)(2,1)}), bf16[4,68,1152]{2,1,0:T(8,128)(2,1)S(1)}, u32[]{:S(2)}, u32[]{:S(2)}) async-start(bf16[4,68,1152]{2,1,0:T(8,128)(2,1)} %broadcast_in_dim.7), calls=%async_computation.1 | async-start | bytes 1327104 | tf_op jit(solution)/shard_map/all_to_all | solution.py:73
  82.5 2.2 copy-start
  84.7 1.1 copy-start.2
  87.9 16.8 %collective-permute-start.4 = (f32[256,1152]{1,0:T(8,128)}, f32[256,1152]{1,0:T(8,128)}, u32[]{:S(2)}, u32[]{:S(2)}) collective-permute-start(f32[256,1152]{1,0:T(8,128)} %fusion.7), channel_id=1, source_target_pairs={{0,1},{1,0},{2,3},{3,2},{4,5},{5,4},{6,7},{7,6},{8,9},{9,8},{10,11... | collective-permute-start | bytes 3538952 | tf_op jit(solution)/shard_map/ppermute | solution.py:69
  96.0 58.8 %collective-permute-start.8 = (bf16[1152,1152]{1,0:T(8,128)(2,1)S(1)}, bf16[1152,1152]{1,0:T(8,128)(2,1)}, u32[]{:S(2)}, u32[]{:S(2)}) collective-permute-start(bf16[1152,1152]{1,0:T(8,128)(2,1)S(1)} %bitcast.34), channel_id=1, source_target_pairs={{0,1},{1,0},{2,3},{3,2},{4,5},{5,4},{6,7},{7,6},{8,9},{9,8},{10,11... | collective-permute-start | bytes 7962632 | tf_op jit(solution)/shard_map/ppermute | solution.py:69
  98.0 2.4 %copy-start.1 = (bf16[4,4,136,1152]{3,2,1,0:T(8,128)(2,1)S(1)}, bf16[4,4,136,1152]{3,2,1,0:T(8,128)(2,1)}, u32[]{:S(2)}) copy-start(bf16[4,4,136,1152]{3,2,1,0:T(8,128)(2,1)} %copy-done) | copy-start | bytes 15040516
  111.9 45.1 %all-to-all-start.3 = ((bf16[16,72,1152]{2,1,0:T(8,128)(2,1)}), bf16[16,72,1152]{2,1,0:T(8,128)(2,1)}, u32[]{:S(2)}, u32[]{:S(2)}) async-start(bf16[16,72,1152]{2,1,0:T(8,128)(2,1)} %bitcast.36), calls=%async_computation.3 | async-start | bytes 5308416 | tf_op jit(solution)/shard_map/all_to_all | solution.py:73
  117.5 10.5 %collective-permute-start.5 = (bf16[128,1152]{1,0:T(8,128)(2,1)S(1)}, bf16[128,1152]{1,0:T(8,128)(2,1)S(1)}, u32[]{:S(2)}, u32[]{:S(2)}) collective-permute-start(bf16[128,1152]{1,0:T(8,128)(2,1)S(1)} %dynamic-slice_convert_fusion), channel_id=1, source_target_pairs={{0,64},{1,65},{2,66},{3,67},{4,68},{5,69},{6,70},{7,71},{8,72},{9,... | collective-permute-start | bytes 884744 | tf_op jit(solution)/shard_map/ppermute | solution.py:69
  129.1 11.4 %collective-permute-start.6 = (bf16[64,1152]{1,0:T(8,128)(2,1)S(1)}, bf16[64,1152]{1,0:T(8,128)(2,1)}, u32[]{:S(2)}, u32[]{:S(2)}) collective-permute-start(bf16[64,1152]{1,0:T(8,128)(2,1)S(1)} %dynamic-slice_convert_fusion.1), channel_id=1, source_target_pairs={{0,128},{1,129},{2,130},{3,131},{4,132},{5,133},{6,134},{7,135},{8... | collective-permute-start | bytes 442376 | tf_op jit(solution)/shard_map/ppermute | solution.py:69
  141.5 13.3 %collective-permute-start.7 = (bf16[32,1152]{1,0:T(8,128)(2,1)S(1)}, bf16[32,1152]{1,0:T(8,128)(2,1)S(1)}, u32[]{:S(2)}, u32[]{:S(2)}) collective-permute-start(bf16[32,1152]{1,0:T(8,128)(2,1)S(1)} %dynamic-slice_convert_fusion.2), channel_id=1, source_target_pairs={{0,256},{1,257},{2,258},{3,259},{4,260},{5,261},{6,262},{7,263},{8... | collective-permute-start | bytes 221192 | tf_op jit(solution)/shard_map/ppermute | solution.py:69
  159.2 15.1 %collective-permute-start.9 = (bf16[32,1152]{1,0:T(8,128)(2,1)S(1)}, bf16[32,1152]{1,0:T(8,128)(2,1)S(1)}, u32[]{:S(2)}, u32[]{:S(2)}) collective-permute-start(bf16[32,1152]{1,0:T(8,128)(2,1)S(1)} %add_convert_fusion.2), channel_id=1, source_target_pairs={{0,256},{1,257},{2,258},{3,259},{4,260},{5,261},{6,262},{7,263},{8... | collective-permute-start | bytes 221192 | tf_op jit(solution)/shard_map/ppermute | solution.py:69
  167.1 14.5 %collective-permute-start.13 = (bf16[36,1152]{1,0:T(8,128)(2,1)S(1)}, bf16[36,1152]{1,0:T(8,128)(2,1)S(1)}, u32[]{:S(2)}, u32[]{:S(2)}) collective-permute-start(bf16[36,1152]{1,0:T(8,128)(2,1)S(1)} %select_convert_fusion), channel_id=1, source_target_pairs={{0,456},{1,457},{2,458},{3,459},{4,460},{5,461},{6,462},{7,463},{8... | collective-permute-start | bytes 248840 | tf_op jit(solution)/shard_map/ppermute | solution.py:69
  181.7 14.6 %collective-permute-start.14 = (bf16[36,1152]{1,0:T(8,128)(2,1)S(1)}, bf16[36,1152]{1,0:T(8,128)(2,1)S(1)}, u32[]{:S(2)}, u32[]{:S(2)}) collective-permute-start(bf16[36,1152]{1,0:T(8,128)(2,1)S(1)} %add_convert_fusion.1), channel_id=1, source_target_pairs={{0,256},{1,257},{2,258},{3,259},{4,260},{5,261},{6,262},{7,263},{8... | collective-permute-start | bytes 248840 | tf_op jit(solution)/shard_map/ppermute | solution.py:69
  185.3 20.3 %collective-permute-start.10 = (bf16[64,1152]{1,0:T(8,128)(2,1)S(1)}, bf16[64,1152]{1,0:T(8,128)(2,1)S(1)}, u32[]{:S(2)}, u32[]{:S(2)}) collective-permute-start(bf16[64,1152]{1,0:T(8,128)(2,1)S(1)} %pad_maximum_fusion.7), channel_id=1, source_target_pairs={{0,128},{1,129},{2,130},{3,131},{4,132},{5,133},{6,134},{7,135},{8... | collective-permute-start | bytes 442376 | tf_op jit(solution)/shard_map/ppermute | solution.py:69
  196.3 11.3 %collective-permute-start.15 = (bf16[36,1152]{1,0:T(8,128)(2,1)S(1)}, bf16[36,1152]{1,0:T(8,128)(2,1)S(1)}, u32[]{:S(2)}, u32[]{:S(2)}) collective-permute-start(bf16[36,1152]{1,0:T(8,128)(2,1)S(1)} %add_convert_fusion), channel_id=1, source_target_pairs={{0,64},{1,65},{2,66},{3,67},{4,68},{5,69},{6,70},{7,71},{8,72},{9,... | collective-permute-start | bytes 248840 | tf_op jit(solution)/shard_map/ppermute | solution.py:69
  198.3 9.4 %collective-permute-start.16 = (bf16[36,1152]{1,0:T(8,128)(2,1)S(1)}, bf16[36,1152]{1,0:T(8,128)(2,1)S(1)}, u32[]{:S(2)}, u32[]{:S(2)}) collective-permute-start(bf16[36,1152]{1,0:T(8,128)(2,1)S(1)} %add_convert_fusion), channel_id=1, source_target_pairs={{0,128},{1,129},{2,130},{3,131},{4,132},{5,133},{6,134},{7,135},{8... | collective-permute-start | bytes 248840 | tf_op jit(solution)/shard_map/ppermute | solution.py:69
  200.2 7.8 %collective-permute-start.17 = (bf16[36,1152]{1,0:T(8,128)(2,1)S(1)}, bf16[36,1152]{1,0:T(8,128)(2,1)S(1)}, u32[]{:S(2)}, u32[]{:S(2)}) collective-permute-start(bf16[36,1152]{1,0:T(8,128)(2,1)S(1)} %add_convert_fusion), channel_id=1, source_target_pairs={{0,192},{1,193},{2,194},{3,195},{4,196},{5,197},{6,198},{7,199},{8... | collective-permute-start | bytes 248840 | tf_op jit(solution)/shard_map/ppermute | solution.py:69
  205.7 9.2 %collective-permute-start.11 = (bf16[128,1152]{1,0:T(8,128)(2,1)S(1)}, bf16[128,1152]{1,0:T(8,128)(2,1)S(1)}, u32[]{:S(2)}, u32[]{:S(2)}) collective-permute-start(bf16[128,1152]{1,0:T(8,128)(2,1)S(1)} %pad_maximum_fusion.4), channel_id=1, source_target_pairs={{0,64},{1,65},{2,66},{3,67},{4,68},{5,69},{6,70},{7,71},{8,72},{9,... | collective-permute-start | bytes 884744 | tf_op jit(solution)/shard_map/ppermute | solution.py:69
  217.9 8.1 %collective-permute-start.12 = (f32[128,1152]{1,0:T(8,128)S(1)}, f32[128,1152]{1,0:T(8,128)S(1)}, u32[]{:S(2)}, u32[]{:S(2)}) collective-permute-start(f32[128,1152]{1,0:T(8,128)S(1)} %bitcast.44), channel_id=1, source_target_pairs={{0,1},{1,0},{2,3},{3,2},{4,5},{5,4},{6,7},{7,6},{8,9},{9,8},{10,11... | collective-permute-start | bytes 1769480 | tf_op jit(solution)/shard_map/ppermute | solution.py:69
  222.1 3.2 %collective-permute-start.18 = (f32[18,1152]{1,0:T(8,128)S(1)}, f32[18,1152]{1,0:T(8,128)S(1)}, u32[]{:S(2)}, u32[]{:S(2)}) collective-permute-start(f32[18,1152]{1,0:T(8,128)S(1)} %slice_select_fusion.1), channel_id=1, source_target_pairs={{0,1},{1,0},{2,3},{3,2},{4,5},{5,4},{6,7},{7,6},{8,9},{9,8},{10,11... | collective-permute-start | bytes 248840 | tf_op jit(solution)/shard_map/ppermute | solution.py:69

commit v11 on v10

--- a/solution.py
+++ b/solution.py
@@ -261,22 +261,30 @@
     part = partial_grads(at, jnp.stack([scale, shift_by, weight]), made, others, picked)
 
     terms = contract_first(part, feat).astype(bf16)
-    part, terms = lax.optimization_barrier((part, terms))
+    part, terms, late_proj = lax.optimization_barrier((part, terms, proj))
     terms = exchanged(terms.reshape(N_Y * N_X, embed // (N_Y * N_X), width), PLANE)
-    held = part.astype(f32)
-    for bit, hop in ((4, 1), (2, 2), (1, 4)):
-        count = held.shape[0] // 2
-        high = (sub & bit) // bit
-        send = lax.dynamic_slice_in_dim(held, (1 - high) * count, count, 0).astype(bf16)
-        stay = lax.dynamic_slice_in_dim(held, high * count, count, 0)
-        held = stay + permuted(send, along(hop)).astype(f32)
+    quarter = own // 4
+    at_quarter = sub // 2
+
+    def quarter_of(index):
+        return lax.dynamic_slice_in_dim(part, index * quarter, quarter, 0)
+
+    held = summed(
+        quarter_of(at_quarter),
+        permuted(quarter_of(at_quarter ^ 2), along(1)),
+        permuted(quarter_of(at_quarter ^ 1), along(2)),
+        permuted(quarter_of(at_quarter ^ 3), along(3)),
+    ).astype(bf16)
+    held = held.astype(f32) + permuted(held, along(4)).astype(f32)
     du, terms, other_proj = lax.optimization_barrier(
-        (held.astype(bf16), terms, permuted(proj, sibling))
-    )
-    for bit, hop in ((1, 4), (2, 2), (4, 1)):
-        came = permuted(du, along(hop))
-        high = (sub & bit) > 0
-        du = jnp.concatenate([jnp.where(high, came, du), jnp.where(high, du, came)], 0)
+        (held.astype(bf16), terms, permuted(late_proj, sibling))
+    )
+    pieces = [du] + [permuted(du, along(hop)) for hop in (2, 1, 3)]
+    swap = (at_quarter & 1) == 1
+    pieces = [jnp.where(swap, pieces[index ^ 1], pieces[index]) for index in range(4)]
+    swap = (at_quarter & 2) == 2
+    pieces = [jnp.where(swap, pieces[index ^ 2], pieces[index]) for index in range(4)]
+    du = jnp.concatenate(pieces, 0)
 
     terms = jnp.sum(terms.astype(f32), 0)
     lower, upper = terms[:pair], terms[pair:]

time: 228 us -> 214 us (0.939)
  waiting for transfers between devices: 59.4 us -> 38.6 us
  starting transfers between devices: 93.9 us -> 104 us
  other arithmetic: 11.3 us -> 8.92 us
    ppermute x19 -> x20, waiting for transfers between devices: 48.8 us -> 30.1 us  [permuted(): return lax.ppermute(value, BOTH, pairs)]
    ppermute x19 -> x20, starting transfers between devices: 81.8 us -> 92.1 us  [permuted(): return lax.ppermute(value, BOTH, pairs)]
  transfers between devices with their start and end apart: 22 -> 23, of which waited for: 12 -> 7; matrix products, arithmetic and copies ran while one was open for 5% -> 4% of each run, Pallas kernels for 3% -> 2%
where the time goes in v11:
time: 214 us; the launch traced here: 213 us
  starting transfers between devices  104 us (49%)
  waiting for transfers between devices  38.6 us (18%)
  blocking collectives  34.8 us (16%)
  other arithmetic  8.92 us (4%)
  local copies, waits for them, and re-layouts  8.09 us (4%)
  Pallas kernels  7.88 us (4%)
  matrix products  7.35 us (3%)
  between operations  3.27 us (2%)
    ppermute x20, starting transfers between devices, permuted(): return lax.ppermute(value, BOTH, pairs)  92.1 us
    all_to_all x1, blocking collectives, exchanged(): lax.all_to_all(value, BOTH, 0, 0, axis_index_groups=groups, tiled=True)  34.8 us
    ppermute x20, waiting for transfers between devices, permuted(): return lax.ppermute(value, BOTH, pairs)  30.1 us
    all_to_all x3, starting transfers between devices, exchanged(): lax.all_to_all(value, BOTH, 0, 0, axis_index_groups=groups, tiled=True)  12.1 us
    all_to_all x3, waiting for transfers between devices, exchanged(): lax.all_to_all(value, BOTH, 0, 0, axis_index_groups=groups, tiled=True)  8.51 us
    unnamed x10, local copies, waits for them, and re-layouts  4.72 us
  transfers between devices with their start and end apart: 23, of which 7 were waited for; matrix products, arithmetic and copies ran while one was open for 4% of the time, Pallas kernels for 2%

profile of v11, /device:TPU:1, one launch (start us, length us, event | category | flops | bytes accessed | tf_op | source)
XLA Modules:
  0.0 213.2 jit_solution(12466428138173412676)
XLA Ops:
  2.7 8.8 %collective-permute-start = (bf16[34,1152]{1,0:T(8,128)(2,1)S(1)}, bf16[34,1152]{1,0:T(8,128)(2,1)S(1)}, u32[]{:S(2)}, u32[]{:S(2)}) collective-permute-start(bf16[34,1152]{1,0:T(8,128)(2,1)S(1)} %pad_maximum_fusion.6), channel_id=1, source_target_pairs={{0,1},{1,0},{2,3},{3,2},{4,5},{5,4},{6,7},{7,6},{8,9},{9,8},{10,11... | collective-permute-start | bytes 235016 | tf_op jit(solution)/shard_map/ppermute | solution.py:69
  11.5 5.6 %collective-permute-start.2 = (bf16[34,1152]{1,0:T(8,128)(2,1)S(1)}, bf16[34,1152]{1,0:T(8,128)(2,1)S(1)}, u32[]{:S(2)}, u32[]{:S(2)}) collective-permute-start(bf16[34,1152]{1,0:T(8,128)(2,1)S(1)} %pad_maximum_fusion.6), channel_id=1, source_target_pairs={{0,457},{1,456},{2,459},{3,458},{4,461},{5,460},{6,463},{7,462},{8... | collective-permute-start | bytes 235016 | tf_op jit(solution)/shard_map/ppermute | solution.py:69
  17.2 2.4 %collective-permute-start.3 = (bf16[256,1152]{1,0:T(8,128)(2,1)S(1)}, bf16[256,1152]{1,0:T(8,128)(2,1)S(1)}, u32[]{:S(2)}, u32[]{:S(2)}) collective-permute-start(bf16[256,1152]{1,0:T(8,128)(2,1)S(1)} %pad_maximum_fusion.1), channel_id=1, source_target_pairs={{0,1},{1,0},{2,3},{3,2},{4,5},{5,4},{6,7},{7,6},{8,9},{9,8},{10,11... | collective-permute-start | bytes 1769480 | tf_op jit(solution)/shard_map/ppermute | solution.py:69
  22.6 4.2 %all-to-all-start = ((bf16[4,68,1152]{2,1,0:T(8,128)(2,1)}), bf16[4,68,1152]{2,1,0:T(8,128)(2,1)S(1)}, u32[]{:S(2)}, u32[]{:S(2)}) async-start(bf16[4,68,1152]{2,1,0:T(8,128)(2,1)} %broadcast_in_dim.6), calls=%async_computation | async-start | bytes 1327104 | tf_op jit(solution)/shard_map/all_to_all | solution.py:73
  26.8 6.2 %collective-permute-done.1 = bf16[34,1152]{1,0:T(8,128)(2,1)S(1)} collective-permute-done((bf16[34,1152]{1,0:T(8,128)(2,1)S(1)}, bf16[34,1152]{1,0:T(8,128)(2,1)S(1)}, u32[]{:S(2)}, u32[]{:S(2)}) %collective-permute-start.1) | collective-permute-done | bytes 78368 | tf_op jit(solution)/shard_map/ppermute | solution.py:69
  35.7 3.5 %all-to-all-start.1 = ((bf16[4,68,1152]{2,1,0:T(8,128)(2,1)}), bf16[4,68,1152]{2,1,0:T(8,128)(2,1)S(1)}, u32[]{:S(2)}, u32[]{:S(2)}) async-start(bf16[4,68,1152]{2,1,0:T(8,128)(2,1)} %broadcast_in_dim.7), calls=%async_computation.1 | async-start | bytes 1327104 | tf_op jit(solution)/shard_map/all_to_all | solution.py:73
  40.2 6.6 %all-to-all-done.1 = bf16[4,68,1152]{2,1,0:T(8,128)(2,1)S(1)} async-done(((bf16[4,68,1152]{2,1,0:T(8,128)(2,1)}), bf16[4,68,1152]{2,1,0:T(8,128)(2,1)S(1)}, u32[]{:S(2)}, u32[]{:S(2)}) %all-to-all-start.1) | async-done | bytes 626720 | tf_op jit(solution)/shard_map/all_to_all | solution.py:73
  47.4 34.8 %all_to_all.20 = bf16[4,4,136,1152]{3,2,1,0:T(8,128)(2,1)S(1)} all-to-all(bf16[4,4,136,1152]{3,2,1,0:T(8,128)(2,1)S(1)} %broadcast_in_dim.8), channel_id=1, replica_groups={{0,16,32,48},{2,18,34,50},{4,20,36,52},{6,22,38,54},{1,3,5,7},{17,19,21..., dimensions={0} | all-to-all | bytes 10027008 | tf_op jit(solution)/shard_map/all_to_all | solution.py:73
  82.5 2.3 %copy-done = bf16[4,4,136,1152]{3,2,1,0:T(8,128)(2,1)} copy-done((bf16[4,4,136,1152]{3,2,1,0:T(8,128)(2,1)}, bf16[4,4,136,1152]{3,2,1,0:T(8,128)(2,1)S(1)}, u32[]{:S(2)}) %copy-start) | copy-done | bytes 5013528
  85.0 2.1 fusion.11
  87.1 6.0 %collective-permute-start.4 = (f32[256,1152]{1,0:T(8,128)}, f32[256,1152]{1,0:T(8,128)}, u32[]{:S(2)}, u32[]{:S(2)}) collective-permute-start(f32[256,1152]{1,0:T(8,128)} %fusion.11), channel_id=1, source_target_pairs={{0,1},{1,0},{2,3},{3,2},{4,5},{5,4},{6,7},{7,6},{8,9},{9,8},{10,11... | collective-permute-start | bytes 3538952 | tf_op jit(solution)/shard_map/ppermute | solution.py:69
  95.3 2.4 %copy-done.1 = bf16[4,4,136,1152]{3,2,1,0:T(8,128)(2,1)S(1)} copy-done((bf16[4,4,136,1152]{3,2,1,0:T(8,128)(2,1)S(1)}, bf16[4,4,136,1152]{3,2,1,0:T(8,128)(2,1)}, u32[]{:S(2)}) %copy-start.1) | copy-done | bytes 5013528
  97.7 4.3 %shard_map.102.others_ref = bf16[1024,1152]{1,0:T(8,128)(2,1)S(1)} custom-call(bf16[16,136,1152]{2,1,0:T(8,128)(2,1)S(1)} %bitcast.32, bf16[1152,1152]{1,0:T(8,128)(2,1)S(1)} %bitcast.34), custom_call_target="tpu_custom_call" | custom-call | flops 2717908992 | bytes 7372800 | tf_op jit(solution)/shard_map/pallas_call | solution.py:110
  102.0 3.6 %shard_map.103 = bf16[256,1152]{1,0:T(8,128)(2,1)S(1)} custom-call(s32[2]{0:T(128)S(1)} %pad_add_fusion.at_ref, f32[3]{0:T(128)S(1)} %pad_maximum_fusion.8.par_ref, f32[256,1152]{1,0:T(8,128)} %collective-permute-done.4.made_ref, bf16[1024,1152]{1,0:T(8,128)(2,1)S(1)} %shard_map.102.others_ref), custom_call_target="tpu_custom_call" | custom-call | flops 1207959552 | bytes 4128768 | tf_op jit(solution)/shard_map/pallas_call | solution.py:164
  105.6 2.5 %convolution_convert_fusion = bf16[1152,1152]{1,0:T(8,128)(2,1)} fusion(bf16[256,1152]{1,0:T(8,128)(2,1)S(1)} %shard_map.103, bf16[256,1152]{1,0:T(8,128)(2,1)S(1)} %bitcast.39), kind=kOutput, calls=%fused_computation | convolution fusion | flops 680804352 | bytes 3833856 | tf_op jit(solution)/shard_map/dot_general | solution.py:94
  110.0 4.5 %all-to-all-start.3 = ((bf16[16,72,1152]{2,1,0:T(8,128)(2,1)}), bf16[16,72,1152]{2,1,0:T(8,128)(2,1)}, u32[]{:S(2)}, u32[]{:S(2)}) async-start(bf16[16,72,1152]{2,1,0:T(8,128)(2,1)} %bitcast.36), calls=%async_computation.3 | async-start | bytes 5308416 | tf_op jit(solution)/shard_map/all_to_all | solution.py:73
  115.3 3.5 %collective-permute-start.5 = (bf16[64,1152]{1,0:T(8,128)(2,1)}, bf16[64,1152]{1,0:T(8,128)(2,1)S(1)}, u32[]{:S(2)}, u32[]{:S(2)}) collective-permute-start(bf16[64,1152]{1,0:T(8,128)(2,1)} %get-tuple-element.34), channel_id=1, source_target_pairs={{0,64},{1,65},{2,66},{3,67},{4,68},{5,69},{6,70},{7,71},{8,72},{9,... | collective-permute-start | bytes 442376 | tf_op jit(solution)/shard_map/ppermute | solution.py:69
  118.9 4.9 %collective-permute-start.6 = (bf16[64,1152]{1,0:T(8,128)(2,1)}, bf16[64,1152]{1,0:T(8,128)(2,1)S(1)}, u32[]{:S(2)}, u32[]{:S(2)}) collective-permute-start(bf16[64,1152]{1,0:T(8,128)(2,1)} %get-tuple-element.36), channel_id=1, source_target_pairs={{0,128},{1,129},{2,130},{3,131},{4,132},{5,133},{6,134},{7,135},{8... | collective-permute-start | bytes 442376 | tf_op jit(solution)/shard_map/ppermute | solution.py:69
  125.7 8.5 %collective-permute-done.6 = bf16[64,1152]{1,0:T(8,128)(2,1)S(1)} collective-permute-done((bf16[64,1152]{1,0:T(8,128)(2,1)}, bf16[64,1152]{1,0:T(8,128)(2,1)S(1)}, u32[]{:S(2)}, u32[]{:S(2)}) %collective-permute-start.6) | collective-permute-done | bytes 147488 | tf_op jit(solution)/shard_map/ppermute | solution.py:69
  135.2 5.2 %collective-permute-start.8 = (bf16[64,1152]{1,0:T(8,128)(2,1)S(1)}, bf16[64,1152]{1,0:T(8,128)(2,1)S(1)}, u32[]{:S(2)}, u32[]{:S(2)}) collective-permute-start(bf16[64,1152]{1,0:T(8,128)(2,1)S(1)} %add_convert_fusion.1), channel_id=1, source_target_pairs={{0,256},{1,257},{2,258},{3,259},{4,260},{5,261},{6,262},{7,263},{8... | collective-permute-start | bytes 442376 | tf_op jit(solution)/shard_map/ppermute | solution.py:69
  140.4 14.5 %collective-permute-done.8 = bf16[64,1152]{1,0:T(8,128)(2,1)S(1)} collective-permute-done((bf16[64,1152]{1,0:T(8,128)(2,1)S(1)}, bf16[64,1152]{1,0:T(8,128)(2,1)S(1)}, u32[]{:S(2)}, u32[]{:S(2)}) %collective-permute-start.8) | collective-permute-done | bytes 147488 | tf_op jit(solution)/shard_map/ppermute | solution.py:69
  155.1 2.2 %convert_reduce_fusion = f32[72,1152]{1,0:T(8,128)S(1)} fusion(bf16[16,72,1152]{2,1,0:T(8,128)(2,1)} %all-to-all-done.3), kind=kLoop, calls=%fused_computation.1 | loop fusion | flops 2571264 | bytes 2985984 | tf_op jit(solution)/shard_map/reduce_sum | solution.py:289
  157.3 4.5 %collective-permute-start.14 = (bf16[36,1152]{1,0:T(8,128)(2,1)S(1)}, bf16[36,1152]{1,0:T(8,128)(2,1)S(1)}, u32[]{:S(2)}, u32[]{:S(2)}) collective-permute-start(bf16[36,1152]{1,0:T(8,128)(2,1)S(1)} %select_convert_fusion), channel_id=1, source_target_pairs={{0,456},{1,457},{2,458},{3,459},{4,460},{5,461},{6,462},{7,463},{8... | collective-permute-start | bytes 248840 | tf_op jit(solution)/shard_map/ppermute | solution.py:69
  161.8 11.6 %collective-permute-start.10 = (bf16[64,1152]{1,0:T(8,128)(2,1)S(1)}, bf16[64,1152]{1,0:T(8,128)(2,1)S(1)}, u32[]{:S(2)}, u32[]{:S(2)}) collective-permute-start(bf16[64,1152]{1,0:T(8,128)(2,1)S(1)} %add_convert_fusion), channel_id=1, source_target_pairs={{0,192},{1,193},{2,194},{3,195},{4,196},{5,197},{6,198},{7,199},{8... | collective-permute-start | bytes 442376 | tf_op jit(solution)/shard_map/ppermute | solution.py:69
  175.4 2.2 %collective-permute-start.12 = (bf16[64,1152]{1,0:T(8,128)(2,1)S(1)}, bf16[64,1152]{1,0:T(8,128)(2,1)S(1)}, u32[]{:S(2)}, u32[]{:S(2)}) collective-permute-start(bf16[64,1152]{1,0:T(8,128)(2,1)S(1)} %add_convert_fusion), channel_id=1, source_target_pairs={{0,128},{1,129},{2,130},{3,131},{4,132},{5,133},{6,134},{7,135},{8... | collective-permute-start | bytes 442376 | tf_op jit(solution)/shard_map/ppermute | solution.py:69
  177.6 6.9 %collective-permute-start.15 = (bf16[36,1152]{1,0:T(8,128)(2,1)S(1)}, bf16[36,1152]{1,0:T(8,128)(2,1)S(1)}, u32[]{:S(2)}, u32[]{:S(2)}) collective-permute-start(bf16[36,1152]{1,0:T(8,128)(2,1)S(1)} %add_convert_fusion.3), channel_id=1, source_target_pairs={{0,256},{1,257},{2,258},{3,259},{4,260},{5,261},{6,262},{7,263},{8... | collective-permute-start | bytes 248840 | tf_op jit(solution)/shard_map/ppermute | solution.py:69
  184.6 2.7 %fusion = f32[256,1152]{1,0:T(8,128)S(1)} fusion(bf16[1152,1152]{1,0:T(8,128)(2,1)} %collective-permute-done.9, bf16[64,1152]{1,0:T(8,128)(2,1)S(1)} %get-tuple-element.33, bf16[64,1152]{1,0:T(8,128)(2,1)S(1)} %get-tuple-element.32, bf16[64,1152]{1,0:T(8,128)(2,1)S(1)} %get-tuple-element.31, bf16[64,1152]{1,0:T(8,128)(2,1)S(1)} %get-tuple-element.30), kind=kOutput, calls=%fused_computation.7 | convolution fusion | flops 681836544 | bytes 4423680 | tf_op jit(solution)/shard_map/dot_general | solution.py:300
  187.4 3.2 %collective-permute-start.16 = (bf16[36,1152]{1,0:T(8,128)(2,1)S(1)}, bf16[36,1152]{1,0:T(8,128)(2,1)S(1)}, u32[]{:S(2)}, u32[]{:S(2)}) collective-permute-start(bf16[36,1152]{1,0:T(8,128)(2,1)S(1)} %add_convert_fusion.2), channel_id=1, source_target_pairs={{0,64},{1,65},{2,66},{3,67},{4,68},{5,69},{6,70},{7,71},{8,72},{9,... | collective-permute-start | bytes 248840 | tf_op jit(solution)/shard_map/ppermute | solution.py:69
  190.7 6.5 %collective-permute-start.17 = (bf16[36,1152]{1,0:T(8,128)(2,1)S(1)}, bf16[36,1152]{1,0:T(8,128)(2,1)S(1)}, u32[]{:S(2)}, u32[]{:S(2)}) collective-permute-start(bf16[36,1152]{1,0:T(8,128)(2,1)S(1)} %add_convert_fusion.2), channel_id=1, source_target_pairs={{0,128},{1,129},{2,130},{3,131},{4,132},{5,133},{6,134},{7,135},{8... | collective-permute-start | bytes 248840 | tf_op jit(solution)/shard_map/ppermute | solution.py:69
  197.2 3.1 %collective-permute-start.18 = (bf16[36,1152]{1,0:T(8,128)(2,1)S(1)}, bf16[36,1152]{1,0:T(8,128)(2,1)S(1)}, u32[]{:S(2)}, u32[]{:S(2)}) collective-permute-start(bf16[36,1152]{1,0:T(8,128)(2,1)S(1)} %add_convert_fusion.2), channel_id=1, source_target_pairs={{0,192},{1,193},{2,194},{3,195},{4,196},{5,197},{6,198},{7,199},{8... | collective-permute-start | bytes 248840 | tf_op jit(solution)/shard_map/ppermute | solution.py:69
  200.4 6.0 %collective-permute-start.13 = (f32[128,1152]{1,0:T(8,128)S(1)}, f32[128,1152]{1,0:T(8,128)S(1)}, u32[]{:S(2)}, u32[]{:S(2)}) collective-permute-start(f32[128,1152]{1,0:T(8,128)S(1)} %bitcast.44), channel_id=1, source_target_pairs={{0,1},{1,0},{2,3},{3,2},{4,5},{5,4},{6,7},{7,6},{8,9},{9,8},{10,11... | collective-permute-start | bytes 1769480 | tf_op jit(solution)/shard_map/ppermute | solution.py:69
  206.5 3.9 %collective-permute-start.19 = (f32[18,1152]{1,0:T(8,128)S(1)}, f32[18,1152]{1,0:T(8,128)S(1)}, u32[]{:S(2)}, u32[]{:S(2)}) collective-permute-start(f32[18,1152]{1,0:T(8,128)S(1)} %slice_select_fusion.1), channel_id=1, source_target_pairs={{0,1},{1,0},{2,3},{3,2},{4,5},{5,4},{6,7},{7,6},{8,9},{9,8},{10,11... | collective-permute-start | bytes 248840 | tf_op jit(solution)/shard_map/ppermute | solution.py:69
  (72 shorter events, 20.7 us)
Async XLA Ops:
  0.6 19.0 %copy-start.3 = (bf16[1152,18]{0,1:T(8,128)(2,1)S(1)}, bf16[1152,18]{0,1:T(8,128)(2,1)}, u32[]{:S(2)}) copy-start(bf16[1152,18]{0,1:T(8,128)(2,1)} %param.10) | copy-start | bytes 124420
  0.6 19.0 %copy-start.4 = (bf16[1152,18]{0,1:T(8,128)(2,1)S(1)}, bf16[1152,18]{0,1:T(8,128)(2,1)}, u32[]{:S(2)}) copy-start(bf16[1152,18]{0,1:T(8,128)(2,1)} %param.9) | copy-start | bytes 124420
  2.7 16.9 %collective-permute-start = (bf16[34,1152]{1,0:T(8,128)(2,1)S(1)}, bf16[34,1152]{1,0:T(8,128)(2,1)S(1)}, u32[]{:S(2)}, u32[]{:S(2)}) collective-permute-start(bf16[34,1152]{1,0:T(8,128)(2,1)S(1)} %pad_maximum_fusion.6), channel_id=1, source_target_pairs={{0,1},{1,0},{2,3},{3,2},{4,5},{5,4},{6,7},{7,6},{8,9},{9,8},{10,11... | collective-permute-start | bytes 235016 | tf_op jit(solution)/shard_map/ppermute | solution.py:69
  11.5 15.3 %collective-permute-start.2 = (bf16[34,1152]{1,0:T(8,128)(2,1)S(1)}, bf16[34,1152]{1,0:T(8,128)(2,1)S(1)}, u32[]{:S(2)}, u32[]{:S(2)}) collective-permute-start(bf16[34,1152]{1,0:T(8,128)(2,1)S(1)} %pad_maximum_fusion.6), channel_id=1, source_target_pairs={{0,457},{1,456},{2,459},{3,458},{4,461},{5,460},{6,463},{7,462},{8... | collective-permute-start | bytes 235016 | tf_op jit(solution)/shard_map/ppermute | solution.py:69
  17.2 22.0 %collective-permute-start.3 = (bf16[256,1152]{1,0:T(8,128)(2,1)S(1)}, bf16[256,1152]{1,0:T(8,128)(2,1)S(1)}, u32[]{:S(2)}, u32[]{:S(2)}) collective-permute-start(bf16[256,1152]{1,0:T(8,128)(2,1)S(1)} %pad_maximum_fusion.1), channel_id=1, source_target_pairs={{0,1},{1,0},{2,3},{3,2},{4,5},{5,4},{6,7},{7,6},{8,9},{9,8},{10,11... | collective-permute-start | bytes 1769480 | tf_op jit(solution)/shard_map/ppermute | solution.py:69
  19.7 13.3 %collective-permute-start.1 = (bf16[34,1152]{1,0:T(8,128)(2,1)S(1)}, bf16[34,1152]{1,0:T(8,128)(2,1)S(1)}, u32[]{:S(2)}, u32[]{:S(2)}) collective-permute-start(bf16[34,1152]{1,0:T(8,128)(2,1)S(1)} %pad_maximum_fusion.7), channel_id=1, source_target_pairs={{0,456},{1,457},{2,458},{3,459},{4,460},{5,461},{6,462},{7,463},{8... | collective-permute-start | bytes 235016 | tf_op jit(solution)/shard_map/ppermute | solution.py:69
  22.6 12.2 %all-to-all-start = ((bf16[4,68,1152]{2,1,0:T(8,128)(2,1)}), bf16[4,68,1152]{2,1,0:T(8,128)(2,1)S(1)}, u32[]{:S(2)}, u32[]{:S(2)}) async-start(bf16[4,68,1152]{2,1,0:T(8,128)(2,1)} %broadcast_in_dim.6), calls=%async_computation | async-start | bytes 1327104 | tf_op jit(solution)/shard_map/all_to_all | solution.py:73
  35.7 11.1 %all-to-all-start.1 = ((bf16[4,68,1152]{2,1,0:T(8,128)(2,1)}), bf16[4,68,1152]{2,1,0:T(8,128)(2,1)S(1)}, u32[]{:S(2)}, u32[]{:S(2)}) async-start(bf16[4,68,1152]{2,1,0:T(8,128)(2,1)} %broadcast_in_dim.7), calls=%async_computation.1 | async-start | bytes 1327104 | tf_op jit(solution)/shard_map/all_to_all | solution.py:73
  82.5 2.3 %copy-start = (bf16[4,4,136,1152]{3,2,1,0:T(8,128)(2,1)}, bf16[4,4,136,1152]{3,2,1,0:T(8,128)(2,1)S(1)}, u32[]{:S(2)}) copy-start(bf16[4,4,136,1152]{3,2,1,0:T(8,128)(2,1)S(1)} %all_to_all.20) | copy-start | bytes 15040516
  87.1 14.9 %collective-permute-start.4 = (f32[256,1152]{1,0:T(8,128)}, f32[256,1152]{1,0:T(8,128)}, u32[]{:S(2)}, u32[]{:S(2)}) collective-permute-start(f32[256,1152]{1,0:T(8,128)} %fusion.11), channel_id=1, source_target_pairs={{0,1},{1,0},{2,3},{3,2},{4,5},{5,4},{6,7},{7,6},{8,9},{9,8},{10,11... | collective-permute-start | bytes 3538952 | tf_op jit(solution)/shard_map/ppermute | solution.py:69
  95.3 2.4 %copy-start.1 = (bf16[4,4,136,1152]{3,2,1,0:T(8,128)(2,1)S(1)}, bf16[4,4,136,1152]{3,2,1,0:T(8,128)(2,1)}, u32[]{:S(2)}) copy-start(bf16[4,4,136,1152]{3,2,1,0:T(8,128)(2,1)} %copy-done) | copy-start | bytes 15040516
  102.0 3.6 %copy-start.2 = (bf16[8,2,16,1152]{3,2,1,0:T(8,128)(2,1)S(1)}, bf16[8,2,16,1152]{3,2,1,0:T(8,128)(2,1)}, u32[]{:S(2)}) copy-start(bf16[8,2,16,1152]{3,2,1,0:T(8,128)(2,1)} %pad_maximum_fusion.2) | copy-start | bytes 1769476
  108.1 47.0 %collective-permute-start.9 = (bf16[1152,1152]{1,0:T(8,128)(2,1)S(1)}, bf16[1152,1152]{1,0:T(8,128)(2,1)}, u32[]{:S(2)}, u32[]{:S(2)}) collective-permute-start(bf16[1152,1152]{1,0:T(8,128)(2,1)S(1)} %bitcast.35), channel_id=1, source_target_pairs={{0,1},{1,0},{2,3},{3,2},{4,5},{5,4},{6,7},{7,6},{8,9},{9,8},{10,11... | collective-permute-start | bytes 7962632 | tf_op jit(solution)/shard_map/ppermute | solution.py:69
  110.0 45.1 %all-to-all-start.3 = ((bf16[16,72,1152]{2,1,0:T(8,128)(2,1)}), bf16[16,72,1152]{2,1,0:T(8,128)(2,1)}, u32[]{:S(2)}, u32[]{:S(2)}) async-start(bf16[16,72,1152]{2,1,0:T(8,128)(2,1)} %bitcast.36), calls=%async_computation.3 | async-start | bytes 5308416 | tf_op jit(solution)/shard_map/all_to_all | solution.py:73
  115.3 10.3 %collective-permute-start.5 = (bf16[64,1152]{1,0:T(8,128)(2,1)}, bf16[64,1152]{1,0:T(8,128)(2,1)S(1)}, u32[]{:S(2)}, u32[]{:S(2)}) collective-permute-start(bf16[64,1152]{1,0:T(8,128)(2,1)} %get-tuple-element.34), channel_id=1, source_target_pairs={{0,64},{1,65},{2,66},{3,67},{4,68},{5,69},{6,70},{7,71},{8,72},{9,... | collective-permute-start | bytes 442376 | tf_op jit(solution)/shard_map/ppermute | solution.py:69
  118.9 15.3 %collective-permute-start.6 = (bf16[64,1152]{1,0:T(8,128)(2,1)}, bf16[64,1152]{1,0:T(8,128)(2,1)S(1)}, u32[]{:S(2)}, u32[]{:S(2)}) collective-permute-start(bf16[64,1152]{1,0:T(8,128)(2,1)} %get-tuple-element.36), channel_id=1, source_target_pairs={{0,128},{1,129},{2,130},{3,131},{4,132},{5,133},{6,134},{7,135},{8... | collective-permute-start | bytes 442376 | tf_op jit(solution)/shard_map/ppermute | solution.py:69
  123.8 10.5 %collective-permute-start.7 = (bf16[64,1152]{1,0:T(8,128)(2,1)}, bf16[64,1152]{1,0:T(8,128)(2,1)}, u32[]{:S(2)}, u32[]{:S(2)}) collective-permute-start(bf16[64,1152]{1,0:T(8,128)(2,1)} %get-tuple-element.35), channel_id=1, source_target_pairs={{0,192},{1,193},{2,194},{3,195},{4,196},{5,197},{6,198},{7,199},{8... | collective-permute-start | bytes 442376 | tf_op jit(solution)/shard_map/ppermute | solution.py:69
  135.2 19.7 %collective-permute-start.8 = (bf16[64,1152]{1,0:T(8,128)(2,1)S(1)}, bf16[64,1152]{1,0:T(8,128)(2,1)S(1)}, u32[]{:S(2)}, u32[]{:S(2)}) collective-permute-start(bf16[64,1152]{1,0:T(8,128)(2,1)S(1)} %add_convert_fusion.1), channel_id=1, source_target_pairs={{0,256},{1,257},{2,258},{3,259},{4,260},{5,261},{6,262},{7,263},{8... | collective-permute-start | bytes 442376 | tf_op jit(solution)/shard_map/ppermute | solution.py:69
  157.3 20.2 %collective-permute-start.14 = (bf16[36,1152]{1,0:T(8,128)(2,1)S(1)}, bf16[36,1152]{1,0:T(8,128)(2,1)S(1)}, u32[]{:S(2)}, u32[]{:S(2)}) collective-permute-start(bf16[36,1152]{1,0:T(8,128)(2,1)S(1)} %select_convert_fusion), channel_id=1, source_target_pairs={{0,456},{1,457},{2,458},{3,459},{4,460},{5,461},{6,462},{7,463},{8... | collective-permute-start | bytes 248840 | tf_op jit(solution)/shard_map/ppermute | solution.py:69
  161.8 22.7 %collective-permute-start.10 = (bf16[64,1152]{1,0:T(8,128)(2,1)S(1)}, bf16[64,1152]{1,0:T(8,128)(2,1)S(1)}, u32[]{:S(2)}, u32[]{:S(2)}) collective-permute-start(bf16[64,1152]{1,0:T(8,128)(2,1)S(1)} %add_convert_fusion), channel_id=1, source_target_pairs={{0,192},{1,193},{2,194},{3,195},{4,196},{5,197},{6,198},{7,199},{8... | collective-permute-start | bytes 442376 | tf_op jit(solution)/shard_map/ppermute | solution.py:69
  173.4 11.1 %collective-permute-start.11 = (bf16[64,1152]{1,0:T(8,128)(2,1)S(1)}, bf16[64,1152]{1,0:T(8,128)(2,1)S(1)}, u32[]{:S(2)}, u32[]{:S(2)}) collective-permute-start(bf16[64,1152]{1,0:T(8,128)(2,1)S(1)} %add_convert_fusion), channel_id=1, source_target_pairs={{0,64},{1,65},{2,66},{3,67},{4,68},{5,69},{6,70},{7,71},{8,72},{9,... | collective-permute-start | bytes 442376 | tf_op jit(solution)/shard_map/ppermute | solution.py:69
  175.4 9.1 %collective-permute-start.12 = (bf16[64,1152]{1,0:T(8,128)(2,1)S(1)}, bf16[64,1152]{1,0:T(8,128)(2,1)S(1)}, u32[]{:S(2)}, u32[]{:S(2)}) collective-permute-start(bf16[64,1152]{1,0:T(8,128)(2,1)S(1)} %add_convert_fusion), channel_id=1, source_target_pairs={{0,128},{1,129},{2,130},{3,131},{4,132},{5,133},{6,134},{7,135},{8... | collective-permute-start | bytes 442376 | tf_op jit(solution)/shard_map/ppermute | solution.py:69
  177.6 9.7 %collective-permute-start.15 = (bf16[36,1152]{1,0:T(8,128)(2,1)S(1)}, bf16[36,1152]{1,0:T(8,128)(2,1)S(1)}, u32[]{:S(2)}, u32[]{:S(2)}) collective-permute-start(bf16[36,1152]{1,0:T(8,128)(2,1)S(1)} %add_convert_fusion.3), channel_id=1, source_target_pairs={{0,256},{1,257},{2,258},{3,259},{4,260},{5,261},{6,262},{7,263},{8... | collective-permute-start | bytes 248840 | tf_op jit(solution)/shard_map/ppermute | solution.py:69
  187.4 19.0 %collective-permute-start.16 = (bf16[36,1152]{1,0:T(8,128)(2,1)S(1)}, bf16[36,1152]{1,0:T(8,128)(2,1)S(1)}, u32[]{:S(2)}, u32[]{:S(2)}) collective-permute-start(bf16[36,1152]{1,0:T(8,128)(2,1)S(1)} %add_convert_fusion.2), channel_id=1, source_target_pairs={{0,64},{1,65},{2,66},{3,67},{4,68},{5,69},{6,70},{7,71},{8,72},{9,... | collective-permute-start | bytes 248840 | tf_op jit(solution)/shard_map/ppermute | solution.py:69
  190.7 15.8 %collective-permute-start.17 = (bf16[36,1152]{1,0:T(8,128)(2,1)S(1)}, bf16[36,1152]{1,0:T(8,128)(2,1)S(1)}, u32[]{:S(2)}, u32[]{:S(2)}) collective-permute-start(bf16[36,1152]{1,0:T(8,128)(2,1)S(1)} %add_convert_fusion.2), channel_id=1, source_target_pairs={{0,128},{1,129},{2,130},{3,131},{4,132},{5,133},{6,134},{7,135},{8... | collective-permute-start | bytes 248840 | tf_op jit(solution)/shard_map/ppermute | solution.py:69
  197.2 9.3 %collective-permute-start.18 = (bf16[36,1152]{1,0:T(8,128)(2,1)S(1)}, bf16[36,1152]{1,0:T(8,128)(2,1)S(1)}, u32[]{:S(2)}, u32[]{:S(2)}) collective-permute-start(bf16[36,1152]{1,0:T(8,128)(2,1)S(1)} %add_convert_fusion.2), channel_id=1, source_target_pairs={{0,192},{1,193},{2,194},{3,195},{4,196},{5,197},{6,198},{7,199},{8... | collective-permute-start | bytes 248840 | tf_op jit(solution)/shard_map/ppermute | solution.py:69
  200.4 11.8 %collective-permute-start.13 = (f32[128,1152]{1,0:T(8,128)S(1)}, f32[128,1152]{1,0:T(8,128)S(1)}, u32[]{:S(2)}, u32[]{:S(2)}) collective-permute-start(f32[128,1152]{1,0:T(8,128)S(1)} %bitcast.44), channel_id=1, source_target_pairs={{0,1},{1,0},{2,3},{3,2},{4,5},{5,4},{6,7},{7,6},{8,9},{9,8},{10,11... | collective-permute-start | bytes 1769480 | tf_op jit(solution)/shard_map/ppermute | solution.py:69
  206.5 4.9 %collective-permute-start.19 = (f32[18,1152]{1,0:T(8,128)S(1)}, f32[18,1152]{1,0:T(8,128)S(1)}, u32[]{:S(2)}, u32[]{:S(2)}) collective-permute-start(f32[18,1152]{1,0:T(8,128)S(1)} %slice_select_fusion.1), channel_id=1, source_target_pairs={{0,1},{1,0},{2,3},{3,2},{4,5},{5,4},{6,7},{7,6},{8,9},{9,8},{10,11... | collective-permute-start | bytes 248840 | tf_op jit(solution)/shard_map/ppermute | solution.py:69

commit v12 on v11

--- a/solution.py
+++ b/solution.py
@@ -116,7 +116,7 @@
         ],
         out_specs=pl.BlockSpec((group * picked, embed), lambda i: (i, 0)),
         out_shape=jax.ShapeDtypeStruct((rows, embed), jnp.bfloat16),
-        compiler_params=pltpu.CompilerParams(vmem_limit_bytes=40 * 2**20),
+        compiler_params=pltpu.CompilerParams(vmem_limit_bytes=20 * 2**20),
         cost_estimate=pl.CostEstimate(
             flops=2 * rows * embed * width,
             bytes_accessed=2 * (rows * width + rows * embed + embed * width),
@@ -176,7 +176,7 @@
             pltpu.VMEM((own, embed), jnp.bfloat16),
             pltpu.VMEM((own, embed), jnp.float32),
         ],
-        compiler_params=pltpu.CompilerParams(vmem_limit_bytes=40 * 2**20),
+        compiler_params=pltpu.CompilerParams(vmem_limit_bytes=20 * 2**20),
         cost_estimate=pl.CostEstimate(
             flops=4 * own * count * embed,
             bytes_accessed=2 * count * embed + 6 * own * embed,
@@ -275,9 +275,13 @@
         permuted(quarter_of(at_quarter ^ 1), along(2)),
         permuted(quarter_of(at_quarter ^ 3), along(3)),
     ).astype(bf16)
+    held, late_proj = lax.optimization_barrier((held, late_proj))
     held = held.astype(f32) + permuted(held, along(4)).astype(f32)
-    du, terms, other_proj = lax.optimization_barrier(
-        (held.astype(bf16), terms, permuted(late_proj, sibling))
+    terms = jnp.sum(terms.astype(f32), 0)
+    lower, upper = terms[:pair], terms[pair:]
+    came = permuted(jnp.where(low, upper, lower).astype(bf16), mirror)
+    du, came, other_proj = lax.optimization_barrier(
+        (held.astype(bf16), came, permuted(late_proj, sibling))
     )
     pieces = [du] + [permuted(du, along(hop)) for hop in (2, 1, 3)]
     swap = (at_quarter & 1) == 1
@@ -286,9 +290,6 @@
     pieces = [jnp.where(swap, pieces[index ^ 2], pieces[index]) for index in range(4)]
     du = jnp.concatenate(pieces, 0)
 
-    terms = jnp.sum(terms.astype(f32), 0)
-    lower, upper = terms[:pair], terms[pair:]
-    came = permuted(jnp.where(low, upper, lower).astype(bf16), mirror)
     total = (jnp.where(low, lower, upper) + came.astype(f32)).astype(bf16)
     total = (total.astype(f32) + permuted(total, along(4)).astype(f32)).astype(bf16)
     total = summed(total, *(permuted(total, along(hop)) for hop in (1, 2, 3)))

time: 214 us -> 210 us (0.981)
  starting transfers between devices: 104 us -> 100 us
    all_to_all x3, waiting for transfers between devices: 8.51 us -> 20.7 us  [exchanged(): lax.all_to_all(value, BOTH, 0, 0, axis_index_groups=groups, tiled=True)]
    ppermute x20, waiting for transfers between devices: 30.1 us -> 18.1 us  [permuted(): return lax.ppermute(value, BOTH, pairs)]
    ppermute x20, starting transfers between devices: 92.1 us -> 88 us  [permuted(): return lax.ppermute(value, BOTH, pairs)]
  transfers between devices with their start and end apart: 23 -> 23, of which waited for: 7 -> 7; matrix products, arithmetic and copies ran while one was open for 4% -> 5% of each run, Pallas kernels for 2% -> 2%
where the time goes in v12:
time: 210 us; the launch traced here: 209 us
  starting transfers between devices  100 us (48%)
  waiting for transfers between devices  38.8 us (18%)
  blocking collectives  34.8 us (17%)
  other arithmetic  9.01 us (4%)
  local copies, waits for them, and re-layouts  8.07 us (4%)
  Pallas kernels  7.88 us (4%)
  matrix products  7.36 us (4%)
  between operations  3.27 us (2%)
    ppermute x20, starting transfers between devices, permuted(): return lax.ppermute(value, BOTH, pairs)  88 us
    all_to_all x1, blocking collectives, exchanged(): lax.all_to_all(value, BOTH, 0, 0, axis_index_groups=groups, tiled=True)  34.8 us
    all_to_all x3, waiting for transfers between devices, exchanged(): lax.all_to_all(value, BOTH, 0, 0, axis_index_groups=groups, tiled=True)  20.7 us
    ppermute x20, waiting for transfers between devices, permuted(): return lax.ppermute(value, BOTH, pairs)  18.1 us
    all_to_all x3, starting transfers between devices, exchanged(): lax.all_to_all(value, BOTH, 0, 0, axis_index_groups=groups, tiled=True)  12.1 us
    unnamed x10, local copies, waits for them, and re-layouts  4.72 us
    pallas_call x1, Pallas kernels, embedded(): pl.pallas_call(embed_kernel, grid=(count // group,), in_specs=[pl.BlockSp...  4.28 us
  transfers between devices with their start and end apart: 23, of which 7 were waited for; matrix products, arithmetic and copies ran while one was open for 5% of the time, Pallas kernels for 2%

profile of v12, /device:TPU:1, one launch (start us, length us, event | category | flops | bytes accessed | tf_op | source)
XLA Modules:
  0.0 209.3 jit_solution(6885126171248146721)
XLA Ops:
  2.7 8.8 %collective-permute-start = (bf16[34,1152]{1,0:T(8,128)(2,1)S(1)}, bf16[34,1152]{1,0:T(8,128)(2,1)S(1)}, u32[]{:S(2)}, u32[]{:S(2)}) collective-permute-start(bf16[34,1152]{1,0:T(8,128)(2,1)S(1)} %pad_maximum_fusion.6), channel_id=1, source_target_pairs={{0,1},{1,0},{2,3},{3,2},{4,5},{5,4},{6,7},{7,6},{8,9},{9,8},{10,11... | collective-permute-start | bytes 235016 | tf_op jit(solution)/shard_map/ppermute | solution.py:69
  11.5 5.6 %collective-permute-start.2 = (bf16[34,1152]{1,0:T(8,128)(2,1)S(1)}, bf16[34,1152]{1,0:T(8,128)(2,1)S(1)}, u32[]{:S(2)}, u32[]{:S(2)}) collective-permute-start(bf16[34,1152]{1,0:T(8,128)(2,1)S(1)} %pad_maximum_fusion.6), channel_id=1, source_target_pairs={{0,457},{1,456},{2,459},{3,458},{4,461},{5,460},{6,463},{7,462},{8... | collective-permute-start | bytes 235016 | tf_op jit(solution)/shard_map/ppermute | solution.py:69
  17.2 2.4 %collective-permute-start.3 = (bf16[256,1152]{1,0:T(8,128)(2,1)S(1)}, bf16[256,1152]{1,0:T(8,128)(2,1)S(1)}, u32[]{:S(2)}, u32[]{:S(2)}) collective-permute-start(bf16[256,1152]{1,0:T(8,128)(2,1)S(1)} %pad_maximum_fusion.1), channel_id=1, source_target_pairs={{0,1},{1,0},{2,3},{3,2},{4,5},{5,4},{6,7},{7,6},{8,9},{9,8},{10,11... | collective-permute-start | bytes 1769480 | tf_op jit(solution)/shard_map/ppermute | solution.py:69
  22.6 4.2 %all-to-all-start = ((bf16[4,68,1152]{2,1,0:T(8,128)(2,1)}), bf16[4,68,1152]{2,1,0:T(8,128)(2,1)S(1)}, u32[]{:S(2)}, u32[]{:S(2)}) async-start(bf16[4,68,1152]{2,1,0:T(8,128)(2,1)} %broadcast_in_dim.6), calls=%async_computation | async-start | bytes 1327104 | tf_op jit(solution)/shard_map/all_to_all | solution.py:73
  26.8 6.2 %collective-permute-done.1 = bf16[34,1152]{1,0:T(8,128)(2,1)S(1)} collective-permute-done((bf16[34,1152]{1,0:T(8,128)(2,1)S(1)}, bf16[34,1152]{1,0:T(8,128)(2,1)S(1)}, u32[]{:S(2)}, u32[]{:S(2)}) %collective-permute-start.1) | collective-permute-done | bytes 78368 | tf_op jit(solution)/shard_map/ppermute | solution.py:69
  35.7 3.5 %all-to-all-start.1 = ((bf16[4,68,1152]{2,1,0:T(8,128)(2,1)}), bf16[4,68,1152]{2,1,0:T(8,128)(2,1)S(1)}, u32[]{:S(2)}, u32[]{:S(2)}) async-start(bf16[4,68,1152]{2,1,0:T(8,128)(2,1)} %broadcast_in_dim.7), calls=%async_computation.1 | async-start | bytes 1327104 | tf_op jit(solution)/shard_map/all_to_all | solution.py:73
  40.2 6.6 %all-to-all-done.1 = bf16[4,68,1152]{2,1,0:T(8,128)(2,1)S(1)} async-done(((bf16[4,68,1152]{2,1,0:T(8,128)(2,1)}), bf16[4,68,1152]{2,1,0:T(8,128)(2,1)S(1)}, u32[]{:S(2)}, u32[]{:S(2)}) %all-to-all-start.1) | async-done | bytes 626720 | tf_op jit(solution)/shard_map/all_to_all | solution.py:73
  47.4 34.8 %all_to_all.20 = bf16[4,4,136,1152]{3,2,1,0:T(8,128)(2,1)S(1)} all-to-all(bf16[4,4,136,1152]{3,2,1,0:T(8,128)(2,1)S(1)} %broadcast_in_dim.8), channel_id=1, replica_groups={{0,16,32,48},{2,18,34,50},{4,20,36,52},{6,22,38,54},{1,3,5,7},{17,19,21..., dimensions={0} | all-to-all | bytes 10027008 | tf_op jit(solution)/shard_map/all_to_all | solution.py:73
  82.5 2.3 %copy-done = bf16[4,4,136,1152]{3,2,1,0:T(8,128)(2,1)} copy-done((bf16[4,4,136,1152]{3,2,1,0:T(8,128)(2,1)}, bf16[4,4,136,1152]{3,2,1,0:T(8,128)(2,1)S(1)}, u32[]{:S(2)}) %copy-start) | copy-done | bytes 5013528
  85.0 2.1 fusion.11
  87.1 6.0 %collective-permute-start.4 = (f32[256,1152]{1,0:T(8,128)}, f32[256,1152]{1,0:T(8,128)}, u32[]{:S(2)}, u32[]{:S(2)}) collective-permute-start(f32[256,1152]{1,0:T(8,128)} %fusion.11), channel_id=1, source_target_pairs={{0,1},{1,0},{2,3},{3,2},{4,5},{5,4},{6,7},{7,6},{8,9},{9,8},{10,11... | collective-permute-start | bytes 3538952 | tf_op jit(solution)/shard_map/ppermute | solution.py:69
  95.3 2.4 %copy-done.1 = bf16[4,4,136,1152]{3,2,1,0:T(8,128)(2,1)S(1)} copy-done((bf16[4,4,136,1152]{3,2,1,0:T(8,128)(2,1)S(1)}, bf16[4,4,136,1152]{3,2,1,0:T(8,128)(2,1)}, u32[]{:S(2)}) %copy-start.1) | copy-done | bytes 5013528
  97.7 4.3 %shard_map.102.others_ref = bf16[1024,1152]{1,0:T(8,128)(2,1)S(1)} custom-call(bf16[16,136,1152]{2,1,0:T(8,128)(2,1)S(1)} %bitcast.32, bf16[1152,1152]{1,0:T(8,128)(2,1)S(1)} %bitcast.34), custom_call_target="tpu_custom_call" | custom-call | flops 2717908992 | bytes 7372800 | tf_op jit(solution)/shard_map/pallas_call | solution.py:110
  102.0 3.6 %shard_map.103 = bf16[256,1152]{1,0:T(8,128)(2,1)S(1)} custom-call(s32[2]{0:T(128)S(1)} %pad_add_fusion.at_ref, f32[3]{0:T(128)S(1)} %pad_maximum_fusion.8.par_ref, f32[256,1152]{1,0:T(8,128)} %collective-permute-done.4.made_ref, bf16[1024,1152]{1,0:T(8,128)(2,1)S(1)} %shard_map.102.others_ref), custom_call_target="tpu_custom_call" | custom-call | flops 1207959552 | bytes 4128768 | tf_op jit(solution)/shard_map/pallas_call | solution.py:164
  105.6 2.5 %convolution_convert_fusion = bf16[1152,1152]{1,0:T(8,128)(2,1)} fusion(bf16[256,1152]{1,0:T(8,128)(2,1)S(1)} %shard_map.103, bf16[256,1152]{1,0:T(8,128)(2,1)S(1)} %bitcast.39), kind=kOutput, calls=%fused_computation | convolution fusion | flops 680804352 | bytes 3833856 | tf_op jit(solution)/shard_map/dot_general | solution.py:94
  108.1 4.5 %all-to-all-start.3 = ((bf16[16,72,1152]{2,1,0:T(8,128)(2,1)}), bf16[16,72,1152]{2,1,0:T(8,128)(2,1)}, u32[]{:S(2)}, u32[]{:S(2)}) async-start(bf16[16,72,1152]{2,1,0:T(8,128)(2,1)} %bitcast.36), calls=%async_computation.3 | async-start | bytes 5308416 | tf_op jit(solution)/shard_map/all_to_all | solution.py:73
  113.4 3.5 %collective-permute-start.5 = (bf16[64,1152]{1,0:T(8,128)(2,1)}, bf16[64,1152]{1,0:T(8,128)(2,1)S(1)}, u32[]{:S(2)}, u32[]{:S(2)}) collective-permute-start(bf16[64,1152]{1,0:T(8,128)(2,1)} %get-tuple-element.38), channel_id=1, source_target_pairs={{0,64},{1,65},{2,66},{3,67},{4,68},{5,69},{6,70},{7,71},{8,72},{9,... | collective-permute-start | bytes 442376 | tf_op jit(solution)/shard_map/ppermute | solution.py:69
  116.9 4.9 %collective-permute-start.6 = (bf16[64,1152]{1,0:T(8,128)(2,1)}, bf16[64,1152]{1,0:T(8,128)(2,1)}, u32[]{:S(2)}, u32[]{:S(2)}) collective-permute-start(bf16[64,1152]{1,0:T(8,128)(2,1)} %get-tuple-element.40), channel_id=1, source_target_pairs={{0,128},{1,129},{2,130},{3,131},{4,132},{5,133},{6,134},{7,135},{8... | collective-permute-start | bytes 442376 | tf_op jit(solution)/shard_map/ppermute | solution.py:69
  121.8 1.9 collective-permute-start.7
  123.7 8.7 %collective-permute-done.6 = bf16[64,1152]{1,0:T(8,128)(2,1)} collective-permute-done((bf16[64,1152]{1,0:T(8,128)(2,1)}, bf16[64,1152]{1,0:T(8,128)(2,1)}, u32[]{:S(2)}, u32[]{:S(2)}) %collective-permute-start.6) | collective-permute-done | bytes 147488 | tf_op jit(solution)/shard_map/ppermute | solution.py:69
  133.5 3.1 %collective-permute-start.10 = (bf16[1152,1152]{1,0:T(8,128)(2,1)S(1)}, bf16[1152,1152]{1,0:T(8,128)(2,1)}, u32[]{:S(2)}, u32[]{:S(2)}) collective-permute-start(bf16[1152,1152]{1,0:T(8,128)(2,1)S(1)} %bitcast.35), channel_id=1, source_target_pairs={{0,1},{1,0},{2,3},{3,2},{4,5},{5,4},{6,7},{7,6},{8,9},{9,8},{10,11... | collective-permute-start | bytes 7962632 | tf_op jit(solution)/shard_map/ppermute | solution.py:69
  136.6 5.8 %collective-permute-start.8 = (bf16[64,1152]{1,0:T(8,128)(2,1)S(1)}, bf16[64,1152]{1,0:T(8,128)(2,1)S(1)}, u32[]{:S(2)}, u32[]{:S(2)}) collective-permute-start(bf16[64,1152]{1,0:T(8,128)(2,1)S(1)} %add_convert_fusion.1), channel_id=1, source_target_pairs={{0,256},{1,257},{2,258},{3,259},{4,260},{5,261},{6,262},{7,263},{8... | collective-permute-start | bytes 442376 | tf_op jit(solution)/shard_map/ppermute | solution.py:69
  142.4 12.3 %all-to-all-done.3 = bf16[16,72,1152]{2,1,0:T(8,128)(2,1)} async-done(((bf16[16,72,1152]{2,1,0:T(8,128)(2,1)}), bf16[16,72,1152]{2,1,0:T(8,128)(2,1)}, u32[]{:S(2)}, u32[]{:S(2)}) %all-to-all-start.3) | async-done | bytes 2654240 | tf_op jit(solution)/shard_map/all_to_all | solution.py:73
  154.7 2.2 %convert_reduce_fusion = f32[72,1152]{1,0:T(8,128)S(1)} fusion(bf16[16,72,1152]{2,1,0:T(8,128)(2,1)} %all-to-all-done.3), kind=kLoop, calls=%fused_computation.1 | loop fusion | flops 2571264 | bytes 2985984 | tf_op jit(solution)/shard_map/reduce_sum | solution.py:280
  156.9 4.5 %collective-permute-start.9 = (bf16[36,1152]{1,0:T(8,128)(2,1)S(1)}, bf16[36,1152]{1,0:T(8,128)(2,1)S(1)}, u32[]{:S(2)}, u32[]{:S(2)}) collective-permute-start(bf16[36,1152]{1,0:T(8,128)(2,1)S(1)} %select_convert_fusion), channel_id=1, source_target_pairs={{0,456},{1,457},{2,458},{3,459},{4,460},{5,461},{6,462},{7,463},{8... | collective-permute-start | bytes 248840 | tf_op jit(solution)/shard_map/ppermute | solution.py:69
  161.5 1.9 collective-permute-done.9
  163.5 13.3 %collective-permute-start.15 = (bf16[36,1152]{1,0:T(8,128)(2,1)S(1)}, bf16[36,1152]{1,0:T(8,128)(2,1)S(1)}, u32[]{:S(2)}, u32[]{:S(2)}) collective-permute-start(bf16[36,1152]{1,0:T(8,128)(2,1)S(1)} %add_convert_fusion.3), channel_id=1, source_target_pairs={{0,256},{1,257},{2,258},{3,259},{4,260},{5,261},{6,262},{7,263},{8... | collective-permute-start | bytes 248840 | tf_op jit(solution)/shard_map/ppermute | solution.py:69
  180.6 5.4 %collective-permute-start.13 = (bf16[64,1152]{1,0:T(8,128)(2,1)S(1)}, bf16[64,1152]{1,0:T(8,128)(2,1)S(1)}, u32[]{:S(2)}, u32[]{:S(2)}) collective-permute-start(bf16[64,1152]{1,0:T(8,128)(2,1)S(1)} %add_convert_fusion), channel_id=1, source_target_pairs={{0,128},{1,129},{2,130},{3,131},{4,132},{5,133},{6,134},{7,135},{8... | collective-permute-start | bytes 442376 | tf_op jit(solution)/shard_map/ppermute | solution.py:69
  188.0 2.2 %collective-permute-start.17 = (bf16[36,1152]{1,0:T(8,128)(2,1)S(1)}, bf16[36,1152]{1,0:T(8,128)(2,1)S(1)}, u32[]{:S(2)}, u32[]{:S(2)}) collective-permute-start(bf16[36,1152]{1,0:T(8,128)(2,1)S(1)} %add_convert_fusion.2), channel_id=1, source_target_pairs={{0,128},{1,129},{2,130},{3,131},{4,132},{5,133},{6,134},{7,135},{8... | collective-permute-start | bytes 248840 | tf_op jit(solution)/shard_map/ppermute | solution.py:69
  190.2 5.2 %collective-permute-start.18 = (bf16[36,1152]{1,0:T(8,128)(2,1)S(1)}, bf16[36,1152]{1,0:T(8,128)(2,1)S(1)}, u32[]{:S(2)}, u32[]{:S(2)}) collective-permute-start(bf16[36,1152]{1,0:T(8,128)(2,1)S(1)} %add_convert_fusion.2), channel_id=1, source_target_pairs={{0,192},{1,193},{2,194},{3,195},{4,196},{5,197},{6,198},{7,199},{8... | collective-permute-start | bytes 248840 | tf_op jit(solution)/shard_map/ppermute | solution.py:69
  195.5 2.8 %fusion = f32[256,1152]{1,0:T(8,128)S(1)} fusion(bf16[1152,1152]{1,0:T(8,128)(2,1)} %collective-permute-done.10, bf16[64,1152]{1,0:T(8,128)(2,1)S(1)} %get-tuple-element.37, bf16[64,1152]{1,0:T(8,128)(2,1)S(1)} %get-tuple-element.36, bf16[64,1152]{1,0:T(8,128)(2,1)S(1)} %get-tuple-element.35, bf16[64,1152]{1,0:T(8,128)(2,1)S(1)} %get-tuple-element.34), kind=kOutput, calls=%fused_computation.7 | convolution fusion | flops 681836544 | bytes 4423680 | tf_op jit(solution)/shard_map/dot_general | solution.py:301
  198.4 5.8 %collective-permute-start.14 = (f32[128,1152]{1,0:T(8,128)S(1)}, f32[128,1152]{1,0:T(8,128)S(1)}, u32[]{:S(2)}, u32[]{:S(2)}) collective-permute-start(f32[128,1152]{1,0:T(8,128)S(1)} %bitcast.44), channel_id=1, source_target_pairs={{0,1},{1,0},{2,3},{3,2},{4,5},{5,4},{6,7},{7,6},{8,9},{9,8},{10,11... | collective-permute-start | bytes 1769480 | tf_op jit(solution)/shard_map/ppermute | solution.py:69
  (72 shorter events, 22.9 us)
Async XLA Ops:
  0.6 19.0 %copy-start.3 = (bf16[1152,18]{0,1:T(8,128)(2,1)S(1)}, bf16[1152,18]{0,1:T(8,128)(2,1)}, u32[]{:S(2)}) copy-start(bf16[1152,18]{0,1:T(8,128)(2,1)} %param.10) | copy-start | bytes 124420
  0.6 19.0 %copy-start.4 = (bf16[1152,18]{0,1:T(8,128)(2,1)S(1)}, bf16[1152,18]{0,1:T(8,128)(2,1)}, u32[]{:S(2)}) copy-start(bf16[1152,18]{0,1:T(8,128)(2,1)} %param.9) | copy-start | bytes 124420
  2.7 16.9 %collective-permute-start = (bf16[34,1152]{1,0:T(8,128)(2,1)S(1)}, bf16[34,1152]{1,0:T(8,128)(2,1)S(1)}, u32[]{:S(2)}, u32[]{:S(2)}) collective-permute-start(bf16[34,1152]{1,0:T(8,128)(2,1)S(1)} %pad_maximum_fusion.6), channel_id=1, source_target_pairs={{0,1},{1,0},{2,3},{3,2},{4,5},{5,4},{6,7},{7,6},{8,9},{9,8},{10,11... | collective-permute-start | bytes 235016 | tf_op jit(solution)/shard_map/ppermute | solution.py:69
  11.5 15.3 %collective-permute-start.2 = (bf16[34,1152]{1,0:T(8,128)(2,1)S(1)}, bf16[34,1152]{1,0:T(8,128)(2,1)S(1)}, u32[]{:S(2)}, u32[]{:S(2)}) collective-permute-start(bf16[34,1152]{1,0:T(8,128)(2,1)S(1)} %pad_maximum_fusion.6), channel_id=1, source_target_pairs={{0,457},{1,456},{2,459},{3,458},{4,461},{5,460},{6,463},{7,462},{8... | collective-permute-start | bytes 235016 | tf_op jit(solution)/shard_map/ppermute | solution.py:69
  17.2 22.0 %collective-permute-start.3 = (bf16[256,1152]{1,0:T(8,128)(2,1)S(1)}, bf16[256,1152]{1,0:T(8,128)(2,1)S(1)}, u32[]{:S(2)}, u32[]{:S(2)}) collective-permute-start(bf16[256,1152]{1,0:T(8,128)(2,1)S(1)} %pad_maximum_fusion.1), channel_id=1, source_target_pairs={{0,1},{1,0},{2,3},{3,2},{4,5},{5,4},{6,7},{7,6},{8,9},{9,8},{10,11... | collective-permute-start | bytes 1769480 | tf_op jit(solution)/shard_map/ppermute | solution.py:69
  19.7 13.3 %collective-permute-start.1 = (bf16[34,1152]{1,0:T(8,128)(2,1)S(1)}, bf16[34,1152]{1,0:T(8,128)(2,1)S(1)}, u32[]{:S(2)}, u32[]{:S(2)}) collective-permute-start(bf16[34,1152]{1,0:T(8,128)(2,1)S(1)} %pad_maximum_fusion.7), channel_id=1, source_target_pairs={{0,456},{1,457},{2,458},{3,459},{4,460},{5,461},{6,462},{7,463},{8... | collective-permute-start | bytes 235016 | tf_op jit(solution)/shard_map/ppermute | solution.py:69
  22.6 12.2 %all-to-all-start = ((bf16[4,68,1152]{2,1,0:T(8,128)(2,1)}), bf16[4,68,1152]{2,1,0:T(8,128)(2,1)S(1)}, u32[]{:S(2)}, u32[]{:S(2)}) async-start(bf16[4,68,1152]{2,1,0:T(8,128)(2,1)} %broadcast_in_dim.6), calls=%async_computation | async-start | bytes 1327104 | tf_op jit(solution)/shard_map/all_to_all | solution.py:73
  35.7 11.1 %all-to-all-start.1 = ((bf16[4,68,1152]{2,1,0:T(8,128)(2,1)}), bf16[4,68,1152]{2,1,0:T(8,128)(2,1)S(1)}, u32[]{:S(2)}, u32[]{:S(2)}) async-start(bf16[4,68,1152]{2,1,0:T(8,128)(2,1)} %broadcast_in_dim.7), calls=%async_computation.1 | async-start | bytes 1327104 | tf_op jit(solution)/shard_map/all_to_all | solution.py:73
  82.5 2.3 %copy-start = (bf16[4,4,136,1152]{3,2,1,0:T(8,128)(2,1)}, bf16[4,4,136,1152]{3,2,1,0:T(8,128)(2,1)S(1)}, u32[]{:S(2)}) copy-start(bf16[4,4,136,1152]{3,2,1,0:T(8,128)(2,1)S(1)} %all_to_all.20) | copy-start | bytes 15040516
  87.1 14.9 %collective-permute-start.4 = (f32[256,1152]{1,0:T(8,128)}, f32[256,1152]{1,0:T(8,128)}, u32[]{:S(2)}, u32[]{:S(2)}) collective-permute-start(f32[256,1152]{1,0:T(8,128)} %fusion.11), channel_id=1, source_target_pairs={{0,1},{1,0},{2,3},{3,2},{4,5},{5,4},{6,7},{7,6},{8,9},{9,8},{10,11... | collective-permute-start | bytes 3538952 | tf_op jit(solution)/shard_map/ppermute | solution.py:69
  95.3 2.4 %copy-start.1 = (bf16[4,4,136,1152]{3,2,1,0:T(8,128)(2,1)S(1)}, bf16[4,4,136,1152]{3,2,1,0:T(8,128)(2,1)}, u32[]{:S(2)}) copy-start(bf16[4,4,136,1152]{3,2,1,0:T(8,128)(2,1)} %copy-done) | copy-start | bytes 15040516
  102.0 3.6 %copy-start.2 = (bf16[8,2,16,1152]{3,2,1,0:T(8,128)(2,1)S(1)}, bf16[8,2,16,1152]{3,2,1,0:T(8,128)(2,1)}, u32[]{:S(2)}) copy-start(bf16[8,2,16,1152]{3,2,1,0:T(8,128)(2,1)} %pad_maximum_fusion.2) | copy-start | bytes 1769476
  108.1 46.6 %all-to-all-start.3 = ((bf16[16,72,1152]{2,1,0:T(8,128)(2,1)}), bf16[16,72,1152]{2,1,0:T(8,128)(2,1)}, u32[]{:S(2)}, u32[]{:S(2)}) async-start(bf16[16,72,1152]{2,1,0:T(8,128)(2,1)} %bitcast.36), calls=%async_computation.3 | async-start | bytes 5308416 | tf_op jit(solution)/shard_map/all_to_all | solution.py:73
  113.4 10.3 %collective-permute-start.5 = (bf16[64,1152]{1,0:T(8,128)(2,1)}, bf16[64,1152]{1,0:T(8,128)(2,1)S(1)}, u32[]{:S(2)}, u32[]{:S(2)}) collective-permute-start(bf16[64,1152]{1,0:T(8,128)(2,1)} %get-tuple-element.38), channel_id=1, source_target_pairs={{0,64},{1,65},{2,66},{3,67},{4,68},{5,69},{6,70},{7,71},{8,72},{9,... | collective-permute-start | bytes 442376 | tf_op jit(solution)/shard_map/ppermute | solution.py:69
  116.9 15.5 %collective-permute-start.6 = (bf16[64,1152]{1,0:T(8,128)(2,1)}, bf16[64,1152]{1,0:T(8,128)(2,1)}, u32[]{:S(2)}, u32[]{:S(2)}) collective-permute-start(bf16[64,1152]{1,0:T(8,128)(2,1)} %get-tuple-element.40), channel_id=1, source_target_pairs={{0,128},{1,129},{2,130},{3,131},{4,132},{5,133},{6,134},{7,135},{8... | collective-permute-start | bytes 442376 | tf_op jit(solution)/shard_map/ppermute | solution.py:69
  121.8 10.6 %collective-permute-start.7 = (bf16[64,1152]{1,0:T(8,128)(2,1)S(1)}, bf16[64,1152]{1,0:T(8,128)(2,1)}, u32[]{:S(2)}, u32[]{:S(2)}) collective-permute-start(bf16[64,1152]{1,0:T(8,128)(2,1)S(1)} %get-tuple-element.39), channel_id=1, source_target_pairs={{0,192},{1,193},{2,194},{3,195},{4,196},{5,197},{6,198},{7,199},{8... | collective-permute-start | bytes 442376 | tf_op jit(solution)/shard_map/ppermute | solution.py:69
  133.5 30.0 %collective-permute-start.10 = (bf16[1152,1152]{1,0:T(8,128)(2,1)S(1)}, bf16[1152,1152]{1,0:T(8,128)(2,1)}, u32[]{:S(2)}, u32[]{:S(2)}) collective-permute-start(bf16[1152,1152]{1,0:T(8,128)(2,1)S(1)} %bitcast.35), channel_id=1, source_target_pairs={{0,1},{1,0},{2,3},{3,2},{4,5},{5,4},{6,7},{7,6},{8,9},{9,8},{10,11... | collective-permute-start | bytes 7962632 | tf_op jit(solution)/shard_map/ppermute | solution.py:69
  136.6 24.9 %collective-permute-start.8 = (bf16[64,1152]{1,0:T(8,128)(2,1)S(1)}, bf16[64,1152]{1,0:T(8,128)(2,1)S(1)}, u32[]{:S(2)}, u32[]{:S(2)}) collective-permute-start(bf16[64,1152]{1,0:T(8,128)(2,1)S(1)} %add_convert_fusion.1), channel_id=1, source_target_pairs={{0,256},{1,257},{2,258},{3,259},{4,260},{5,261},{6,262},{7,263},{8... | collective-permute-start | bytes 442376 | tf_op jit(solution)/shard_map/ppermute | solution.py:69
  156.9 6.5 %collective-permute-start.9 = (bf16[36,1152]{1,0:T(8,128)(2,1)S(1)}, bf16[36,1152]{1,0:T(8,128)(2,1)S(1)}, u32[]{:S(2)}, u32[]{:S(2)}) collective-permute-start(bf16[36,1152]{1,0:T(8,128)(2,1)S(1)} %select_convert_fusion), channel_id=1, source_target_pairs={{0,456},{1,457},{2,458},{3,459},{4,460},{5,461},{6,462},{7,463},{8... | collective-permute-start | bytes 248840 | tf_op jit(solution)/shard_map/ppermute | solution.py:69
  163.5 22.6 %collective-permute-start.15 = (bf16[36,1152]{1,0:T(8,128)(2,1)S(1)}, bf16[36,1152]{1,0:T(8,128)(2,1)S(1)}, u32[]{:S(2)}, u32[]{:S(2)}) collective-permute-start(bf16[36,1152]{1,0:T(8,128)(2,1)S(1)} %add_convert_fusion.3), channel_id=1, source_target_pairs={{0,256},{1,257},{2,258},{3,259},{4,260},{5,261},{6,262},{7,263},{8... | collective-permute-start | bytes 248840 | tf_op jit(solution)/shard_map/ppermute | solution.py:69
  176.8 13.5 %collective-permute-start.11 = (bf16[64,1152]{1,0:T(8,128)(2,1)S(1)}, bf16[64,1152]{1,0:T(8,128)(2,1)S(1)}, u32[]{:S(2)}, u32[]{:S(2)}) collective-permute-start(bf16[64,1152]{1,0:T(8,128)(2,1)S(1)} %add_convert_fusion), channel_id=1, source_target_pairs={{0,192},{1,193},{2,194},{3,195},{4,196},{5,197},{6,198},{7,199},{8... | collective-permute-start | bytes 442376 | tf_op jit(solution)/shard_map/ppermute | solution.py:69
  178.7 16.7 %collective-permute-start.12 = (bf16[64,1152]{1,0:T(8,128)(2,1)S(1)}, bf16[64,1152]{1,0:T(8,128)(2,1)S(1)}, u32[]{:S(2)}, u32[]{:S(2)}) collective-permute-start(bf16[64,1152]{1,0:T(8,128)(2,1)S(1)} %add_convert_fusion), channel_id=1, source_target_pairs={{0,64},{1,65},{2,66},{3,67},{4,68},{5,69},{6,70},{7,71},{8,72},{9,... | collective-permute-start | bytes 442376 | tf_op jit(solution)/shard_map/ppermute | solution.py:69
  180.6 14.8 %collective-permute-start.13 = (bf16[64,1152]{1,0:T(8,128)(2,1)S(1)}, bf16[64,1152]{1,0:T(8,128)(2,1)S(1)}, u32[]{:S(2)}, u32[]{:S(2)}) collective-permute-start(bf16[64,1152]{1,0:T(8,128)(2,1)S(1)} %add_convert_fusion), channel_id=1, source_target_pairs={{0,128},{1,129},{2,130},{3,131},{4,132},{5,133},{6,134},{7,135},{8... | collective-permute-start | bytes 442376 | tf_op jit(solution)/shard_map/ppermute | solution.py:69
  186.1 18.1 %collective-permute-start.16 = (bf16[36,1152]{1,0:T(8,128)(2,1)S(1)}, bf16[36,1152]{1,0:T(8,128)(2,1)S(1)}, u32[]{:S(2)}, u32[]{:S(2)}) collective-permute-start(bf16[36,1152]{1,0:T(8,128)(2,1)S(1)} %add_convert_fusion.2), channel_id=1, source_target_pairs={{0,64},{1,65},{2,66},{3,67},{4,68},{5,69},{6,70},{7,71},{8,72},{9,... | collective-permute-start | bytes 248840 | tf_op jit(solution)/shard_map/ppermute | solution.py:69
  188.0 16.2 %collective-permute-start.17 = (bf16[36,1152]{1,0:T(8,128)(2,1)S(1)}, bf16[36,1152]{1,0:T(8,128)(2,1)S(1)}, u32[]{:S(2)}, u32[]{:S(2)}) collective-permute-start(bf16[36,1152]{1,0:T(8,128)(2,1)S(1)} %add_convert_fusion.2), channel_id=1, source_target_pairs={{0,128},{1,129},{2,130},{3,131},{4,132},{5,133},{6,134},{7,135},{8... | collective-permute-start | bytes 248840 | tf_op jit(solution)/shard_map/ppermute | solution.py:69
  190.2 14.0 %collective-permute-start.18 = (bf16[36,1152]{1,0:T(8,128)(2,1)S(1)}, bf16[36,1152]{1,0:T(8,128)(2,1)S(1)}, u32[]{:S(2)}, u32[]{:S(2)}) collective-permute-start(bf16[36,1152]{1,0:T(8,128)(2,1)S(1)} %add_convert_fusion.2), channel_id=1, source_target_pairs={{0,192},{1,193},{2,194},{3,195},{4,196},{5,197},{6,198},{7,199},{8... | collective-permute-start | bytes 248840 | tf_op jit(solution)/shard_map/ppermute | solution.py:69
  198.4 9.9 %collective-permute-start.14 = (f32[128,1152]{1,0:T(8,128)S(1)}, f32[128,1152]{1,0:T(8,128)S(1)}, u32[]{:S(2)}, u32[]{:S(2)}) collective-permute-start(f32[128,1152]{1,0:T(8,128)S(1)} %bitcast.44), channel_id=1, source_target_pairs={{0,1},{1,0},{2,3},{3,2},{4,5},{5,4},{6,7},{7,6},{8,9},{9,8},{10,11... | collective-permute-start | bytes 1769480 | tf_op jit(solution)/shard_map/ppermute | solution.py:69
  204.3 3.2 %collective-permute-start.19 = (f32[18,1152]{1,0:T(8,128)S(1)}, f32[18,1152]{1,0:T(8,128)S(1)}, u32[]{:S(2)}, u32[]{:S(2)}) collective-permute-start(f32[18,1152]{1,0:T(8,128)S(1)} %slice_select_fusion.1), channel_id=1, source_target_pairs={{0,1},{1,0},{2,3},{3,2},{4,5},{5,4},{6,7},{7,6},{8,9},{9,8},{10,11... | collective-permute-start | bytes 248840 | tf_op jit(solution)/shard_map/ppermute | solution.py:69

commit v13 on v12

--- a/solution.py
+++ b/solution.py
@@ -56,12 +56,6 @@
 
 
 INNER, OUTER = crossed("x"), crossed("y")
-PLANE = [
-    [place(blk, y, zh, x, core) for y in range(N_Y) for x in range(N_X)]
-    for blk in range(N_BLK)
-    for zh in range(N_ZH)
-    for core in range(N_CORE)
-]
 
 
 def permuted(value, target):
@@ -251,18 +245,20 @@
 
     both = gathered(both, OUTER)
     proj = both[:, :, N_ZH * picked :]
-    proj = jnp.where(first, proj, proj.transpose(1, 0, 2, 3)).reshape(-1, width)
+    flipped = proj.transpose(1, 0, 2, 3).reshape(-1, width)
+    proj = proj.reshape(-1, width)
     embed = proj.shape[0]
 
-    made = permuted(contract_last(sib_rows, proj), sibling)
+    made = permuted(contract_last(sib_rows, flipped), sibling)
     others = embedded(both.reshape(N_Y * N_X, -1, width), N_ZH * picked, proj)
     spot = jnp.where(first, y * N_X + x, x * N_Y + y) * (N_ZH * picked)
     at = jnp.stack([sub * picked, spot]).astype(jnp.int32)
     part = partial_grads(at, jnp.stack([scale, shift_by, weight]), made, others, picked)
 
     terms = contract_first(part, feat).astype(bf16)
-    part, terms, late_proj = lax.optimization_barrier((part, terms, proj))
-    terms = exchanged(terms.reshape(N_Y * N_X, embed // (N_Y * N_X), width), PLANE)
+    part, terms, late_proj = lax.optimization_barrier((part, terms, flipped))
+    terms = exchanged(terms.reshape(4, embed // 4, width), OUTER)
+    terms = jnp.sum(terms.astype(f32), 0).astype(bf16)
     quarter = own // 4
     at_quarter = sub // 2
 
@@ -275,7 +271,8 @@
         permuted(quarter_of(at_quarter ^ 1), along(2)),
         permuted(quarter_of(at_quarter ^ 3), along(3)),
     ).astype(bf16)
-    held, late_proj = lax.optimization_barrier((held, late_proj))
+    held, terms, late_proj = lax.optimization_barrier((held, terms, late_proj))
+    terms = exchanged(terms.reshape(4, embed // 16, width), INNER)
     held = held.astype(f32) + permuted(held, along(4)).astype(f32)
     terms = jnp.sum(terms.astype(f32), 0)
     lower, upper = terms[:pair], terms[pair:]

time: 210 us -> 209 us (level)
  waiting for transfers between devices: 38.8 us -> 32.2 us
  starting transfers between devices: 100 us -> 104 us
    all_to_all x3 -> x4, waiting for transfers between devices: 20.7 us -> 10.5 us  [exchanged(): lax.all_to_all(value, BOTH, 0, 0, axis_index_groups=groups, tiled=True)]
    ppermute x20, waiting for transfers between devices: 18.1 us -> 21.7 us  [permuted(): return lax.ppermute(value, BOTH, pairs)]
    all_to_all x3 -> x4, starting transfers between devices: 12.1 us -> 14.8 us  [exchanged(): lax.all_to_all(value, BOTH, 0, 0, axis_index_groups=groups, tiled=True)]
    unnamed x10 -> x13, local copies, waits for them, and re-layouts: 4.72 us -> 6.21 us
  transfers between devices with their start and end apart: 23 -> 24, of which waited for: 7 -> 7; matrix products, arithmetic and copies ran while one was open for 5% -> 4% of each run, Pallas kernels for 2% -> 2%
where the time goes in v13:
time: 209 us; the launch traced here: 207 us
  starting transfers between devices  104 us (50%)
  blocking collectives  34.8 us (17%)
  waiting for transfers between devices  32.2 us (15%)
  local copies, waits for them, and re-layouts  9.56 us (5%)
  other arithmetic  8.06 us (4%)
  Pallas kernels  7.82 us (4%)
  matrix products  7.39 us (4%)
  between operations  3.27 us (2%)
    ppermute x20, starting transfers between devices, permuted(): return lax.ppermute(value, BOTH, pairs)  89.5 us
    all_to_all x1, blocking collectives, exchanged(): lax.all_to_all(value, BOTH, 0, 0, axis_index_groups=groups, tiled=True)  34.8 us
    ppermute x20, waiting for transfers between devices, permuted(): return lax.ppermute(value, BOTH, pairs)  21.7 us
    all_to_all x4, starting transfers between devices, exchanged(): lax.all_to_all(value, BOTH, 0, 0, axis_index_groups=groups, tiled=True)  14.8 us
    all_to_all x4, waiting for transfers between devices, exchanged(): lax.all_to_all(value, BOTH, 0, 0, axis_index_groups=groups, tiled=True)  10.5 us
    unnamed x13, local copies, waits for them, and re-layouts  6.21 us
    pallas_call x1, Pallas kernels, embedded(): pl.pallas_call(embed_kernel, grid=(count // group,), in_specs=[pl.BlockSp...  4.28 us
  transfers between devices with their start and end apart: 24, of which 7 were waited for; matrix products, arithmetic and copies ran while one was open for 4% of the time, Pallas kernels for 2%

profile of v13, /device:TPU:1, one launch (start us, length us, event | category | flops | bytes accessed | tf_op | source)
XLA Modules:
  0.0 207.4 jit_solution(2919687644551265351)
XLA Ops:
  2.7 8.8 %collective-permute-start = (bf16[34,1152]{1,0:T(8,128)(2,1)S(1)}, bf16[34,1152]{1,0:T(8,128)(2,1)S(1)}, u32[]{:S(2)}, u32[]{:S(2)}) collective-permute-start(bf16[34,1152]{1,0:T(8,128)(2,1)S(1)} %pad_maximum_fusion.6), channel_id=1, source_target_pairs={{0,1},{1,0},{2,3},{3,2},{4,5},{5,4},{6,7},{7,6},{8,9},{9,8},{10,11... | collective-permute-start | bytes 235016 | tf_op jit(solution)/shard_map/ppermute | solution.py:63
  11.5 5.6 %collective-permute-start.2 = (bf16[34,1152]{1,0:T(8,128)(2,1)S(1)}, bf16[34,1152]{1,0:T(8,128)(2,1)S(1)}, u32[]{:S(2)}, u32[]{:S(2)}) collective-permute-start(bf16[34,1152]{1,0:T(8,128)(2,1)S(1)} %pad_maximum_fusion.6), channel_id=1, source_target_pairs={{0,457},{1,456},{2,459},{3,458},{4,461},{5,460},{6,463},{7,462},{8... | collective-permute-start | bytes 235016 | tf_op jit(solution)/shard_map/ppermute | solution.py:63
  17.2 2.4 %collective-permute-start.3 = (bf16[256,1152]{1,0:T(8,128)(2,1)S(1)}, bf16[256,1152]{1,0:T(8,128)(2,1)S(1)}, u32[]{:S(2)}, u32[]{:S(2)}) collective-permute-start(bf16[256,1152]{1,0:T(8,128)(2,1)S(1)} %pad_maximum_fusion.1), channel_id=1, source_target_pairs={{0,1},{1,0},{2,3},{3,2},{4,5},{5,4},{6,7},{7,6},{8,9},{9,8},{10,11... | collective-permute-start | bytes 1769480 | tf_op jit(solution)/shard_map/ppermute | solution.py:63
  22.6 4.2 %all-to-all-start = ((bf16[4,68,1152]{2,1,0:T(8,128)(2,1)}), bf16[4,68,1152]{2,1,0:T(8,128)(2,1)S(1)}, u32[]{:S(2)}, u32[]{:S(2)}) async-start(bf16[4,68,1152]{2,1,0:T(8,128)(2,1)} %broadcast_in_dim.6), calls=%async_computation | async-start | bytes 1327104 | tf_op jit(solution)/shard_map/all_to_all | solution.py:67
  26.8 6.2 %collective-permute-done.1 = bf16[34,1152]{1,0:T(8,128)(2,1)S(1)} collective-permute-done((bf16[34,1152]{1,0:T(8,128)(2,1)S(1)}, bf16[34,1152]{1,0:T(8,128)(2,1)S(1)}, u32[]{:S(2)}, u32[]{:S(2)}) %collective-permute-start.1) | collective-permute-done | bytes 78368 | tf_op jit(solution)/shard_map/ppermute | solution.py:63
  35.7 3.5 %all-to-all-start.1 = ((bf16[4,68,1152]{2,1,0:T(8,128)(2,1)}), bf16[4,68,1152]{2,1,0:T(8,128)(2,1)S(1)}, u32[]{:S(2)}, u32[]{:S(2)}) async-start(bf16[4,68,1152]{2,1,0:T(8,128)(2,1)} %broadcast_in_dim.7), calls=%async_computation.1 | async-start | bytes 1327104 | tf_op jit(solution)/shard_map/all_to_all | solution.py:67
  40.2 6.6 %all-to-all-done.1 = bf16[4,68,1152]{2,1,0:T(8,128)(2,1)S(1)} async-done(((bf16[4,68,1152]{2,1,0:T(8,128)(2,1)}), bf16[4,68,1152]{2,1,0:T(8,128)(2,1)S(1)}, u32[]{:S(2)}, u32[]{:S(2)}) %all-to-all-start.1) | async-done | bytes 626720 | tf_op jit(solution)/shard_map/all_to_all | solution.py:67
  47.4 34.8 %all_to_all.25 = bf16[4,4,136,1152]{3,2,1,0:T(8,128)(2,1)S(1)} all-to-all(bf16[4,4,136,1152]{3,2,1,0:T(8,128)(2,1)S(1)} %broadcast_in_dim.8), channel_id=1, replica_groups={{0,16,32,48},{2,18,34,50},{4,20,36,52},{6,22,38,54},{1,3,5,7},{17,19,21..., dimensions={0} | all-to-all | bytes 10027008 | tf_op jit(solution)/shard_map/all_to_all | solution.py:67
  82.5 2.1 %copy-done = bf16[4,4,136,1152]{3,2,1,0:T(8,128)(2,1)} copy-done((bf16[4,4,136,1152]{3,2,1,0:T(8,128)(2,1)}, bf16[4,4,136,1152]{3,2,1,0:T(8,128)(2,1)S(1)}, u32[]{:S(2)}) %copy-start) | copy-done | bytes 5013528
  86.3 2.1 %fusion.11 = f32[256,1152]{1,0:T(8,128)} fusion(bf16[256,1152]{1,0:T(8,128)(2,1)S(1)} %bitcast.53, bf16[1152,1152]{1,0:T(8,128)(2,1)S(1)} %bitcast.46), kind=kOutput, calls=%fused_computation.58 | convolution fusion | flops 679477248 | bytes 4423680 | tf_op jit(solution)/shard_map/dot_general | solution.py:82
  88.4 6.0 %collective-permute-start.4 = (f32[256,1152]{1,0:T(8,128)}, f32[256,1152]{1,0:T(8,128)}, u32[]{:S(2)}, u32[]{:S(2)}) collective-permute-start(f32[256,1152]{1,0:T(8,128)} %fusion.11), channel_id=1, source_target_pairs={{0,1},{1,0},{2,3},{3,2},{4,5},{5,4},{6,7},{7,6},{8,9},{9,8},{10,11... | collective-permute-start | bytes 3538952 | tf_op jit(solution)/shard_map/ppermute | solution.py:63
  96.6 2.4 %copy-done.1 = bf16[4,4,136,1152]{3,2,1,0:T(8,128)(2,1)S(1)} copy-done((bf16[4,4,136,1152]{3,2,1,0:T(8,128)(2,1)S(1)}, bf16[4,4,136,1152]{3,2,1,0:T(8,128)(2,1)}, u32[]{:S(2)}) %copy-start.1) | copy-done | bytes 5013528
  99.0 4.3 %shard_map.102.others_ref = bf16[1024,1152]{1,0:T(8,128)(2,1)S(1)} custom-call(bf16[16,136,1152]{2,1,0:T(8,128)(2,1)S(1)} %bitcast.42, bf16[1152,1152]{1,0:T(8,128)(2,1)S(1)} %bitcast.43), custom_call_target="tpu_custom_call" | custom-call | flops 2717908992 | bytes 7372800 | tf_op jit(solution)/shard_map/pallas_call | solution.py:104
  103.3 3.5 %shard_map.103 = bf16[256,1152]{1,0:T(8,128)(2,1)S(1)} custom-call(s32[2]{0:T(128)S(1)} %pad_add_fusion.at_ref, f32[3]{0:T(128)S(1)} %pad_maximum_fusion.8.par_ref, f32[256,1152]{1,0:T(8,128)} %collective-permute-done.4.made_ref, bf16[1024,1152]{1,0:T(8,128)(2,1)S(1)} %shard_map.102.others_ref), custom_call_target="tpu_custom_call" | custom-call | flops 1207959552 | bytes 4128768 | tf_op jit(solution)/shard_map/pallas_call | solution.py:158
  106.8 2.5 %convolution_convert_fusion = bf16[1152,1152]{1,0:T(8,128)(2,1)} fusion(bf16[256,1152]{1,0:T(8,128)(2,1)S(1)} %shard_map.103, bf16[256,1152]{1,0:T(8,128)(2,1)S(1)} %bitcast.49), kind=kOutput, calls=%fused_computation | convolution fusion | flops 680804352 | bytes 3833856 | tf_op jit(solution)/shard_map/dot_general | solution.py:88
  109.3 3.7 %all-to-all-start.3 = ((bf16[4,288,1152]{2,1,0:T(8,128)(2,1)}), bf16[4,288,1152]{2,1,0:T(8,128)(2,1)S(1)}, u32[]{:S(2)}, u32[]{:S(2)}) async-start(bf16[4,288,1152]{2,1,0:T(8,128)(2,1)} %bitcast.18), calls=%async_computation.3 | async-start | bytes 5308416 | tf_op jit(solution)/shard_map/all_to_all | solution.py:67
  113.8 3.5 %collective-permute-start.5 = (bf16[64,1152]{1,0:T(8,128)(2,1)}, bf16[64,1152]{1,0:T(8,128)(2,1)S(1)}, u32[]{:S(2)}, u32[]{:S(2)}) collective-permute-start(bf16[64,1152]{1,0:T(8,128)(2,1)} %get-tuple-element.40), channel_id=1, source_target_pairs={{0,64},{1,65},{2,66},{3,67},{4,68},{5,69},{6,70},{7,71},{8,72},{9,... | collective-permute-start | bytes 442376 | tf_op jit(solution)/shard_map/ppermute | solution.py:63
  117.3 4.9 %collective-permute-start.6 = (bf16[64,1152]{1,0:T(8,128)(2,1)}, bf16[64,1152]{1,0:T(8,128)(2,1)}, u32[]{:S(2)}, u32[]{:S(2)}) collective-permute-start(bf16[64,1152]{1,0:T(8,128)(2,1)} %get-tuple-element.42), channel_id=1, source_target_pairs={{0,128},{1,129},{2,130},{3,131},{4,132},{5,133},{6,134},{7,135},{8... | collective-permute-start | bytes 442376 | tf_op jit(solution)/shard_map/ppermute | solution.py:63
  122.2 1.9 collective-permute-start.7
  124.1 8.7 %collective-permute-done.6 = bf16[64,1152]{1,0:T(8,128)(2,1)} collective-permute-done((bf16[64,1152]{1,0:T(8,128)(2,1)}, bf16[64,1152]{1,0:T(8,128)(2,1)}, u32[]{:S(2)}, u32[]{:S(2)}) %collective-permute-start.6) | collective-permute-done | bytes 147488 | tf_op jit(solution)/shard_map/ppermute | solution.py:63
  135.3 3.1 %collective-permute-start.10 = (bf16[1152,1152]{1,0:T(8,128)(2,1)}, bf16[1152,1152]{1,0:T(8,128)(2,1)}, u32[]{:S(2)}, u32[]{:S(2)}) collective-permute-start(bf16[1152,1152]{1,0:T(8,128)(2,1)} %bitcast.47), channel_id=1, source_target_pairs={{0,1},{1,0},{2,3},{3,2},{4,5},{5,4},{6,7},{7,6},{8,9},{9,8},{10,11... | collective-permute-start | bytes 7962632 | tf_op jit(solution)/shard_map/ppermute | solution.py:63
  138.4 3.5 %all-to-all-start.4 = ((bf16[4,72,1152]{2,1,0:T(8,128)(2,1)}), bf16[4,72,1152]{2,1,0:T(8,128)(2,1)S(1)}, u32[]{:S(2)}, u32[]{:S(2)}) async-start(bf16[4,72,1152]{2,1,0:T(8,128)(2,1)} %bitcast.48), calls=%async_computation.4 | async-start | bytes 1327104 | tf_op jit(solution)/shard_map/all_to_all | solution.py:67
  141.9 5.8 %collective-permute-start.8 = (bf16[64,1152]{1,0:T(8,128)(2,1)S(1)}, bf16[64,1152]{1,0:T(8,128)(2,1)S(1)}, u32[]{:S(2)}, u32[]{:S(2)}) collective-permute-start(bf16[64,1152]{1,0:T(8,128)(2,1)S(1)} %add_convert_fusion.1), channel_id=1, source_target_pairs={{0,256},{1,257},{2,258},{3,259},{4,260},{5,261},{6,262},{7,263},{8... | collective-permute-start | bytes 442376 | tf_op jit(solution)/shard_map/ppermute | solution.py:63
  147.7 2.1 %all-to-all-done.4 = bf16[4,72,1152]{2,1,0:T(8,128)(2,1)S(1)} async-done(((bf16[4,72,1152]{2,1,0:T(8,128)(2,1)}), bf16[4,72,1152]{2,1,0:T(8,128)(2,1)S(1)}, u32[]{:S(2)}, u32[]{:S(2)}) %all-to-all-start.4) | async-done | bytes 663584 | tf_op jit(solution)/shard_map/all_to_all | solution.py:67
  149.9 7.2 %collective-permute-start.9 = (bf16[36,1152]{1,0:T(8,128)(2,1)S(1)}, bf16[36,1152]{1,0:T(8,128)(2,1)S(1)}, u32[]{:S(2)}, u32[]{:S(2)}) collective-permute-start(bf16[36,1152]{1,0:T(8,128)(2,1)S(1)} %select_convert_fusion), channel_id=1, source_target_pairs={{0,456},{1,457},{2,458},{3,459},{4,460},{5,461},{6,462},{7,463},{8... | collective-permute-start | bytes 248840 | tf_op jit(solution)/shard_map/ppermute | solution.py:63
  157.1 5.5 %collective-permute-done.8 = bf16[64,1152]{1,0:T(8,128)(2,1)S(1)} collective-permute-done((bf16[64,1152]{1,0:T(8,128)(2,1)S(1)}, bf16[64,1152]{1,0:T(8,128)(2,1)S(1)}, u32[]{:S(2)}, u32[]{:S(2)}) %collective-permute-start.8) | collective-permute-done | bytes 147488 | tf_op jit(solution)/shard_map/ppermute | solution.py:63
  162.7 13.2 %collective-permute-start.15 = (bf16[36,1152]{1,0:T(8,128)(2,1)S(1)}, bf16[36,1152]{1,0:T(8,128)(2,1)S(1)}, u32[]{:S(2)}, u32[]{:S(2)}) collective-permute-start(bf16[36,1152]{1,0:T(8,128)(2,1)S(1)} %add_convert_fusion.3), channel_id=1, source_target_pairs={{0,256},{1,257},{2,258},{3,259},{4,260},{5,261},{6,262},{7,263},{8... | collective-permute-start | bytes 248840 | tf_op jit(solution)/shard_map/ppermute | solution.py:63
  179.8 5.4 %collective-permute-start.13 = (bf16[64,1152]{1,0:T(8,128)(2,1)S(1)}, bf16[64,1152]{1,0:T(8,128)(2,1)S(1)}, u32[]{:S(2)}, u32[]{:S(2)}) collective-permute-start(bf16[64,1152]{1,0:T(8,128)(2,1)S(1)} %add_convert_fusion), channel_id=1, source_target_pairs={{0,128},{1,129},{2,130},{3,131},{4,132},{5,133},{6,134},{7,135},{8... | collective-permute-start | bytes 442376 | tf_op jit(solution)/shard_map/ppermute | solution.py:63
  187.2 2.2 %collective-permute-start.17 = (bf16[36,1152]{1,0:T(8,128)(2,1)S(1)}, bf16[36,1152]{1,0:T(8,128)(2,1)S(1)}, u32[]{:S(2)}, u32[]{:S(2)}) collective-permute-start(bf16[36,1152]{1,0:T(8,128)(2,1)S(1)} %add_convert_fusion.2), channel_id=1, source_target_pairs={{0,128},{1,129},{2,130},{3,131},{4,132},{5,133},{6,134},{7,135},{8... | collective-permute-start | bytes 248840 | tf_op jit(solution)/shard_map/ppermute | solution.py:63
  189.4 5.2 %collective-permute-start.18 = (bf16[36,1152]{1,0:T(8,128)(2,1)S(1)}, bf16[36,1152]{1,0:T(8,128)(2,1)S(1)}, u32[]{:S(2)}, u32[]{:S(2)}) collective-permute-start(bf16[36,1152]{1,0:T(8,128)(2,1)S(1)} %add_convert_fusion.2), channel_id=1, source_target_pairs={{0,192},{1,193},{2,194},{3,195},{4,196},{5,197},{6,198},{7,199},{8... | collective-permute-start | bytes 248840 | tf_op jit(solution)/shard_map/ppermute | solution.py:63
  194.7 2.8 %fusion = f32[256,1152]{1,0:T(8,128)S(1)} fusion(bf16[1152,1152]{1,0:T(8,128)(2,1)} %collective-permute-done.10, bf16[64,1152]{1,0:T(8,128)(2,1)S(1)} %get-tuple-element.39, bf16[64,1152]{1,0:T(8,128)(2,1)S(1)} %get-tuple-element.38, bf16[64,1152]{1,0:T(8,128)(2,1)S(1)} %get-tuple-element.37, bf16[64,1152]{1,0:T(8,128)(2,1)S(1)} %get-tuple-element.36), kind=kOutput, calls=%fused_computation.6 | convolution fusion | flops 681836544 | bytes 4423680 | tf_op jit(solution)/shard_map/dot_general | solution.py:298
  197.6 4.7 %collective-permute-start.14 = (f32[128,1152]{1,0:T(8,128)S(1)}, f32[128,1152]{1,0:T(8,128)S(1)}, u32[]{:S(2)}, u32[]{:S(2)}) collective-permute-start(f32[128,1152]{1,0:T(8,128)S(1)} %bitcast.54), channel_id=1, source_target_pairs={{0,1},{1,0},{2,3},{3,2},{4,5},{5,4},{6,7},{7,6},{8,9},{9,8},{10,11... | collective-permute-start | bytes 1769480 | tf_op jit(solution)/shard_map/ppermute | solution.py:63
  (77 shorter events, 25.8 us)
Async XLA Ops:
  0.6 19.0 %copy-start.4 = (bf16[1152,18]{0,1:T(8,128)(2,1)S(1)}, bf16[1152,18]{0,1:T(8,128)(2,1)}, u32[]{:S(2)}) copy-start(bf16[1152,18]{0,1:T(8,128)(2,1)} %param.10) | copy-start | bytes 124420
  0.6 19.0 %copy-start.5 = (bf16[1152,18]{0,1:T(8,128)(2,1)S(1)}, bf16[1152,18]{0,1:T(8,128)(2,1)}, u32[]{:S(2)}) copy-start(bf16[1152,18]{0,1:T(8,128)(2,1)} %param.9) | copy-start | bytes 124420
  2.7 16.9 %collective-permute-start = (bf16[34,1152]{1,0:T(8,128)(2,1)S(1)}, bf16[34,1152]{1,0:T(8,128)(2,1)S(1)}, u32[]{:S(2)}, u32[]{:S(2)}) collective-permute-start(bf16[34,1152]{1,0:T(8,128)(2,1)S(1)} %pad_maximum_fusion.6), channel_id=1, source_target_pairs={{0,1},{1,0},{2,3},{3,2},{4,5},{5,4},{6,7},{7,6},{8,9},{9,8},{10,11... | collective-permute-start | bytes 235016 | tf_op jit(solution)/shard_map/ppermute | solution.py:63
  11.5 15.3 %collective-permute-start.2 = (bf16[34,1152]{1,0:T(8,128)(2,1)S(1)}, bf16[34,1152]{1,0:T(8,128)(2,1)S(1)}, u32[]{:S(2)}, u32[]{:S(2)}) collective-permute-start(bf16[34,1152]{1,0:T(8,128)(2,1)S(1)} %pad_maximum_fusion.6), channel_id=1, source_target_pairs={{0,457},{1,456},{2,459},{3,458},{4,461},{5,460},{6,463},{7,462},{8... | collective-permute-start | bytes 235016 | tf_op jit(solution)/shard_map/ppermute | solution.py:63
  17.2 22.0 %collective-permute-start.3 = (bf16[256,1152]{1,0:T(8,128)(2,1)S(1)}, bf16[256,1152]{1,0:T(8,128)(2,1)S(1)}, u32[]{:S(2)}, u32[]{:S(2)}) collective-permute-start(bf16[256,1152]{1,0:T(8,128)(2,1)S(1)} %pad_maximum_fusion.1), channel_id=1, source_target_pairs={{0,1},{1,0},{2,3},{3,2},{4,5},{5,4},{6,7},{7,6},{8,9},{9,8},{10,11... | collective-permute-start | bytes 1769480 | tf_op jit(solution)/shard_map/ppermute | solution.py:63
  19.7 13.3 %collective-permute-start.1 = (bf16[34,1152]{1,0:T(8,128)(2,1)S(1)}, bf16[34,1152]{1,0:T(8,128)(2,1)S(1)}, u32[]{:S(2)}, u32[]{:S(2)}) collective-permute-start(bf16[34,1152]{1,0:T(8,128)(2,1)S(1)} %pad_maximum_fusion.7), channel_id=1, source_target_pairs={{0,456},{1,457},{2,458},{3,459},{4,460},{5,461},{6,462},{7,463},{8... | collective-permute-start | bytes 235016 | tf_op jit(solution)/shard_map/ppermute | solution.py:63
  22.6 12.2 %all-to-all-start = ((bf16[4,68,1152]{2,1,0:T(8,128)(2,1)}), bf16[4,68,1152]{2,1,0:T(8,128)(2,1)S(1)}, u32[]{:S(2)}, u32[]{:S(2)}) async-start(bf16[4,68,1152]{2,1,0:T(8,128)(2,1)} %broadcast_in_dim.6), calls=%async_computation | async-start | bytes 1327104 | tf_op jit(solution)/shard_map/all_to_all | solution.py:67
  35.7 11.1 %all-to-all-start.1 = ((bf16[4,68,1152]{2,1,0:T(8,128)(2,1)}), bf16[4,68,1152]{2,1,0:T(8,128)(2,1)S(1)}, u32[]{:S(2)}, u32[]{:S(2)}) async-start(bf16[4,68,1152]{2,1,0:T(8,128)(2,1)} %broadcast_in_dim.7), calls=%async_computation.1 | async-start | bytes 1327104 | tf_op jit(solution)/shard_map/all_to_all | solution.py:67
  82.3 2.3 %copy-start = (bf16[4,4,136,1152]{3,2,1,0:T(8,128)(2,1)}, bf16[4,4,136,1152]{3,2,1,0:T(8,128)(2,1)S(1)}, u32[]{:S(2)}) copy-start(bf16[4,4,136,1152]{3,2,1,0:T(8,128)(2,1)S(1)} %all_to_all.25) | copy-start | bytes 15040516
  84.5 1.7 copy-start.3
  84.8 1.5 copy-start.2
  88.4 14.9 %collective-permute-start.4 = (f32[256,1152]{1,0:T(8,128)}, f32[256,1152]{1,0:T(8,128)}, u32[]{:S(2)}, u32[]{:S(2)}) collective-permute-start(f32[256,1152]{1,0:T(8,128)} %fusion.11), channel_id=1, source_target_pairs={{0,1},{1,0},{2,3},{3,2},{4,5},{5,4},{6,7},{7,6},{8,9},{9,8},{10,11... | collective-permute-start | bytes 3538952 | tf_op jit(solution)/shard_map/ppermute | solution.py:63
  96.6 2.4 %copy-start.1 = (bf16[4,4,136,1152]{3,2,1,0:T(8,128)(2,1)S(1)}, bf16[4,4,136,1152]{3,2,1,0:T(8,128)(2,1)}, u32[]{:S(2)}) copy-start(bf16[4,4,136,1152]{3,2,1,0:T(8,128)(2,1)} %copy-done) | copy-start | bytes 15040516
  109.3 24.6 %all-to-all-start.3 = ((bf16[4,288,1152]{2,1,0:T(8,128)(2,1)}), bf16[4,288,1152]{2,1,0:T(8,128)(2,1)S(1)}, u32[]{:S(2)}, u32[]{:S(2)}) async-start(bf16[4,288,1152]{2,1,0:T(8,128)(2,1)} %bitcast.18), calls=%async_computation.3 | async-start | bytes 5308416 | tf_op jit(solution)/shard_map/all_to_all | solution.py:67
  113.8 10.3 %collective-permute-start.5 = (bf16[64,1152]{1,0:T(8,128)(2,1)}, bf16[64,1152]{1,0:T(8,128)(2,1)S(1)}, u32[]{:S(2)}, u32[]{:S(2)}) collective-permute-start(bf16[64,1152]{1,0:T(8,128)(2,1)} %get-tuple-element.40), channel_id=1, source_target_pairs={{0,64},{1,65},{2,66},{3,67},{4,68},{5,69},{6,70},{7,71},{8,72},{9,... | collective-permute-start | bytes 442376 | tf_op jit(solution)/shard_map/ppermute | solution.py:63
  117.3 15.5 %collective-permute-start.6 = (bf16[64,1152]{1,0:T(8,128)(2,1)}, bf16[64,1152]{1,0:T(8,128)(2,1)}, u32[]{:S(2)}, u32[]{:S(2)}) collective-permute-start(bf16[64,1152]{1,0:T(8,128)(2,1)} %get-tuple-element.42), channel_id=1, source_target_pairs={{0,128},{1,129},{2,130},{3,131},{4,132},{5,133},{6,134},{7,135},{8... | collective-permute-start | bytes 442376 | tf_op jit(solution)/shard_map/ppermute | solution.py:63
  122.2 10.6 %collective-permute-start.7 = (bf16[64,1152]{1,0:T(8,128)(2,1)S(1)}, bf16[64,1152]{1,0:T(8,128)(2,1)}, u32[]{:S(2)}, u32[]{:S(2)}) collective-permute-start(bf16[64,1152]{1,0:T(8,128)(2,1)S(1)} %get-tuple-element.41), channel_id=1, source_target_pairs={{0,192},{1,193},{2,194},{3,195},{4,196},{5,197},{6,198},{7,199},{8... | collective-permute-start | bytes 442376 | tf_op jit(solution)/shard_map/ppermute | solution.py:63
  135.3 27.4 %collective-permute-start.10 = (bf16[1152,1152]{1,0:T(8,128)(2,1)}, bf16[1152,1152]{1,0:T(8,128)(2,1)}, u32[]{:S(2)}, u32[]{:S(2)}) collective-permute-start(bf16[1152,1152]{1,0:T(8,128)(2,1)} %bitcast.47), channel_id=1, source_target_pairs={{0,1},{1,0},{2,3},{3,2},{4,5},{5,4},{6,7},{7,6},{8,9},{9,8},{10,11... | collective-permute-start | bytes 7962632 | tf_op jit(solution)/shard_map/ppermute | solution.py:63
  138.4 11.4 %all-to-all-start.4 = ((bf16[4,72,1152]{2,1,0:T(8,128)(2,1)}), bf16[4,72,1152]{2,1,0:T(8,128)(2,1)S(1)}, u32[]{:S(2)}, u32[]{:S(2)}) async-start(bf16[4,72,1152]{2,1,0:T(8,128)(2,1)} %bitcast.48), calls=%async_computation.4 | async-start | bytes 1327104 | tf_op jit(solution)/shard_map/all_to_all | solution.py:67
  141.9 20.7 %collective-permute-start.8 = (bf16[64,1152]{1,0:T(8,128)(2,1)S(1)}, bf16[64,1152]{1,0:T(8,128)(2,1)S(1)}, u32[]{:S(2)}, u32[]{:S(2)}) collective-permute-start(bf16[64,1152]{1,0:T(8,128)(2,1)S(1)} %add_convert_fusion.1), channel_id=1, source_target_pairs={{0,256},{1,257},{2,258},{3,259},{4,260},{5,261},{6,262},{7,263},{8... | collective-permute-start | bytes 442376 | tf_op jit(solution)/shard_map/ppermute | solution.py:63
  149.9 12.7 %collective-permute-start.9 = (bf16[36,1152]{1,0:T(8,128)(2,1)S(1)}, bf16[36,1152]{1,0:T(8,128)(2,1)S(1)}, u32[]{:S(2)}, u32[]{:S(2)}) collective-permute-start(bf16[36,1152]{1,0:T(8,128)(2,1)S(1)} %select_convert_fusion), channel_id=1, source_target_pairs={{0,456},{1,457},{2,458},{3,459},{4,460},{5,461},{6,462},{7,463},{8... | collective-permute-start | bytes 248840 | tf_op jit(solution)/shard_map/ppermute | solution.py:63
  162.7 22.5 %collective-permute-start.15 = (bf16[36,1152]{1,0:T(8,128)(2,1)S(1)}, bf16[36,1152]{1,0:T(8,128)(2,1)S(1)}, u32[]{:S(2)}, u32[]{:S(2)}) collective-permute-start(bf16[36,1152]{1,0:T(8,128)(2,1)S(1)} %add_convert_fusion.3), channel_id=1, source_target_pairs={{0,256},{1,257},{2,258},{3,259},{4,260},{5,261},{6,262},{7,263},{8... | collective-permute-start | bytes 248840 | tf_op jit(solution)/shard_map/ppermute | solution.py:63
  175.9 13.5 %collective-permute-start.11 = (bf16[64,1152]{1,0:T(8,128)(2,1)S(1)}, bf16[64,1152]{1,0:T(8,128)(2,1)S(1)}, u32[]{:S(2)}, u32[]{:S(2)}) collective-permute-start(bf16[64,1152]{1,0:T(8,128)(2,1)S(1)} %add_convert_fusion), channel_id=1, source_target_pairs={{0,192},{1,193},{2,194},{3,195},{4,196},{5,197},{6,198},{7,199},{8... | collective-permute-start | bytes 442376 | tf_op jit(solution)/shard_map/ppermute | solution.py:63
  177.9 16.7 %collective-permute-start.12 = (bf16[64,1152]{1,0:T(8,128)(2,1)S(1)}, bf16[64,1152]{1,0:T(8,128)(2,1)S(1)}, u32[]{:S(2)}, u32[]{:S(2)}) collective-permute-start(bf16[64,1152]{1,0:T(8,128)(2,1)S(1)} %add_convert_fusion), channel_id=1, source_target_pairs={{0,64},{1,65},{2,66},{3,67},{4,68},{5,69},{6,70},{7,71},{8,72},{9,... | collective-permute-start | bytes 442376 | tf_op jit(solution)/shard_map/ppermute | solution.py:63
  179.8 14.8 %collective-permute-start.13 = (bf16[64,1152]{1,0:T(8,128)(2,1)S(1)}, bf16[64,1152]{1,0:T(8,128)(2,1)S(1)}, u32[]{:S(2)}, u32[]{:S(2)}) collective-permute-start(bf16[64,1152]{1,0:T(8,128)(2,1)S(1)} %add_convert_fusion), channel_id=1, source_target_pairs={{0,128},{1,129},{2,130},{3,131},{4,132},{5,133},{6,134},{7,135},{8... | collective-permute-start | bytes 442376 | tf_op jit(solution)/shard_map/ppermute | solution.py:63
  185.3 17.0 %collective-permute-start.16 = (bf16[36,1152]{1,0:T(8,128)(2,1)S(1)}, bf16[36,1152]{1,0:T(8,128)(2,1)S(1)}, u32[]{:S(2)}, u32[]{:S(2)}) collective-permute-start(bf16[36,1152]{1,0:T(8,128)(2,1)S(1)} %add_convert_fusion.2), channel_id=1, source_target_pairs={{0,64},{1,65},{2,66},{3,67},{4,68},{5,69},{6,70},{7,71},{8,72},{9,... | collective-permute-start | bytes 248840 | tf_op jit(solution)/shard_map/ppermute | solution.py:63
  187.2 15.1 %collective-permute-start.17 = (bf16[36,1152]{1,0:T(8,128)(2,1)S(1)}, bf16[36,1152]{1,0:T(8,128)(2,1)S(1)}, u32[]{:S(2)}, u32[]{:S(2)}) collective-permute-start(bf16[36,1152]{1,0:T(8,128)(2,1)S(1)} %add_convert_fusion.2), channel_id=1, source_target_pairs={{0,128},{1,129},{2,130},{3,131},{4,132},{5,133},{6,134},{7,135},{8... | collective-permute-start | bytes 248840 | tf_op jit(solution)/shard_map/ppermute | solution.py:63
  189.4 12.9 %collective-permute-start.18 = (bf16[36,1152]{1,0:T(8,128)(2,1)S(1)}, bf16[36,1152]{1,0:T(8,128)(2,1)S(1)}, u32[]{:S(2)}, u32[]{:S(2)}) collective-permute-start(bf16[36,1152]{1,0:T(8,128)(2,1)S(1)} %add_convert_fusion.2), channel_id=1, source_target_pairs={{0,192},{1,193},{2,194},{3,195},{4,196},{5,197},{6,198},{7,199},{8... | collective-permute-start | bytes 248840 | tf_op jit(solution)/shard_map/ppermute | solution.py:63
  197.6 8.8 %collective-permute-start.14 = (f32[128,1152]{1,0:T(8,128)S(1)}, f32[128,1152]{1,0:T(8,128)S(1)}, u32[]{:S(2)}, u32[]{:S(2)}) collective-permute-start(f32[128,1152]{1,0:T(8,128)S(1)} %bitcast.54), channel_id=1, source_target_pairs={{0,1},{1,0},{2,3},{3,2},{4,5},{5,4},{6,7},{7,6},{8,9},{9,8},{10,11... | collective-permute-start | bytes 1769480 | tf_op jit(solution)/shard_map/ppermute | solution.py:63
  202.4 3.2 %collective-permute-start.19 = (f32[18,1152]{1,0:T(8,128)S(1)}, f32[18,1152]{1,0:T(8,128)S(1)}, u32[]{:S(2)}, u32[]{:S(2)}) collective-permute-start(f32[18,1152]{1,0:T(8,128)S(1)} %slice_select_fusion.1), channel_id=1, source_target_pairs={{0,1},{1,0},{2,3},{3,2},{4,5},{5,4},{6,7},{7,6},{8,9},{9,8},{10,11... | collective-permute-start | bytes 248840 | tf_op jit(solution)/shard_map/ppermute | solution.py:63

commit v14 on v13

--- a/solution.py
+++ b/solution.py
@@ -250,7 +250,8 @@
     embed = proj.shape[0]
 
     made = permuted(contract_last(sib_rows, flipped), sibling)
-    others = embedded(both.reshape(N_Y * N_X, -1, width), N_ZH * picked, proj)
+    others = both[:, :, : N_ZH * picked].reshape(N_Y * N_X, -1, width)
+    others = embedded(others, N_ZH * picked, proj)
     spot = jnp.where(first, y * N_X + x, x * N_Y + y) * (N_ZH * picked)
     at = jnp.stack([sub * picked, spot]).astype(jnp.int32)
     part = partial_grads(at, jnp.stack([scale, shift_by, weight]), made, others, picked)

time: 209 us -> 208 us (level)
    unnamed x13 -> x11, local copies, waits for them, and re-layouts: 6.21 us -> 3.76 us
  transfers between devices with their start and end apart: 24 -> 24, of which waited for: 7 -> 7; matrix products, arithmetic and copies ran while one was open for 4% -> 5% of each run, Pallas kernels for 2% -> 2%
where the time goes in v14:
time: 208 us; the launch traced here: 207 us
  starting transfers between devices  104 us (50%)
  blocking collectives  34.8 us (17%)
  waiting for transfers between devices  32.2 us (15%)
  local copies, waits for them, and re-layouts  9.02 us (4%)
  other arithmetic  8.07 us (4%)
  Pallas kernels  7.56 us (4%)
  matrix products  7.37 us (4%)
  between operations  3.28 us (2%)
    ppermute x20, starting transfers between devices, permuted(): return lax.ppermute(value, BOTH, pairs)  89.5 us
    all_to_all x1, blocking collectives, exchanged(): lax.all_to_all(value, BOTH, 0, 0, axis_index_groups=groups, tiled=True)  34.8 us
    ppermute x20, waiting for transfers between devices, permuted(): return lax.ppermute(value, BOTH, pairs)  21.7 us
    all_to_all x4, starting transfers between devices, exchanged(): lax.all_to_all(value, BOTH, 0, 0, axis_index_groups=groups, tiled=True)  14.8 us
    all_to_all x4, waiting for transfers between devices, exchanged(): lax.all_to_all(value, BOTH, 0, 0, axis_index_groups=groups, tiled=True)  10.5 us
  transfers between devices with their start and end apart: 24, of which 7 were waited for; matrix products, arithmetic and copies ran while one was open for 5% of the time, Pallas kernels for 2%

profile of v14, /device:TPU:1, one launch (start us, length us, event | category | flops | bytes accessed | tf_op | source)
XLA Modules:
  0.0 206.6 jit_solution(12743717692822390340)
XLA Ops:
  2.7 8.8 %collective-permute-start = (bf16[34,1152]{1,0:T(8,128)(2,1)S(1)}, bf16[34,1152]{1,0:T(8,128)(2,1)S(1)}, u32[]{:S(2)}, u32[]{:S(2)}) collective-permute-start(bf16[34,1152]{1,0:T(8,128)(2,1)S(1)} %pad_maximum_fusion.6), channel_id=1, source_target_pairs={{0,1},{1,0},{2,3},{3,2},{4,5},{5,4},{6,7},{7,6},{8,9},{9,8},{10,11... | collective-permute-start | bytes 235016 | tf_op jit(solution)/shard_map/ppermute | solution.py:63
  11.5 5.6 %collective-permute-start.2 = (bf16[34,1152]{1,0:T(8,128)(2,1)S(1)}, bf16[34,1152]{1,0:T(8,128)(2,1)S(1)}, u32[]{:S(2)}, u32[]{:S(2)}) collective-permute-start(bf16[34,1152]{1,0:T(8,128)(2,1)S(1)} %pad_maximum_fusion.6), channel_id=1, source_target_pairs={{0,457},{1,456},{2,459},{3,458},{4,461},{5,460},{6,463},{7,462},{8... | collective-permute-start | bytes 235016 | tf_op jit(solution)/shard_map/ppermute | solution.py:63
  17.2 2.4 %collective-permute-start.3 = (bf16[256,1152]{1,0:T(8,128)(2,1)S(1)}, bf16[256,1152]{1,0:T(8,128)(2,1)S(1)}, u32[]{:S(2)}, u32[]{:S(2)}) collective-permute-start(bf16[256,1152]{1,0:T(8,128)(2,1)S(1)} %pad_maximum_fusion.1), channel_id=1, source_target_pairs={{0,1},{1,0},{2,3},{3,2},{4,5},{5,4},{6,7},{7,6},{8,9},{9,8},{10,11... | collective-permute-start | bytes 1769480 | tf_op jit(solution)/shard_map/ppermute | solution.py:63
  19.7 1.9 collective-permute-start.1
  22.6 4.2 %all-to-all-start = ((bf16[4,68,1152]{2,1,0:T(8,128)(2,1)}), bf16[4,68,1152]{2,1,0:T(8,128)(2,1)S(1)}, u32[]{:S(2)}, u32[]{:S(2)}) async-start(bf16[4,68,1152]{2,1,0:T(8,128)(2,1)} %broadcast_in_dim.6), calls=%async_computation | async-start | bytes 1327104 | tf_op jit(solution)/shard_map/all_to_all | solution.py:67
  26.8 6.2 %collective-permute-done.1 = bf16[34,1152]{1,0:T(8,128)(2,1)S(1)} collective-permute-done((bf16[34,1152]{1,0:T(8,128)(2,1)S(1)}, bf16[34,1152]{1,0:T(8,128)(2,1)S(1)}, u32[]{:S(2)}, u32[]{:S(2)}) %collective-permute-start.1) | collective-permute-done | bytes 78368 | tf_op jit(solution)/shard_map/ppermute | solution.py:63
  35.7 3.5 %all-to-all-start.1 = ((bf16[4,68,1152]{2,1,0:T(8,128)(2,1)}), bf16[4,68,1152]{2,1,0:T(8,128)(2,1)S(1)}, u32[]{:S(2)}, u32[]{:S(2)}) async-start(bf16[4,68,1152]{2,1,0:T(8,128)(2,1)} %broadcast_in_dim.7), calls=%async_computation.1 | async-start | bytes 1327104 | tf_op jit(solution)/shard_map/all_to_all | solution.py:67
  40.2 6.6 %all-to-all-done.1 = bf16[4,68,1152]{2,1,0:T(8,128)(2,1)S(1)} async-done(((bf16[4,68,1152]{2,1,0:T(8,128)(2,1)}), bf16[4,68,1152]{2,1,0:T(8,128)(2,1)S(1)}, u32[]{:S(2)}, u32[]{:S(2)}) %all-to-all-start.1) | async-done | bytes 626720 | tf_op jit(solution)/shard_map/all_to_all | solution.py:67
  47.4 34.8 %all_to_all.25 = bf16[4,4,136,1152]{3,2,1,0:T(8,128)(2,1)S(1)} all-to-all(bf16[4,4,136,1152]{3,2,1,0:T(8,128)(2,1)S(1)} %broadcast_in_dim.8), channel_id=1, replica_groups={{0,16,32,48},{2,18,34,50},{4,20,36,52},{6,22,38,54},{1,3,5,7},{17,19,21..., dimensions={0} | all-to-all | bytes 10027008 | tf_op jit(solution)/shard_map/all_to_all | solution.py:67
  82.5 2.0 copy-done
  86.2 2.1 %fusion.11 = f32[256,1152]{1,0:T(8,128)} fusion(bf16[256,1152]{1,0:T(8,128)(2,1)S(1)} %bitcast.53, bf16[1152,1152]{1,0:T(8,128)(2,1)S(1)} %bitcast.46), kind=kOutput, calls=%fused_computation.58 | convolution fusion | flops 679477248 | bytes 4423680 | tf_op jit(solution)/shard_map/dot_general | solution.py:82
  88.4 6.0 %collective-permute-start.4 = (f32[256,1152]{1,0:T(8,128)}, f32[256,1152]{1,0:T(8,128)}, u32[]{:S(2)}, u32[]{:S(2)}) collective-permute-start(f32[256,1152]{1,0:T(8,128)} %fusion.11), channel_id=1, source_target_pairs={{0,1},{1,0},{2,3},{3,2},{4,5},{5,4},{6,7},{7,6},{8,9},{9,8},{10,11... | collective-permute-start | bytes 3538952 | tf_op jit(solution)/shard_map/ppermute | solution.py:63
  98.4 4.1 %shard_map.102.others_ref = bf16[1024,1152]{1,0:T(8,128)(2,1)S(1)} custom-call(bf16[16,64,1152]{2,1,0:T(8,128)(2,1)S(1)} %bitcast.43, bf16[1152,1152]{1,0:T(8,128)(2,1)S(1)} %bitcast.42), custom_call_target="tpu_custom_call" | custom-call | flops 2717908992 | bytes 7372800 | tf_op jit(solution)/shard_map/pallas_call | solution.py:104
  102.5 3.4 %shard_map.103 = bf16[256,1152]{1,0:T(8,128)(2,1)S(1)} custom-call(s32[2]{0:T(128)S(1)} %pad_add_fusion.at_ref, f32[3]{0:T(128)S(1)} %pad_maximum_fusion.8.par_ref, f32[256,1152]{1,0:T(8,128)} %collective-permute-done.4.made_ref, bf16[1024,1152]{1,0:T(8,128)(2,1)S(1)} %shard_map.102.others_ref), custom_call_target="tpu_custom_call" | custom-call | flops 1207959552 | bytes 4128768 | tf_op jit(solution)/shard_map/pallas_call | solution.py:158
  106.0 2.5 %convolution_convert_fusion = bf16[1152,1152]{1,0:T(8,128)(2,1)} fusion(bf16[256,1152]{1,0:T(8,128)(2,1)S(1)} %shard_map.103, bf16[256,1152]{1,0:T(8,128)(2,1)S(1)} %bitcast.49), kind=kOutput, calls=%fused_computation | convolution fusion | flops 680804352 | bytes 3833856 | tf_op jit(solution)/shard_map/dot_general | solution.py:88
  108.5 3.7 %all-to-all-start.3 = ((bf16[4,288,1152]{2,1,0:T(8,128)(2,1)}), bf16[4,288,1152]{2,1,0:T(8,128)(2,1)S(1)}, u32[]{:S(2)}, u32[]{:S(2)}) async-start(bf16[4,288,1152]{2,1,0:T(8,128)(2,1)} %bitcast.18), calls=%async_computation.3 | async-start | bytes 5308416 | tf_op jit(solution)/shard_map/all_to_all | solution.py:67
  112.9 3.5 %collective-permute-start.5 = (bf16[64,1152]{1,0:T(8,128)(2,1)}, bf16[64,1152]{1,0:T(8,128)(2,1)S(1)}, u32[]{:S(2)}, u32[]{:S(2)}) collective-permute-start(bf16[64,1152]{1,0:T(8,128)(2,1)} %get-tuple-element.40), channel_id=1, source_target_pairs={{0,64},{1,65},{2,66},{3,67},{4,68},{5,69},{6,70},{7,71},{8,72},{9,... | collective-permute-start | bytes 442376 | tf_op jit(solution)/shard_map/ppermute | solution.py:63
  116.5 4.9 %collective-permute-start.6 = (bf16[64,1152]{1,0:T(8,128)(2,1)}, bf16[64,1152]{1,0:T(8,128)(2,1)}, u32[]{:S(2)}, u32[]{:S(2)}) collective-permute-start(bf16[64,1152]{1,0:T(8,128)(2,1)} %get-tuple-element.42), channel_id=1, source_target_pairs={{0,128},{1,129},{2,130},{3,131},{4,132},{5,133},{6,134},{7,135},{8... | collective-permute-start | bytes 442376 | tf_op jit(solution)/shard_map/ppermute | solution.py:63
  121.4 1.9 collective-permute-start.7
  123.3 8.7 %collective-permute-done.6 = bf16[64,1152]{1,0:T(8,128)(2,1)} collective-permute-done((bf16[64,1152]{1,0:T(8,128)(2,1)}, bf16[64,1152]{1,0:T(8,128)(2,1)}, u32[]{:S(2)}, u32[]{:S(2)}) %collective-permute-start.6) | collective-permute-done | bytes 147488 | tf_op jit(solution)/shard_map/ppermute | solution.py:63
  134.5 3.1 %collective-permute-start.10 = (bf16[1152,1152]{1,0:T(8,128)(2,1)}, bf16[1152,1152]{1,0:T(8,128)(2,1)}, u32[]{:S(2)}, u32[]{:S(2)}) collective-permute-start(bf16[1152,1152]{1,0:T(8,128)(2,1)} %bitcast.47), channel_id=1, source_target_pairs={{0,1},{1,0},{2,3},{3,2},{4,5},{5,4},{6,7},{7,6},{8,9},{9,8},{10,11... | collective-permute-start | bytes 7962632 | tf_op jit(solution)/shard_map/ppermute | solution.py:63
  137.6 3.5 %all-to-all-start.4 = ((bf16[4,72,1152]{2,1,0:T(8,128)(2,1)}), bf16[4,72,1152]{2,1,0:T(8,128)(2,1)S(1)}, u32[]{:S(2)}, u32[]{:S(2)}) async-start(bf16[4,72,1152]{2,1,0:T(8,128)(2,1)} %bitcast.48), calls=%async_computation.4 | async-start | bytes 1327104 | tf_op jit(solution)/shard_map/all_to_all | solution.py:67
  141.1 5.8 %collective-permute-start.8 = (bf16[64,1152]{1,0:T(8,128)(2,1)S(1)}, bf16[64,1152]{1,0:T(8,128)(2,1)S(1)}, u32[]{:S(2)}, u32[]{:S(2)}) collective-permute-start(bf16[64,1152]{1,0:T(8,128)(2,1)S(1)} %add_convert_fusion.1), channel_id=1, source_target_pairs={{0,256},{1,257},{2,258},{3,259},{4,260},{5,261},{6,262},{7,263},{8... | collective-permute-start | bytes 442376 | tf_op jit(solution)/shard_map/ppermute | solution.py:63
  146.9 2.1 %all-to-all-done.4 = bf16[4,72,1152]{2,1,0:T(8,128)(2,1)S(1)} async-done(((bf16[4,72,1152]{2,1,0:T(8,128)(2,1)}), bf16[4,72,1152]{2,1,0:T(8,128)(2,1)S(1)}, u32[]{:S(2)}, u32[]{:S(2)}) %all-to-all-start.4) | async-done | bytes 663584 | tf_op jit(solution)/shard_map/all_to_all | solution.py:67
  149.1 7.2 %collective-permute-start.9 = (bf16[36,1152]{1,0:T(8,128)(2,1)S(1)}, bf16[36,1152]{1,0:T(8,128)(2,1)S(1)}, u32[]{:S(2)}, u32[]{:S(2)}) collective-permute-start(bf16[36,1152]{1,0:T(8,128)(2,1)S(1)} %select_convert_fusion), channel_id=1, source_target_pairs={{0,456},{1,457},{2,458},{3,459},{4,460},{5,461},{6,462},{7,463},{8... | collective-permute-start | bytes 248840 | tf_op jit(solution)/shard_map/ppermute | solution.py:63
  156.3 5.5 %collective-permute-done.8 = bf16[64,1152]{1,0:T(8,128)(2,1)S(1)} collective-permute-done((bf16[64,1152]{1,0:T(8,128)(2,1)S(1)}, bf16[64,1152]{1,0:T(8,128)(2,1)S(1)}, u32[]{:S(2)}, u32[]{:S(2)}) %collective-permute-start.8) | collective-permute-done | bytes 147488 | tf_op jit(solution)/shard_map/ppermute | solution.py:63
  161.9 13.2 %collective-permute-start.15 = (bf16[36,1152]{1,0:T(8,128)(2,1)S(1)}, bf16[36,1152]{1,0:T(8,128)(2,1)S(1)}, u32[]{:S(2)}, u32[]{:S(2)}) collective-permute-start(bf16[36,1152]{1,0:T(8,128)(2,1)S(1)} %add_convert_fusion.3), channel_id=1, source_target_pairs={{0,256},{1,257},{2,258},{3,259},{4,260},{5,261},{6,262},{7,263},{8... | collective-permute-start | bytes 248840 | tf_op jit(solution)/shard_map/ppermute | solution.py:63
  179.0 5.4 %collective-permute-start.13 = (bf16[64,1152]{1,0:T(8,128)(2,1)S(1)}, bf16[64,1152]{1,0:T(8,128)(2,1)S(1)}, u32[]{:S(2)}, u32[]{:S(2)}) collective-permute-start(bf16[64,1152]{1,0:T(8,128)(2,1)S(1)} %add_convert_fusion), channel_id=1, source_target_pairs={{0,128},{1,129},{2,130},{3,131},{4,132},{5,133},{6,134},{7,135},{8... | collective-permute-start | bytes 442376 | tf_op jit(solution)/shard_map/ppermute | solution.py:63
  186.4 2.2 %collective-permute-start.17 = (bf16[36,1152]{1,0:T(8,128)(2,1)S(1)}, bf16[36,1152]{1,0:T(8,128)(2,1)S(1)}, u32[]{:S(2)}, u32[]{:S(2)}) collective-permute-start(bf16[36,1152]{1,0:T(8,128)(2,1)S(1)} %add_convert_fusion.2), channel_id=1, source_target_pairs={{0,128},{1,129},{2,130},{3,131},{4,132},{5,133},{6,134},{7,135},{8... | collective-permute-start | bytes 248840 | tf_op jit(solution)/shard_map/ppermute | solution.py:63
  188.7 5.2 %collective-permute-start.18 = (bf16[36,1152]{1,0:T(8,128)(2,1)S(1)}, bf16[36,1152]{1,0:T(8,128)(2,1)S(1)}, u32[]{:S(2)}, u32[]{:S(2)}) collective-permute-start(bf16[36,1152]{1,0:T(8,128)(2,1)S(1)} %add_convert_fusion.2), channel_id=1, source_target_pairs={{0,192},{1,193},{2,194},{3,195},{4,196},{5,197},{6,198},{7,199},{8... | collective-permute-start | bytes 248840 | tf_op jit(solution)/shard_map/ppermute | solution.py:63
  193.9 2.8 %fusion = f32[256,1152]{1,0:T(8,128)S(1)} fusion(bf16[1152,1152]{1,0:T(8,128)(2,1)} %collective-permute-done.10, bf16[64,1152]{1,0:T(8,128)(2,1)S(1)} %get-tuple-element.39, bf16[64,1152]{1,0:T(8,128)(2,1)S(1)} %get-tuple-element.38, bf16[64,1152]{1,0:T(8,128)(2,1)S(1)} %get-tuple-element.37, bf16[64,1152]{1,0:T(8,128)(2,1)S(1)} %get-tuple-element.36), kind=kOutput, calls=%fused_computation.6 | convolution fusion | flops 681836544 | bytes 4423680 | tf_op jit(solution)/shard_map/dot_general | solution.py:299
  196.8 4.7 %collective-permute-start.14 = (f32[128,1152]{1,0:T(8,128)S(1)}, f32[128,1152]{1,0:T(8,128)S(1)}, u32[]{:S(2)}, u32[]{:S(2)}) collective-permute-start(f32[128,1152]{1,0:T(8,128)S(1)} %bitcast.54), channel_id=1, source_target_pairs={{0,1},{1,0},{2,3},{3,2},{4,5},{5,4},{6,7},{7,6},{8,9},{9,8},{10,11... | collective-permute-start | bytes 1769480 | tf_op jit(solution)/shard_map/ppermute | solution.py:63
  (76 shorter events, 25.8 us)
Async XLA Ops:
  0.6 19.0 %copy-start.3 = (bf16[1152,18]{0,1:T(8,128)(2,1)S(1)}, bf16[1152,18]{0,1:T(8,128)(2,1)}, u32[]{:S(2)}) copy-start(bf16[1152,18]{0,1:T(8,128)(2,1)} %param.10) | copy-start | bytes 124420
  0.6 19.0 %copy-start.4 = (bf16[1152,18]{0,1:T(8,128)(2,1)S(1)}, bf16[1152,18]{0,1:T(8,128)(2,1)}, u32[]{:S(2)}) copy-start(bf16[1152,18]{0,1:T(8,128)(2,1)} %param.9) | copy-start | bytes 124420
  2.7 16.9 %collective-permute-start = (bf16[34,1152]{1,0:T(8,128)(2,1)S(1)}, bf16[34,1152]{1,0:T(8,128)(2,1)S(1)}, u32[]{:S(2)}, u32[]{:S(2)}) collective-permute-start(bf16[34,1152]{1,0:T(8,128)(2,1)S(1)} %pad_maximum_fusion.6), channel_id=1, source_target_pairs={{0,1},{1,0},{2,3},{3,2},{4,5},{5,4},{6,7},{7,6},{8,9},{9,8},{10,11... | collective-permute-start | bytes 235016 | tf_op jit(solution)/shard_map/ppermute | solution.py:63
  11.5 15.3 %collective-permute-start.2 = (bf16[34,1152]{1,0:T(8,128)(2,1)S(1)}, bf16[34,1152]{1,0:T(8,128)(2,1)S(1)}, u32[]{:S(2)}, u32[]{:S(2)}) collective-permute-start(bf16[34,1152]{1,0:T(8,128)(2,1)S(1)} %pad_maximum_fusion.6), channel_id=1, source_target_pairs={{0,457},{1,456},{2,459},{3,458},{4,461},{5,460},{6,463},{7,462},{8... | collective-permute-start | bytes 235016 | tf_op jit(solution)/shard_map/ppermute | solution.py:63
  17.2 22.0 %collective-permute-start.3 = (bf16[256,1152]{1,0:T(8,128)(2,1)S(1)}, bf16[256,1152]{1,0:T(8,128)(2,1)S(1)}, u32[]{:S(2)}, u32[]{:S(2)}) collective-permute-start(bf16[256,1152]{1,0:T(8,128)(2,1)S(1)} %pad_maximum_fusion.1), channel_id=1, source_target_pairs={{0,1},{1,0},{2,3},{3,2},{4,5},{5,4},{6,7},{7,6},{8,9},{9,8},{10,11... | collective-permute-start | bytes 1769480 | tf_op jit(solution)/shard_map/ppermute | solution.py:63
  19.7 13.3 %collective-permute-start.1 = (bf16[34,1152]{1,0:T(8,128)(2,1)S(1)}, bf16[34,1152]{1,0:T(8,128)(2,1)S(1)}, u32[]{:S(2)}, u32[]{:S(2)}) collective-permute-start(bf16[34,1152]{1,0:T(8,128)(2,1)S(1)} %pad_maximum_fusion.7), channel_id=1, source_target_pairs={{0,456},{1,457},{2,458},{3,459},{4,460},{5,461},{6,462},{7,463},{8... | collective-permute-start | bytes 235016 | tf_op jit(solution)/shard_map/ppermute | solution.py:63
  22.6 12.2 %all-to-all-start = ((bf16[4,68,1152]{2,1,0:T(8,128)(2,1)}), bf16[4,68,1152]{2,1,0:T(8,128)(2,1)S(1)}, u32[]{:S(2)}, u32[]{:S(2)}) async-start(bf16[4,68,1152]{2,1,0:T(8,128)(2,1)} %broadcast_in_dim.6), calls=%async_computation | async-start | bytes 1327104 | tf_op jit(solution)/shard_map/all_to_all | solution.py:67
  35.7 11.1 %all-to-all-start.1 = ((bf16[4,68,1152]{2,1,0:T(8,128)(2,1)}), bf16[4,68,1152]{2,1,0:T(8,128)(2,1)S(1)}, u32[]{:S(2)}, u32[]{:S(2)}) async-start(bf16[4,68,1152]{2,1,0:T(8,128)(2,1)} %broadcast_in_dim.7), calls=%async_computation.1 | async-start | bytes 1327104 | tf_op jit(solution)/shard_map/all_to_all | solution.py:67
  82.3 2.3 %copy-start = (bf16[4,4,136,1152]{3,2,1,0:T(8,128)(2,1)}, bf16[4,4,136,1152]{3,2,1,0:T(8,128)(2,1)S(1)}, u32[]{:S(2)}) copy-start(bf16[4,4,136,1152]{3,2,1,0:T(8,128)(2,1)S(1)} %all_to_all.25) | copy-start | bytes 15040516
  84.5 1.7 copy-start.2
  84.7 1.5 copy-start.1
  88.4 14.2 %collective-permute-start.4 = (f32[256,1152]{1,0:T(8,128)}, f32[256,1152]{1,0:T(8,128)}, u32[]{:S(2)}, u32[]{:S(2)}) collective-permute-start(f32[256,1152]{1,0:T(8,128)} %fusion.11), channel_id=1, source_target_pairs={{0,1},{1,0},{2,3},{3,2},{4,5},{5,4},{6,7},{7,6},{8,9},{9,8},{10,11... | collective-permute-start | bytes 3538952 | tf_op jit(solution)/shard_map/ppermute | solution.py:63
  108.5 24.6 %all-to-all-start.3 = ((bf16[4,288,1152]{2,1,0:T(8,128)(2,1)}), bf16[4,288,1152]{2,1,0:T(8,128)(2,1)S(1)}, u32[]{:S(2)}, u32[]{:S(2)}) async-start(bf16[4,288,1152]{2,1,0:T(8,128)(2,1)} %bitcast.18), calls=%async_computation.3 | async-start | bytes 5308416 | tf_op jit(solution)/shard_map/all_to_all | solution.py:67
  112.9 10.4 %collective-permute-start.5 = (bf16[64,1152]{1,0:T(8,128)(2,1)}, bf16[64,1152]{1,0:T(8,128)(2,1)S(1)}, u32[]{:S(2)}, u32[]{:S(2)}) collective-permute-start(bf16[64,1152]{1,0:T(8,128)(2,1)} %get-tuple-element.40), channel_id=1, source_target_pairs={{0,64},{1,65},{2,66},{3,67},{4,68},{5,69},{6,70},{7,71},{8,72},{9,... | collective-permute-start | bytes 442376 | tf_op jit(solution)/shard_map/ppermute | solution.py:63
  116.5 15.5 %collective-permute-start.6 = (bf16[64,1152]{1,0:T(8,128)(2,1)}, bf16[64,1152]{1,0:T(8,128)(2,1)}, u32[]{:S(2)}, u32[]{:S(2)}) collective-permute-start(bf16[64,1152]{1,0:T(8,128)(2,1)} %get-tuple-element.42), channel_id=1, source_target_pairs={{0,128},{1,129},{2,130},{3,131},{4,132},{5,133},{6,134},{7,135},{8... | collective-permute-start | bytes 442376 | tf_op jit(solution)/shard_map/ppermute | solution.py:63
  121.4 10.6 %collective-permute-start.7 = (bf16[64,1152]{1,0:T(8,128)(2,1)S(1)}, bf16[64,1152]{1,0:T(8,128)(2,1)}, u32[]{:S(2)}, u32[]{:S(2)}) collective-permute-start(bf16[64,1152]{1,0:T(8,128)(2,1)S(1)} %get-tuple-element.41), channel_id=1, source_target_pairs={{0,192},{1,193},{2,194},{3,195},{4,196},{5,197},{6,198},{7,199},{8... | collective-permute-start | bytes 442376 | tf_op jit(solution)/shard_map/ppermute | solution.py:63
  134.5 27.4 %collective-permute-start.10 = (bf16[1152,1152]{1,0:T(8,128)(2,1)}, bf16[1152,1152]{1,0:T(8,128)(2,1)}, u32[]{:S(2)}, u32[]{:S(2)}) collective-permute-start(bf16[1152,1152]{1,0:T(8,128)(2,1)} %bitcast.47), channel_id=1, source_target_pairs={{0,1},{1,0},{2,3},{3,2},{4,5},{5,4},{6,7},{7,6},{8,9},{9,8},{10,11... | collective-permute-start | bytes 7962632 | tf_op jit(solution)/shard_map/ppermute | solution.py:63
  137.6 11.4 %all-to-all-start.4 = ((bf16[4,72,1152]{2,1,0:T(8,128)(2,1)}), bf16[4,72,1152]{2,1,0:T(8,128)(2,1)S(1)}, u32[]{:S(2)}, u32[]{:S(2)}) async-start(bf16[4,72,1152]{2,1,0:T(8,128)(2,1)} %bitcast.48), calls=%async_computation.4 | async-start | bytes 1327104 | tf_op jit(solution)/shard_map/all_to_all | solution.py:67
  141.1 20.7 %collective-permute-start.8 = (bf16[64,1152]{1,0:T(8,128)(2,1)S(1)}, bf16[64,1152]{1,0:T(8,128)(2,1)S(1)}, u32[]{:S(2)}, u32[]{:S(2)}) collective-permute-start(bf16[64,1152]{1,0:T(8,128)(2,1)S(1)} %add_convert_fusion.1), channel_id=1, source_target_pairs={{0,256},{1,257},{2,258},{3,259},{4,260},{5,261},{6,262},{7,263},{8... | collective-permute-start | bytes 442376 | tf_op jit(solution)/shard_map/ppermute | solution.py:63
  149.1 12.7 %collective-permute-start.9 = (bf16[36,1152]{1,0:T(8,128)(2,1)S(1)}, bf16[36,1152]{1,0:T(8,128)(2,1)S(1)}, u32[]{:S(2)}, u32[]{:S(2)}) collective-permute-start(bf16[36,1152]{1,0:T(8,128)(2,1)S(1)} %select_convert_fusion), channel_id=1, source_target_pairs={{0,456},{1,457},{2,458},{3,459},{4,460},{5,461},{6,462},{7,463},{8... | collective-permute-start | bytes 248840 | tf_op jit(solution)/shard_map/ppermute | solution.py:63
  161.9 22.5 %collective-permute-start.15 = (bf16[36,1152]{1,0:T(8,128)(2,1)S(1)}, bf16[36,1152]{1,0:T(8,128)(2,1)S(1)}, u32[]{:S(2)}, u32[]{:S(2)}) collective-permute-start(bf16[36,1152]{1,0:T(8,128)(2,1)S(1)} %add_convert_fusion.3), channel_id=1, source_target_pairs={{0,256},{1,257},{2,258},{3,259},{4,260},{5,261},{6,262},{7,263},{8... | collective-permute-start | bytes 248840 | tf_op jit(solution)/shard_map/ppermute | solution.py:63
  175.2 13.5 %collective-permute-start.11 = (bf16[64,1152]{1,0:T(8,128)(2,1)S(1)}, bf16[64,1152]{1,0:T(8,128)(2,1)S(1)}, u32[]{:S(2)}, u32[]{:S(2)}) collective-permute-start(bf16[64,1152]{1,0:T(8,128)(2,1)S(1)} %add_convert_fusion), channel_id=1, source_target_pairs={{0,192},{1,193},{2,194},{3,195},{4,196},{5,197},{6,198},{7,199},{8... | collective-permute-start | bytes 442376 | tf_op jit(solution)/shard_map/ppermute | solution.py:63
  177.1 16.7 %collective-permute-start.12 = (bf16[64,1152]{1,0:T(8,128)(2,1)S(1)}, bf16[64,1152]{1,0:T(8,128)(2,1)S(1)}, u32[]{:S(2)}, u32[]{:S(2)}) collective-permute-start(bf16[64,1152]{1,0:T(8,128)(2,1)S(1)} %add_convert_fusion), channel_id=1, source_target_pairs={{0,64},{1,65},{2,66},{3,67},{4,68},{5,69},{6,70},{7,71},{8,72},{9,... | collective-permute-start | bytes 442376 | tf_op jit(solution)/shard_map/ppermute | solution.py:63
  179.0 14.8 %collective-permute-start.13 = (bf16[64,1152]{1,0:T(8,128)(2,1)S(1)}, bf16[64,1152]{1,0:T(8,128)(2,1)S(1)}, u32[]{:S(2)}, u32[]{:S(2)}) collective-permute-start(bf16[64,1152]{1,0:T(8,128)(2,1)S(1)} %add_convert_fusion), channel_id=1, source_target_pairs={{0,128},{1,129},{2,130},{3,131},{4,132},{5,133},{6,134},{7,135},{8... | collective-permute-start | bytes 442376 | tf_op jit(solution)/shard_map/ppermute | solution.py:63
  184.5 17.0 %collective-permute-start.16 = (bf16[36,1152]{1,0:T(8,128)(2,1)S(1)}, bf16[36,1152]{1,0:T(8,128)(2,1)S(1)}, u32[]{:S(2)}, u32[]{:S(2)}) collective-permute-start(bf16[36,1152]{1,0:T(8,128)(2,1)S(1)} %add_convert_fusion.2), channel_id=1, source_target_pairs={{0,64},{1,65},{2,66},{3,67},{4,68},{5,69},{6,70},{7,71},{8,72},{9,... | collective-permute-start | bytes 248840 | tf_op jit(solution)/shard_map/ppermute | solution.py:63
  186.4 15.1 %collective-permute-start.17 = (bf16[36,1152]{1,0:T(8,128)(2,1)S(1)}, bf16[36,1152]{1,0:T(8,128)(2,1)S(1)}, u32[]{:S(2)}, u32[]{:S(2)}) collective-permute-start(bf16[36,1152]{1,0:T(8,128)(2,1)S(1)} %add_convert_fusion.2), channel_id=1, source_target_pairs={{0,128},{1,129},{2,130},{3,131},{4,132},{5,133},{6,134},{7,135},{8... | collective-permute-start | bytes 248840 | tf_op jit(solution)/shard_map/ppermute | solution.py:63
  188.7 12.9 %collective-permute-start.18 = (bf16[36,1152]{1,0:T(8,128)(2,1)S(1)}, bf16[36,1152]{1,0:T(8,128)(2,1)S(1)}, u32[]{:S(2)}, u32[]{:S(2)}) collective-permute-start(bf16[36,1152]{1,0:T(8,128)(2,1)S(1)} %add_convert_fusion.2), channel_id=1, source_target_pairs={{0,192},{1,193},{2,194},{3,195},{4,196},{5,197},{6,198},{7,199},{8... | collective-permute-start | bytes 248840 | tf_op jit(solution)/shard_map/ppermute | solution.py:63
  196.8 8.8 %collective-permute-start.14 = (f32[128,1152]{1,0:T(8,128)S(1)}, f32[128,1152]{1,0:T(8,128)S(1)}, u32[]{:S(2)}, u32[]{:S(2)}) collective-permute-start(f32[128,1152]{1,0:T(8,128)S(1)} %bitcast.54), channel_id=1, source_target_pairs={{0,1},{1,0},{2,3},{3,2},{4,5},{5,4},{6,7},{7,6},{8,9},{9,8},{10,11... | collective-permute-start | bytes 1769480 | tf_op jit(solution)/shard_map/ppermute | solution.py:63
  201.6 3.2 %collective-permute-start.19 = (f32[18,1152]{1,0:T(8,128)S(1)}, f32[18,1152]{1,0:T(8,128)S(1)}, u32[]{:S(2)}, u32[]{:S(2)}) collective-permute-start(f32[18,1152]{1,0:T(8,128)S(1)} %slice_select_fusion.1), channel_id=1, source_target_pairs={{0,1},{1,0},{2,3},{3,2},{4,5},{5,4},{6,7},{7,6},{8,9},{9,8},{10,11... | collective-permute-start | bytes 248840 | tf_op jit(solution)/shard_map/ppermute | solution.py:63
